TPU v7x, 32 devices: a whole 2x2x4 slice. The times are simulated.
32 devices in a mesh: dp: 8 (over z, y), ctx: 4 (over x, core).
Axes of the slice: x: 2, y: 2, z: 4, core: 2. Of those that a mesh axis runs over, the one named last changes fastest.
Arguments:
- tokens_in: bfloat16 [32, 1024, 768], P('dp', 'ctx'), may hold values from -6 to 6
- segments: int32 [32, 1024], P('dp', 'ctx'), may hold values from 0 to 3, as said below
- cotangent: bfloat16 [32, 1024, 768], P('dp', 'ctx'), may hold values from -6 to 6
- joint_weight: float32 [768, 2304], P(('dp', 'ctx')), may hold values from -0.21875 to 0.21875
- output_weight: float32 [768, 768], P(('dp', 'ctx')), may hold values from -1.75 to 1.75
- expand_weight: float32 [768, 3072], P(('dp', 'ctx')), may hold values from -0.21875 to 0.21875
- shrink_weight: float32 [3072, 768], P(('dp', 'ctx')), may hold values from -0.109375 to 0.109375
- momentum_joint: float32 [768, 2304], P(('dp', 'ctx')), may hold values from -97.75044 to 97.75044
- momentum_output: float32 [768, 768], P(('dp', 'ctx')), may hold values from -23.894552 to 23.894552
- momentum_expand: float32 [768, 3072], P(('dp', 'ctx')), may hold values from -30.41125 to 30.41125
- momentum_shrink: float32 [3072, 768], P(('dp', 'ctx')), may hold values from -72.40774 to 72.40774
- variance_joint: float32 [768, 2304], P(('dp', 'ctx')), may hold values from 19.6608 to 78.6432
- variance_output: float32 [768, 768], P(('dp', 'ctx')), may hold values from 1.31072 to 5.24288
- variance_expand: float32 [768, 3072], P(('dp', 'ctx')), may hold values from 1.96608 to 7.86432
- variance_shrink: float32 [3072, 768], P(('dp', 'ctx')), may hold values from 11.79648 to 47.18592
- small_params: float32 [12, 768], P(None, ('dp', 'ctx')), may hold values from -0.5 to 1.2, as said below
- momentum_small: float32 [12, 768], P(None, ('dp', 'ctx')), may hold values from -85.07909 to 85.07909
- variance_small: float32 [12, 768], P(None, ('dp', 'ctx')), may hold values from 16.384 to 65.536
Outputs:
- block_output: bfloat16 [32, 1024, 768], P('dp', 'ctx')
- input_grad: float32 [32, 1024, 768], P('dp', 'ctx')
- new_joint: float32 [768, 2304], P(('dp', 'ctx'))
- new_output: float32 [768, 768], P(('dp', 'ctx'))
- new_expand: float32 [768, 3072], P(('dp', 'ctx'))
- new_shrink: float32 [3072, 768], P(('dp', 'ctx'))
- first_joint: float32 [768, 2304], P(('dp', 'ctx'))
- first_output: float32 [768, 768], P(('dp', 'ctx'))
- first_expand: float32 [768, 3072], P(('dp', 'ctx'))
- first_shrink: float32 [3072, 768], P(('dp', 'ctx'))
- second_joint: float32 [768, 2304], P(('dp', 'ctx'))
- second_output: float32 [768, 768], P(('dp', 'ctx'))
- second_expand: float32 [768, 3072], P(('dp', 'ctx'))
- second_shrink: float32 [3072, 768], P(('dp', 'ctx'))
- new_small: float32 [12, 768], P(None, ('dp', 'ctx'))
- first_small: float32 [12, 768], P(None, ('dp', 'ctx'))
- second_small: float32 [12, 768], P(None, ('dp', 'ctx'))
Inputs may be any that keep to these rules, and one draw needn't show every extreme that they name: `segments`: along each sequence the numbers start at 0, never fall, and step up by one at exactly 3 places, so each sequence holds 4 documents. `small_params`: rows 0 and 5 (the gains) lie in 0.8 to 1.2, the other rows in -0.5 to 0.5.
All inputs are finite; a program needn't handle non-finite values.
Results may differ from a plain program's by a relative error of at most 0.009.
The roundings to bfloat16 on the way count: a program that leaves them out, or rounds other values in their place, can miss the bound.
Values may be sent and summed in bfloat16 or wider, within the bound.
No kernel may reach another device: no remote copies, remote signals or barrier semaphores. Data moves between devices by JAX's collectives and lax.ppermute only.
A program may use at most 192 MiB of HBM per device.

v0:
```python
import math

import jax
import jax.numpy as jnp
from jax import lax
from jax.sharding import PartitionSpec as P

HDIM = 64
STEP = 10


NORM_EPSILON = 1e-05
MASKED_SCORE = -1000000000.0
BETA_ONE = 0.9
BETA_TWO = 0.999
ADAM_EPSILON = 1e-08
RATE_MATRIX = 0.05
RATE_VECTOR = 0.3
WEIGHT_DECAY = 0.1


def norm_rows(values, gain, shift):
    centre = values - jnp.mean(values, axis=-1, keepdims=True)
    spread = jnp.mean(centre * centre, axis=-1, keepdims=True)
    return centre * lax.rsqrt(spread + NORM_EPSILON) * gain + shift


def allowed_pairs(query_seg, key_seg, query_start):
    query_pos = query_start + jnp.arange(query_seg.shape[0])
    key_pos = jnp.arange(key_seg.shape[0])
    return (key_pos[None, :] <= query_pos[:, None]) & (key_seg[None, :] == query_seg[:, None])


def adam_step(weight, gradient, first, second, rate, decay):
    first_new = BETA_ONE * first + (1.0 - BETA_ONE) * gradient
    second_new = BETA_TWO * second + (1.0 - BETA_TWO) * gradient * gradient
    first_hat = first_new / (1.0 - BETA_ONE**STEP)
    second_hat = second_new / (1.0 - BETA_TWO**STEP)
    updated = weight - rate * (first_hat / (jnp.sqrt(second_hat) + ADAM_EPSILON) + decay * weight)
    return (updated, first_new, second_new)


def per_device(
    tokens_in,
    segments,
    cotangent,
    joint_weight,
    output_weight,
    expand_weight,
    shrink_weight,
    momentum_joint,
    momentum_output,
    momentum_expand,
    momentum_shrink,
    variance_joint,
    variance_output,
    variance_expand,
    variance_shrink,
    small_params,
    momentum_small,
    variance_small,
):
    bf16 = jnp.bfloat16
    f32 = jnp.float32
    joint_cast = joint_weight.astype(bf16)
    output_cast = output_weight.astype(bf16)
    expand_cast = expand_weight.astype(bf16)
    shrink_cast = shrink_weight.astype(bf16)
    small_cast = small_params.astype(bf16)
    weights = (
        lax.all_gather(joint_cast, ("dp", "ctx"), axis=0, tiled=True),
        lax.all_gather(output_cast, ("dp", "ctx"), axis=0, tiled=True),
        lax.all_gather(expand_cast, ("dp", "ctx"), axis=0, tiled=True),
        lax.all_gather(shrink_cast, ("dp", "ctx"), axis=0, tiled=True),
        lax.all_gather(small_cast, ("dp", "ctx"), axis=1, tiled=True),
    )
    joint_lo, output_lo, expand_lo, shrink_lo, small_lo = weights
    params = small_lo.astype(f32)
    width = joint_lo.shape[0]
    hidden = expand_lo.shape[1]
    spans = hidden // width
    heads = width // HDIM
    seqs_here, stretch, _unused = tokens_in.shape
    rows = seqs_here * stretch
    start = lax.axis_index("ctx") * stretch
    scale = 1.0 / math.sqrt(HDIM)
    flat_in = tokens_in.reshape(rows, width).astype(f32)
    normed_one, norm_one_back = jax.vjp(norm_rows, flat_in, params[0], params[1])
    normed_lo = normed_one.astype(bf16)
    joint_bias = jnp.concatenate([params[2], jnp.zeros((width,), f32), params[3]])
    joint_out = jnp.dot(normed_lo, joint_lo, preferred_element_type=f32) + joint_bias
    joint_round = joint_out.astype(bf16)
    queries = joint_round[:, :width].reshape(seqs_here, stretch, heads, HDIM)
    keys_here = joint_round[:, width : 2 * width].reshape(seqs_here, stretch, width)
    values_here = joint_round[:, 2 * width :].reshape(seqs_here, stretch, width)
    segs_lo = segments.astype(bf16)
    keys_all, values_all, key_segs_lo = (
        lax.all_gather(keys_here, "ctx", axis=1, tiled=True),
        lax.all_gather(values_here, "ctx", axis=1, tiled=True),
        lax.all_gather(segs_lo, "ctx", axis=1, tiled=True),
    )
    key_segs = key_segs_lo.astype(jnp.int32)
    seq_len = keys_all.shape[1]

    def scores_for(query_set, key_set, query_seg, key_seg):
        raw = (
            jnp.einsum(
                "qhd,khd->hqk",
                query_set,
                key_set.reshape(seq_len, heads, HDIM),
                preferred_element_type=f32,
            )
            * scale
        )
        return jnp.where(allowed_pairs(query_seg, key_seg, start)[None], raw, MASKED_SCORE)

    def attend_forward(item):
        query_set, key_set, value_set, query_seg, key_seg = item
        scores = scores_for(query_set, key_set, query_seg, key_seg)
        row_max = jnp.max(scores, axis=-1, keepdims=True)
        exponent = jnp.exp(scores - row_max)
        row_sum = jnp.sum(exponent, axis=-1, keepdims=True)
        weights_lo = (exponent / row_sum).astype(bf16)
        mixed = jnp.einsum(
            "hqk,khd->qhd",
            weights_lo,
            value_set.reshape(seq_len, heads, HDIM),
            preferred_element_type=f32,
        )
        return (mixed.reshape(stretch, width).astype(bf16), (row_max + jnp.log(row_sum))[..., 0])

    attended, log_totals = lax.map(
        attend_forward, (queries, keys_all, values_all, segments, key_segs)
    )
    mixed_rows = attended.reshape(rows, width)
    branch = jnp.dot(mixed_rows, output_lo, preferred_element_type=f32) + params[4]
    residual = flat_in + branch
    normed_two, norm_two_back = jax.vjp(norm_rows, residual, params[5], params[6])
    normed_two_lo = normed_two.astype(bf16)
    expanded = jnp.dot(normed_two_lo, expand_lo, preferred_element_type=f32) + params[
        7 : 7 + spans
    ].reshape(hidden)
    activated, gelu_back = jax.vjp(jax.nn.gelu, expanded)
    activated_lo = activated.astype(bf16)
    result = (
        residual + jnp.dot(activated_lo, shrink_lo, preferred_element_type=f32) + params[7 + spans]
    )
    block_output = result.reshape(tokens_in.shape).astype(bf16)
    upstream = cotangent.reshape(rows, width)
    grad_shrink = jnp.einsum("rf,rd->fd", activated_lo, upstream, preferred_element_type=f32)
    grad_bias_shrink = jnp.sum(upstream, axis=0, dtype=f32)
    grad_act = jnp.einsum("rd,fd->rf", upstream, shrink_lo, preferred_element_type=f32)
    (grad_pre,) = gelu_back(grad_act)
    grad_pre_lo = grad_pre.astype(bf16)
    grad_expand = jnp.einsum("rd,rf->df", normed_two_lo, grad_pre_lo, preferred_element_type=f32)
    grad_bias_expand = jnp.sum(grad_pre_lo, axis=0, dtype=f32)
    grad_normed_two = jnp.einsum("rf,df->rd", grad_pre_lo, expand_lo, preferred_element_type=f32)
    grad_resid_norm, grad_gain_two, grad_shift_two = norm_two_back(grad_normed_two)
    grad_resid = upstream.astype(f32) + grad_resid_norm
    grad_branch_lo = grad_resid.astype(bf16)
    grad_bias_out = jnp.sum(grad_branch_lo, axis=0, dtype=f32)
    grad_output = jnp.einsum("rd,re->de", mixed_rows, grad_branch_lo, preferred_element_type=f32)
    grad_mixed = jnp.einsum("re,de->rd", grad_branch_lo, output_lo, preferred_element_type=f32)
    grad_mixed = grad_mixed.astype(bf16).reshape(seqs_here, stretch, heads, HDIM)
    keys_back, values_back, key_segs_back = (keys_all, values_all, key_segs)

    def attend_backward(item):
        query_set, grad_set, log_total, key_set, value_set, query_seg, key_seg = item
        key_heads = key_set.reshape(seq_len, heads, HDIM)
        value_heads = value_set.reshape(seq_len, heads, HDIM)
        scores = scores_for(query_set, key_set, query_seg, key_seg)
        probs = jnp.exp(scores - log_total[..., None])
        weights_lo = probs.astype(bf16)
        grad_probs = jnp.einsum("qhd,khd->hqk", grad_set, value_heads, preferred_element_type=f32)
        grad_value = jnp.einsum("hqk,qhd->khd", weights_lo, grad_set, preferred_element_type=f32)
        inner = jnp.sum(probs * grad_probs, axis=-1, keepdims=True)
        grad_scores = (probs * (grad_probs - inner)).astype(bf16)
        grad_query = (
            jnp.einsum("hqk,khd->qhd", grad_scores, key_heads, preferred_element_type=f32) * scale
        )
        grad_key = (
            jnp.einsum("hqk,qhd->khd", grad_scores, query_set, preferred_element_type=f32) * scale
        )
        return (
            grad_query.reshape(stretch, width),
            grad_key.reshape(seq_len, width).astype(bf16),
            grad_value.reshape(seq_len, width).astype(bf16),
        )

    grad_queries, key_terms, value_terms = lax.map(
        attend_backward,
        (queries, grad_mixed, log_totals, keys_back, values_back, segments, key_segs_back),
    )
    grad_keys, grad_values = (
        lax.psum_scatter(key_terms, "ctx", scatter_dimension=1, tiled=True).astype(jnp.float32),
        lax.psum_scatter(value_terms, "ctx", scatter_dimension=1, tiled=True).astype(jnp.float32),
    )
    grad_joint_lo = jnp.concatenate(
        [grad_queries.astype(bf16), grad_keys.astype(bf16), grad_values.astype(bf16)], axis=-1
    ).reshape(rows, 3 * width)
    grad_joint = jnp.einsum("rd,re->de", normed_lo, grad_joint_lo, preferred_element_type=f32)
    grad_bias_query = jnp.sum(grad_joint_lo[:, :width], axis=0, dtype=f32)
    grad_bias_value = jnp.sum(grad_joint_lo[:, 2 * width :], axis=0, dtype=f32)
    grad_normed_one = jnp.einsum("re,de->rd", grad_joint_lo, joint_lo, preferred_element_type=f32)
    grad_in_norm, grad_gain_one, grad_shift_one = norm_one_back(grad_normed_one)
    input_grad = (grad_resid + grad_in_norm).reshape(tokens_in.shape)
    grad_small = jnp.concatenate(
        [
            jnp.stack(
                [
                    grad_gain_one,
                    grad_shift_one,
                    grad_bias_query,
                    grad_bias_value,
                    grad_bias_out,
                    grad_gain_two,
                    grad_shift_two,
                ]
            ),
            grad_bias_expand.reshape(spans, width),
            grad_bias_shrink[None],
        ],
        axis=0,
    )
    reduced = (
        lax.psum_scatter(grad_joint, ("dp", "ctx"), scatter_dimension=0, tiled=True),
        lax.psum_scatter(grad_output, ("dp", "ctx"), scatter_dimension=0, tiled=True),
        lax.psum_scatter(grad_expand, ("dp", "ctx"), scatter_dimension=0, tiled=True),
        lax.psum_scatter(grad_shrink, ("dp", "ctx"), scatter_dimension=0, tiled=True),
        lax.psum_scatter(grad_small, ("dp", "ctx"), scatter_dimension=1, tiled=True),
    )
    new_joint, first_joint, second_joint = adam_step(
        joint_weight, reduced[0], momentum_joint, variance_joint, RATE_MATRIX, WEIGHT_DECAY
    )
    new_output, first_output, second_output = adam_step(
        output_weight, reduced[1], momentum_output, variance_output, RATE_MATRIX, WEIGHT_DECAY
    )
    new_expand, first_expand, second_expand = adam_step(
        expand_weight, reduced[2], momentum_expand, variance_expand, RATE_MATRIX, WEIGHT_DECAY
    )
    new_shrink, first_shrink, second_shrink = adam_step(
        shrink_weight, reduced[3], momentum_shrink, variance_shrink, RATE_MATRIX, WEIGHT_DECAY
    )
    new_small, first_small, second_small = adam_step(
        small_params, reduced[4], momentum_small, variance_small, RATE_VECTOR, 0.0
    )
    return (
        block_output,
        input_grad,
        new_joint,
        new_output,
        new_expand,
        new_shrink,
        first_joint,
        first_output,
        first_expand,
        first_shrink,
        second_joint,
        second_output,
        second_expand,
        second_shrink,
        new_small,
        first_small,
        second_small,
    )


def solution(mesh):
    return jax.shard_map(
        per_device,
        mesh=mesh,
        in_specs=(
            P("dp", "ctx", None),
            P("dp", "ctx"),
            P("dp", "ctx", None),
            P(("dp", "ctx"), None),
            P(("dp", "ctx"), None),
            P(("dp", "ctx"), None),
            P(("dp", "ctx"), None),
            P(("dp", "ctx"), None),
            P(("dp", "ctx"), None),
            P(("dp", "ctx"), None),
            P(("dp", "ctx"), None),
            P(("dp", "ctx"), None),
            P(("dp", "ctx"), None),
            P(("dp", "ctx"), None),
            P(("dp", "ctx"), None),
            P(None, ("dp", "ctx")),
            P(None, ("dp", "ctx")),
            P(None, ("dp", "ctx")),
        ),
        out_specs=(
            P("dp", "ctx", None),
            P("dp", "ctx", None),
            P(("dp", "ctx"), None),
            P(("dp", "ctx"), None),
            P(("dp", "ctx"), None),
            P(("dp", "ctx"), None),
            P(("dp", "ctx"), None),
            P(("dp", "ctx"), None),
            P(("dp", "ctx"), None),
            P(("dp", "ctx"), None),
            P(("dp", "ctx"), None),
            P(("dp", "ctx"), None),
            P(("dp", "ctx"), None),
            P(("dp", "ctx"), None),
            P(None, ("dp", "ctx")),
            P(None, ("dp", "ctx")),
            P(None, ("dp", "ctx")),
        ),
        check_vma=False,
    )
```

profile of v0, /device:TPU:0, one launch (start us, length us, event | category | flops | bytes accessed | tf_op | source)
XLA Modules:
  0.0 1253.0 jit_solution(10605953294036540499)
XLA Ops:
  14.0 43.7 %all-gather = bf16[32,24,12]{1,2,0:T(8,128)(2,1)S(1)} all-gather(bf16[1,24,12]{1,2,0:T(8,128)(2,1)S(1)} %convert_bitcast_fusion), channel_id=1, replica_groups=mesh['dp'=8,'ctx'=4] {'dp','ctx'}, dimensions={0}, use_global_device_ids=true | all-gather | bytes 19008 | tf_op jit(solution)/shard_map/all_gather | solution.py:75
  59.9 14.5 %all-gather.8.cloned.1.call-done = bf16[768,2304]{1,0:T(8,128)(2,1)} async-done(((bf16[24,2304]{1,0:T(8,128)(2,1)}), bf16[768,2304]{1,0:T(8,128)(2,1)}) %all-gather.8.cloned.1.call-update) | async-done | bytes 3538960 | tf_op jit(solution)/shard_map/all_gather | solution.py:71
  74.4 6.0 add_convert_fusion
  81.9 2.6 copy.74
  89.2 5.4 all_gather.27
  98.0 32.7 %all-gather.12.cloned.1.call-done = bf16[4,1024,768]{1,2,0:T(8,128)(2,1)} async-done(((bf16[4,256,768]{1,2,0:T(8,128)(2,1)}), bf16[4,1024,768]{1,2,0:T(8,128)(2,1)}) %all-gather.12.cloned.1.call-update) | async-done | bytes 6291472 | tf_op jit(solution)/shard_map/all_gather | solution.py:98
  130.7 49.4 %all-gather.10.cloned.1.call-done = bf16[4,1024,768]{1,2,0:T(8,128)(2,1)} async-done(((bf16[4,256,768]{1,2,0:T(8,128)(2,1)}), bf16[4,1024,768]{1,2,0:T(8,128)(2,1)}) %all-gather.10.cloned.1.call-update) | async-done | bytes 6291472 | tf_op jit(solution)/shard_map/all_gather | solution.py:99
  180.1 71.0 %while.26 = (s32[]{:T(128)}, bf16[4,256,768]{2,1,0:T(8,128)(2,1)}, f32[4,12,256]{2,1,0:T(8,128)}, bf16[4,1024,768]{1,2,0:T(8,128)(2,1)}, s32[]{:T(128)}, /*index...) while((s32[]{:T(128)}, bf16[4,256,768]{2,1,0:T(8,128)(2,1)}, ...), condition=%wide.region_5.6_spmd, body=%wide.region_2.5_spmd.sunk | while | flops 844035328 | bytes 50767012 | solution.py:132
  186.4 3.6 fusion.134
  190.0 4.6 fusion.135
  204.1 3.6 fusion.134
  207.8 4.6 fusion.135
  221.8 3.6 fusion.134
  225.5 4.6 fusion.135
  239.6 3.6 fusion.134
  243.2 4.6 fusion.135
  251.1 3.3 fusion.85
  256.6 46.7 %all-gather.16.cloned.1.call-done = bf16[768,3072]{1,0:T(8,128)(2,1)} async-done(((bf16[24,3072]{1,0:T(8,128)(2,1)}), bf16[768,3072]{1,0:T(8,128)(2,1)}) %all-gather.16.cloned.1.call-update) | async-done | bytes 4718608 | tf_op jit(solution)/shard_map/all_gather | solution.py:73
  303.4 8.3 fusion.74
  311.7 4.5 copy-done.63
  316.2 10.7 fusion.75
  327.0 134.5 %reduce-scatter.18.cloned.1.call-done = f32[96,768]{1,0:T(8,128)} async-done(((f32[3072,768]{1,0:T(8,128)}), f32[96,768]{1,0:T(8,128)}) %reduce-scatter.18.cloned.1.call-update) | async-done | bytes 294928 | tf_op jit(solution)/shard_map/reduce_scatter | solution.py:229
  463.9 64.2 %all-gather.18.cloned.1.call-done = bf16[3072,768]{1,0:T(8,128)(2,1)} async-done(((bf16[96,768]{1,0:T(8,128)(2,1)}), bf16[3072,768]{1,0:T(8,128)(2,1)}) %all-gather.18.cloned.1.call-update) | async-done | bytes 4718608 | tf_op jit(solution)/shard_map/all_gather | solution.py:74
  528.1 15.5 %convert_reduce_fusion = (f32[3072]{0:T(1024)}, bf16[1024,3072]{1,0:T(8,128)(2,1)S(1)}) fusion(f32[1024,3072]{1,0:T(8,128)} %copy-done.63, f32[3072]{0:T(1024)S(1)} %copy-done.52, bf16[1024,768]{1,0:T(8,128)(2,1)S(1)} %bitcast.185, bf16[3072,768]{1,0:T(8,128)(2,1)} %all-gather.18.cloned.1.call-done), kind=kOutput, calls=%fused_computation.67 | convolution fusion | flops 4904186880 | bytes 25190400 | tf_op jit(solution)/shard_map/rd,fd->rf/dot_general | solution.py:152
  543.6 10.8 multiply_reduce_fusion.1
  565.7 2.8 copy.79
  568.5 186.4 %while.27 = (s32[]{:T(128)}, bf16[4,256,768]{2,1,0:T(8,128)(2,1)}, bf16[4,1024,768]{2,1,0:T(8,128)(2,1)}, bf16[4,1024,768]{2,1,0:T(8,128)(2,1)}, bf16[4,1024,768...) while((s32[]{:T(128)}, bf16[4,256,768]{2,1,0:T(8,128)(2,1)}, ...), condition=%wide.region_12.13_spmd, body=%wide.region_10.12_spmd.sunk | while | flops 2063987968 | bytes 245339408 | solution.py:190
  574.2 2.8 fusion.145
  577.0 5.9 fusion.147
  583.0 2.6 copy.120
  585.6 11.5 multiply_reduce_fusion.5
  598.2 6.7 multiply_convert_fusion.7
  611.7 3.4 constant_dynamic-update-slice_fusion.9
  620.7 2.8 fusion.145
  623.5 5.9 fusion.147
  629.5 2.6 copy.120
  632.0 11.4 multiply_reduce_fusion.5
  644.7 6.7 multiply_convert_fusion.7
  658.2 3.4 constant_dynamic-update-slice_fusion.9
  667.1 2.8 fusion.145
  670.0 5.9 fusion.147
  675.9 2.6 copy.120
  678.5 11.4 multiply_reduce_fusion.5
  691.1 6.7 multiply_convert_fusion.7
  704.7 3.5 constant_dynamic-update-slice_fusion.9
  713.7 2.8 fusion.145
  716.5 5.9 fusion.147
  722.5 2.6 copy.120
  725.1 11.4 multiply_reduce_fusion.5
  737.7 6.7 multiply_convert_fusion.7
  751.2 3.4 constant_dynamic-update-slice_fusion.9
  755.7 4.9 fusion.86
  760.8 12.0 fusion.73
  772.9 39.3 %reduce-scatter.10.cloned.1.call-done = bf16[4,256,768]{2,1,0:T(8,128)(2,1)} async-done(((bf16[4,1024,768]{2,1,0:T(8,128)(2,1)}), bf16[4,256,768]{2,1,0:T(8,128)(2,1)}) %reduce-scatter.10.cloned.1.call-update) | async-done | bytes 1572880 | tf_op jit(solution)/shard_map/reduce_scatter | solution.py:196
  812.2 61.0 %reduce-scatter.8.cloned.1.call-done = bf16[4,256,768]{2,1,0:T(8,128)(2,1)} async-done(((bf16[4,1024,768]{2,1,0:T(8,128)(2,1)}), bf16[4,256,768]{2,1,0:T(8,128)(2,1)}) %reduce-scatter.8.cloned.1.call-update) | async-done | bytes 1572880 | tf_op jit(solution)/shard_map/reduce_scatter | solution.py:195
  873.2 8.9 convolution_bitcast_fusion
  884.0 13.8 %add_convert_fusion.1 = bf16[1024,768]{1,0:T(8,128)(2,1)} fusion(f32[1024,768]{1,0:T(8,128)} %copy-done.8, bf16[3072,768]{1,0:T(8,128)(2,1)} %all-gather.18.cloned.1.call-done, f32[768]{0:T(1024)S(1)} %copy-done.57, f32[1024,3072]{1,0:T(8,128)} %copy-done.63, f32[3072]{0:T(1024)S(1)} %copy-done.53), kind=kOutput, calls=%fused_computation.101 | convolution fusion | flops 4865654784 | bytes 22035456 | tf_op jit(solution)/shard_map/dot_general | solution.py:146
  897.8 80.4 %reduce-scatter.14.cloned.1.call-done = f32[24,768]{1,0:T(8,128)} async-done(((f32[768,768]{1,0:T(8,128)}), f32[24,768]{1,0:T(8,128)}) %reduce-scatter.14.cloned.1.call-update) | async-done | bytes 73744 | tf_op jit(solution)/shard_map/reduce_scatter | solution.py:227
  979.8 2.6 pad_maximum_fusion
  983.3 4.1 fusion.76
  991.0 40.4 %all-reduce = f32[12,768]{1,0:T(8,128)S(1)} all-reduce(f32[12,768]{1,0:T(8,128)S(1)} %concatenate.11), channel_id=8, replica_groups=mesh['dp'=8,'ctx'=4] {'dp','ctx'}, use_global_device_ids=true, to_apply=%region_30.31.clone | all-reduce | flops 9216 | bytes 73728
  1032.2 4.8 add_add_fusion.2
  1037.0 81.9 %reduce-scatter.16.cloned.1.call-done = f32[24,3072]{1,0:T(8,128)} async-done(((f32[768,3072]{1,0:T(8,128)}), f32[24,3072]{1,0:T(8,128)}) %reduce-scatter.16.cloned.1.call-update) | async-done | bytes 294928 | tf_op jit(solution)/shard_map/reduce_scatter | solution.py:228
  1121.1 122.4 %reduce-scatter.12.cloned.1.call-done = f32[24,2304]{1,0:T(8,128)} async-done(((f32[768,2304]{1,0:T(8,128)}), f32[24,2304]{1,0:T(8,128)}) %reduce-scatter.12.cloned.1.call-update) | async-done | bytes 221200 | tf_op jit(solution)/shard_map/reduce_scatter | solution.py:226
  (334 shorter events, 139.8 us)
Async XLA Ops:
  7.2 52.1 %copy-start.3 = (bf16[4,256,768]{2,1,0:T(8,128)(2,1)S(1)}, bf16[4,256,768]{2,1,0:T(8,128)(2,1)}, u32[]{:S(2)}) copy-start(bf16[4,256,768]{2,1,0:T(8,128)(2,1)} %param.22) | copy-start | bytes 4718596
  7.2 6.8 copy-start.45
  7.2 67.2 %all-gather.8.cloned.1.call-start = ((), (), s32[]{:S(2)}) async-start(), calls=%async_computation.6 | async-start | bytes 3649536 | tf_op jit(solution)/shard_map/all_gather | solution.py:71
  9.0 121.7 %all-gather.12.cloned.1.call-start = ((), (), s32[]{:S(2)}) async-start(), calls=%async_computation.8 | async-start | bytes 7864320 | tf_op jit(solution)/shard_map/all_gather | solution.py:98
  10.8 69.7 %copy-start.37 = (f32[1,2,4,128]{3,1,2,0:T(2,128)}, f32[1,2,4,128]{3,1,2,0:T(2,128)S(1)}, u32[]{:S(2)}) copy-start(f32[1,2,4,128]{3,1,2,0:T(2,128)S(1)} %copy.112) | copy-start | bytes 12292
  14.0 66.5 %copy-start.39 = (f32[1024]{0:T(1024)}, f32[1024]{0:T(1024)S(1)}, u32[]{:S(2)}) copy-start(f32[1024]{0:T(1024)S(1)} %rsqrt.23) | copy-start | bytes 12292
  84.5 95.5 %all-gather.10.cloned.1.call-start = ((), (), s32[]{:S(2)}) async-start(), calls=%async_computation.7 | async-start | bytes 7864320 | tf_op jit(solution)/shard_map/all_gather | solution.py:99
  86.2 165.0 %all-gather.14.cloned.1.call-start = ((), (), s32[]{:S(2)}) async-start(), calls=%async_computation.9 | async-start | bytes 1216512 | tf_op jit(solution)/shard_map/all_gather | solution.py:72
  86.9 216.5 %all-gather.16.cloned.1.call-start = ((), (), s32[]{:S(2)}) async-start(), calls=%async_computation.10 | async-start | bytes 4866048 | tf_op jit(solution)/shard_map/all_gather | solution.py:73
  87.6 373.9 %reduce-scatter.18.cloned.1.call-start = ((), (), s32[]{:S(2)}) async-start(), calls=%async_computation.17 | async-start | bytes 9732096 | tf_op jit(solution)/shard_map/reduce_scatter | solution.py:229
  180.1 71.1 %copy-start.4 = (bf16[4,256,768]{2,1,0:T(8,128)(2,1)S(1)}, bf16[4,256,768]{2,1,0:T(8,128)(2,1)}, u32[]{:S(2)}) copy-start(bf16[4,256,768]{2,1,0:T(8,128)(2,1)} %param.22) | copy-start | bytes 4718596
  190.0 4.6 copy-start.16
  207.7 4.6 copy-start.16
  225.5 4.6 copy-start.16
  243.2 4.6 copy-start.16
  254.4 49.0 %copy-start.29 = (f32[768]{0:T(1024)S(1)}, f32[768]{0:T(1024)}, u32[]{:S(2)}) copy-start(f32[768]{0:T(1024)} %get-tuple-element.227) | copy-start | bytes 9220
  254.5 48.9 %copy-start.35 = (f32[768]{0:T(1024)S(1)}, f32[768]{0:T(1024)}, u32[]{:S(2)}) copy-start(f32[768]{0:T(1024)} %get-tuple-element.229) | copy-start | bytes 9220
  254.5 300.0 %copy-start.21 = (f32[1024]{0:T(1024)}, f32[1024]{0:T(1024)S(1)}, u32[]{:S(2)}) copy-start(f32[1024]{0:T(1024)S(1)} %broadcast_multiply_fusion) | copy-start | bytes 12292
  256.6 297.8 %copy-start.26 = (f32[1024]{0:T(1024)}, f32[1024]{0:T(1024)S(1)}, u32[]{:S(2)}) copy-start(f32[1024]{0:T(1024)S(1)} %fusion.68) | copy-start | bytes 12292
  303.4 12.8 %copy-start.12 = (bf16[4,256,768]{2,1,0:T(8,128)(2,1)S(1)}, bf16[4,256,768]{2,1,0:T(8,128)(2,1)}, u32[]{:S(2)}) copy-start(bf16[4,256,768]{2,1,0:T(8,128)(2,1)} %param.24) | copy-start | bytes 4718596
  303.4 12.8 %copy-start.52 = (f32[3072]{0:T(1024)S(1)}, f32[3072]{0:T(1024)}, u32[]{:S(2)}) copy-start(f32[3072]{0:T(1024)} %add.251) | copy-start | bytes 36868
  311.7 4.5 copy-start.63
  327.0 134.6 %copy-start.23 = (f32[96,768]{1,0:T(8,128)S(1)}, f32[96,768]{1,0:T(8,128)}, u32[]{:S(2)}) copy-start(f32[96,768]{1,0:T(8,128)} %param.28) | copy-start | bytes 884740
  327.0 201.1 %all-gather.18.cloned.1.call-start = ((), (), s32[]{:S(2)}) async-start(), calls=%async_computation.11 | async-start | bytes 4866048 | tf_op jit(solution)/shard_map/all_gather | solution.py:74
  463.8 348.4 %reduce-scatter.10.cloned.1.call-start = ((), (), s32[]{:S(2)}) async-start(), calls=%async_computation.13 | async-start | bytes 7864320 | tf_op jit(solution)/shard_map/reduce_scatter | solution.py:196
  528.1 15.5 %copy-start.9 = (f32[1024,768]{1,0:T(8,128)S(1)}, f32[1024,768]{1,0:T(8,128)}, u32[]{:S(2)}) copy-start(f32[1024,768]{1,0:T(8,128)} %copy-done.8) | copy-start | bytes 9437188
  543.6 10.8 copy-start.15
  577.0 6.0 copy-start
  585.6 12.6 %copy-start.1 = (f32[12,256,1024]{2,1,0:T(8,128)S(1)}, f32[12,256,1024]{2,1,0:T(8,128)}, u32[]{:S(2)}) copy-start(f32[12,256,1024]{2,1,0:T(8,128)} %copy-done) | copy-start | bytes 37748740 | tf_op jit(solution)/shard_map/while
  611.7 3.4 copy-start.7
  623.5 5.9 copy-start
  632.0 12.6 %copy-start.1 = (f32[12,256,1024]{2,1,0:T(8,128)S(1)}, f32[12,256,1024]{2,1,0:T(8,128)}, u32[]{:S(2)}) copy-start(f32[12,256,1024]{2,1,0:T(8,128)} %copy-done) | copy-start | bytes 37748740 | tf_op jit(solution)/shard_map/while
  670.0 5.9 copy-start
  678.5 12.6 %copy-start.1 = (f32[12,256,1024]{2,1,0:T(8,128)S(1)}, f32[12,256,1024]{2,1,0:T(8,128)}, u32[]{:S(2)}) copy-start(f32[12,256,1024]{2,1,0:T(8,128)} %copy-done) | copy-start | bytes 37748740 | tf_op jit(solution)/shard_map/while
  704.7 3.5 copy-start.7
  716.5 5.9 copy-start
  725.0 12.6 %copy-start.1 = (f32[12,256,1024]{2,1,0:T(8,128)S(1)}, f32[12,256,1024]{2,1,0:T(8,128)}, u32[]{:S(2)}) copy-start(f32[12,256,1024]{2,1,0:T(8,128)} %copy-done) | copy-start | bytes 37748740 | tf_op jit(solution)/shard_map/while
  751.2 3.5 copy-start.7
  754.9 118.3 %reduce-scatter.8.cloned.1.call-start = ((), (), s32[]{:S(2)}) async-start(), calls=%async_computation.12 | async-start | bytes 7864320 | tf_op jit(solution)/shard_map/reduce_scatter | solution.py:195
  755.6 5.1 copy-start.10
  755.6 5.1 copy-start.22
  755.7 5.1 copy-start.27
  755.7 5.1 copy-start.30
  755.7 5.1 copy-start.36
  755.7 222.6 %reduce-scatter.14.cloned.1.call-start = ((), (), s32[]{:S(2)}) async-start(), calls=%async_computation.15 | async-start | bytes 2433024 | tf_op jit(solution)/shard_map/reduce_scatter | solution.py:227
  760.7 358.2 %reduce-scatter.16.cloned.1.call-start = ((), (), s32[]{:S(2)}) async-start(), calls=%async_computation.16 | async-start | bytes 9732096 | tf_op jit(solution)/shard_map/reduce_scatter | solution.py:228
  772.8 100.4 %copy-start.5 = (bf16[4,256,768]{2,1,0:T(8,128)(2,1)S(1)}, bf16[4,256,768]{2,1,0:T(8,128)(2,1)}, u32[]{:S(2)}) copy-start(bf16[4,256,768]{2,1,0:T(8,128)(2,1)} %param.22) | copy-start | bytes 4718596
  772.8 100.4 %copy-start.17 = (bf16[4,256,768]{2,1,0:T(8,128)(2,1)S(1)}, bf16[4,256,768]{2,1,0:T(8,128)(2,1)}, u32[]{:S(2)}) copy-start(bf16[4,256,768]{2,1,0:T(8,128)(2,1)} %get-tuple-element.131) | copy-start | bytes 4718596
  772.8 100.4 %copy-start.34 = (f32[768]{0:T(1024)S(1)}, f32[768]{0:T(1024)}, u32[]{:S(2)}) copy-start(f32[768]{0:T(1024)} %copy-done.33) | copy-start | bytes 9220
  772.8 100.4 %copy-start.48 = (f32[768]{0:T(1024)S(1)}, f32[768]{0:T(1024)}, u32[]{:S(2)}) copy-start(f32[768]{0:T(1024)} %copy-done.47) | copy-start | bytes 9220
  772.8 100.4 %copy-start.50 = (f32[4,256]{1,0:T(4,128)S(1)}, f32[4,256]{1,0:T(4,128)}, u32[]{:S(2)}) copy-start(f32[4,256]{1,0:T(4,128)} %copy-done.49) | copy-start | bytes 12292
  772.8 100.4 %copy-start.58 = (f32[4,256]{1,0:T(4,128)S(1)}, f32[4,256]{1,0:T(4,128)}, u32[]{:S(2)}) copy-start(f32[4,256]{1,0:T(4,128)} %get-tuple-element.308) | copy-start | bytes 12292
  772.8 470.6 %reduce-scatter.12.cloned.1.call-start = ((), (), s32[]{:S(2)}) async-start(), calls=%async_computation.14 | async-start | bytes 7299072 | tf_op jit(solution)/shard_map/reduce_scatter | solution.py:226
  883.9 94.3 %copy-start.25 = (f32[24,768]{1,0:T(8,128)S(1)}, f32[24,768]{1,0:T(8,128)}, u32[]{:S(2)}) copy-start(f32[24,768]{1,0:T(8,128)} %param.26) | copy-start | bytes 221188
  883.9 94.3 %copy-start.31 = (f32[24,768]{1,0:T(8,128)S(1)}, f32[24,768]{1,0:T(8,128)}, u32[]{:S(2)}) copy-start(f32[24,768]{1,0:T(8,128)} %param.30) | copy-start | bytes 221188
  884.0 94.3 %copy-start.32 = (f32[24,768]{1,0:T(8,128)S(1)}, f32[24,768]{1,0:T(8,128)}, u32[]{:S(2)}) copy-start(f32[24,768]{1,0:T(8,128)} %param.34) | copy-start | bytes 221188
  979.8 3.4 copy-start.61
  983.3 4.2 copy-start.44
  983.3 5.8 copy-start.40
  987.5 44.0 %copy-start.46 = (f32[12,24]{1,0:T(8,128)S(1)}, f32[12,24]{1,0:T(8,128)}, u32[]{:S(2)}) copy-start(f32[12,24]{1,0:T(8,128)} %param.37) | copy-start | bytes 3460
  987.5 44.0 %copy-start.55 = (f32[12,24]{1,0:T(8,128)S(1)}, f32[12,24]{1,0:T(8,128)}, u32[]{:S(2)}) copy-start(f32[12,24]{1,0:T(8,128)} %param.38) | copy-start | bytes 3460
  987.5 44.0 %copy-start.56 = (f32[12,24]{1,0:T(8,128)S(1)}, f32[12,24]{1,0:T(8,128)}, u32[]{:S(2)}) copy-start(f32[12,24]{1,0:T(8,128)} %param.39) | copy-start | bytes 3460
  987.5 44.7 %copy-start.42 = (f32[1024]{0:T(1024)S(1)}, f32[1024]{0:T(1024)}, u32[]{:S(2)}) copy-start(f32[1024]{0:T(1024)} %copy-done.41) | copy-start | bytes 12292
  1032.2 86.7 %copy-start.20 = (f32[24,3072]{1,0:T(8,128)S(1)}, f32[24,3072]{1,0:T(8,128)}, u32[]{:S(2)}) copy-start(f32[24,3072]{1,0:T(8,128)} %param.27) | copy-start | bytes 884740
  (30 other events, 52.5 us)
Sparse Core Ops, SparseCore 0:
  11.5 62.8 all-gather.7
  84.6 45.9 all-gather.11
  132.8 47.2 all-gather.9
  183.4 54.0 all-gather.13
  240.8 62.5 all-gather.15
  327.1 134.3 reduce-scatter.17
  465.4 62.6 all-gather.17
  755.0 57.1 reduce-scatter.9
  814.8 58.3 reduce-scatter.7
  879.2 99.0 reduce-scatter.13
  984.1 134.7 reduce-scatter.15
  1125.4 118.0 reduce-scatter.11
where the time goes:
time: 1260 us; the launch traced here: 1250 us
  waiting for transfers between devices  728 us (58%)
  matrix products  226 us (18%)
  local copies, waits for them, and re-layouts  112 us (9%)
  blocking collectives  89.5 us (7%)
  other arithmetic  80.3 us (6%)
  between operations  15.5 us (1%)
    reduce_scatter x1, waiting for transfers between devices, per_device(): lax.psum_scatter(grad_shrink, ('dp', 'ctx'), scatter_dimension=0, tiled=T...  135 us
    reduce_scatter x1, waiting for transfers between devices, per_device(): lax.psum_scatter(grad_joint, ('dp', 'ctx'), scatter_dimension=0, tiled=True)  122 us
    reduce_scatter x1, waiting for transfers between devices, per_device(): lax.psum_scatter(grad_expand, ('dp', 'ctx'), scatter_dimension=0, tiled=T...  81.9 us
    reduce_scatter x1, waiting for transfers between devices, per_device(): lax.psum_scatter(grad_output, ('dp', 'ctx'), scatter_dimension=0, tiled=T...  80.4 us
    all_gather x1, waiting for transfers between devices, per_device(): lax.all_gather(shrink_cast, ('dp', 'ctx'), axis=0, tiled=True)  64.2 us
    reduce_scatter x1, waiting for transfers between devices, per_device(): lax.psum_scatter(key_terms, 'ctx', scatter_dimension=1, tiled=True)  61 us
    all_gather x1, waiting for transfers between devices, per_device(): lax.all_gather(values_here, 'ctx', axis=1, tiled=True)  49.4 us
    all_gather x1, waiting for transfers between devices, per_device(): lax.all_gather(expand_cast, ('dp', 'ctx'), axis=0, tiled=True)  46.7 us
  transfers between devices with their start and end apart: 12, of which 11 were waited for; matrix products, arithmetic and copies ran while one was open for 12% of the time, Pallas kernels for 0%

commit v1 on v0

v1 whole, which is shorter than its diff:
```python
import functools

import jax
import jax.numpy as jnp
from jax import lax
from jax.experimental import pallas as pl
from jax.experimental.pallas import tpu as pltpu
from jax.sharding import PartitionSpec as P

HDIM = 64
STEP = 10

NORM_EPSILON = 1e-05
MASKED_SCORE = -1000000000.0
BETA_ONE = 0.9
BETA_TWO = 0.999
ADAM_EPSILON = 1e-08
RATE_MATRIX = 0.05
RATE_VECTOR = 0.3
WEIGHT_DECAY = 0.1

BF16 = jnp.bfloat16
F32 = jnp.float32


def norm_rows(values, gain, shift):
    centre = values - jnp.mean(values, axis=-1, keepdims=True)
    spread = jnp.mean(centre * centre, axis=-1, keepdims=True)
    return centre * lax.rsqrt(spread + NORM_EPSILON) * gain + shift


def norm_plain(values):
    centre = values - jnp.mean(values, axis=-1, keepdims=True)
    spread = jnp.mean(centre * centre, axis=-1, keepdims=True)
    return centre * lax.rsqrt(spread + NORM_EPSILON)


def adam_step(weight, gradient, first, second, rate, decay):
    first_new = BETA_ONE * first + (1.0 - BETA_ONE) * gradient
    second_new = BETA_TWO * second + (1.0 - BETA_TWO) * gradient * gradient
    first_hat = first_new / (1.0 - BETA_ONE**STEP)
    second_hat = second_new / (1.0 - BETA_TWO**STEP)
    updated = weight - rate * (first_hat / (jnp.sqrt(second_hat) + ADAM_EPSILON) + decay * weight)
    return (updated, first_new, second_new)


def dot(left, right, dims):
    return lax.dot_general(left, right, (dims, ((), ())), preferred_element_type=F32)


def fill_bias(bias, start_ref, n_blk, blk, block):
    keys = (block + 1) * blk
    key_pos = lax.broadcasted_iota(jnp.int32, (keys, blk), 0)
    query_pos = lax.broadcasted_iota(jnp.int32, (keys, blk), 1) + block * blk
    first = start_ref[0, :, block * blk : (block + 1) * blk]
    allowed = (key_pos >= first) & (key_pos <= query_pos)
    bias[:keys, :] = jnp.where(allowed, 0.0, MASKED_SCORE)


def forward_kernel(n_blk, blk, heads, me_ref, joint_ref, start_ref, out_ref, log_ref, joint, bias):
    me = me_ref[0]
    group = heads * HDIM
    for block in range(n_blk):
        joint[block * blk : (block + 1) * blk, :] = joint_ref[lax.bitwise_xor(me, block), 0]
    for block in range(n_blk):
        rows = slice(block * blk, (block + 1) * blk)
        keys = (block + 1) * blk
        fill_bias(bias, start_ref, n_blk, blk, block)
        for head in range(heads):
            low = head * HDIM
            query = joint[rows, low : low + HDIM] * 0.125
            key = joint[:keys, group + low : group + low + HDIM]
            value = joint[:keys, 2 * group + low : 2 * group + low + HDIM]
            scores = dot(key, query, ((1,), (1,))) + bias[:keys, :]
            top = jnp.max(scores, axis=0, keepdims=True)
            exponent = jnp.exp(scores - top)
            total = jnp.sum(exponent, axis=0, keepdims=True)
            weights = (exponent * (1.0 / total)).astype(BF16)
            mixed = dot(value, weights, ((0,), (0,)))
            out_ref[lax.bitwise_xor(me, block), 0, :, low : low + HDIM] = mixed.T.astype(BF16)
            log_ref[0, head : head + 1, rows] = top + jnp.log(total)


def backward_kernel(
    n_blk, blk, heads, me_ref, joint_ref, grad_ref, start_ref, log_ref, out_ref, joint, bias, grad_key, grad_value
):
    me = me_ref[0]
    group = heads * HDIM
    for block in range(n_blk):
        joint[block * blk : (block + 1) * blk, :] = joint_ref[lax.bitwise_xor(me, block), 0]
    for block in reversed(range(n_blk)):
        rows = slice(block * blk, (block + 1) * blk)
        keys = (block + 1) * blk
        fill_bias(bias, start_ref, n_blk, blk, block)
        place = lax.bitwise_xor(me, block)
        for head in range(heads):
            low = head * HDIM
            query = joint[rows, low : low + HDIM] * 0.125
            key = joint[:keys, group + low : group + low + HDIM]
            value = joint[:keys, 2 * group + low : 2 * group + low + HDIM]
            grad = grad_ref[place, 0, :, low : low + HDIM]
            scores = dot(key, query, ((1,), (1,))) + bias[:keys, :]
            probs = jnp.exp(scores - log_ref[0, head : head + 1, rows])
            grad_probs = dot(value, grad, ((1,), (1,)))
            inner = jnp.sum(probs * grad_probs, axis=0, keepdims=True)
            grad_scores = (probs * (grad_probs - inner)).astype(BF16)
            key_term = dot(grad_scores, query, ((1,), (0,)))
            value_term = dot(probs.astype(BF16), grad, ((1,), (0,)))
            if block == n_blk - 1:
                grad_key[head, :keys, :] = key_term
                grad_value[head, :keys, :] = value_term
            else:
                grad_key[head, :keys, :] += key_term
                grad_value[head, :keys, :] += value_term
            grad_query = dot(key, grad_scores, ((0,), (0,)))
            out_ref[place, 0, :, low : low + HDIM] = (grad_query.T * 0.125).astype(BF16)
    for block in range(n_blk):
        rows = slice(block * blk, (block + 1) * blk)
        place = lax.bitwise_xor(me, block)
        for head in range(heads):
            low = head * HDIM
            out_ref[place, 0, :, group + low : group + low + HDIM] = grad_key[head, rows, :].astype(BF16)
            out_ref[place, 0, :, 2 * group + low : 2 * group + low + HDIM] = grad_value[head, rows, :].astype(BF16)


def attend_forward(me, joint, start):
    n_blk, seqs, blk, cols = joint.shape
    group = cols // 3
    heads = group // HDIM
    length = n_blk * blk
    return pl.pallas_call(
        functools.partial(forward_kernel, n_blk, blk, heads),
        grid_spec=pltpu.PrefetchScalarGridSpec(
            num_scalar_prefetch=1,
            grid=(seqs,),
            in_specs=[
                pl.BlockSpec((n_blk, 1, blk, cols), lambda s, m: (0, s, 0, 0)),
                pl.BlockSpec((1, 1, length), lambda s, m: (s, 0, 0)),
            ],
            out_specs=[
                pl.BlockSpec((n_blk, 1, blk, group), lambda s, m: (0, s, 0, 0)),
                pl.BlockSpec((1, heads, length), lambda s, m: (s, 0, 0)),
            ],
            scratch_shapes=[pltpu.VMEM((length, cols), BF16), pltpu.VMEM((length, blk), F32)],
        ),
        out_shape=[
            jax.ShapeDtypeStruct((n_blk, seqs, blk, group), BF16),
            jax.ShapeDtypeStruct((seqs, heads, length), F32),
        ],
        compiler_params=pltpu.CompilerParams(vmem_limit_bytes=48 * 1024 * 1024),
        cost_estimate=pl.CostEstimate(
            flops=seqs * heads * length * length * HDIM * 3,
            bytes_accessed=seqs * length * cols * 3,
            transcendentals=seqs * heads * length * length,
        ),
        name="attend_forward",
    )(me, joint, start)


def attend_backward(me, joint, grad, start, logs):
    n_blk, seqs, blk, cols = joint.shape
    group = cols // 3
    heads = group // HDIM
    length = n_blk * blk
    return pl.pallas_call(
        functools.partial(backward_kernel, n_blk, blk, heads),
        grid_spec=pltpu.PrefetchScalarGridSpec(
            num_scalar_prefetch=1,
            grid=(seqs,),
            in_specs=[
                pl.BlockSpec((n_blk, 1, blk, cols), lambda s, m: (0, s, 0, 0)),
                pl.BlockSpec((n_blk, 1, blk, group), lambda s, m: (0, s, 0, 0)),
                pl.BlockSpec((1, 1, length), lambda s, m: (s, 0, 0)),
                pl.BlockSpec((1, heads, length), lambda s, m: (s, 0, 0)),
            ],
            out_specs=pl.BlockSpec((n_blk, 1, blk, cols), lambda s, m: (0, s, 0, 0)),
            scratch_shapes=[
                pltpu.VMEM((length, cols), BF16),
                pltpu.VMEM((length, blk), F32),
                pltpu.VMEM((heads, length, HDIM), F32),
                pltpu.VMEM((heads, length, HDIM), F32),
            ],
        ),
        out_shape=jax.ShapeDtypeStruct((n_blk, seqs, blk, cols), BF16),
        compiler_params=pltpu.CompilerParams(vmem_limit_bytes=48 * 1024 * 1024),
        cost_estimate=pl.CostEstimate(
            flops=seqs * heads * length * length * HDIM * 7,
            bytes_accessed=seqs * length * cols * 6,
            transcendentals=seqs * heads * length * length,
        ),
        name="attend_backward",
    )(me, joint, grad, start, logs)


def build(sizes):
    n_dp, n_ctx = sizes["dp"], sizes["ctx"]
    dp_bits = [bit for bit in range(16) if (1 << bit) < n_dp]
    ctx_bits = [bit for bit in range(16) if (1 << bit) < n_ctx]

    def swap(value, axis, mask):
        return lax.ppermute(value, axis, [(place, place ^ mask) for place in range(sizes[axis])])

    def reorder(items, me):
        stacked = jnp.stack(items)
        return [
            lax.dynamic_index_in_dim(stacked, lax.bitwise_xor(me, j), 0, keepdims=False) for j in range(len(items))
        ]

    def halve(value, labels, order, spots):
        labels = list(labels)
        for axis, bit in order:
            pos = labels.index((axis, bit))
            mine = (spots[axis] >> bit) & 1
            send = lax.dynamic_index_in_dim(value, 1 - mine, pos, keepdims=False).astype(BF16)
            keep = lax.dynamic_index_in_dim(value, mine, pos, keepdims=False)
            value = keep + swap(send, axis, 1 << bit).astype(F32)
            labels.pop(pos)
        return value

    def per_device(
        tokens_in,
        segments,
        cotangent,
        joint_weight,
        output_weight,
        expand_weight,
        shrink_weight,
        momentum_joint,
        momentum_output,
        momentum_expand,
        momentum_shrink,
        variance_joint,
        variance_output,
        variance_expand,
        variance_shrink,
        small_params,
        momentum_small,
        variance_small,
    ):
        seqs, stretch, width = tokens_in.shape
        hidden = expand_weight.shape[1]
        spans = hidden // width
        part = joint_weight.shape[0]
        group = width // n_ctx
        cols = 3 * group
        rows = seqs * stretch
        vectors = small_params.shape[0]
        me_dp, me = lax.axis_index("dp"), lax.axis_index("ctx")
        spots = {"dp": me_dp, "ctx": me}
        me_arr = me.astype(jnp.int32).reshape(1)

        joint_cast, small_cast, output_cast, expand_cast, shrink_cast = lax.optimization_barrier(
            (
                joint_weight.astype(BF16),
                small_params.astype(BF16),
                output_weight.astype(BF16),
                expand_weight.astype(BF16),
                shrink_weight.astype(BF16),
            )
        )
        shrink_wide = shrink_cast.reshape(spans, part, width).transpose(1, 0, 2).reshape(part, hidden)
        rest = lax.all_gather(
            jnp.concatenate([output_cast, expand_cast, shrink_wide], axis=1), ("dp", "ctx"), axis=0, tiled=True
        )

        extra = -(-vectors * part // cols)
        pad = extra * cols - vectors * part
        small_rows = jnp.pad(small_cast.reshape(-1), (0, pad)).reshape(extra, cols)
        joint_cols = joint_cast.reshape(part, 3, n_ctx, group)

        def columns_for(k):
            picked = lax.dynamic_index_in_dim(joint_cols, lax.bitwise_xor(me, k), 2, keepdims=False)
            return jnp.concatenate([picked.reshape(part, cols), small_rows], axis=0)

        pieces = [columns_for(0)] + [swap(columns_for(k), "ctx", k) for k in range(1, n_ctx)]
        gathered = jnp.stack(reorder(pieces, me))
        for bit in reversed(dp_bits):
            other = swap(gathered, "dp", 1 << bit)
            upper = ((me_dp >> bit) & 1) == 1
            gathered = jnp.where(upper, jnp.stack([other, gathered]), jnp.stack([gathered, other]))
        n_bits = len(dp_bits)
        gathered = gathered.transpose(tuple(reversed(range(n_bits))) + tuple(range(n_bits, n_bits + 3)))
        gathered = gathered.reshape(n_dp, n_ctx, part + extra, cols)
        joint_lo = gathered[:, :, :part].reshape(width, cols)
        small_lo = gathered[:, :, part:].reshape(n_dp, n_ctx, extra * cols)[:, :, : vectors * part]
        params = small_lo.reshape(n_dp, n_ctx, vectors, part).transpose(2, 0, 1, 3).reshape(vectors, width).astype(F32)

        blocks = {0: tokens_in}
        for bit in reversed(ctx_bits):
            blocks.update({k ^ (1 << bit): swap(value, "ctx", 1 << bit) for k, value in list(blocks.items())})
        tokens_all = jnp.stack([blocks[k] for k in range(n_ctx)]).reshape(n_ctx * rows, width)

        segs_all = lax.all_gather(segments.astype(BF16), "ctx", axis=1, tiled=True)
        start = jnp.sum(
            (segs_all[:, :, None] > segs_all[:, None, :]).astype(F32), axis=2
        ).astype(jnp.int32)[:, None, :]

        normed_lo = norm_rows(tokens_all.astype(F32), params[0], params[1]).astype(BF16)
        mine_bias = lax.dynamic_slice(params[2:4], (0, me * group), (2, group))
        joint_bias = jnp.concatenate([mine_bias[0], jnp.zeros((group,), F32), mine_bias[1]])
        joint_lo_out = (dot(normed_lo, joint_lo, ((1,), (0,))) + joint_bias).astype(BF16)
        joint_blocks = joint_lo_out.reshape(n_ctx, seqs, stretch, cols)
        attended, logs = attend_forward(me_arr, joint_blocks, start)
        mixed = jnp.concatenate(
            [attended[0]] + [swap(attended[k], "ctx", k) for k in range(1, n_ctx)], axis=-1
        ).reshape(rows, width)

        output_lo = rest[:, :width].reshape(n_ctx, group, width)
        output_lo = jnp.concatenate(reorder([output_lo[j] for j in range(n_ctx)], me), axis=0)
        expand_lo = rest[:, width : width + hidden]
        shrink_lo = (
            rest[:, width + hidden :].reshape(n_dp * n_ctx, part, spans, width).transpose(0, 2, 1, 3)
        ).reshape(hidden, width)

        flat_in = tokens_in.reshape(rows, width).astype(F32)
        residual = flat_in + (dot(mixed, output_lo, ((1,), (0,))) + params[4])
        normed_two, norm_two_back = jax.vjp(norm_rows, residual, params[5], params[6])
        normed_two_lo = normed_two.astype(BF16)
        expanded = dot(normed_two_lo, expand_lo, ((1,), (0,))) + params[7 : 7 + spans].reshape(hidden)
        activated, gelu_back = jax.vjp(jax.nn.gelu, expanded)
        activated_lo = activated.astype(BF16)
        result = residual + dot(activated_lo, shrink_lo, ((1,), (0,))) + params[7 + spans]
        block_output = result.reshape(tokens_in.shape).astype(BF16)

        labels = [("dp", bit) for bit in reversed(dp_bits)] + [("ctx", bit) for bit in reversed(ctx_bits)]
        bit_dims = (2,) * len(labels)
        near_first = [("ctx", bit) for bit in ctx_bits] + [("dp", bit) for bit in dp_bits]
        far_last = [("ctx", ctx_bits[0])] + [("dp", bit) for bit in dp_bits[1:]]
        far_last += [("dp", dp_bits[0])] + [("ctx", bit) for bit in ctx_bits[1:]]

        upstream = cotangent.reshape(rows, width)
        grad_shrink = dot(activated_lo, upstream, ((0,), (0,)))
        sum_shrink = halve(grad_shrink.reshape(bit_dims + (spans * part, width)), labels, near_first, spots)
        grad_bias_shrink = jnp.sum(upstream, axis=0, dtype=F32)
        grad_act = dot(upstream, shrink_lo, ((1,), (1,)))
        (grad_pre,) = gelu_back(grad_act)
        grad_pre_lo = grad_pre.astype(BF16)
        grad_expand = dot(normed_two_lo, grad_pre_lo, ((0,), (0,)))
        sum_expand = halve(grad_expand.reshape(bit_dims + (part, hidden)), labels, far_last, spots)
        grad_bias_expand = jnp.sum(grad_pre_lo, axis=0, dtype=F32)
        grad_normed_two = dot(grad_pre_lo, expand_lo, ((1,), (1,)))
        grad_resid_norm, grad_gain_two, grad_shift_two = norm_two_back(grad_normed_two)
        grad_resid = upstream.astype(F32) + grad_resid_norm
        grad_branch_lo = grad_resid.astype(BF16)
        grad_bias_out = jnp.sum(grad_branch_lo, axis=0, dtype=F32)
        grad_mixed = dot(grad_branch_lo, output_lo, ((1,), (1,))).astype(BF16).reshape(seqs, stretch, n_ctx, group)
        grad_pieces = jnp.stack(
            [grad_mixed[:, :, 0]] + [swap(grad_mixed[:, :, k], "ctx", k) for k in range(1, n_ctx)]
        )
        grad_output = dot(mixed, grad_branch_lo, ((0,), (0,))).reshape(n_ctx, group, width)
        grad_output = jnp.concatenate(reorder([grad_output[k] for k in range(n_ctx)], me), axis=0)
        sum_output = halve(grad_output.reshape(bit_dims + (part, width)), labels, near_first, spots)

        grad_joint_lo = attend_backward(me_arr, joint_blocks, grad_pieces, start, logs).reshape(n_ctx * rows, cols)

        grad_share = dot(grad_joint_lo, joint_lo, ((1,), (1,)))
        plain_all = norm_plain(tokens_all.astype(F32))
        grad_gain_one = jnp.sum(grad_share * plain_all, axis=0)
        grad_shift_one = jnp.sum(grad_share, axis=0)
        shares = {k: value for k, value in enumerate(grad_share.reshape(n_ctx, rows, width))}
        for bit in ctx_bits:
            mask = 1 << bit
            kept = {k: value for k, value in shares.items() if not k & mask}
            shares = {k: value + swap(shares[k | mask].astype(BF16), "ctx", mask).astype(F32) for k, value in kept.items()}
        _, norm_one_back = jax.vjp(norm_rows, flat_in, params[0], params[1])
        input_grad = (grad_resid + norm_one_back(shares[0])[0]).reshape(tokens_in.shape)

        grad_joint = dot(normed_lo, grad_joint_lo, ((0,), (0,)))
        grad_bias_joint = jnp.sum(grad_joint_lo, axis=0, dtype=F32)
        placed = lax.dynamic_update_slice(
            jnp.zeros((2, width), F32),
            jnp.stack([grad_bias_joint[:group], grad_bias_joint[2 * group :]]),
            (0, me * group),
        )
        grad_small = jnp.concatenate(
            [
                grad_gain_one[None],
                grad_shift_one[None],
                placed,
                grad_bias_out[None],
                grad_gain_two[None],
                grad_shift_two[None],
                grad_bias_expand.reshape(spans, width),
                grad_bias_shrink[None],
            ],
            axis=0,
        )
        small_terms = grad_small.reshape(vectors, n_dp, n_ctx, part).transpose(1, 2, 0, 3)
        small_terms = jnp.pad(small_terms.reshape(n_dp, n_ctx, vectors * part), ((0, 0), (0, 0), (0, pad)))
        terms = jnp.concatenate(
            [grad_joint.reshape(n_dp, n_ctx, part, cols), small_terms.reshape(n_dp, n_ctx, extra, cols)], axis=2
        ).reshape((2,) * n_bits + (n_ctx, part + extra, cols))
        dp_labels = [("dp", bit) for bit in reversed(dp_bits)]
        terms = halve(terms, dp_labels, [("dp", bit) for bit in dp_bits], spots)

        def terms_for(k):
            return lax.dynamic_index_in_dim(terms, lax.bitwise_xor(me, k), 0, keepdims=False)

        arrived = [terms_for(0)] + [
            swap(terms_for(k).astype(BF16), "ctx", k).astype(F32) for k in range(1, n_ctx)
        ]
        small_sum = sum(item[part:] for item in arrived).reshape(-1)[: vectors * part].reshape(vectors, part)
        sum_joint = jnp.stack([item[:part].reshape(part, 3, group) for item in reorder(arrived, me)], axis=2)
        sum_joint = sum_joint.reshape(part, 3 * width)

        new_joint, first_joint, second_joint = adam_step(
            joint_weight, sum_joint, momentum_joint, variance_joint, RATE_MATRIX, WEIGHT_DECAY
        )
        new_output, first_output, second_output = adam_step(
            output_weight, sum_output, momentum_output, variance_output, RATE_MATRIX, WEIGHT_DECAY
        )
        new_expand, first_expand, second_expand = adam_step(
            expand_weight, sum_expand, momentum_expand, variance_expand, RATE_MATRIX, WEIGHT_DECAY
        )
        new_shrink, first_shrink, second_shrink = adam_step(
            shrink_weight, sum_shrink, momentum_shrink, variance_shrink, RATE_MATRIX, WEIGHT_DECAY
        )
        new_small, first_small, second_small = adam_step(
            small_params, small_sum, momentum_small, variance_small, RATE_VECTOR, 0.0
        )
        return (
            block_output,
            input_grad,
            new_joint,
            new_output,
            new_expand,
            new_shrink,
            first_joint,
            first_output,
            first_expand,
            first_shrink,
            second_joint,
            second_output,
            second_expand,
            second_shrink,
            new_small,
            first_small,
            second_small,
        )

    return per_device


def solution(mesh):
    sizes = {axis: mesh.shape[axis] for axis in ("dp", "ctx")}
    tokens = P("dp", "ctx", None)
    matrix = P(("dp", "ctx"), None)
    table = P(None, ("dp", "ctx"))
    return jax.shard_map(
        build(sizes),
        mesh=mesh,
        in_specs=(tokens, P("dp", "ctx"), tokens) + (matrix,) * 12 + (table,) * 3,
        out_specs=(tokens, tokens) + (matrix,) * 12 + (table,) * 3,
        check_vma=False,
    )
```

time: 1260 us -> 615 us (0.49)
  waiting for transfers between devices: 728 us -> 157 us
  matrix products: 226 us -> 107 us
  Pallas kernels: 0 us -> 66.8 us
  starting transfers between devices: 0.49 us -> 45.8 us
  blocking collectives: 89.5 us -> 45.2 us
    reduce_scatter x6 -> x0, waiting for transfers between devices: 520 us -> none  [the longest x1 135 us: per_device(): lax.psum_scatter(grad_shrink, ('dp', 'ctx'), scatter_dimension=0, tiled=T...]
    all_gather x6 -> x1, waiting for transfers between devices: 208 us -> 0.01 us  [per_device(): lax.all_gather(jnp.concatenate([output_cast, expand_cast, shrink_wide], a...]
    ppermute x0 -> x39, waiting for transfers between devices: none -> 157 us  [swap(): lax.ppermute(value, axis, [(place, place ^ mask) for place in range(sizes...]
    dot_general x40 -> x12, matrix products: 226 us -> 107 us  [dot(): lax.dot_general(left, right, (dims, ((), ())), preferred_element_type=F32)]
    pallas_call x0 -> x2, Pallas kernels: none -> 66.8 us  [the longest x1 36.3 us: attend_backward(): pl.pallas_call(functools.partial(backward_kernel, n_blk, blk, heads), gri...]
    ppermute x0 -> x39, starting transfers between devices: none -> 45.8 us  [swap(): lax.ppermute(value, axis, [(place, place ^ mask) for place in range(sizes...]
    dynamic_update_slice x28 -> x1, local copies, waits for them, and re-layouts: 42.1 us -> 0.17 us  [per_device(): lax.dynamic_update_slice(jnp.zeros((2, width), F32), jnp.stack([grad_bias...]
    unnamed x1 -> x0, blocking collectives: 40.4 us -> none
  transfers between devices with their start and end apart: 12 -> 40, of which waited for: 11 -> 21; matrix products, arithmetic and copies ran while one was open for 12% -> 29% of each run, Pallas kernels for 0% -> 11%
where the time goes in v1:
time: 615 us; the launch traced here: 606 us
  waiting for transfers between devices  157 us (26%)
  matrix products  107 us (17%)
  local copies, waits for them, and re-layouts  100 us (16%)
  other arithmetic  68.2 us (11%)
  Pallas kernels  66.8 us (11%)
  starting transfers between devices  45.8 us (7%)
  blocking collectives  45.2 us (7%)
  between operations  15.7 us (3%)
    ppermute x39, waiting for transfers between devices, swap(): lax.ppermute(value, axis, [(place, place ^ mask) for place in range(sizes...  157 us
    dot_general x12, matrix products, dot(): lax.dot_general(left, right, (dims, ((), ())), preferred_element_type=F32)  107 us
    ppermute x39, starting transfers between devices, swap(): lax.ppermute(value, axis, [(place, place ^ mask) for place in range(sizes...  45.8 us
    all_gather x1, blocking collectives, per_device(): segs_all = lax.all_gather(segments.astype(BF16), 'ctx', axis=1, tiled=True)  45.2 us
    pallas_call x1, Pallas kernels, attend_backward(): pl.pallas_call(functools.partial(backward_kernel, n_blk, blk, heads), gri...  36.3 us
    pallas_call x1, Pallas kernels, attend_forward(): pl.pallas_call(functools.partial(forward_kernel, n_blk, blk, heads), grid...  30.4 us
    add x15, other arithmetic, halve(): value = keep + swap(send, axis, 1 << bit).astype(F32)  13.4 us
  transfers between devices with their start and end apart: 40, of which 21 were waited for; matrix products, arithmetic and copies ran while one was open for 29% of the time, Pallas kernels for 11%

profile of v1, /device:TPU:0, one launch (start us, length us, event | category | flops | bytes accessed | tf_op | source)
XLA Modules:
  0.0 606.3 jit_solution(11386101162664617323)
XLA Ops:
  13.2 2.6 collective-permute-start.1
  19.4 45.2 %all_gather.6 = bf16[4,1024]{1,0:T(4,128)(2,1)S(1)} all-gather(bf16[4,256]{1,0:T(4,128)(2,1)S(1)} %convert_element_type.351), channel_id=1, replica_groups=mesh['dp'=8,'ctx'=4] {'ctx'}, dimensions={1}, use_global_device_ids=true | all-gather | bytes 10240 | tf_op jit(solution)/shard_map/all_gather | solution.py:293
  64.6 2.5 convert_reduce_fusion
  68.2 3.6 collective-permute-start.6
  72.4 8.2 %collective-permute-done.6 = bf16[4,25,576]{2,1,0:T(8,128)(2,1)S(1)} collective-permute-done((bf16[4,25,576]{2,1,0:T(8,128)(2,1)S(1)}, bf16[4,25,576]{2,1,0:T(8,128)(2,1)S(1)}, u32[]{:S(2)}, u32[]{:S(2)}) %collective-permute-start.6) | collective-permute-done | bytes 115232 | tf_op jit(solution)/shard_map/ppermute | solution.py:201
  84.0 25.4 %collective-permute-done.7 = bf16[2,4,25,576]{3,2,1,0:T(8,128)(2,1)} collective-permute-done((bf16[2,4,25,576]{3,2,1,0:T(8,128)(2,1)}, bf16[2,4,25,576]{3,2,1,0:T(8,128)(2,1)}, u32[]{:S(2)}, u32[]{:S(2)}) %collective-permute-start.7) | collective-permute-done | bytes 230432 | tf_op jit(solution)/shard_map/ppermute | solution.py:201
  117.0 8.5 %collective-permute-done.8 = bf16[2,2,4,25,576]{4,2,3,1,0:T(4,128)(2,1)} collective-permute-done((bf16[2,2,4,25,576]{4,2,3,1,0:T(4,128)(2,1)}, bf16[2,2,4,25,576]{4,2,3,1,0:T(4,128)(2,1)}, u32[]{:S(2)}, u32[]{:S(2)}) %collective-permute-start.8) | collective-permute-done | bytes 460832 | tf_op jit(solution)/shard_map/ppermute | solution.py:201
  129.1 2.3 copy.253
  135.8 4.5 convert_reduce_fusion.2
  140.9 4.3 multiply_reduce_fusion.1
  145.9 4.6 add_convert_fusion.1
  150.5 5.8 add_convert_fusion.2
  156.2 7.6 %copy.255 = bf16[4096,576]{1,0:T(8,128)(2,1)} copy(bf16[4096,576]{0,1:T(8,128)(2,1)} %add_convert_fusion.2) | data formatting | bytes 9437184 | tf_op jit(solution)/shard_map/convert_element_type | solution.py:301
  163.9 30.4 %attend_forward.1 = (bf16[4,4,256,192]{3,2,1,0:T(8,128)(2,1)S(1)}, f32[4,3,1024]{2,1,0:T(4,128)S(1)}) custom-call(s32[1]{0:T(128)} %bitcast.1.me_ref, bf16[4,4,256,576]{3,2,1,0:T(8,128)(2,1)} %bitcast.314, s32[4,1,1024]{2,1,0:T(1,128)S(1)} %convert_element_type.354.start_ref), custom_call_target="tpu_custom_call" | custom-call | flops 2415919104 | bytes 7077888 | tf_op jit(solution)/shard_map/attend_forward/pallas_call | solution.py:131
  199.7 4.8 slice.247
  204.5 9.9 %reshape.627 = bf16[32,24,4,768]{3,2,1,0:T(4,128)(2,1)} reshape(bf16[768,3072]{1,0:T(8,128)(2,1)} %slice.247) | data formatting | bytes 9437184 | tf_op jit(solution)/shard_map/reshape | solution.py:312
  214.4 3.3 copy.261
  218.1 3.4 collective-permute-done.10
  221.5 3.0 fusion.93
  225.3 14.5 %fusion.14 = (bf16[3072,1024]{0,1:T(8,128)(2,1)}, f32[1024,3072]{1,0:T(8,128)}) fusion(f32[3072]{0:T(1024)S(1)} %copy-done.38, bf16[768,6912]{1,0:T(8,128)(2,1)} %all-gather.2.cloned.1.call-done, f32[1024,768]{1,0:T(8,128)S(1)} %get-tuple-element.126, f32[768]{0:T(1024)S(1)} %add.419, f32[768]{0:T(1024)S(1)} %mul.387, f32[1024]{0:T(1024)S(1)} %fusion.62, ...), kind=kOutput, calls=%fused_computation.18 | convolution fusion | flops 4867227648 | bytes 26765312 | tf_op jit(solution)/shard_map/dot_general | solution.py:48
  239.8 14.0 %convert_reduce_fusion.1 = (f32[3072]{0:T(1024)S(1)}, bf16[1024,3072]{1,0:T(8,128)(2,1)S(1)}) fusion(f32[1024,3072]{1,0:T(8,128)} %get-tuple-element.132, f32[3072]{0:T(1024)S(1)} %copy-done.38, bf16[3072,768]{1,0:T(8,128)(2,1)S(1)} %bitcast.318, bf16[1024,768]{1,0:T(8,128)(2,1)S(1)} %bitcast.302), kind=kOutput, calls=%fused_computation.26 | convolution fusion | flops 4904186880 | bytes 25190400 | tf_op jit(solution)/shard_map/dot_general | solution.py:48
  253.9 8.7 %fusion.77 = f32[768,3072]{1,0:T(8,128)} fusion(bf16[1024,3072]{1,0:T(8,128)(2,1)S(1)} %get-tuple-element.130, f32[1024,768]{1,0:T(8,128)S(1)} %get-tuple-element.126, f32[768]{0:T(1024)S(1)} %add.419, f32[768]{0:T(1024)S(1)} %mul.387, f32[1024]{0:T(1024)S(1)} %fusion.62, f32[1024]{0:T(1024)S(1)} %broadcast_multiply_fusion.2), kind=kOutput, calls=%fused_computation.260 | convolution fusion | flops 4835770368 | bytes 18888704 | tf_op jit(solution)/shard_map/dot_general | solution.py:48
  262.6 8.0 %multiply_reduce_fusion.2 = (f32[768]{0:T(1024)S(1)}, f32[1024]{0:T(1024)S(1)}, f32[768]{0:T(1024)S(1)}, f32[1024,768]{1,0:T(8,128)S(1)}) fusion(f32[1024,768]{1,0:T(8,128)S(1)} %get-tuple-element.126, f32[1024]{0:T(1024)S(1)} %fusion.62, f32[1024]{0:T(1024)S(1)} %broadcast_multiply_fusion.2, f32[768]{0:T(1024)S(1)} %mul.387, ...), kind=kOutput, calls=%fused_computation.64 | convolution fusion | flops 4838126592 | bytes 17323008 | tf_op jit(solution)/shard_map/dot_general | solution.py:48
  273.8 4.5 fusion.61
  278.3 2.6 convolution_convert_fusion
  280.9 8.7 %copy.279 = bf16[3072,1024]{1,0:T(8,128)(2,1)} copy(bf16[3072,1024]{0,1:T(8,128)(2,1)} %get-tuple-element.131) | data formatting | bytes 12582912 | tf_op jit(solution)/shard_map/convert_element_type | solution.py:321
  289.6 13.8 %add_convert_fusion.3 = bf16[1024,768]{1,0:T(8,128)(2,1)} fusion(f32[1024,768]{1,0:T(8,128)} %copy-done.1, bf16[3072,768]{1,0:T(8,128)(2,1)} %bitcast.319, f32[1024,3072]{1,0:T(8,128)} %get-tuple-element.132, f32[3072]{0:T(1024)S(1)} %copy-done.38, f32[768]{0:T(1024)S(1)} %copy-done.41), kind=kOutput, calls=%fused_computation.69 | convolution fusion | flops 4865654784 | bytes 22035456 | tf_op jit(solution)/shard_map/dot_general | solution.py:48
  307.2 5.3 reshape.644
  315.4 3.3 fusion.88
  321.3 4.1 fusion.33
  325.7 5.1 fusion.95
  333.8 10.8 %collective-permute-done.13 = bf16[4,256,192]{2,1,0:T(8,128)(2,1)S(1)} collective-permute-done((bf16[4,256,192]{2,1,0:T(8,128)(2,1)S(1)}, bf16[4,256,192]{2,1,0:T(8,128)(2,1)S(1)}, u32[]{:S(2)}, u32[]{:S(2)}) %collective-permute-start.13) | collective-permute-done | bytes 393248 | tf_op jit(solution)/shard_map/ppermute | solution.py:201
  345.2 36.3 %attend_backward.1 = bf16[4,4,256,576]{3,2,1,0:T(8,128)(2,1)} custom-call(s32[1]{0:T(128)} %bitcast.1.me_ref, bf16[4,4,256,576]{3,2,1,0:T(8,128)(2,1)} %bitcast.315, bf16[4,4,256,192]{3,2,1,0:T(8,128)(2,1)S(1)} %pad_maximum_fusion.3.grad_ref, s32[4,1,1024]{2,1,0:T(1,128)S(1)} %convert_element_type.354.start_ref, f32[4,3,1024]{2,1,0:T(4,128)S(1)} %get-tuple-element.30.log_ref), custom_call_target="tpu_custom_call" | custom-call | flops 5637144576 | bytes 14155776 | tf_op jit(solution)/shard_map/attend_backward/pallas_call | solution.py:165
  381.5 3.4 convert_reduce_fusion.3
  385.3 18.4 %fusion.78 = (f32[768]{0:T(1024)S(1)}, f32[768]{0:T(1024)S(1)}, bf16[4096,768]{1,0:T(8,128)(2,1)}, bf16[4096,768]{1,0:T(8,128)(2,1)}, f32[4096,768]{1,0:T(8,128)}) fusion(f32[4096]{0:T(1024)S(1)} %bitcast.354, f32[4096]{0:T(1024)S(1)} %bitcast.353, bf16[1,4,256,768]{3,2,1,0:T(8,128)(2,1)} %bitcast.5, bf16[1,4,256,768]{3,2,1,0:T(8,128)(2,1)} %bitcast.4, ...), kind=kOutput, calls=%fused_computation.261 | convolution fusion | flops 3664771584 | bytes 37105664 | tf_op jit(solution)/shard_map/dot_general | solution.py:48
  404.4 3.8 fusion.87
  408.2 8.7 %copy.268 = bf16[768,4096]{1,0:T(8,128)(2,1)} copy(bf16[768,4096]{0,1:T(8,128)(2,1)} %bitcast.311) | data formatting | bytes 12582912 | tf_op jit(solution)/shard_map/dot_general | solution.py:48
  419.3 8.9 %fusion.94 = f32[2,2,2,4,24,576]{5,4,3,2,1,0:T(8,128)S(1)} fusion(bf16[2,2,2,4,24,4096]{5,4,3,2,1,0:T(8,128)(2,1)} %bitcast.312, bf16[4096,576,1,1,1,1]{1,0,5,4,3,2:T(8,128)(2,1)} %bitcast.317), kind=kOutput, calls=%fused_computation.271 | convolution fusion | flops 3623878656 | bytes 12779520 | tf_op jit(solution)/shard_map/dot_general | solution.py:48
  430.2 12.2 %collective-permute-done.18 = bf16[2,2,4,25,576]{4,2,3,1,0:T(4,128)(2,1)S(1)} collective-permute-done((bf16[2,2,4,25,576]{4,2,3,1,0:T(4,128)(2,1)S(1)}, bf16[2,2,4,25,576]{4,2,3,1,0:T(4,128)(2,1)S(1)}, u32[]{:S(2)}, u32[]{:S(2)}) %collective-permute-start.18) | collective-permute-done | bytes 460832 | tf_op jit(solution)/shard_map/ppermute | solution.py:201
  444.5 3.0 collective-permute-done.26
  447.6 6.5 %collective-permute-done.19 = bf16[2,4,25,576]{3,1,2,0:T(4,128)(2,1)S(1)} collective-permute-done((bf16[2,4,25,576]{3,1,2,0:T(4,128)(2,1)S(1)}, bf16[2,4,25,576]{3,1,2,0:T(4,128)(2,1)S(1)}, u32[]{:S(2)}, u32[]{:S(2)}) %collective-permute-start.19) | collective-permute-done | bytes 230432 | tf_op jit(solution)/shard_map/ppermute | solution.py:201
  454.3 4.2 collective-permute-done.27
  458.5 6.1 %collective-permute-start.28 = (bf16[24,768]{1,0:T(8,128)(2,1)S(1)}, bf16[24,768]{1,0:T(8,128)(2,1)S(1)}, u32[]{:S(2)}, u32[]{:S(2)}) collective-permute-start(bf16[24,768]{1,0:T(8,128)(2,1)S(1)} %fusion.59), channel_id=1, source_target_pairs={{0,16},{4,20},{8,24},{12,28},{16,0},{20,4},{24,8},{28,12},{1,17},{... | collective-permute-start | bytes 110600 | tf_op jit(solution)/shard_map/ppermute | solution.py:201
  464.7 2.2 collective-permute-done.28
  466.9 3.1 collective-permute-start.20
  470.7 2.2 collective-permute-done.20
  473.4 3.9 collective-permute-done.22
  478.6 3.3 collective-permute-done.23
  487.4 2.2 multiply_subtract_fusion.2
  491.7 3.7 bitcast_add_fusion.1
  495.4 2.2 copy-done.5
  498.8 2.5 collective-permute-start.30
  501.4 2.8 fusion.24
  504.4 3.7 bitcast_add_fusion
  511.0 16.9 %collective-permute-done.30 = bf16[2,2,2,24,3072]{4,3,2,1,0:T(8,128)(2,1)} collective-permute-done((bf16[2,2,2,24,3072]{4,3,2,1,0:T(8,128)(2,1)}, bf16[2,2,2,24,3072]{4,3,2,1,0:T(8,128)(2,1)}, u32[]{:S(2)}, u32[]{:S(2)}) %collective-permute-start.30) | collective-permute-done | bytes 1179680 | tf_op jit(solution)/shard_map/ppermute | solution.py:201
  530.5 3.3 collective-permute-start.31
  533.7 32.1 %collective-permute-done.35 = bf16[2,2,2,96,768]{4,3,2,1,0:T(8,128)(2,1)S(1)} collective-permute-done((bf16[2,2,2,96,768]{4,3,2,1,0:T(8,128)(2,1)S(1)}, bf16[2,2,2,96,768]{4,3,2,1,0:T(8,128)(2,1)S(1)}, u32[]{:S(2)}, u32[]{:S(2)}) %collective-permute-start.35) | collective-permute-done | bytes 1179680 | tf_op jit(solution)/shard_map/ppermute | solution.py:201
  567.0 2.6 fusion.29
  569.7 3.1 fusion.85
  572.8 2.4 add_add_fusion.2
  577.8 4.7 collective-permute-done.36
  583.1 3.8 collective-permute-done.32
  589.6 4.9 collective-permute-start.38
  595.6 2.6 collective-permute-done.38
  (336 shorter events, 87.5 us)
Async XLA Ops:
  7.2 59.9 %copy-start = (bf16[4,256,768]{2,1,0:T(8,128)(2,1)S(1)}, bf16[4,256,768]{2,1,0:T(8,128)(2,1)}, u32[]{:S(2)}) copy-start(bf16[4,256,768]{2,1,0:T(8,128)(2,1)} %param.18) | copy-start | bytes 4718596
  7.2 12.2 %copy-start.42 = (s32[4,256]{1,0:T(4,128)S(1)}, s32[4,256]{1,0:T(4,128)}, u32[]{:S(2)}) copy-start(s32[4,256]{1,0:T(4,128)} %param.19) | copy-start | bytes 12292
  7.2 190.4 %all-gather.2.cloned.1.call-start = ((), (), s32[]{:S(2)}) async-start(), calls=%async_computation | async-start | bytes 10948608 | tf_op jit(solution)/shard_map/all_gather | solution.py:262
  12.7 123.2 %collective-permute-start = (bf16[4,256,768]{2,1,0:T(8,128)(2,1)}, bf16[4,256,768]{2,1,0:T(8,128)(2,1)}, u32[]{:S(2)}, u32[]{:S(2)}) collective-permute-start(bf16[4,256,768]{2,1,0:T(8,128)(2,1)} %param.18), channel_id=1, source_target_pairs={{0,1},{1,0},{2,3},{3,2},{4,5},{5,4},{6,7},{7,6},{8,9},{9,8},{10,11... | collective-permute-start | bytes 4718600 | tf_op jit(solution)/shard_map/ppermute | solution.py:201
  13.2 70.8 %collective-permute-start.1 = (bf16[4,256,768]{2,1,0:T(8,128)(2,1)}, bf16[4,256,768]{2,1,0:T(8,128)(2,1)}, u32[]{:S(2)}, u32[]{:S(2)}) collective-permute-start(bf16[4,256,768]{2,1,0:T(8,128)(2,1)} %param.18), channel_id=1, source_target_pairs={{0,2},{1,3},{2,0},{3,1},{4,6},{5,7},{6,4},{7,5},{8,10},{9,11},{10,... | collective-permute-start | bytes 4718600 | tf_op jit(solution)/shard_map/ppermute | solution.py:201
  17.5 50.5 %collective-permute-start.3 = (bf16[25,576]{1,0:T(8,128)(2,1)S(1)}, bf16[25,576]{1,0:T(8,128)(2,1)S(1)}, u32[]{:S(2)}, u32[]{:S(2)}) collective-permute-start(bf16[25,576]{1,0:T(8,128)(2,1)S(1)} %get-tuple-element.122), channel_id=1, source_target_pairs={{0,1},{1,0},{2,3},{3,2},{4,5},{5,4},{6,7},{7,6},{8,9},{9,8},{10,11... | collective-permute-start | bytes 86408 | tf_op jit(solution)/shard_map/ppermute | solution.py:201
  17.7 50.3 %collective-permute-start.4 = (bf16[25,576]{1,0:T(8,128)(2,1)S(1)}, bf16[25,576]{1,0:T(8,128)(2,1)S(1)}, u32[]{:S(2)}, u32[]{:S(2)}) collective-permute-start(bf16[25,576]{1,0:T(8,128)(2,1)S(1)} %get-tuple-element.123), channel_id=1, source_target_pairs={{0,2},{1,3},{2,0},{3,1},{4,6},{5,7},{6,4},{7,5},{8,10},{9,11},{10,... | collective-permute-start | bytes 86408 | tf_op jit(solution)/shard_map/ppermute | solution.py:201
  18.0 50.0 %collective-permute-start.5 = (bf16[25,576]{1,0:T(8,128)(2,1)S(1)}, bf16[25,576]{1,0:T(8,128)(2,1)S(1)}, u32[]{:S(2)}, u32[]{:S(2)}) collective-permute-start(bf16[25,576]{1,0:T(8,128)(2,1)S(1)} %get-tuple-element.124), channel_id=1, source_target_pairs={{0,3},{1,2},{2,1},{3,0},{4,7},{5,6},{6,5},{7,4},{8,11},{9,10},{10,... | collective-permute-start | bytes 86408 | tf_op jit(solution)/shard_map/ppermute | solution.py:201
  68.1 46.4 %copy-start.36 = (f32[4,1024]{1,0:T(4,128)S(1)}, f32[4,1024]{1,0:T(4,128)}, u32[]{:S(2)}) copy-start(f32[4,1024]{1,0:T(4,128)} %convert_reduce_fusion) | copy-start | bytes 49156
  68.1 46.4 %copy-start.6 = (bf16[4,256,768]{2,1,0:T(8,128)(2,1)S(1)}, bf16[4,256,768]{2,1,0:T(8,128)(2,1)}, u32[]{:S(2)}) copy-start(bf16[4,256,768]{2,1,0:T(8,128)(2,1)} %param.20) | copy-start | bytes 4718596
  68.2 12.5 %collective-permute-start.6 = (bf16[4,25,576]{2,1,0:T(8,128)(2,1)S(1)}, bf16[4,25,576]{2,1,0:T(8,128)(2,1)S(1)}, u32[]{:S(2)}, u32[]{:S(2)}) collective-permute-start(bf16[4,25,576]{2,1,0:T(8,128)(2,1)S(1)} %get-tuple-element.104), channel_id=1, source_target_pairs={{0,16},{4,20},{8,24},{12,28},{16,0},{20,4},{24,8},{28,12},{1,17},{... | collective-permute-start | bytes 345608 | tf_op jit(solution)/shard_map/ppermute | solution.py:201
  81.5 28.0 %collective-permute-start.7 = (bf16[2,4,25,576]{3,2,1,0:T(8,128)(2,1)}, bf16[2,4,25,576]{3,2,1,0:T(8,128)(2,1)}, u32[]{:S(2)}, u32[]{:S(2)}) collective-permute-start(bf16[2,4,25,576]{3,2,1,0:T(8,128)(2,1)} %maximum_select_fusion.3), channel_id=1, source_target_pairs={{0,8},{4,12},{8,0},{12,4},{16,24},{20,28},{24,16},{28,20},{1,9},{5... | collective-permute-start | bytes 691208 | tf_op jit(solution)/shard_map/ppermute | solution.py:201
  83.9 51.9 %collective-permute-start.2 = (bf16[4,256,768]{2,1,0:T(8,128)(2,1)}, bf16[4,256,768]{2,1,0:T(8,128)(2,1)}, u32[]{:S(2)}, u32[]{:S(2)}) collective-permute-start(bf16[4,256,768]{2,1,0:T(8,128)(2,1)} %collective-permute-done.1), channel_id=1, source_target_pairs={{0,1},{1,0},{2,3},{3,2},{4,5},{5,4},{6,7},{7,6},{8,9},{9,8},{10,11... | collective-permute-start | bytes 4718600 | tf_op jit(solution)/shard_map/ppermute | solution.py:201
  111.8 13.7 %collective-permute-start.8 = (bf16[2,2,4,25,576]{4,2,3,1,0:T(4,128)(2,1)}, bf16[2,2,4,25,576]{4,2,3,1,0:T(4,128)(2,1)}, u32[]{:S(2)}, u32[]{:S(2)}) collective-permute-start(bf16[2,2,4,25,576]{4,2,3,1,0:T(4,128)(2,1)} %copy.247), channel_id=1, source_target_pairs={{0,4},{4,0},{8,12},{12,8},{16,20},{20,16},{24,28},{28,24},{1,5},{5... | collective-permute-start | bytes 1382408 | tf_op jit(solution)/shard_map/ppermute | solution.py:201
  135.5 10.4 %copy-start.32 = (f32[768]{0:T(1024)}, f32[768]{0:T(1024)S(1)}, u32[]{:S(2)}) copy-start(f32[768]{0:T(1024)S(1)} %add.408) | copy-start | bytes 9220
  195.7 22.4 %collective-permute-start.11 = (bf16[4,256,192]{2,1,0:T(8,128)(2,1)}, bf16[4,256,192]{2,1,0:T(8,128)(2,1)}, u32[]{:S(2)}, u32[]{:S(2)}) collective-permute-start(bf16[4,256,192]{2,1,0:T(8,128)(2,1)} %get-tuple-element.86), channel_id=1, source_target_pairs={{0,3},{1,2},{2,1},{3,0},{4,7},{5,6},{6,5},{7,4},{8,11},{9,10},{10,... | collective-permute-start | bytes 1179656 | tf_op jit(solution)/shard_map/ppermute | solution.py:201
  196.0 25.5 %collective-permute-start.10 = (bf16[4,256,192]{2,1,0:T(8,128)(2,1)}, bf16[4,256,192]{2,1,0:T(8,128)(2,1)}, u32[]{:S(2)}, u32[]{:S(2)}) collective-permute-start(bf16[4,256,192]{2,1,0:T(8,128)(2,1)} %get-tuple-element.87), channel_id=1, source_target_pairs={{0,2},{1,3},{2,0},{3,1},{4,6},{5,7},{6,4},{7,5},{8,10},{9,11},{10,... | collective-permute-start | bytes 1179656 | tf_op jit(solution)/shard_map/ppermute | solution.py:201
  197.3 24.2 %collective-permute-start.9 = (bf16[4,256,192]{2,1,0:T(8,128)(2,1)}, bf16[4,256,192]{2,1,0:T(8,128)(2,1)}, u32[]{:S(2)}, u32[]{:S(2)}) collective-permute-start(bf16[4,256,192]{2,1,0:T(8,128)(2,1)} %get-tuple-element.88), channel_id=1, source_target_pairs={{0,1},{1,0},{2,3},{3,2},{4,5},{5,4},{6,7},{7,6},{8,9},{9,8},{10,11... | collective-permute-start | bytes 1179656 | tf_op jit(solution)/shard_map/ppermute | solution.py:201
  217.8 22.0 %copy-start.9 = (bf16[32,4,24,768]{3,2,1,0:T(8,128)(2,1)}, bf16[32,4,24,768]{3,2,1,0:T(8,128)(2,1)S(1)}, u32[]{:S(2)}) copy-start(bf16[32,4,24,768]{3,2,1,0:T(8,128)(2,1)S(1)} %copy.261) | copy-start | bytes 14155780
  224.5 46.1 %copy-start.1 = (f32[1024,768]{1,0:T(8,128)}, f32[1024,768]{1,0:T(8,128)S(1)}, u32[]{:S(2)}) copy-start(f32[1024,768]{1,0:T(8,128)S(1)} %get-tuple-element.126) | copy-start | bytes 9437188
  315.4 101.6 %collective-permute-start.24 = (bf16[2,2,2,2,24,768]{5,4,3,2,1,0:T(8,128)(2,1)}, bf16[2,2,2,2,24,768]{5,4,3,2,1,0:T(8,128)(2,1)}, u32[]{:S(2)}, u32[]{:S(2)}) collective-permute-start(bf16[2,2,2,2,24,768]{5,4,3,2,1,0:T(8,128)(2,1)} %fusion.42), channel_id=1, source_target_pairs={{0,1},{1,0},{2,3},{3,2},{4,5},{5,4},{6,7},{7,6},{8,9},{9,8},{10,11... | collective-permute-start | bytes 1769480 | tf_op jit(solution)/shard_map/ppermute | solution.py:201
  319.1 13.7 %collective-permute-start.14 = (bf16[4,256,192]{2,1,0:T(8,128)(2,1)S(1)}, bf16[4,256,192]{2,1,0:T(8,128)(2,1)S(1)}, u32[]{:S(2)}, u32[]{:S(2)}) collective-permute-start(bf16[4,256,192]{2,1,0:T(8,128)(2,1)S(1)} %bitcast.337), channel_id=1, source_target_pairs={{0,3},{1,2},{2,1},{3,0},{4,7},{5,6},{6,5},{7,4},{8,11},{9,10},{10,... | collective-permute-start | bytes 1179656 | tf_op jit(solution)/shard_map/ppermute | solution.py:201
  319.4 14.4 %collective-permute-start.12 = (bf16[4,256,192]{2,1,0:T(8,128)(2,1)S(1)}, bf16[4,256,192]{2,1,0:T(8,128)(2,1)S(1)}, u32[]{:S(2)}, u32[]{:S(2)}) collective-permute-start(bf16[4,256,192]{2,1,0:T(8,128)(2,1)S(1)} %bitcast.336), channel_id=1, source_target_pairs={{0,1},{1,0},{2,3},{3,2},{4,5},{5,4},{6,7},{7,6},{8,9},{9,8},{10,11... | collective-permute-start | bytes 1179656 | tf_op jit(solution)/shard_map/ppermute | solution.py:201
  319.9 24.7 %collective-permute-start.13 = (bf16[4,256,192]{2,1,0:T(8,128)(2,1)S(1)}, bf16[4,256,192]{2,1,0:T(8,128)(2,1)S(1)}, u32[]{:S(2)}, u32[]{:S(2)}) collective-permute-start(bf16[4,256,192]{2,1,0:T(8,128)(2,1)S(1)} %bitcast.335), channel_id=1, source_target_pairs={{0,2},{1,3},{2,0},{3,1},{4,6},{5,7},{6,4},{7,5},{8,10},{9,11},{10,... | collective-permute-start | bytes 1179656 | tf_op jit(solution)/shard_map/ppermute | solution.py:201
  325.5 166.3 %collective-permute-start.29 = (bf16[2,2,2,2,24,3072]{5,4,3,2,0,1:T(8,128)(2,1)}, bf16[2,2,2,2,24,3072]{5,4,3,2,0,1:T(8,128)(2,1)}, u32[]{:S(2)}, u32[]{:S(2)}) collective-permute-start(bf16[2,2,2,2,24,3072]{5,4,3,2,0,1:T(8,128)(2,1)} %fusion.33), channel_id=1, source_target_pairs={{0,1},{1,0},{2,3},{3,2},{4,5},{5,4},{6,7},{7,6},{8,9},{9,8},{10,11... | collective-permute-start | bytes 7077896 | tf_op jit(solution)/shard_map/ppermute | solution.py:201
  330.8 13.9 %copy-start.8 = (f32[2,2,2,2,2,96,768]{6,5,4,3,2,1,0:T(8,128)}, f32[2,2,2,2,2,96,768]{6,5,4,3,2,1,0:T(8,128)S(1)}, u32[]{:S(2)}) copy-start(f32[2,2,2,2,2,96,768]{6,5,4,3,2,1,0:T(8,128)S(1)} %fusion.95) | copy-start | bytes 28311556
  332.8 171.6 %collective-permute-start.34 = (bf16[2,2,2,2,96,768]{5,4,3,2,1,0:T(8,128)(2,1)}, bf16[2,2,2,2,96,768]{5,4,3,2,1,0:T(8,128)(2,1)}, u32[]{:S(2)}, u32[]{:S(2)}) collective-permute-start(bf16[2,2,2,2,96,768]{5,4,3,2,1,0:T(8,128)(2,1)} %fusion.32), channel_id=1, source_target_pairs={{0,1},{1,0},{2,3},{3,2},{4,5},{5,4},{6,7},{7,6},{8,9},{9,8},{10,11... | collective-permute-start | bytes 7077896 | tf_op jit(solution)/shard_map/ppermute | solution.py:201
  385.3 18.7 %copy-start.26 = (f32[1,8,4,24]{3,2,1,0:T(4,128)S(1)}, f32[1,8,4,24]{3,2,1,0:T(4,128)}, u32[]{:S(2)}) copy-start(f32[1,8,4,24]{3,2,1,0:T(4,128)} %concatenate.127) | copy-start | bytes 9220
  408.2 158.8 %collective-permute-start.15 = (bf16[1024,768]{1,0:T(8,128)(2,1)}, bf16[1024,768]{1,0:T(8,128)(2,1)}, u32[]{:S(2)}, u32[]{:S(2)}) collective-permute-start(bf16[1024,768]{1,0:T(8,128)(2,1)} %get-tuple-element.71), channel_id=1, source_target_pairs={{0,1},{1,0},{2,3},{3,2},{4,5},{5,4},{6,7},{7,6},{8,9},{9,8},{10,11... | collective-permute-start | bytes 4718600 | tf_op jit(solution)/shard_map/ppermute | solution.py:201
  418.6 11.4 %collective-permute-start.25 = (bf16[2,2,2,24,768]{4,3,2,1,0:T(8,128)(2,1)S(1)}, bf16[2,2,2,24,768]{4,3,2,1,0:T(8,128)(2,1)S(1)}, u32[]{:S(2)}, u32[]{:S(2)}) collective-permute-start(bf16[2,2,2,24,768]{4,3,2,1,0:T(8,128)(2,1)S(1)} %fusion.47), channel_id=1, source_target_pairs={{0,2},{1,3},{2,0},{3,1},{4,6},{5,7},{6,4},{7,5},{8,10},{9,11},{10,... | collective-permute-start | bytes 884744 | tf_op jit(solution)/shard_map/ppermute | solution.py:201
  428.6 13.9 %collective-permute-start.18 = (bf16[2,2,4,25,576]{4,2,3,1,0:T(4,128)(2,1)S(1)}, bf16[2,2,4,25,576]{4,2,3,1,0:T(4,128)(2,1)S(1)}, u32[]{:S(2)}, u32[]{:S(2)}) collective-permute-start(bf16[2,2,4,25,576]{4,2,3,1,0:T(4,128)(2,1)S(1)} %copy.273), channel_id=1, source_target_pairs={{0,4},{4,0},{8,12},{12,8},{16,20},{20,16},{24,28},{28,24},{1,5},{5... | collective-permute-start | bytes 1382408 | tf_op jit(solution)/shard_map/ppermute | solution.py:201
  430.0 71.4 %collective-permute-start.16 = (bf16[1024,768]{1,0:T(8,128)(2,1)}, bf16[1024,768]{1,0:T(8,128)(2,1)}, u32[]{:S(2)}, u32[]{:S(2)}) collective-permute-start(bf16[1024,768]{1,0:T(8,128)(2,1)} %get-tuple-element.72), channel_id=1, source_target_pairs={{0,1},{1,0},{2,3},{3,2},{4,5},{5,4},{6,7},{7,6},{8,9},{9,8},{10,11... | collective-permute-start | bytes 4718600 | tf_op jit(solution)/shard_map/ppermute | solution.py:201
  430.2 39.8 %copy-start.21 = (f32[24,768]{1,0:T(8,128)S(1)}, f32[24,768]{1,0:T(8,128)}, u32[]{:S(2)}) copy-start(f32[24,768]{1,0:T(8,128)} %param.22) | copy-start | bytes 221188
  430.2 39.8 %copy-start.22 = (f32[24,768]{1,0:T(8,128)S(1)}, f32[24,768]{1,0:T(8,128)}, u32[]{:S(2)}) copy-start(f32[24,768]{1,0:T(8,128)} %param.26) | copy-start | bytes 221188
  430.2 39.8 %copy-start.23 = (f32[24,768]{1,0:T(8,128)S(1)}, f32[24,768]{1,0:T(8,128)}, u32[]{:S(2)}) copy-start(f32[24,768]{1,0:T(8,128)} %param.30) | copy-start | bytes 221188
  442.4 5.2 collective-permute-start.26
  447.6 6.6 %collective-permute-start.19 = (bf16[2,4,25,576]{3,1,2,0:T(4,128)(2,1)S(1)}, bf16[2,4,25,576]{3,1,2,0:T(4,128)(2,1)S(1)}, u32[]{:S(2)}, u32[]{:S(2)}) collective-permute-start(bf16[2,4,25,576]{3,1,2,0:T(4,128)(2,1)S(1)} %fusion.50), channel_id=1, source_target_pairs={{0,8},{4,12},{8,0},{12,4},{16,24},{20,28},{24,16},{28,20},{1,9},{5... | collective-permute-start | bytes 691208 | tf_op jit(solution)/shard_map/ppermute | solution.py:201
  454.2 4.4 collective-permute-start.27
  458.5 8.4 %collective-permute-start.28 = (bf16[24,768]{1,0:T(8,128)(2,1)S(1)}, bf16[24,768]{1,0:T(8,128)(2,1)S(1)}, u32[]{:S(2)}, u32[]{:S(2)}) collective-permute-start(bf16[24,768]{1,0:T(8,128)(2,1)S(1)} %fusion.59), channel_id=1, source_target_pairs={{0,16},{4,20},{8,24},{12,28},{16,0},{20,4},{24,8},{28,12},{1,17},{... | collective-permute-start | bytes 110600 | tf_op jit(solution)/shard_map/ppermute | solution.py:201
  466.9 6.0 collective-permute-start.20
  473.2 4.1 collective-permute-start.22
  477.2 1.2 collective-permute-start.21
  478.5 3.5 collective-permute-start.23
  498.8 29.1 %collective-permute-start.30 = (bf16[2,2,2,24,3072]{4,3,2,1,0:T(8,128)(2,1)}, bf16[2,2,2,24,3072]{4,3,2,1,0:T(8,128)(2,1)}, u32[]{:S(2)}, u32[]{:S(2)}) collective-permute-start(bf16[2,2,2,24,3072]{4,3,2,1,0:T(8,128)(2,1)} %fusion.39), channel_id=1, source_target_pairs={{0,8},{4,12},{8,0},{12,4},{16,24},{20,28},{24,16},{28,20},{1,9},{5... | collective-permute-start | bytes 3538952 | tf_op jit(solution)/shard_map/ppermute | solution.py:201
  501.4 26.5 %slice-start = ((s8[4718592]{0:T(1024)(128)(4,1)}), s8[4194304]{0:T(1024)(128)(4,1)S(1)}, s32[]{:S(2)}) async-start(s8[4718592]{0:T(1024)(128)(4,1)} %bitcast.300), calls=%async_computation.1 | async-start | bytes 8388608
  504.3 23.6 %slice-start.1 = ((s8[4718592]{0:T(1024)(128)(4,1)}), s8[524288]{0:T(1024)(128)(4,1)S(1)}, s32[]{:S(2)}) async-start(s8[4718592]{0:T(1024)(128)(4,1)} %bitcast.300), calls=%async_computation.2 | async-start | bytes 1048576
  504.3 62.7 %collective-permute-start.17 = (bf16[1024,768]{1,0:T(8,128)(2,1)S(1)}, bf16[1024,768]{1,0:T(8,128)(2,1)S(1)}, u32[]{:S(2)}, u32[]{:S(2)}) collective-permute-start(bf16[1024,768]{1,0:T(8,128)(2,1)S(1)} %fusion.24), channel_id=1, source_target_pairs={{0,2},{1,3},{2,0},{3,1},{4,6},{5,7},{6,4},{7,5},{8,10},{9,11},{10,... | collective-permute-start | bytes 4718600 | tf_op jit(solution)/shard_map/ppermute | solution.py:201
  504.4 62.6 %slice-start.2 = ((s8[12582912]{0:T(1024)(128)(4,1)}), s8[4194304]{0:T(1024)(128)(4,1)S(1)}, s32[]{:S(2)}) async-start(s8[12582912]{0:T(1024)(128)(4,1)} %bitcast.306), calls=%async_computation.3 | async-start | bytes 8388608
  504.4 62.6 %slice-start.3 = ((s8[12582912]{0:T(1024)(128)(4,1)}), s8[4194304]{0:T(1024)(128)(4,1)S(1)}, s32[]{:S(2)}) async-start(s8[12582912]{0:T(1024)(128)(4,1)} %bitcast.306), calls=%async_computation.4 | async-start | bytes 8388608
  508.3 57.5 %collective-permute-start.35 = (bf16[2,2,2,96,768]{4,3,2,1,0:T(8,128)(2,1)S(1)}, bf16[2,2,2,96,768]{4,3,2,1,0:T(8,128)(2,1)S(1)}, u32[]{:S(2)}, u32[]{:S(2)}) collective-permute-start(bf16[2,2,2,96,768]{4,3,2,1,0:T(8,128)(2,1)S(1)} %fusion.40), channel_id=1, source_target_pairs={{0,2},{1,3},{2,0},{3,1},{4,6},{5,7},{6,4},{7,5},{8,10},{9,11},{10,... | collective-permute-start | bytes 3538952 | tf_op jit(solution)/shard_map/ppermute | solution.py:201
  511.0 56.0 %slice-start.4 = ((s8[12582912]{0:T(1024)(128)(4,1)}), s8[4194304]{0:T(1024)(128)(4,1)S(1)}, s32[]{:S(2)}) async-start(s8[12582912]{0:T(1024)(128)(4,1)} %bitcast.306), calls=%async_computation.5 | async-start | bytes 8388608
  530.5 36.6 %copy-start.30 = (f32[1,2,4,128]{3,1,2,0:T(2,128)S(1)}, f32[1,2,4,128]{3,1,2,0:T(2,128)}, u32[]{:S(2)}) copy-start(f32[1,2,4,128]{3,1,2,0:T(2,128)} %copy.300) | copy-start | bytes 12292
  530.5 44.7 %collective-permute-start.31 = (bf16[2,2,24,3072]{3,2,1,0:T(8,128)(2,1)}, bf16[2,2,24,3072]{3,2,1,0:T(8,128)(2,1)}, u32[]{:S(2)}, u32[]{:S(2)}) collective-permute-start(bf16[2,2,24,3072]{3,2,1,0:T(8,128)(2,1)} %fusion.43), channel_id=1, source_target_pairs={{0,16},{4,20},{8,24},{12,28},{16,0},{20,4},{24,8},{28,12},{1,17},{... | collective-permute-start | bytes 1769480 | tf_op jit(solution)/shard_map/ppermute | solution.py:201
  566.2 16.3 %collective-permute-start.36 = (bf16[2,2,96,768]{3,2,1,0:T(8,128)(2,1)S(1)}, bf16[2,2,96,768]{3,2,1,0:T(8,128)(2,1)S(1)}, u32[]{:S(2)}, u32[]{:S(2)}) collective-permute-start(bf16[2,2,96,768]{3,2,1,0:T(8,128)(2,1)S(1)} %fusion.44), channel_id=1, source_target_pairs={{0,4},{4,0},{8,12},{12,8},{16,20},{20,16},{24,28},{28,24},{1,5},{5... | collective-permute-start | bytes 1769480 | tf_op jit(solution)/shard_map/ppermute | solution.py:201
  576.4 18.1 %copy-start.13 = (f32[24,3072]{1,0:T(8,128)S(1)}, f32[24,3072]{1,0:T(8,128)}, u32[]{:S(2)}) copy-start(f32[24,3072]{1,0:T(8,128)} %param.23) | copy-start | bytes 884740
  576.4 18.1 %copy-start.17 = (f32[24,3072]{1,0:T(8,128)S(1)}, f32[24,3072]{1,0:T(8,128)}, u32[]{:S(2)}) copy-start(f32[24,3072]{1,0:T(8,128)} %param.27) | copy-start | bytes 884740
  576.4 18.1 %copy-start.18 = (f32[24,3072]{1,0:T(8,128)S(1)}, f32[24,3072]{1,0:T(8,128)}, u32[]{:S(2)}) copy-start(f32[24,3072]{1,0:T(8,128)} %param.31) | copy-start | bytes 884740
  576.5 10.4 %collective-permute-start.32 = (bf16[2,24,3072]{2,1,0:T(8,128)(2,1)S(1)}, bf16[2,24,3072]{2,1,0:T(8,128)(2,1)S(1)}, u32[]{:S(2)}, u32[]{:S(2)}) collective-permute-start(bf16[2,24,3072]{2,1,0:T(8,128)(2,1)S(1)} %fusion.48), channel_id=1, source_target_pairs={{0,4},{4,0},{8,12},{12,8},{16,20},{20,16},{24,28},{28,24},{1,5},{5... | collective-permute-start | bytes 884744 | tf_op jit(solution)/shard_map/ppermute | solution.py:201
  582.6 15.6 %copy-start.14 = (f32[96,768]{1,0:T(8,128)S(1)}, f32[96,768]{1,0:T(8,128)}, u32[]{:S(2)}) copy-start(f32[96,768]{1,0:T(8,128)} %param.24) | copy-start | bytes 884740
  582.6 15.6 %copy-start.19 = (f32[96,768]{1,0:T(8,128)S(1)}, f32[96,768]{1,0:T(8,128)}, u32[]{:S(2)}) copy-start(f32[96,768]{1,0:T(8,128)} %param.28) | copy-start | bytes 884740
  582.7 15.5 %copy-start.20 = (f32[96,768]{1,0:T(8,128)S(1)}, f32[96,768]{1,0:T(8,128)}, u32[]{:S(2)}) copy-start(f32[96,768]{1,0:T(8,128)} %param.32) | copy-start | bytes 884740
  582.7 6.8 %collective-permute-start.37 = (bf16[2,96,768]{2,1,0:T(8,128)(2,1)S(1)}, bf16[2,96,768]{2,1,0:T(8,128)(2,1)S(1)}, u32[]{:S(2)}, u32[]{:S(2)}) collective-permute-start(bf16[2,96,768]{2,1,0:T(8,128)(2,1)S(1)} %fusion.49), channel_id=1, source_target_pairs={{0,8},{4,12},{8,0},{12,4},{16,24},{20,28},{24,16},{28,20},{1,9},{5... | collective-permute-start | bytes 884744 | tf_op jit(solution)/shard_map/ppermute | solution.py:201
  586.9 7.6 %collective-permute-start.33 = (bf16[24,3072]{1,0:T(8,128)(2,1)S(1)}, bf16[24,3072]{1,0:T(8,128)(2,1)S(1)}, u32[]{:S(2)}, u32[]{:S(2)}) collective-permute-start(bf16[24,3072]{1,0:T(8,128)(2,1)S(1)} %fusion.53), channel_id=1, source_target_pairs={{0,2},{1,3},{2,0},{3,1},{4,6},{5,7},{6,4},{7,5},{8,10},{9,11},{10,... | collective-permute-start | bytes 442376 | tf_op jit(solution)/shard_map/ppermute | solution.py:201
  589.6 8.6 %collective-permute-start.38 = (bf16[96,768]{1,0:T(8,128)(2,1)S(1)}, bf16[96,768]{1,0:T(8,128)(2,1)S(1)}, u32[]{:S(2)}, u32[]{:S(2)}) collective-permute-start(bf16[96,768]{1,0:T(8,128)(2,1)S(1)} %fusion.54), channel_id=1, source_target_pairs={{0,16},{4,20},{8,24},{12,28},{16,0},{20,4},{24,8},{28,12},{1,17},{... | collective-permute-start | bytes 442376 | tf_op jit(solution)/shard_map/ppermute | solution.py:201
  (26 other events, 113.3 us)
Sparse Core Ops, SparseCore 0:
  12.8 105.6 all-gather.1

commit v2 on v1

v2 whole, which is shorter than its diff:
```python
import functools

import jax
import jax.numpy as jnp
from jax import lax
from jax.experimental import pallas as pl
from jax.experimental.pallas import tpu as pltpu
from jax.sharding import PartitionSpec as P

HDIM = 64
STEP = 10

NORM_EPSILON = 1e-05
MASKED_SCORE = -1000000000.0
BETA_ONE = 0.9
BETA_TWO = 0.999
ADAM_EPSILON = 1e-08
RATE_MATRIX = 0.05
RATE_VECTOR = 0.3
WEIGHT_DECAY = 0.1
DOCS = 4
GELU_ROOT = 0.7978845608028654
GELU_CUBE = 0.044715
VMEM_BYTES = 56 * 1024 * 1024

BF16 = jnp.bfloat16
F32 = jnp.float32


def norm_parts(values):
    centre = values - jnp.mean(values, axis=-1, keepdims=True)
    scale = lax.rsqrt(jnp.mean(centre * centre, axis=-1, keepdims=True) + NORM_EPSILON)
    return centre * scale, scale


def norm_back(plain, scale, grad, gain):
    grad_plain = grad * gain
    along = jnp.mean(grad_plain * plain, axis=-1, keepdims=True)
    return (grad_plain - jnp.mean(grad_plain, axis=-1, keepdims=True) - plain * along) * scale


def column_sum(values):
    return jnp.sum(values, axis=0, keepdims=True)


def adam_step(weight, gradient, first, second, rate, decay):
    first_new = BETA_ONE * first + (1.0 - BETA_ONE) * gradient
    second_new = BETA_TWO * second + (1.0 - BETA_TWO) * gradient * gradient
    first_hat = first_new / (1.0 - BETA_ONE**STEP)
    second_hat = second_new / (1.0 - BETA_TWO**STEP)
    updated = weight - rate * (first_hat / (jnp.sqrt(second_hat) + ADAM_EPSILON) + decay * weight)
    return (updated, first_new, second_new)


def dot(left, right, dims):
    return lax.dot_general(left, right, (dims, ((), ())), preferred_element_type=F32)


def project_kernel(n_blk, *refs):
    tokens, (params_ref, weight_ref, bias_ref, joint_ref) = refs[:n_blk], refs[n_blk:]
    for place in range(n_blk):
        plain, _ = norm_parts(tokens[place][0].astype(F32))
        normed = (plain * params_ref[0:1, :] + params_ref[1:2, :]).astype(BF16)
        joint = dot(normed, weight_ref[...], ((1,), (0,))) + bias_ref[...]
        joint_ref[place, 0] = joint.astype(BF16)


def project(tokens, params, weight, bias):
    n_blk = len(tokens)
    seqs, blk, width = tokens[0].shape
    cols = weight.shape[1]
    return pl.pallas_call(
        functools.partial(project_kernel, n_blk),
        grid=(seqs,),
        in_specs=[pl.BlockSpec((1, blk, width), lambda s: (s, 0, 0))] * n_blk
        + [
            pl.BlockSpec(params.shape, lambda s: (0, 0)),
            pl.BlockSpec(weight.shape, lambda s: (0, 0)),
            pl.BlockSpec(bias.shape, lambda s: (0, 0)),
        ],
        out_specs=pl.BlockSpec((n_blk, 1, blk, cols), lambda s: (0, s, 0, 0)),
        out_shape=jax.ShapeDtypeStruct((n_blk, seqs, blk, cols), BF16),
        compiler_params=pltpu.CompilerParams(vmem_limit_bytes=VMEM_BYTES),
        cost_estimate=pl.CostEstimate(
            flops=2 * n_blk * seqs * blk * width * cols,
            bytes_accessed=2 * n_blk * seqs * blk * (width + cols),
            transcendentals=0,
        ),
        name="project",
    )(*tokens, params, weight, bias)


def fill_bias(bias, start_ref, n_blk, blk):
    offsets = []
    offset = 0
    for block in range(n_blk):
        keys = (block + 1) * blk
        key_pos = lax.broadcasted_iota(jnp.int32, (keys, blk), 0)
        query_pos = lax.broadcasted_iota(jnp.int32, (keys, blk), 1) + block * blk
        first = start_ref[0, :, block * blk : (block + 1) * blk]
        allowed = (key_pos >= first) & (key_pos <= query_pos)
        bias[offset : offset + keys, :] = jnp.where(allowed, 0.0, MASKED_SCORE)
        offsets.append(offset)
        offset += keys
    return offsets


def bias_rows(n_blk, blk):
    return n_blk * (n_blk + 1) // 2 * blk


def forward_kernel(n_blk, blk, heads, me_ref, joint_ref, start_ref, out_ref, log_ref, joint, bias):
    me = me_ref[0]
    group = heads * HDIM
    for block in range(n_blk):
        joint[block * blk : (block + 1) * blk, :] = joint_ref[lax.bitwise_xor(me, block), 0]
    offsets = fill_bias(bias, start_ref, n_blk, blk)
    tasks = [(block, head) for block in reversed(range(n_blk)) for head in range(heads)]

    def raw_scores(task):
        block, head = task
        low = head * HDIM
        query = joint[block * blk : (block + 1) * blk, low : low + HDIM] * 0.125
        return dot(joint[: (block + 1) * blk, group + low : group + low + HDIM], query, ((1,), (1,)))

    ahead = raw_scores(tasks[0])
    mixed = []
    for number, (block, head) in enumerate(tasks):
        scores = ahead
        if number + 1 < len(tasks):
            ahead = raw_scores(tasks[number + 1])
        keys = (block + 1) * blk
        low = head * HDIM
        scores = scores + bias[offsets[block] : offsets[block] + keys, :]
        top = jnp.max(scores, axis=0, keepdims=True)
        exponent = jnp.exp(scores - top)
        total = jnp.sum(exponent, axis=0, keepdims=True)
        value = joint[:keys, 2 * group + low : 2 * group + low + HDIM]
        mixed.append(dot(value, exponent.astype(BF16), ((0,), (0,))) * (1.0 / total))
        log_ref[0, head : head + 1, block * blk : (block + 1) * blk] = top + jnp.log(total)
        if head == heads - 1:
            out_ref[lax.bitwise_xor(me, block), 0] = jnp.concatenate(mixed, axis=0).T.astype(BF16)
            mixed = []


def attend_forward(me, joint, start):
    n_blk, seqs, blk, cols = joint.shape
    group = cols // 3
    heads = group // HDIM
    length = n_blk * blk
    return pl.pallas_call(
        functools.partial(forward_kernel, n_blk, blk, heads),
        grid_spec=pltpu.PrefetchScalarGridSpec(
            num_scalar_prefetch=1,
            grid=(seqs,),
            in_specs=[
                pl.BlockSpec((n_blk, 1, blk, cols), lambda s, m: (0, s, 0, 0)),
                pl.BlockSpec((1, 1, length), lambda s, m: (s, 0, 0)),
            ],
            out_specs=[
                pl.BlockSpec((n_blk, 1, blk, group), lambda s, m: (0, s, 0, 0)),
                pl.BlockSpec((1, heads, length), lambda s, m: (s, 0, 0)),
            ],
            scratch_shapes=[pltpu.VMEM((length, cols), BF16), pltpu.VMEM((bias_rows(n_blk, blk), blk), F32)],
        ),
        out_shape=[
            jax.ShapeDtypeStruct((n_blk, seqs, blk, group), BF16),
            jax.ShapeDtypeStruct((seqs, heads, length), F32),
        ],
        compiler_params=pltpu.CompilerParams(vmem_limit_bytes=VMEM_BYTES),
        cost_estimate=pl.CostEstimate(
            flops=seqs * heads * length * length * HDIM * 12,
            bytes_accessed=seqs * length * cols * 3,
            transcendentals=seqs * heads * length * length,
        ),
        name="attend_forward",
    )(me, joint, start)


def layer_kernel(
    n_ctx,
    spans,
    me_ref,
    x_ref,
    y_ref,
    *refs,
):
    mixed_refs = refs[:n_ctx]
    rest_ref, params_ref, result_ref, resid_ref, branch_ref, normed_ref, act_ref, pre_ref, mix_ref, sums_ref = refs[n_ctx:]
    me = me_ref[0]
    width = x_ref.shape[-1]
    group = width // n_ctx
    base = width * (1 + spans)

    def output_rows(place):
        first = pl.multiple_of(lax.bitwise_xor(me, place) * group, group)
        return rest_ref[pl.ds(first, group), 0:width]

    def param(row):
        return params_ref[row : row + 1, :]

    upstream = y_ref[0]
    residual = x_ref[0].astype(F32) + param(4)
    for place in range(n_ctx):
        residual = residual + dot(mixed_refs[place][0], output_rows(place), ((1,), (0,)))
    plain, scale = norm_parts(residual)
    normed = (plain * param(5) + param(6)).astype(BF16)
    normed_ref[0] = normed
    result = residual + param(7 + spans)
    grad_normed = jnp.zeros(residual.shape, F32)
    sums = []
    for span in range(spans):
        expand = rest_ref[:, width * (1 + span) : width * (2 + span)]
        shrink = rest_ref[:, base + width * span : base + width * (span + 1)]
        pre = dot(normed, expand, ((1,), (0,))) + param(7 + span)
        square = pre * pre
        bent = jnp.tanh(GELU_ROOT * (pre + GELU_CUBE * (square * pre)))
        half = 0.5 * (1.0 + bent)
        activated = (pre * half).astype(BF16)
        slope = half + (0.5 * pre) * (1.0 - bent * bent) * (GELU_ROOT + (3.0 * GELU_ROOT * GELU_CUBE) * square)
        act_ref[0, :, width * span : width * (span + 1)] = activated
        result = result + dot(activated, shrink, ((1,), (0,)))
        grad_pre = (dot(upstream, shrink, ((1,), (1,))) * slope).astype(BF16)
        pre_ref[0, :, width * span : width * (span + 1)] = grad_pre
        grad_normed = grad_normed + dot(grad_pre, expand, ((1,), (1,)))
        sums.append(column_sum(grad_pre.astype(F32)))
    result_ref[0] = result.astype(BF16)
    gain_sum = column_sum(grad_normed * plain)
    shift_sum = column_sum(grad_normed)
    upstream_wide = upstream.astype(F32)
    grad_resid = upstream_wide + norm_back(plain, scale, grad_normed, param(5))
    resid_ref[0] = grad_resid
    branch = grad_resid.astype(BF16)
    branch_ref[0] = branch
    for place in range(n_ctx):
        mix_ref[place, 0] = dot(branch, output_rows(place), ((1,), (1,))).astype(BF16)
    table = jnp.concatenate(
        [column_sum(branch.astype(F32)), gain_sum, shift_sum] + sums + [column_sum(upstream_wide)], axis=0
    )

    @pl.when(pl.program_id(0) == 0)
    def _():
        sums_ref[...] = table

    @pl.when(pl.program_id(0) > 0)
    def _():
        sums_ref[...] += table


def layer(me, tokens, cotangent, mixed, rest, params):
    n_ctx = len(mixed)
    seqs, blk, width = tokens.shape
    group = width // n_ctx
    spans = (rest.shape[1] // width - 1) // 2
    hidden = spans * width

    def by_seq(*shape):
        return pl.BlockSpec((1,) + shape, lambda s, m: (s,) + (0,) * len(shape))

    def whole(shape):
        return pl.BlockSpec(shape, lambda s, m: (0,) * len(shape), pipeline_mode=pl.Buffered(1))

    return pl.pallas_call(
        functools.partial(layer_kernel, n_ctx, spans),
        grid_spec=pltpu.PrefetchScalarGridSpec(
            num_scalar_prefetch=1,
            grid=(seqs,),
            in_specs=[by_seq(blk, width)] * 2
            + [by_seq(blk, group)] * n_ctx
            + [whole(rest.shape), whole(params.shape)],
            out_specs=[
                by_seq(blk, width),
                by_seq(blk, width),
                by_seq(blk, width),
                by_seq(blk, width),
                by_seq(blk, hidden),
                by_seq(blk, hidden),
                pl.BlockSpec((n_ctx, 1, blk, group), lambda s, m: (0, s, 0, 0)),
                pl.BlockSpec((4 + spans, width), lambda s, m: (0, 0)),
            ],
        ),
        out_shape=[
            jax.ShapeDtypeStruct((seqs, blk, width), BF16),
            jax.ShapeDtypeStruct((seqs, blk, width), F32),
            jax.ShapeDtypeStruct((seqs, blk, width), BF16),
            jax.ShapeDtypeStruct((seqs, blk, width), BF16),
            jax.ShapeDtypeStruct((seqs, blk, hidden), BF16),
            jax.ShapeDtypeStruct((seqs, blk, hidden), BF16),
            jax.ShapeDtypeStruct((n_ctx, seqs, blk, group), BF16),
            jax.ShapeDtypeStruct((4 + spans, width), F32),
        ],
        compiler_params=pltpu.CompilerParams(vmem_limit_bytes=VMEM_BYTES),
        cost_estimate=pl.CostEstimate(
            flops=2 * seqs * blk * width * (2 * width + 4 * hidden),
            bytes_accessed=rest.size * 2 + seqs * blk * (hidden * 4 + width * 14),
            transcendentals=seqs * blk * hidden,
        ),
        name="layer",
    )(me, tokens, cotangent, *mixed, rest, params)


def backward_kernel(
    n_blk, blk, heads, me_ref, joint_ref, *refs
):
    grad_refs = refs[:n_blk]
    start_ref, log_ref, out_ref, joint, grads, bias, totals = refs[n_blk:]
    me = me_ref[0]
    group = heads * HDIM
    for place in range(n_blk):
        rows = pl.ds(pl.multiple_of(lax.bitwise_xor(me, place) * blk, blk), blk)
        joint[rows, :] = joint_ref[place, 0]
        grads[rows, :] = grad_refs[place][0]
    offsets = fill_bias(bias, start_ref, n_blk, blk)
    tasks = [(block, head) for block in reversed(range(n_blk)) for head in range(heads)]

    def products(task):
        block, head = task
        low = head * HDIM
        keys = (block + 1) * blk
        rows = slice(block * blk, keys)
        query = joint[rows, low : low + HDIM] * 0.125
        grad = grads[rows, low : low + HDIM]
        scores = dot(joint[:keys, group + low : group + low + HDIM], query, ((1,), (1,)))
        grad_probs = dot(joint[:keys, 2 * group + low : 2 * group + low + HDIM], grad, ((1,), (1,)))
        zeros = jnp.zeros((blk, HDIM), BF16)
        pair = jnp.concatenate(
            [jnp.concatenate([query, zeros], axis=1), jnp.concatenate([zeros, grad], axis=1)], axis=0
        )
        return scores, grad_probs, pair

    ahead = products(tasks[0])
    grad_queries = []
    for number, (block, head) in enumerate(tasks):
        scores, grad_probs, pair = ahead
        if number + 1 < len(tasks):
            ahead = products(tasks[number + 1])
        keys = (block + 1) * blk
        low = head * HDIM
        scores = scores + bias[offsets[block] : offsets[block] + keys, :]
        probs = jnp.exp(scores - log_ref[0, head : head + 1, block * blk : keys])
        inner = jnp.sum(probs * grad_probs, axis=0, keepdims=True)
        grad_scores = (probs * (grad_probs - inner)).astype(BF16)
        terms = dot(jnp.concatenate([grad_scores, probs.astype(BF16)], axis=1), pair, ((1,), (0,)))
        if block == n_blk - 1:
            totals[head, :keys, :] = terms
        else:
            totals[head, :keys, :] += terms
        key = joint[:keys, group + low : group + low + HDIM]
        grad_queries.append(dot(key, grad_scores, ((0,), (0,))) * 0.125)
        if head == heads - 1:
            out_ref[lax.bitwise_xor(me, block), 0, :, :group] = jnp.concatenate(grad_queries, axis=0).T.astype(BF16)
            grad_queries = []
    for block in range(n_blk):
        rows = slice(block * blk, (block + 1) * blk)
        place = lax.bitwise_xor(me, block)
        sides = [totals[head, rows, :].astype(BF16) for head in range(heads)]
        out_ref[place, 0, :, group:] = jnp.concatenate(
            [side[:, :HDIM] for side in sides] + [side[:, HDIM:] for side in sides], axis=1
        )


def attend_backward(me, joint, grads, start, logs, first, count):
    n_blk, _, blk, cols = joint.shape
    group = cols // 3
    heads = group // HDIM
    length = n_blk * blk
    return pl.pallas_call(
        functools.partial(backward_kernel, n_blk, blk, heads),
        grid_spec=pltpu.PrefetchScalarGridSpec(
            num_scalar_prefetch=1,
            grid=(count,),
            in_specs=[pl.BlockSpec((n_blk, 1, blk, cols), lambda s, m: (0, s + first, 0, 0))]
            + [pl.BlockSpec((1, blk, group), lambda s, m: (s + first, 0, 0))] * n_blk
            + [
                pl.BlockSpec((1, 1, length), lambda s, m: (s + first, 0, 0)),
                pl.BlockSpec((1, heads, length), lambda s, m: (s + first, 0, 0)),
            ],
            out_specs=pl.BlockSpec((n_blk, 1, blk, cols), lambda s, m: (0, s, 0, 0)),
            scratch_shapes=[
                pltpu.VMEM((length, cols), BF16),
                pltpu.VMEM((length, group), BF16),
                pltpu.VMEM((bias_rows(n_blk, blk), blk), F32),
                pltpu.VMEM((heads, length, 2 * HDIM), F32),
            ],
        ),
        out_shape=jax.ShapeDtypeStruct((n_blk, count, blk, cols), BF16),
        compiler_params=pltpu.CompilerParams(vmem_limit_bytes=VMEM_BYTES),
        cost_estimate=pl.CostEstimate(
            flops=count * heads * length * length * HDIM * 30,
            bytes_accessed=count * length * cols * 6,
            transcendentals=count * heads * length * length,
        ),
        name="attend_backward",
    )(me, joint, *grads, start, logs)


def unproject_kernel(n_blk, *refs):
    grad_ref, tokens = refs[0], refs[1 : 1 + n_blk]
    params_ref, weight_ref, share_ref, weight_grad_ref, sums_ref, bias_ref = refs[1 + n_blk :]
    weight_grad = bias_grad = gain_sum = shift_sum = 0.0
    for place in range(n_blk):
        grad = grad_ref[place, 0]
        plain, _ = norm_parts(tokens[place][0].astype(F32))
        normed = (plain * params_ref[0:1, :] + params_ref[1:2, :]).astype(BF16)
        share = dot(grad, weight_ref[...], ((1,), (1,)))
        share_ref[place, 0] = share.astype(BF16)
        gain_sum += column_sum(share * plain)
        shift_sum += column_sum(share)
        bias_grad += column_sum(grad.astype(F32))
        weight_grad += dot(normed, grad, ((0,), (0,)))
    sums = jnp.concatenate([gain_sum, shift_sum], axis=0)

    @pl.when(pl.program_id(0) == 0)
    def _():
        weight_grad_ref[...] = weight_grad
        sums_ref[...] = sums
        bias_ref[...] = bias_grad

    @pl.when(pl.program_id(0) > 0)
    def _():
        weight_grad_ref[...] += weight_grad
        sums_ref[...] += sums
        bias_ref[...] += bias_grad


def unproject(grad, tokens, params, weight, first):
    n_blk, count, blk, cols = grad.shape
    width = tokens[0].shape[-1]
    return pl.pallas_call(
        functools.partial(unproject_kernel, n_blk),
        grid=(count,),
        in_specs=[pl.BlockSpec((n_blk, 1, blk, cols), lambda s: (0, s, 0, 0))]
        + [pl.BlockSpec((1, blk, width), lambda s: (s + first, 0, 0))] * n_blk
        + [pl.BlockSpec(params.shape, lambda s: (0, 0)), pl.BlockSpec(weight.shape, lambda s: (0, 0))],
        out_specs=[
            pl.BlockSpec((n_blk, 1, blk, width), lambda s: (0, s, 0, 0)),
            pl.BlockSpec((width, cols), lambda s: (0, 0)),
            pl.BlockSpec((2, width), lambda s: (0, 0)),
            pl.BlockSpec((1, cols), lambda s: (0, 0)),
        ],
        out_shape=[
            jax.ShapeDtypeStruct((n_blk, count, blk, width), BF16),
            jax.ShapeDtypeStruct((width, cols), F32),
            jax.ShapeDtypeStruct((2, width), F32),
            jax.ShapeDtypeStruct((1, cols), F32),
        ],
        compiler_params=pltpu.CompilerParams(vmem_limit_bytes=VMEM_BYTES),
        cost_estimate=pl.CostEstimate(
            flops=4 * n_blk * count * blk * width * cols,
            bytes_accessed=2 * n_blk * count * blk * (2 * width + cols),
            transcendentals=0,
        ),
        name="unproject",
    )(grad, *tokens, params, weight)


def build(sizes):
    n_dp, n_ctx = sizes["dp"], sizes["ctx"]
    dp_bits = [bit for bit in range(16) if (1 << bit) < n_dp]
    ctx_bits = [bit for bit in range(16) if (1 << bit) < n_ctx]

    def swap(value, axis, mask):
        return lax.ppermute(value, axis, [(place, place ^ mask) for place in range(sizes[axis])])

    def reorder(items, me):
        stacked = jnp.stack(items)
        return [
            lax.dynamic_index_in_dim(stacked, lax.bitwise_xor(me, j), 0, keepdims=False) for j in range(len(items))
        ]

    def halve(value, labels, order, spots):
        labels = list(labels)
        for axis, bit in order:
            pos = labels.index((axis, bit))
            mine = (spots[axis] >> bit) & 1
            send = lax.dynamic_index_in_dim(value, 1 - mine, pos, keepdims=False).astype(BF16)
            keep = lax.dynamic_index_in_dim(value, mine, pos, keepdims=False)
            value = keep + swap(send, axis, 1 << bit).astype(F32)
            labels.pop(pos)
        return value

    def per_device(
        tokens_in,
        segments,
        cotangent,
        joint_weight,
        output_weight,
        expand_weight,
        shrink_weight,
        momentum_joint,
        momentum_output,
        momentum_expand,
        momentum_shrink,
        variance_joint,
        variance_output,
        variance_expand,
        variance_shrink,
        small_params,
        momentum_small,
        variance_small,
    ):
        seqs, stretch, width = tokens_in.shape
        hidden = expand_weight.shape[1]
        spans = hidden // width
        part = joint_weight.shape[0]
        group = width // n_ctx
        cols = 3 * group
        rows = seqs * stretch
        n_dev = n_dp * n_ctx
        vectors = small_params.shape[0]
        me_dp, me = lax.axis_index("dp"), lax.axis_index("ctx")
        spots = {"dp": me_dp, "ctx": me}
        me_arr = me.astype(jnp.int32).reshape(1)

        joint_cast, small_cast, output_cast, expand_cast, shrink_cast = lax.optimization_barrier(
            (
                joint_weight.astype(BF16),
                small_params.astype(BF16),
                output_weight.astype(BF16),
                expand_weight.astype(BF16),
                shrink_weight.astype(BF16),
            )
        )

        blocks, seg_blocks = {0: tokens_in}, {0: segments}
        for bit in reversed(ctx_bits):
            for known in (seg_blocks, blocks):
                known.update({k ^ (1 << bit): swap(value, "ctx", 1 << bit) for k, value in list(known.items())})
        tokens = [blocks[k] for k in range(n_ctx)]
        segs = jnp.concatenate(reorder([seg_blocks[k] for k in range(n_ctx)], me), axis=1)
        start = jnp.zeros_like(segs)
        for number in range(1, DOCS):
            bound = jnp.sum((segs < number).astype(jnp.int32), axis=1, keepdims=True)
            start = jnp.where(segs >= number, bound, start)
        start = start[:, None, :]

        extra = -(-vectors * part // cols)
        pad = extra * cols - vectors * part
        small_rows = jnp.pad(small_cast.reshape(-1), (0, pad)).reshape(extra, cols)
        joint_cols = joint_cast.reshape(part, 3, n_ctx, group)

        def columns_for(k):
            picked = lax.dynamic_index_in_dim(joint_cols, lax.bitwise_xor(me, k), 2, keepdims=False)
            return jnp.concatenate([picked.reshape(part, cols), small_rows], axis=0)

        pieces = [columns_for(0)] + [swap(columns_for(k), "ctx", k) for k in range(1, n_ctx)]
        gathered = jnp.stack(reorder(pieces, me))
        for bit in reversed(dp_bits):
            other = swap(gathered, "dp", 1 << bit)
            upper = ((me_dp >> bit) & 1) == 1
            gathered = jnp.where(upper, jnp.stack([other, gathered]), jnp.stack([gathered, other]))
        n_bits = len(dp_bits)

        expand_wide = expand_cast.reshape(part, n_dev, spans, part).transpose(0, 2, 1, 3).reshape(part, hidden)
        shrink_wide = shrink_cast.reshape(spans, part, width).transpose(1, 0, 2).reshape(part, hidden)
        rest = jnp.concatenate([output_cast, expand_wide, shrink_wide], axis=1)
        rest, gathered = lax.optimization_barrier((rest, gathered))
        rest = lax.all_gather(rest, ("dp", "ctx"), axis=0, tiled=True)

        gathered = gathered.transpose(tuple(reversed(range(n_bits))) + tuple(range(n_bits, n_bits + 3)))
        gathered = gathered.reshape(n_dp, n_ctx, part + extra, cols)
        joint_lo = gathered[:, :, :part].reshape(width, cols)
        small_lo = gathered[:, :, part:].reshape(n_dp, n_ctx, extra * cols)[:, :, : vectors * part]
        params = small_lo.reshape(n_dp, n_ctx, vectors, part).transpose(2, 0, 1, 3).reshape(vectors, width).astype(F32)
        mine_bias = lax.dynamic_slice(params[2:4], (0, me * group), (2, group))
        joint_bias = jnp.concatenate([mine_bias[:1], jnp.zeros((1, group), F32), mine_bias[1:]], axis=1)
        bias_hidden = params[7 : 7 + spans].reshape(n_dev, spans, part).transpose(1, 0, 2).reshape(spans, width)
        params = jnp.concatenate([params[:7], bias_hidden, params[7 + spans :]], axis=0)

        joint = project(tokens, params, joint_lo, joint_bias)
        attended, logs = attend_forward(me_arr, joint, start)
        mixed = [attended[0]] + [swap(attended[k], "ctx", k) for k in range(1, n_ctx)]
        block_output, grad_resid, branch, normed_two, activated, grad_pre, grad_mixed, sums = layer(
            me_arr, tokens_in, cotangent, mixed, rest, params
        )
        grads = [grad_mixed[0]] + [swap(grad_mixed[k], "ctx", k) for k in range(1, n_ctx)]

        upstream = cotangent.reshape(rows, width)
        grad_shrink = dot(activated.reshape(rows, hidden), upstream, ((0,), (0,)))
        grad_expand = dot(normed_two.reshape(rows, width), grad_pre.reshape(rows, hidden), ((0,), (0,)))
        branch = branch.reshape(rows, width)
        grad_output = [dot(item.reshape(rows, group), branch, ((0,), (0,))) for item in mixed]
        grad_output = jnp.concatenate(reorder(grad_output, me), axis=0)

        labels = [("dp", bit) for bit in reversed(dp_bits)] + [("ctx", bit) for bit in reversed(ctx_bits)]
        bit_dims = (2,) * len(labels)
        y_first = [("ctx", ctx_bits[0])] + [("dp", bit) for bit in dp_bits] + [("ctx", bit) for bit in ctx_bits[1:]]
        z_first = [("ctx", ctx_bits[0])] + [("dp", bit) for bit in dp_bits[1:]]
        z_first += [("dp", dp_bits[0])] + [("ctx", bit) for bit in ctx_bits[1:]]
        chains = [
            [grad_shrink.reshape((spans,) + bit_dims + (part, width)), ["span"] + labels, y_first],
            [grad_expand.reshape(bit_dims + (part, hidden)), labels, z_first],
            [grad_output.reshape(bit_dims + (part, width)), labels, y_first],
        ]

        def stage():
            sent = []
            for chain in chains:
                value, names, order = chain
                axis, bit = order[0]
                pos = names.index((axis, bit))
                mine = (spots[axis] >> bit) & 1
                send = lax.dynamic_index_in_dim(value, 1 - mine, pos, keepdims=False).astype(BF16)
                keep = lax.dynamic_index_in_dim(value, mine, pos, keepdims=False)
                sent.append((keep, swap(send, axis, 1 << bit)))
                chain[1] = names[:pos] + names[pos + 1 :]
                chain[2] = order[1:]
            return sent

        def settle(sent, pinned):
            for chain, (keep, got) in zip(chains, sent):
                chain[0] = keep + got.astype(F32)
            out = lax.optimization_barrier((pinned,) + tuple(chain[0] for chain in chains))
            for chain, value in zip(chains, out[1:]):
                chain[0] = value
            return out[0]

        half = max(seqs // 2, 1)
        halves = [(first, half) for first in range(0, seqs, half)]
        sent = stage()
        shares, weight_grads = [], []
        for number, (first, count) in enumerate(halves):
            source = joint
            if number:
                source = settle(sent, joint)
                sent = stage()
            grad_joint = attend_backward(me_arr, source, grads, start, logs, first, count)
            if number == 0:
                grad_joint = settle(sent, grad_joint)
                sent = stage()
            share, weight_grad, norm_sums, bias_sums = unproject(grad_joint, tokens, params, joint_lo, first)
            weight_grads.append((weight_grad, norm_sums, bias_sums))
            known = {k: share[k] for k in range(n_ctx)}
            for bit in ctx_bits:
                mask = 1 << bit
                known = {
                    k: value.astype(F32) + swap(known[k | mask].astype(BF16), "ctx", mask).astype(F32)
                    for k, value in known.items()
                    if not k & mask
                }
            shares.append(known[0])
        weight_grad, norm_sums, bias_sums = [sum(items) for items in zip(*weight_grads)]

        plain, scale = norm_parts(tokens_in.astype(F32))
        input_grad = grad_resid + norm_back(plain, scale, jnp.concatenate(shares, axis=0), params[0])

        placed = lax.dynamic_update_slice(
            jnp.zeros((2, width), F32),
            jnp.concatenate([bias_sums[:, :group], bias_sums[:, 2 * group :]], axis=0),
            (0, me * group),
        )
        sums_hidden = sums[3 : 3 + spans].reshape(spans, n_dev, part).transpose(1, 0, 2).reshape(spans, width)
        grad_small = jnp.concatenate([norm_sums, placed, sums[:3], sums_hidden, sums[3 + spans :]], axis=0)
        small_terms = grad_small.reshape(vectors, n_dp, n_ctx, part).transpose(1, 2, 0, 3)
        small_terms = jnp.pad(small_terms.reshape(n_dp, n_ctx, vectors * part), ((0, 0), (0, 0), (0, pad)))
        terms = jnp.concatenate(
            [weight_grad.reshape(n_dp, n_ctx, part, cols), small_terms.reshape(n_dp, n_ctx, extra, cols)], axis=2
        ).reshape((2,) * n_bits + (n_ctx, part + extra, cols))
        dp_labels = [("dp", bit) for bit in reversed(dp_bits)]
        terms = halve(terms, dp_labels, [("dp", bit) for bit in dp_bits], spots)

        def terms_for(k):
            return lax.dynamic_index_in_dim(terms, lax.bitwise_xor(me, k), 0, keepdims=False)

        arrived = [terms_for(0)] + [
            swap(terms_for(k).astype(BF16), "ctx", k).astype(F32) for k in range(1, n_ctx)
        ]
        small_sum = sum(item[part:] for item in arrived).reshape(-1)[: vectors * part].reshape(vectors, part)
        sum_joint = jnp.stack([item[:part].reshape(part, 3, group) for item in reorder(arrived, me)], axis=2)
        sum_joint = sum_joint.reshape(part, 3 * width)

        for chain, (keep, got) in zip(chains, sent):
            chain[0] = keep + got.astype(F32)
        sum_shrink, sum_expand, sum_output = [halve(value, names, order, spots) for value, names, order in chains]
        sum_shrink = sum_shrink.reshape(spans * part, width)
        sum_expand = sum_expand.reshape(part, spans, n_dev, part).transpose(0, 2, 1, 3).reshape(part, hidden)

        new_joint, first_joint, second_joint = adam_step(
            joint_weight, sum_joint, momentum_joint, variance_joint, RATE_MATRIX, WEIGHT_DECAY
        )
        new_output, first_output, second_output = adam_step(
            output_weight, sum_output, momentum_output, variance_output, RATE_MATRIX, WEIGHT_DECAY
        )
        new_expand, first_expand, second_expand = adam_step(
            expand_weight, sum_expand, momentum_expand, variance_expand, RATE_MATRIX, WEIGHT_DECAY
        )
        new_shrink, first_shrink, second_shrink = adam_step(
            shrink_weight, sum_shrink, momentum_shrink, variance_shrink, RATE_MATRIX, WEIGHT_DECAY
        )
        new_small, first_small, second_small = adam_step(
            small_params, small_sum, momentum_small, variance_small, RATE_VECTOR, 0.0
        )
        return (
            block_output,
            input_grad,
            new_joint,
            new_output,
            new_expand,
            new_shrink,
            first_joint,
            first_output,
            first_expand,
            first_shrink,
            second_joint,
            second_output,
            second_expand,
            second_shrink,
            new_small,
            first_small,
            second_small,
        )

    return per_device


def solution(mesh):
    sizes = {axis: mesh.shape[axis] for axis in ("dp", "ctx")}
    tokens = P("dp", "ctx", None)
    matrix = P(("dp", "ctx"), None)
    table = P(None, ("dp", "ctx"))
    return jax.shard_map(
        build(sizes),
        mesh=mesh,
        in_specs=(tokens, P("dp", "ctx"), tokens) + (matrix,) * 12 + (table,) * 3,
        out_specs=(tokens, tokens) + (matrix,) * 12 + (table,) * 3,
        check_vma=False,
    )
```

time: 615 us -> 520 us (0.85)
  matrix products: 107 us -> 17.4 us
  Pallas kernels: 66.8 us -> 133 us
  local copies, waits for them, and re-layouts: 100 us -> 52.3 us
  blocking collectives: 45.2 us -> 0 us
  waiting for transfers between devices: 157 us -> 199 us
  other arithmetic: 68.2 us -> 49.6 us
    dot_general x12 -> x6, matrix products: 107 us -> 17.4 us  [dot(): lax.dot_general(left, right, (dims, ((), ())), preferred_element_type=F32)]
    pallas_call x0 -> x4, Pallas kernels: none -> 70 us  [the longest x1 38.8 us: layer(): pl.pallas_call(functools.partial(layer_kernel, n_ctx, spans), grid_spec=p...]
    all_gather x1 -> x0, blocking collectives: 45.2 us -> none  [per_device(): segs_all = lax.all_gather(segments.astype(BF16), 'ctx', axis=1, tiled=True)]
    ppermute x39 -> x45, waiting for transfers between devices: 157 us -> 199 us  [swap(): lax.ppermute(value, axis, [(place, place ^ mask) for place in range(sizes...]
    add x1 -> x15, other arithmetic: 2.38 us -> 25.1 us  [the longest x6 15 us: settle(): chain[0] = keep + got.astype(F32)]
    reduce_sum x12 -> x4, other arithmetic: 24.7 us -> 2.26 us  [the longest x1 1.22 us: norm_back(): jnp.mean(grad_plain, axis=-1, keepdims=True)]
    slice x14 -> x12, local copies, waits for them, and re-layouts: 14.3 us -> 0.47 us  [the longest x3 0.23 us: per_device(): params[:7]]
    convert_element_type x3 -> x9, local copies, waits for them, and re-layouts: 16.3 us -> 3.7 us  [stage(): lax.dynamic_index_in_dim(value, 1 - mine, pos, keepdims=False).astype(BF16)]
  transfers between devices with their start and end apart: 40 -> 46, of which waited for: 21 -> 23; matrix products, arithmetic and copies ran while one was open for 29% -> 16% of each run, Pallas kernels for 11% -> 19%
where the time goes in v2:
time: 520 us; the launch traced here: 511 us
  waiting for transfers between devices  199 us (38%)
  Pallas kernels  133 us (26%)
  local copies, waits for them, and re-layouts  52.3 us (10%)
  other arithmetic  49.6 us (10%)
  starting transfers between devices  44 us (8%)
  matrix products  17.4 us (3%)
  between operations  15.8 us (3%)
    ppermute x45, waiting for transfers between devices, swap(): lax.ppermute(value, axis, [(place, place ^ mask) for place in range(sizes...  199 us
    ppermute x45, starting transfers between devices, swap(): lax.ppermute(value, axis, [(place, place ^ mask) for place in range(sizes...  43.9 us
    pallas_call x1, Pallas kernels, layer(): pl.pallas_call(functools.partial(layer_kernel, n_ctx, spans), grid_spec=p...  38.8 us
    pallas_call x2, Pallas kernels, attend_backward(): pl.pallas_call(functools.partial(backward_kernel, n_blk, blk, heads), gri...  38.6 us
    pallas_call x1, Pallas kernels, attend_forward(): pl.pallas_call(functools.partial(forward_kernel, n_blk, blk, heads), grid...  24.9 us
    pallas_call x2, Pallas kernels, unproject(): pl.pallas_call(functools.partial(unproject_kernel, n_blk), grid=(count,),...  20.8 us
    dot_general x6, matrix products, dot(): lax.dot_general(left, right, (dims, ((), ())), preferred_element_type=F32)  17.4 us
    add x6, other arithmetic, settle(): chain[0] = keep + got.astype(F32)  15 us
  transfers between devices with their start and end apart: 46, of which 23 were waited for; matrix products, arithmetic and copies ran while one was open for 16% of the time, Pallas kernels for 19%

profile of v2, /device:TPU:0, one launch (start us, length us, event | category | flops | bytes accessed | tf_op | source)
XLA Modules:
  0.0 511.2 jit_solution(7499116828775119581)
XLA Ops:
  14.0 2.6 collective-permute-start.4
  16.7 2.1 collective-permute-done.4
  18.8 1.4 collective-permute-done.5
  20.3 2.7 collective-permute-start.6
  22.9 8.1 %collective-permute-done.6 = bf16[4,25,576]{2,1,0:T(8,128)(2,1)S(1)} collective-permute-done((bf16[4,25,576]{2,1,0:T(8,128)(2,1)S(1)}, bf16[4,25,576]{2,1,0:T(8,128)(2,1)S(1)}, u32[]{:S(2)}, u32[]{:S(2)}) %collective-permute-start.6) | collective-permute-done | bytes 115232 | tf_op jit(solution)/shard_map/ppermute | solution.py:463
  34.7 5.4 %collective-permute-done.7 = bf16[2,4,25,576]{3,2,1,0:T(8,128)(2,1)S(1)} collective-permute-done((bf16[2,4,25,576]{3,2,1,0:T(8,128)(2,1)S(1)}, bf16[2,4,25,576]{3,2,1,0:T(8,128)(2,1)S(1)}, u32[]{:S(2)}, u32[]{:S(2)}) %collective-permute-start.7) | collective-permute-done | bytes 230432 | tf_op jit(solution)/shard_map/ppermute | solution.py:463
  40.6 1.6 collective-permute-start.8
  43.2 9.4 %collective-permute-done.8 = bf16[2,2,4,25,576]{4,2,3,1,0:T(4,128)(2,1)S(1)} collective-permute-done((bf16[2,2,4,25,576]{4,2,3,1,0:T(4,128)(2,1)S(1)}, bf16[2,2,4,25,576]{4,2,3,1,0:T(4,128)(2,1)S(1)}, u32[]{:S(2)}, u32[]{:S(2)}) %collective-permute-start.8) | collective-permute-done | bytes 460832 | tf_op jit(solution)/shard_map/ppermute | solution.py:463
  55.7 39.7 %collective-permute-done.10 = s32[4,256]{1,0:T(4,128)S(1)} collective-permute-done((s32[4,256]{1,0:T(4,128)S(1)}, s32[4,256]{1,0:T(4,128)S(1)}, u32[]{:S(2)}, u32[]{:S(2)}) %collective-permute-start.10) | collective-permute-done | bytes 4128 | tf_op jit(solution)/shard_map/ppermute | solution.py:463
  102.4 10.4 %project.1.joint_ref = bf16[4,4,256,576]{3,2,1,0:T(8,128)(2,1)} custom-call(bf16[4,256,768]{2,1,0:T(8,128)(2,1)} %refs_1_.3, bf16[4,256,768]{2,1,0:T(8,128)(2,1)} %collective-permute-done.refs_1_.refs_2_, bf16[4,256,768]{2,1,0:T(8,128)(2,1)} %collective-permute-done.1.refs_2_.refs_3_, bf16[4,256,768]{2,1,0:T(8,128)(2,1)} %collective-permute-done.2.refs_3_.refs_4_, ...), custom_call_target="tpu_custom_call" | custom-call | flops 3623878656 | bytes 11010048 | tf_op jit(solution)/shard_map/project/pallas_call | solution.py:72
  112.8 24.9 %attend_forward.1 = (bf16[4,4,256,192]{3,2,1,0:T(8,128)(2,1)}, f32[4,3,1024]{2,1,0:T(4,128)}) custom-call(s32[1]{0:T(128)} %bitcast.me_ref, bf16[4,4,256,576]{3,2,1,0:T(8,128)(2,1)} %project.1.joint_ref, s32[4,1,1024]{2,1,0:T(1,128)} %compare_select_fusion.2.start_ref.refs_4_), custom_call_target="tpu_custom_call" | custom-call | flops 9663676416 | bytes 7077888 | tf_op jit(solution)/shard_map/attend_forward/pallas_call | solution.py:151
  137.7 2.6 fusion.53
  140.7 2.9 collective-permute-start.13
  144.2 12.1 %collective-permute-done.13.refs_2_ = bf16[4,256,192]{2,1,0:T(8,128)(2,1)S(1)} collective-permute-done((bf16[4,256,192]{2,1,0:T(8,128)(2,1)S(1)}, bf16[4,256,192]{2,1,0:T(8,128)(2,1)S(1)}, u32[]{:S(2)}, u32[]{:S(2)}) %collective-permute-start.13) | collective-permute-done | bytes 393248 | tf_op jit(solution)/shard_map/ppermute | solution.py:463
  156.3 9.9 %collective-permute-done.14.refs_3_ = bf16[4,256,192]{2,1,0:T(8,128)(2,1)S(1)} collective-permute-done((bf16[4,256,192]{2,1,0:T(8,128)(2,1)S(1)}, bf16[4,256,192]{2,1,0:T(8,128)(2,1)S(1)}, u32[]{:S(2)}, u32[]{:S(2)}) %collective-permute-start.14) | collective-permute-done | bytes 393248 | tf_op jit(solution)/shard_map/ppermute | solution.py:463
  167.1 38.8 %layer.1 = (bf16[4,256,768]{2,1,0:T(8,128)(2,1)}, f32[4,256,768]{2,1,0:T(8,128)}, bf16[4,256,768]{2,1,0:T(8,128)(2,1)}, bf16[4,256,768]{2,1,0:T(8,128)(2,1)}, bf...) custom-call(s32[1]{0:T(128)} %bitcast.me_ref, ...), custom_call_target="tpu_custom_call" | custom-call | flops 21743271936 | bytes 34209792 | tf_op jit(solution)/shard_map/layer/pallas_call | solution.py:263
  205.9 1.7 copy.154
  207.6 7.2 %fusion.57 = f32[2,2,2,2,2,24,3072]{6,5,4,3,2,1,0:T(8,128)S(1)} fusion(bf16[2,2,2,2,2,24,1024]{6,5,4,3,2,1,0:T(8,128)(2,1)S(1)} %bitcast.259, bf16[1024,3072,1,1,1,1,1]{1,0,6,5,4,3,2:T(8,128)(2,1)} %bitcast.291), kind=kOutput, calls=%fused_computation.200 | convolution fusion | flops 4831838208 | bytes 17301504 | tf_op jit(solution)/shard_map/dot_general | solution.py:56
  214.9 3.6 copy-done.10
  219.4 8.6 %copy.153 = bf16[3072,1024]{1,0:T(8,128)(2,1)} copy(bf16[3072,1024]{0,1:T(8,128)(2,1)} %bitcast.249) | data formatting | bytes 12582912 | tf_op jit(solution)/shard_map/dot_general | solution.py:56
  228.0 8.1 %fusion.56 = f32[4,2,2,2,2,2,24,768]{7,6,5,4,3,2,1,0:T(8,128)S(1)} fusion(bf16[4,2,2,2,2,2,24,1024]{7,6,5,4,3,2,1,0:T(8,128)(2,1)} %bitcast.250, bf16[1024,768,1,1,1,1,1,1]{1,0,7,6,5,4,3,2:T(8,128)(2,1)} %bitcast.290), kind=kOutput, calls=%fused_computation.199 | convolution fusion | flops 4831838208 | bytes 17301504 | tf_op jit(solution)/shard_map/dot_general | solution.py:56
  236.1 1.8 fusion.9
  240.3 1.7 collective-permute-start.16
  245.2 9.8 %collective-permute-done.16.refs_2_ = bf16[4,256,192]{2,1,0:T(8,128)(2,1)S(1)} collective-permute-done((bf16[4,256,192]{2,1,0:T(8,128)(2,1)S(1)}, bf16[4,256,192]{2,1,0:T(8,128)(2,1)S(1)}, u32[]{:S(2)}, u32[]{:S(2)}) %collective-permute-start.16) | collective-permute-done | bytes 393248 | tf_op jit(solution)/shard_map/ppermute | solution.py:463
  255.0 10.4 %collective-permute-done.17.refs_3_ = bf16[4,256,192]{2,1,0:T(8,128)(2,1)S(1)} collective-permute-done((bf16[4,256,192]{2,1,0:T(8,128)(2,1)S(1)}, bf16[4,256,192]{2,1,0:T(8,128)(2,1)S(1)}, u32[]{:S(2)}, u32[]{:S(2)}) %collective-permute-start.17) | collective-permute-done | bytes 393248 | tf_op jit(solution)/shard_map/ppermute | solution.py:463
  266.2 18.9 %attend_backward.2.refs_0_ = bf16[4,2,256,576]{3,2,1,0:T(8,128)(2,1)} custom-call(s32[1]{0:T(128)} %bitcast.me_ref, bf16[4,4,256,576]{3,2,1,0:T(8,128)(2,1)} %project.1.joint_ref, bf16[4,256,192]{2,1,0:T(8,128)(2,1)} %get-tuple-element.123.refs_0_, bf16[4,256,192]{2,1,0:T(8,128)(2,1)} %copy-done.38, bf16[4,256,192]{2,1,0:T(8,128)(2,1)} %copy-done.39, ...), custom_call_target="tpu_custom_call" | custom-call | flops 12079595520 | bytes 7077888 | tf_op jit(solution)/shard_map/attend_backward/pallas_call | solution.py:367
  285.3 4.0 bitcast_add_fusion
  289.3 5.5 %bitcast_add_fusion.1 = f32[4,2,2,2,2,24,768]{6,5,4,3,2,1,0:T(8,128)S(1)} fusion(bf16[4,2,2,2,2,24,768]{6,5,4,3,2,1,0:T(8,128)(2,1)} %collective-permute-done.18, f32[4,2,2,2,2,2,24,768]{7,6,5,4,3,2,1,0:T(8,128)} %copy-done.11, s32[]{:T(128)S(6)} %select_n.219), kind=kLoop, calls=%fused_computation.1 | loop fusion | flops 2359296 | bytes 11796484 | tf_op jit(solution)/shard_map/add | solution.py:612
  294.8 1.4 collective-permute-start.26
  297.0 1.4 collective-permute-start.24
  298.4 10.4 %unproject.2 = (bf16[4,2,256,768]{3,2,1,0:T(8,128)(2,1)}, f32[768,576]{1,0:T(8,128)}, f32[2,768]{1,0:T(2,128)}, f32[1,576]{1,0:T(1,128)}) custom-call(bf16[4,2,256,576]{3,2,1,0:T(8,128)(2,1)} %attend_backward.2.refs_0_, bf16[4,256,768]{2,1,0:T(8,128)(2,1)} %refs_1_.3, bf16[4,256,768]{2,1,0:T(8,128)(2,1)} %collective-permute-done.refs_1_.refs_2_, ...), custom_call_target="tpu_custom_call" | custom-call | flops 3623878656 | bytes 8650752 | tf_op jit(solution)/shard_map/unproject/pallas_call | solution.py:429
  308.9 2.7 slice_bitcast_fusion.3
  312.8 3.7 collective-permute-start.25
  317.4 2.5 fusion.14
  319.9 1.4 collective-permute-start.23
  321.3 8.2 %collective-permute-done.24 = bf16[4,2,2,2,24,768]{5,4,3,2,1,0:T(8,128)(2,1)} collective-permute-done((bf16[4,2,2,2,24,768]{5,4,3,2,1,0:T(8,128)(2,1)S(1)}, bf16[4,2,2,2,24,768]{5,4,3,2,1,0:T(8,128)(2,1)}, u32[]{:S(2)}, u32[]{:S(2)}) %collective-permute-start.24) | collective-permute-done | bytes 1179680 | tf_op jit(solution)/shard_map/ppermute | solution.py:463
  329.5 3.7 bitcast_add_fusion.3
  333.2 10.2 %collective-permute-done.25 = bf16[2,2,2,24,3072]{4,3,2,1,0:T(8,128)(2,1)} collective-permute-done((bf16[2,2,2,24,3072]{4,3,2,1,0:T(8,128)(2,1)}, bf16[2,2,2,24,3072]{4,3,2,1,0:T(8,128)(2,1)}, u32[]{:S(2)}, u32[]{:S(2)}) %collective-permute-start.25) | collective-permute-done | bytes 1179680 | tf_op jit(solution)/shard_map/ppermute | solution.py:463
  343.4 1.6 bitcast_add_fusion.2
  345.0 19.6 %attend_backward.3.refs_0_ = bf16[4,2,256,576]{3,2,1,0:T(8,128)(2,1)} custom-call(s32[1]{0:T(128)} %bitcast.me_ref, bf16[4,4,256,576]{3,2,1,0:T(8,128)(2,1)} %project.1.joint_ref, bf16[4,256,192]{2,1,0:T(8,128)(2,1)} %get-tuple-element.123.refs_0_, bf16[4,256,192]{2,1,0:T(8,128)(2,1)} %copy-done.38, bf16[4,256,192]{2,1,0:T(8,128)(2,1)} %copy-done.39, ...), custom_call_target="tpu_custom_call" | custom-call | flops 12079595520 | bytes 7077888 | tf_op jit(solution)/shard_map/attend_backward/pallas_call | solution.py:367
  364.7 10.4 %unproject.3 = (bf16[4,2,256,768]{3,2,1,0:T(8,128)(2,1)}, f32[768,576]{1,0:T(8,128)}, f32[2,768]{1,0:T(2,128)}, f32[1,576]{1,0:T(1,128)}) custom-call(bf16[4,2,256,576]{3,2,1,0:T(8,128)(2,1)} %attend_backward.3.refs_0_, bf16[4,256,768]{2,1,0:T(8,128)(2,1)} %refs_1_.3, bf16[4,256,768]{2,1,0:T(8,128)(2,1)} %collective-permute-done.refs_1_.refs_2_, ...), custom_call_target="tpu_custom_call" | custom-call | flops 3623878656 | bytes 8650752 | tf_op jit(solution)/shard_map/unproject/pallas_call | solution.py:429
  377.8 2.3 add.329
  381.8 1.8 collective-permute-start.42
  384.1 16.2 %collective-permute-done.36 = bf16[2,2,24,768]{3,2,1,0:T(8,128)(2,1)S(1)} collective-permute-done((bf16[2,2,24,768]{3,2,1,0:T(8,128)(2,1)S(1)}, bf16[2,2,24,768]{3,2,1,0:T(8,128)(2,1)S(1)}, u32[]{:S(2)}, u32[]{:S(2)}) %collective-permute-start.36) | collective-permute-done | bytes 147488 | tf_op jit(solution)/shard_map/ppermute | solution.py:463
  400.4 4.5 collective-permute-start.37
  405.9 2.1 collective-permute-done.37
  408.1 1.4 collective-permute-start.38
  409.6 2.5 collective-permute-done.38
  412.1 2.2 collective-permute-start.39
  415.6 1.9 fusion.15
  417.7 1.8 collective-permute-start.31
  420.5 24.3 %collective-permute-done.39 = bf16[2,2,24,3072]{3,2,1,0:T(8,128)(2,1)S(1)} collective-permute-done((bf16[2,2,24,3072]{3,2,1,0:T(8,128)(2,1)S(1)}, bf16[2,2,24,3072]{3,2,1,0:T(8,128)(2,1)S(1)}, u32[]{:S(2)}, u32[]{:S(2)}) %collective-permute-start.39) | collective-permute-done | bytes 589856 | tf_op jit(solution)/shard_map/ppermute | solution.py:463
  447.6 1.4 collective-permute-start.29
  449.0 8.5 %collective-permute-done.32 = bf16[4,25,576]{2,1,0:T(8,128)(2,1)S(1)} collective-permute-done((bf16[4,25,576]{2,1,0:T(8,128)(2,1)S(1)}, bf16[4,25,576]{2,1,0:T(8,128)(2,1)S(1)}, u32[]{:S(2)}, u32[]{:S(2)}) %collective-permute-start.32) | collective-permute-done | bytes 115232 | tf_op jit(solution)/shard_map/ppermute | solution.py:463
  457.8 7.4 %collective-permute-done.35 = bf16[25,576]{1,0:T(8,128)(2,1)S(1)} collective-permute-done((bf16[25,576]{1,0:T(8,128)(2,1)S(1)}, bf16[25,576]{1,0:T(8,128)(2,1)S(1)}, u32[]{:S(2)}, u32[]{:S(2)}) %collective-permute-start.35) | collective-permute-done | bytes 28832 | tf_op jit(solution)/shard_map/ppermute | solution.py:463
  466.2 3.2 collective-permute-done.34
  472.3 2.0 multiply_subtract_fusion.2
  481.7 3.5 collective-permute-done.44
  485.3 2.3 collective-permute-done.41
  489.9 2.4 copy.169
  492.3 3.3 reshape.651
  495.5 2.1 multiply_subtract_fusion.1
  497.6 2.0 fusion.13
  501.6 2.3 fusion.7
  (300 shorter events, 60.8 us)
Async XLA Ops:
  7.2 159.1 %all-gather.2.cloned.1.call-start = ((), (), s32[]{:S(2)}) async-start(), calls=%async_computation | async-start | bytes 10948608 | tf_op jit(solution)/shard_map/all_gather | solution.py:558
  13.5 3.2 collective-permute-start.3
  14.0 4.7 collective-permute-start.4
  16.6 3.5 collective-permute-start.5
  20.3 10.7 %collective-permute-start.6 = (bf16[4,25,576]{2,1,0:T(8,128)(2,1)S(1)}, bf16[4,25,576]{2,1,0:T(8,128)(2,1)S(1)}, u32[]{:S(2)}, u32[]{:S(2)}) collective-permute-start(bf16[4,25,576]{2,1,0:T(8,128)(2,1)S(1)} %get-tuple-element.135), channel_id=1, source_target_pairs={{0,16},{4,20},{8,24},{12,28},{16,0},{20,4},{24,8},{28,12},{1,17},{... | collective-permute-start | bytes 345608 | tf_op jit(solution)/shard_map/ppermute | solution.py:463
  31.1 9.0 %collective-permute-start.7 = (bf16[2,4,25,576]{3,2,1,0:T(8,128)(2,1)S(1)}, bf16[2,4,25,576]{3,2,1,0:T(8,128)(2,1)S(1)}, u32[]{:S(2)}, u32[]{:S(2)}) collective-permute-start(bf16[2,4,25,576]{3,2,1,0:T(8,128)(2,1)S(1)} %maximum_select_fusion.3), channel_id=1, source_target_pairs={{0,8},{4,12},{8,0},{12,4},{16,24},{20,28},{24,16},{28,20},{1,9},{5... | collective-permute-start | bytes 691208 | tf_op jit(solution)/shard_map/ppermute | solution.py:463
  40.6 12.0 %collective-permute-start.8 = (bf16[2,2,4,25,576]{4,2,3,1,0:T(4,128)(2,1)S(1)}, bf16[2,2,4,25,576]{4,2,3,1,0:T(4,128)(2,1)S(1)}, u32[]{:S(2)}, u32[]{:S(2)}) collective-permute-start(bf16[2,2,4,25,576]{4,2,3,1,0:T(4,128)(2,1)S(1)} %copy.144), channel_id=1, source_target_pairs={{0,4},{4,0},{8,12},{12,8},{16,20},{20,16},{24,28},{28,24},{1,5},{5... | collective-permute-start | bytes 1382408 | tf_op jit(solution)/shard_map/ppermute | solution.py:463
  43.2 9.9 %copy-start = (bf16[4,256,768]{2,1,0:T(8,128)(2,1)S(1)}, bf16[4,256,768]{2,1,0:T(8,128)(2,1)}, u32[]{:S(2)}) copy-start(bf16[4,256,768]{2,1,0:T(8,128)(2,1)} %refs_1_.3) | copy-start | bytes 4718596
  43.2 11.1 %copy-start.36 = (s32[4,256]{1,0:T(4,128)S(1)}, s32[4,256]{1,0:T(4,128)}, u32[]{:S(2)}) copy-start(s32[4,256]{1,0:T(4,128)} %param.19) | copy-start | bytes 12292
  53.1 43.4 %collective-permute-start.1 = (bf16[4,256,768]{2,1,0:T(8,128)(2,1)S(1)}, bf16[4,256,768]{2,1,0:T(8,128)(2,1)}, u32[]{:S(2)}, u32[]{:S(2)}) collective-permute-start(bf16[4,256,768]{2,1,0:T(8,128)(2,1)S(1)} %copy-done), channel_id=1, source_target_pairs={{0,2},{1,3},{2,0},{3,1},{4,6},{5,7},{6,4},{7,5},{8,10},{9,11},{10,... | collective-permute-start | bytes 4718600 | tf_op jit(solution)/shard_map/ppermute | solution.py:463
  54.3 41.1 %collective-permute-start.10 = (s32[4,256]{1,0:T(4,128)S(1)}, s32[4,256]{1,0:T(4,128)S(1)}, u32[]{:S(2)}, u32[]{:S(2)}) collective-permute-start(s32[4,256]{1,0:T(4,128)S(1)} %copy-done.36), channel_id=1, source_target_pairs={{0,2},{1,3},{2,0},{3,1},{4,6},{5,7},{6,4},{7,5},{8,10},{9,11},{10,... | collective-permute-start | bytes 12296 | tf_op jit(solution)/shard_map/ppermute | solution.py:463
  55.2 47.2 %collective-permute-start = (bf16[4,256,768]{2,1,0:T(8,128)(2,1)S(1)}, bf16[4,256,768]{2,1,0:T(8,128)(2,1)}, u32[]{:S(2)}, u32[]{:S(2)}) collective-permute-start(bf16[4,256,768]{2,1,0:T(8,128)(2,1)S(1)} %copy-done), channel_id=1, source_target_pairs={{0,1},{1,0},{2,3},{3,2},{4,5},{5,4},{6,7},{7,6},{8,9},{9,8},{10,11... | collective-permute-start | bytes 4718600 | tf_op jit(solution)/shard_map/ppermute | solution.py:463
  55.2 40.6 %collective-permute-start.9 = (s32[4,256]{1,0:T(4,128)S(1)}, s32[4,256]{1,0:T(4,128)S(1)}, u32[]{:S(2)}, u32[]{:S(2)}) collective-permute-start(s32[4,256]{1,0:T(4,128)S(1)} %copy-done.36), channel_id=1, source_target_pairs={{0,1},{1,0},{2,3},{3,2},{4,5},{5,4},{6,7},{7,6},{8,9},{9,8},{10,11... | collective-permute-start | bytes 12296 | tf_op jit(solution)/shard_map/ppermute | solution.py:463
  95.4 1.2 collective-permute-start.11
  96.6 5.9 %collective-permute-start.2 = (bf16[4,256,768]{2,1,0:T(8,128)(2,1)}, bf16[4,256,768]{2,1,0:T(8,128)(2,1)}, u32[]{:S(2)}, u32[]{:S(2)}) collective-permute-start(bf16[4,256,768]{2,1,0:T(8,128)(2,1)} %collective-permute-done.1.refs_2_.refs_3_), channel_id=1, source_target_pairs={{0,1},{1,0},{2,3},{3,2},{4,5},{5,4},{6,7},{7,6},{8,9},{9,8},{10,11... | collective-permute-start | bytes 4718600 | tf_op jit(solution)/shard_map/ppermute | solution.py:463
  140.3 3.9 collective-permute-start.12
  140.7 15.6 %collective-permute-start.13 = (bf16[4,256,192]{2,1,0:T(8,128)(2,1)S(1)}, bf16[4,256,192]{2,1,0:T(8,128)(2,1)S(1)}, u32[]{:S(2)}, u32[]{:S(2)}) collective-permute-start(bf16[4,256,192]{2,1,0:T(8,128)(2,1)S(1)} %get-tuple-element.118), channel_id=1, source_target_pairs={{0,2},{1,3},{2,0},{3,1},{4,6},{5,7},{6,4},{7,5},{8,10},{9,11},{10,... | collective-permute-start | bytes 1179656 | tf_op jit(solution)/shard_map/ppermute | solution.py:463
  143.6 22.7 %collective-permute-start.14 = (bf16[4,256,192]{2,1,0:T(8,128)(2,1)S(1)}, bf16[4,256,192]{2,1,0:T(8,128)(2,1)S(1)}, u32[]{:S(2)}, u32[]{:S(2)}) collective-permute-start(bf16[4,256,192]{2,1,0:T(8,128)(2,1)S(1)} %get-tuple-element.117), channel_id=1, source_target_pairs={{0,3},{1,2},{2,1},{3,0},{4,7},{5,6},{6,5},{7,4},{8,11},{9,10},{10,... | collective-permute-start | bytes 1179656 | tf_op jit(solution)/shard_map/ppermute | solution.py:463
  144.2 22.1 %copy-start.19 = (bf16[4,256,192]{2,1,0:T(8,128)(2,1)}, bf16[4,256,192]{2,1,0:T(8,128)(2,1)S(1)}, u32[]{:S(2)}) copy-start(bf16[4,256,192]{2,1,0:T(8,128)(2,1)S(1)} %collective-permute-done.12.refs_1_) | copy-start | bytes 1179652
  156.3 10.0 %copy-start.21 = (bf16[4,256,192]{2,1,0:T(8,128)(2,1)}, bf16[4,256,192]{2,1,0:T(8,128)(2,1)S(1)}, u32[]{:S(2)}) copy-start(bf16[4,256,192]{2,1,0:T(8,128)(2,1)S(1)} %collective-permute-done.13.refs_2_) | copy-start | bytes 1179652
  218.8 66.4 %collective-permute-start.19 = (bf16[2,2,2,2,24,3072]{5,4,3,2,1,0:T(8,128)(2,1)S(1)}, bf16[2,2,2,2,24,3072]{5,4,3,2,1,0:T(8,128)(2,1)}, u32[]{:S(2)}, u32[]{:S(2)}) collective-permute-start(bf16[2,2,2,2,24,3072]{5,4,3,2,1,0:T(8,128)(2,1)S(1)} %fusion.10), channel_id=1, source_target_pairs={{0,1},{1,0},{2,3},{3,2},{4,5},{5,4},{6,7},{7,6},{8,9},{9,8},{10,11... | collective-permute-start | bytes 7077896 | tf_op jit(solution)/shard_map/ppermute | solution.py:463
  237.9 51.4 %collective-permute-start.18 = (bf16[4,2,2,2,2,24,768]{6,5,4,3,2,1,0:T(8,128)(2,1)}, bf16[4,2,2,2,2,24,768]{6,5,4,3,2,1,0:T(8,128)(2,1)}, u32[]{:S(2)}, u32[]{:S(2)}) collective-permute-start(bf16[4,2,2,2,2,24,768]{6,5,4,3,2,1,0:T(8,128)(2,1)} %fusion.9), channel_id=1, source_target_pairs={{0,1},{1,0},{2,3},{3,2},{4,5},{5,4},{6,7},{7,6},{8,9},{9,8},{10,11... | collective-permute-start | bytes 7077896 | tf_op jit(solution)/shard_map/ppermute | solution.py:463
  240.2 4.6 collective-permute-start.15
  240.3 14.7 %collective-permute-start.16 = (bf16[4,256,192]{2,1,0:T(8,128)(2,1)S(1)}, bf16[4,256,192]{2,1,0:T(8,128)(2,1)S(1)}, u32[]{:S(2)}, u32[]{:S(2)}) collective-permute-start(bf16[4,256,192]{2,1,0:T(8,128)(2,1)S(1)} %get-tuple-element.121), channel_id=1, source_target_pairs={{0,2},{1,3},{2,0},{3,1},{4,6},{5,7},{6,4},{7,5},{8,10},{9,11},{10,... | collective-permute-start | bytes 1179656 | tf_op jit(solution)/shard_map/ppermute | solution.py:463
  242.0 23.4 %collective-permute-start.17 = (bf16[4,256,192]{2,1,0:T(8,128)(2,1)S(1)}, bf16[4,256,192]{2,1,0:T(8,128)(2,1)S(1)}, u32[]{:S(2)}, u32[]{:S(2)}) collective-permute-start(bf16[4,256,192]{2,1,0:T(8,128)(2,1)S(1)} %get-tuple-element.120), channel_id=1, source_target_pairs={{0,3},{1,2},{2,1},{3,0},{4,7},{5,6},{6,5},{7,4},{8,11},{9,10},{10,... | collective-permute-start | bytes 1179656 | tf_op jit(solution)/shard_map/ppermute | solution.py:463
  244.8 20.6 %copy-start.38 = (bf16[4,256,192]{2,1,0:T(8,128)(2,1)}, bf16[4,256,192]{2,1,0:T(8,128)(2,1)S(1)}, u32[]{:S(2)}) copy-start(bf16[4,256,192]{2,1,0:T(8,128)(2,1)S(1)} %collective-permute-done.15.refs_1_) | copy-start | bytes 1179652
  244.8 40.3 %collective-permute-start.20 = (bf16[2,2,2,2,24,768]{5,4,3,2,1,0:T(8,128)(2,1)S(1)}, bf16[2,2,2,2,24,768]{5,4,3,2,1,0:T(8,128)(2,1)S(1)}, u32[]{:S(2)}, u32[]{:S(2)}) collective-permute-start(bf16[2,2,2,2,24,768]{5,4,3,2,1,0:T(8,128)(2,1)S(1)} %fusion.18), channel_id=1, source_target_pairs={{0,1},{1,0},{2,3},{3,2},{4,5},{5,4},{6,7},{7,6},{8,9},{9,8},{10,11... | collective-permute-start | bytes 1769480 | tf_op jit(solution)/shard_map/ppermute | solution.py:463
  255.0 10.4 %copy-start.39 = (bf16[4,256,192]{2,1,0:T(8,128)(2,1)}, bf16[4,256,192]{2,1,0:T(8,128)(2,1)S(1)}, u32[]{:S(2)}) copy-start(bf16[4,256,192]{2,1,0:T(8,128)(2,1)S(1)} %collective-permute-done.16.refs_2_) | copy-start | bytes 1179652
  289.3 22.3 %copy-start.4 = (f32[2,2,2,2,24,3072]{5,4,3,2,1,0:T(8,128)}, f32[2,2,2,2,24,3072]{5,4,3,2,1,0:T(8,128)S(1)}, u32[]{:S(2)}) copy-start(f32[2,2,2,2,24,3072]{5,4,3,2,1,0:T(8,128)S(1)} %bitcast_add_fusion) | copy-start | bytes 14155780
  294.8 22.5 %collective-permute-start.26 = (bf16[2,2,2,24,768]{4,3,2,1,0:T(8,128)(2,1)S(1)}, bf16[2,2,2,24,768]{4,3,2,1,0:T(8,128)(2,1)S(1)}, u32[]{:S(2)}, u32[]{:S(2)}) collective-permute-start(bf16[2,2,2,24,768]{4,3,2,1,0:T(8,128)(2,1)S(1)} %fusion.25), channel_id=1, source_target_pairs={{0,4},{4,0},{8,12},{12,8},{16,20},{20,16},{24,28},{28,24},{1,5},{5... | collective-permute-start | bytes 884744 | tf_op jit(solution)/shard_map/ppermute | solution.py:463
  297.0 32.4 %collective-permute-start.24 = (bf16[4,2,2,2,24,768]{5,4,3,2,1,0:T(8,128)(2,1)S(1)}, bf16[4,2,2,2,24,768]{5,4,3,2,1,0:T(8,128)(2,1)}, u32[]{:S(2)}, u32[]{:S(2)}) collective-permute-start(bf16[4,2,2,2,24,768]{5,4,3,2,1,0:T(8,128)(2,1)S(1)} %fusion.16), channel_id=1, source_target_pairs={{0,4},{4,0},{8,12},{12,8},{16,20},{20,16},{24,28},{28,24},{1,5},{5... | collective-permute-start | bytes 3538952 | tf_op jit(solution)/shard_map/ppermute | solution.py:463
  311.5 5.9 %collective-permute-start.22 = (bf16[2,256,768]{2,1,0:T(8,128)(2,1)}, bf16[2,256,768]{2,1,0:T(8,128)(2,1)}, u32[]{:S(2)}, u32[]{:S(2)}) collective-permute-start(bf16[2,256,768]{2,1,0:T(8,128)(2,1)} %get-tuple-element.108), channel_id=1, source_target_pairs={{0,1},{1,0},{2,3},{3,2},{4,5},{5,4},{6,7},{7,6},{8,9},{9,8},{10,11... | collective-permute-start | bytes 2359304 | tf_op jit(solution)/shard_map/ppermute | solution.py:463
  312.8 30.6 %collective-permute-start.25 = (bf16[2,2,2,24,3072]{4,3,2,1,0:T(8,128)(2,1)}, bf16[2,2,2,24,3072]{4,3,2,1,0:T(8,128)(2,1)}, u32[]{:S(2)}, u32[]{:S(2)}) collective-permute-start(bf16[2,2,2,24,3072]{4,3,2,1,0:T(8,128)(2,1)} %fusion.17), channel_id=1, source_target_pairs={{0,8},{4,12},{8,0},{12,4},{16,24},{20,28},{24,16},{28,20},{1,9},{5... | collective-permute-start | bytes 3538952 | tf_op jit(solution)/shard_map/ppermute | solution.py:463
  317.0 98.0 %collective-permute-start.21 = (bf16[2,256,768]{2,1,0:T(8,128)(2,1)}, bf16[2,256,768]{2,1,0:T(8,128)(2,1)}, u32[]{:S(2)}, u32[]{:S(2)}) collective-permute-start(bf16[2,256,768]{2,1,0:T(8,128)(2,1)} %get-tuple-element.107), channel_id=1, source_target_pairs={{0,1},{1,0},{2,3},{3,2},{4,5},{5,4},{6,7},{7,6},{8,9},{9,8},{10,11... | collective-permute-start | bytes 2359304 | tf_op jit(solution)/shard_map/ppermute | solution.py:463
  319.9 23.5 %copy-start.5 = (f32[2,2,2,2,24,3072]{5,4,3,2,1,0:T(8,128)S(1)}, f32[2,2,2,2,24,3072]{5,4,3,2,1,0:T(8,128)}, u32[]{:S(2)}) copy-start(f32[2,2,2,2,24,3072]{5,4,3,2,1,0:T(8,128)} %copy-done.4) | copy-start | bytes 14155780
  319.9 95.2 %collective-permute-start.23 = (bf16[2,256,768]{2,1,0:T(8,128)(2,1)}, bf16[2,256,768]{2,1,0:T(8,128)(2,1)}, u32[]{:S(2)}, u32[]{:S(2)}) collective-permute-start(bf16[2,256,768]{2,1,0:T(8,128)(2,1)} %fusion.14), channel_id=1, source_target_pairs={{0,2},{1,3},{2,0},{3,1},{4,6},{5,7},{6,4},{7,5},{8,10},{9,11},{10,... | collective-permute-start | bytes 2359304 | tf_op jit(solution)/shard_map/ppermute | solution.py:463
  345.0 39.0 %copy-start.7 = (f32[2,2,2,24,3072]{4,3,2,1,0:T(8,128)}, f32[2,2,2,24,3072]{4,3,2,1,0:T(8,128)S(1)}, u32[]{:S(2)}) copy-start(f32[2,2,2,24,3072]{4,3,2,1,0:T(8,128)S(1)} %bitcast_add_fusion.2) | copy-start | bytes 7077892
  364.6 10.4 %copy-start.37 = (f32[1,576]{1,0:T(1,128)S(1)}, f32[1,576]{1,0:T(1,128)}, u32[]{:S(2)}) copy-start(f32[1,576]{1,0:T(1,128)} %get-tuple-element.77) | copy-start | bytes 6916
  364.6 11.5 %copy-start.35 = (f32[2,768]{1,0:T(2,128)S(1)}, f32[2,768]{1,0:T(2,128)}, u32[]{:S(2)}) copy-start(f32[2,768]{1,0:T(2,128)} %get-tuple-element.75) | copy-start | bytes 18436
  380.6 24.3 %copy-start.14 = (bf16[4,2,256,768]{3,2,1,0:T(8,128)(2,1)S(1)}, bf16[4,2,256,768]{3,2,1,0:T(8,128)(2,1)}, u32[]{:S(2)}) copy-start(bf16[4,2,256,768]{3,2,1,0:T(8,128)(2,1)} %get-tuple-element.72) | copy-start | bytes 9437188
  380.9 36.6 %collective-permute-start.30 = (bf16[2,2,4,25,576]{4,2,3,1,0:T(4,128)(2,1)S(1)}, bf16[2,2,4,25,576]{4,2,3,1,0:T(4,128)(2,1)S(1)}, u32[]{:S(2)}, u32[]{:S(2)}) collective-permute-start(bf16[2,2,4,25,576]{4,2,3,1,0:T(4,128)(2,1)S(1)} %fusion.21), channel_id=1, source_target_pairs={{0,4},{4,0},{8,12},{12,8},{16,20},{20,16},{24,28},{28,24},{1,5},{5... | collective-permute-start | bytes 1382408 | tf_op jit(solution)/shard_map/ppermute | solution.py:463
  381.8 37.6 %collective-permute-start.42 = (bf16[4,2,2,24,768]{4,3,2,1,0:T(8,128)(2,1)S(1)}, bf16[4,2,2,24,768]{4,3,2,1,0:T(8,128)(2,1)S(1)}, u32[]{:S(2)}, u32[]{:S(2)}) collective-permute-start(bf16[4,2,2,24,768]{4,3,2,1,0:T(8,128)(2,1)S(1)} %fusion.20), channel_id=1, source_target_pairs={{0,8},{4,12},{8,0},{12,4},{16,24},{20,28},{24,16},{28,20},{1,9},{5... | collective-permute-start | bytes 1769480 | tf_op jit(solution)/shard_map/ppermute | solution.py:463
  383.7 16.7 %collective-permute-start.36 = (bf16[2,2,24,768]{3,2,1,0:T(8,128)(2,1)S(1)}, bf16[2,2,24,768]{3,2,1,0:T(8,128)(2,1)S(1)}, u32[]{:S(2)}, u32[]{:S(2)}) collective-permute-start(bf16[2,2,24,768]{3,2,1,0:T(8,128)(2,1)S(1)} %fusion.31), channel_id=1, source_target_pairs={{0,8},{4,12},{8,0},{12,4},{16,24},{20,28},{24,16},{28,20},{1,9},{5... | collective-permute-start | bytes 442376 | tf_op jit(solution)/shard_map/ppermute | solution.py:463
  400.4 7.7 %collective-permute-start.37 = (bf16[2,24,768]{2,1,0:T(8,128)(2,1)S(1)}, bf16[2,24,768]{2,1,0:T(8,128)(2,1)S(1)}, u32[]{:S(2)}, u32[]{:S(2)}) collective-permute-start(bf16[2,24,768]{2,1,0:T(8,128)(2,1)S(1)} %fusion.35), channel_id=1, source_target_pairs={{0,16},{4,20},{8,24},{12,28},{16,0},{20,4},{24,8},{28,12},{1,17},{... | collective-permute-start | bytes 221192 | tf_op jit(solution)/shard_map/ppermute | solution.py:463
  408.1 4.0 collective-permute-start.38
  412.1 32.7 %collective-permute-start.39 = (bf16[2,2,24,3072]{3,2,1,0:T(8,128)(2,1)S(1)}, bf16[2,2,24,3072]{3,2,1,0:T(8,128)(2,1)S(1)}, u32[]{:S(2)}, u32[]{:S(2)}) collective-permute-start(bf16[2,2,24,3072]{3,2,1,0:T(8,128)(2,1)S(1)} %fusion.19), channel_id=1, source_target_pairs={{0,16},{4,20},{8,24},{12,28},{16,0},{20,4},{24,8},{28,12},{1,17},{... | collective-permute-start | bytes 1769480 | tf_op jit(solution)/shard_map/ppermute | solution.py:463
  415.1 31.4 %collective-permute-start.28 = (bf16[2,256,768]{2,1,0:T(8,128)(2,1)S(1)}, bf16[2,256,768]{2,1,0:T(8,128)(2,1)S(1)}, u32[]{:S(2)}, u32[]{:S(2)}) collective-permute-start(bf16[2,256,768]{2,1,0:T(8,128)(2,1)S(1)} %get-tuple-element.110), channel_id=1, source_target_pairs={{0,1},{1,0},{2,3},{3,2},{4,5},{5,4},{6,7},{7,6},{8,9},{9,8},{10,11... | collective-permute-start | bytes 2359304 | tf_op jit(solution)/shard_map/ppermute | solution.py:463
  415.1 82.5 %collective-permute-start.27 = (bf16[2,256,768]{2,1,0:T(8,128)(2,1)}, bf16[2,256,768]{2,1,0:T(8,128)(2,1)}, u32[]{:S(2)}, u32[]{:S(2)}) collective-permute-start(bf16[2,256,768]{2,1,0:T(8,128)(2,1)} %get-tuple-element.109), channel_id=1, source_target_pairs={{0,1},{1,0},{2,3},{3,2},{4,5},{5,4},{6,7},{7,6},{8,9},{9,8},{10,11... | collective-permute-start | bytes 2359304 | tf_op jit(solution)/shard_map/ppermute | solution.py:463
  417.6 27.2 %copy-start.8 = (f32[2,2,2,24,3072]{4,3,2,1,0:T(8,128)S(1)}, f32[2,2,2,24,3072]{4,3,2,1,0:T(8,128)}, u32[]{:S(2)}) copy-start(f32[2,2,2,24,3072]{4,3,2,1,0:T(8,128)} %copy-done.7) | copy-start | bytes 7077892
  417.7 28.6 %collective-permute-start.31 = (bf16[2,4,25,576]{3,2,1,0:T(8,128)(2,1)S(1)}, bf16[2,4,25,576]{3,2,1,0:T(8,128)(2,1)S(1)}, u32[]{:S(2)}, u32[]{:S(2)}) collective-permute-start(bf16[2,4,25,576]{3,2,1,0:T(8,128)(2,1)S(1)} %fusion.22), channel_id=1, source_target_pairs={{0,8},{4,12},{8,0},{12,4},{16,24},{20,28},{24,16},{28,20},{1,9},{5... | collective-permute-start | bytes 691208 | tf_op jit(solution)/shard_map/ppermute | solution.py:463
  419.6 26.7 %copy-start.12 = (f32[4,2,2,24,768]{4,3,2,1,0:T(8,128)}, f32[4,2,2,24,768]{4,3,2,1,0:T(8,128)S(1)}, u32[]{:S(2)}) copy-start(f32[4,2,2,24,768]{4,3,2,1,0:T(8,128)S(1)} %bitcast_add_fusion.5) | copy-start | bytes 3538948
  420.5 56.7 %collective-permute-start.43 = (bf16[4,2,24,768]{3,2,1,0:T(8,128)(2,1)}, bf16[4,2,24,768]{3,2,1,0:T(8,128)(2,1)}, u32[]{:S(2)}, u32[]{:S(2)}) collective-permute-start(bf16[4,2,24,768]{3,2,1,0:T(8,128)(2,1)} %fusion.27), channel_id=1, source_target_pairs={{0,16},{4,20},{8,24},{12,28},{16,0},{20,4},{24,8},{28,12},{1,17},{... | collective-permute-start | bytes 884744 | tf_op jit(solution)/shard_map/ppermute | solution.py:463
  445.7 33.8 %collective-permute-start.40 = (bf16[2,24,3072]{2,1,0:T(8,128)(2,1)}, bf16[2,24,3072]{2,1,0:T(8,128)(2,1)}, u32[]{:S(2)}, u32[]{:S(2)}) collective-permute-start(bf16[2,24,3072]{2,1,0:T(8,128)(2,1)} %fusion.26), channel_id=1, source_target_pairs={{0,4},{4,0},{8,12},{12,8},{16,20},{20,16},{24,28},{28,24},{1,5},{5... | collective-permute-start | bytes 884744 | tf_op jit(solution)/shard_map/ppermute | solution.py:463
  446.4 11.1 %collective-permute-start.32 = (bf16[4,25,576]{2,1,0:T(8,128)(2,1)S(1)}, bf16[4,25,576]{2,1,0:T(8,128)(2,1)S(1)}, u32[]{:S(2)}, u32[]{:S(2)}) collective-permute-start(bf16[4,25,576]{2,1,0:T(8,128)(2,1)S(1)} %fusion.30), channel_id=1, source_target_pairs={{0,16},{4,20},{8,24},{12,28},{16,0},{20,4},{24,8},{28,12},{1,17},{... | collective-permute-start | bytes 345608 | tf_op jit(solution)/shard_map/ppermute | solution.py:463
  447.6 50.0 %collective-permute-start.29 = (bf16[2,256,768]{2,1,0:T(8,128)(2,1)}, bf16[2,256,768]{2,1,0:T(8,128)(2,1)}, u32[]{:S(2)}, u32[]{:S(2)}) collective-permute-start(bf16[2,256,768]{2,1,0:T(8,128)(2,1)} %fusion.12), channel_id=1, source_target_pairs={{0,2},{1,3},{2,0},{3,1},{4,6},{5,7},{6,4},{7,5},{8,10},{9,11},{10,... | collective-permute-start | bytes 2359304 | tf_op jit(solution)/shard_map/ppermute | solution.py:463
  457.5 14.7 %copy-start.18 = (f32[24,2304]{1,0:T(8,128)S(1)}, f32[24,2304]{1,0:T(8,128)}, u32[]{:S(2)}) copy-start(f32[24,2304]{1,0:T(8,128)} %param.21) | copy-start | bytes 663556
  457.6 7.7 %collective-permute-start.35 = (bf16[25,576]{1,0:T(8,128)(2,1)S(1)}, bf16[25,576]{1,0:T(8,128)(2,1)S(1)}, u32[]{:S(2)}, u32[]{:S(2)}) collective-permute-start(bf16[25,576]{1,0:T(8,128)(2,1)S(1)} %get-tuple-element.129), channel_id=1, source_target_pairs={{0,3},{1,2},{2,1},{3,0},{4,7},{5,6},{6,5},{7,4},{8,11},{9,10},{10,... | collective-permute-start | bytes 86408 | tf_op jit(solution)/shard_map/ppermute | solution.py:463
  465.3 4.2 collective-permute-start.34
  469.4 1.2 collective-permute-start.33
  477.1 10.5 %copy-start.16 = (f32[96,768]{1,0:T(8,128)S(1)}, f32[96,768]{1,0:T(8,128)}, u32[]{:S(2)}) copy-start(f32[96,768]{1,0:T(8,128)} %param.24) | copy-start | bytes 884740
  477.1 10.5 %copy-start.26 = (f32[96,768]{1,0:T(8,128)S(1)}, f32[96,768]{1,0:T(8,128)}, u32[]{:S(2)}) copy-start(f32[96,768]{1,0:T(8,128)} %param.28) | copy-start | bytes 884740
  477.1 10.5 %copy-start.27 = (f32[96,768]{1,0:T(8,128)S(1)}, f32[96,768]{1,0:T(8,128)}, u32[]{:S(2)}) copy-start(f32[96,768]{1,0:T(8,128)} %param.32) | copy-start | bytes 884740
  478.5 6.8 %collective-permute-start.44 = (bf16[4,24,768]{2,1,0:T(8,128)(2,1)S(1)}, bf16[4,24,768]{2,1,0:T(8,128)(2,1)S(1)}, u32[]{:S(2)}, u32[]{:S(2)}) collective-permute-start(bf16[4,24,768]{2,1,0:T(8,128)(2,1)S(1)} %fusion.33), channel_id=1, source_target_pairs={{0,2},{1,3},{2,0},{3,1},{4,6},{5,7},{6,4},{7,5},{8,10},{9,11},{10,... | collective-permute-start | bytes 442376 | tf_op jit(solution)/shard_map/ppermute | solution.py:463
  480.5 7.1 %collective-permute-start.41 = (bf16[24,3072]{1,0:T(8,128)(2,1)S(1)}, bf16[24,3072]{1,0:T(8,128)(2,1)S(1)}, u32[]{:S(2)}, u32[]{:S(2)}) collective-permute-start(bf16[24,3072]{1,0:T(8,128)(2,1)S(1)} %fusion.32), channel_id=1, source_target_pairs={{0,2},{1,3},{2,0},{3,1},{4,6},{5,7},{6,4},{7,5},{8,10},{9,11},{10,... | collective-permute-start | bytes 442376 | tf_op jit(solution)/shard_map/ppermute | solution.py:463
  (23 other events, 96.6 us)
Sparse Core Ops, SparseCore 0:
  53.2 97.2 all-gather.1

commit v3 on v2

--- a/solution.py
+++ b/solution.py
@@ -205,7 +205,7 @@
         residual = residual + dot(mixed_refs[place][0], output_rows(place), ((1,), (0,)))
     plain, scale = norm_parts(residual)
     normed = (plain * param(5) + param(6)).astype(BF16)
-    normed_ref[0] = normed
+    normed_ref[...] = normed.T
     result = residual + param(7 + spans)
     grad_normed = jnp.zeros(residual.shape, F32)
     sums = []
@@ -218,7 +218,7 @@
         half = 0.5 * (1.0 + bent)
         activated = (pre * half).astype(BF16)
         slope = half + (0.5 * pre) * (1.0 - bent * bent) * (GELU_ROOT + (3.0 * GELU_ROOT * GELU_CUBE) * square)
-        act_ref[0, :, width * span : width * (span + 1)] = activated
+        act_ref[width * span : width * (span + 1), :] = activated.T
         result = result + dot(activated, shrink, ((1,), (0,)))
         grad_pre = (dot(upstream, shrink, ((1,), (1,))) * slope).astype(BF16)
         pre_ref[0, :, width * span : width * (span + 1)] = grad_pre
@@ -272,8 +272,8 @@
                 by_seq(blk, width),
                 by_seq(blk, width),
                 by_seq(blk, width),
-                by_seq(blk, width),
-                by_seq(blk, hidden),
+                pl.BlockSpec((width, blk), lambda s, m: (0, s)),
+                pl.BlockSpec((hidden, blk), lambda s, m: (0, s)),
                 by_seq(blk, hidden),
                 pl.BlockSpec((n_ctx, 1, blk, group), lambda s, m: (0, s, 0, 0)),
                 pl.BlockSpec((4 + spans, width), lambda s, m: (0, 0)),
@@ -283,8 +283,8 @@
             jax.ShapeDtypeStruct((seqs, blk, width), BF16),
             jax.ShapeDtypeStruct((seqs, blk, width), F32),
             jax.ShapeDtypeStruct((seqs, blk, width), BF16),
-            jax.ShapeDtypeStruct((seqs, blk, width), BF16),
-            jax.ShapeDtypeStruct((seqs, blk, hidden), BF16),
+            jax.ShapeDtypeStruct((width, seqs * blk), BF16),
+            jax.ShapeDtypeStruct((hidden, seqs * blk), BF16),
             jax.ShapeDtypeStruct((seqs, blk, hidden), BF16),
             jax.ShapeDtypeStruct((n_ctx, seqs, blk, group), BF16),
             jax.ShapeDtypeStruct((4 + spans, width), F32),
@@ -507,6 +507,7 @@
         cols = 3 * group
         rows = seqs * stretch
         n_dev = n_dp * n_ctx
+        n_bits = len(dp_bits)
         vectors = small_params.shape[0]
         me_dp, me = lax.axis_index("dp"), lax.axis_index("ctx")
         spots = {"dp": me_dp, "ctx": me}
@@ -545,17 +546,18 @@
 
         pieces = [columns_for(0)] + [swap(columns_for(k), "ctx", k) for k in range(1, n_ctx)]
         gathered = jnp.stack(reorder(pieces, me))
+        expand_wide = expand_cast.reshape(part, n_dev, spans, part).transpose(0, 2, 1, 3).reshape(part, hidden)
+        shrink_wide = shrink_cast.reshape(spans, part, width).transpose(1, 0, 2).reshape(part, hidden)
+        rest = jnp.concatenate([output_cast, expand_wide, shrink_wide], axis=1)
         for bit in reversed(dp_bits):
+            if bit == dp_bits[max(n_bits - 2, 0)]:
+                rest, gathered, start = lax.optimization_barrier((rest, gathered, start))
+                rest = lax.all_gather(rest, ("dp", "ctx"), axis=0, tiled=True)
+            if bit == dp_bits[0]:
+                gathered, *tokens = lax.optimization_barrier((gathered, *tokens))
             other = swap(gathered, "dp", 1 << bit)
             upper = ((me_dp >> bit) & 1) == 1
             gathered = jnp.where(upper, jnp.stack([other, gathered]), jnp.stack([gathered, other]))
-        n_bits = len(dp_bits)
-
-        expand_wide = expand_cast.reshape(part, n_dev, spans, part).transpose(0, 2, 1, 3).reshape(part, hidden)
-        shrink_wide = shrink_cast.reshape(spans, part, width).transpose(1, 0, 2).reshape(part, hidden)
-        rest = jnp.concatenate([output_cast, expand_wide, shrink_wide], axis=1)
-        rest, gathered = lax.optimization_barrier((rest, gathered))
-        rest = lax.all_gather(rest, ("dp", "ctx"), axis=0, tiled=True)
 
         gathered = gathered.transpose(tuple(reversed(range(n_bits))) + tuple(range(n_bits, n_bits + 3)))
         gathered = gathered.reshape(n_dp, n_ctx, part + extra, cols)
@@ -575,70 +577,82 @@
         )
         grads = [grad_mixed[0]] + [swap(grad_mixed[k], "ctx", k) for k in range(1, n_ctx)]
 
-        upstream = cotangent.reshape(rows, width)
-        grad_shrink = dot(activated.reshape(rows, hidden), upstream, ((0,), (0,)))
-        grad_expand = dot(normed_two.reshape(rows, width), grad_pre.reshape(rows, hidden), ((0,), (0,)))
+        activated, grad_pre, normed_two, branch, grads[1] = lax.optimization_barrier(
+            (activated, grad_pre, normed_two, branch, grads[1])
+        )
         branch = branch.reshape(rows, width)
+        grad_shrink = dot(activated, cotangent.reshape(rows, width), ((1,), (0,)))
+        grad_expand = dot(normed_two, grad_pre.reshape(rows, hidden), ((1,), (0,)))
         grad_output = [dot(item.reshape(rows, group), branch, ((0,), (0,))) for item in mixed]
         grad_output = jnp.concatenate(reorder(grad_output, me), axis=0)
 
         labels = [("dp", bit) for bit in reversed(dp_bits)] + [("ctx", bit) for bit in reversed(ctx_bits)]
         bit_dims = (2,) * len(labels)
-        y_first = [("ctx", ctx_bits[0])] + [("dp", bit) for bit in dp_bits] + [("ctx", bit) for bit in ctx_bits[1:]]
-        z_first = [("ctx", ctx_bits[0])] + [("dp", bit) for bit in dp_bits[1:]]
-        z_first += [("dp", dp_bits[0])] + [("ctx", bit) for bit in ctx_bits[1:]]
+        core, far = [("ctx", ctx_bits[0])], [("ctx", bit) for bit in ctx_bits[1:]]
+        inner = [("dp", bit) for bit in dp_bits]
         chains = [
-            [grad_shrink.reshape((spans,) + bit_dims + (part, width)), ["span"] + labels, y_first],
-            [grad_expand.reshape(bit_dims + (part, hidden)), labels, z_first],
-            [grad_output.reshape(bit_dims + (part, width)), labels, y_first],
+            [grad_shrink.reshape((spans,) + bit_dims + (part, width)), None, ["span"] + labels, core + inner + far],
+            [grad_expand.reshape(bit_dims + (part, hidden)), None, labels, core + far + inner],
+            [grad_output.reshape(bit_dims + (part, width)), None, labels, core + far + inner],
         ]
 
-        def stage():
-            sent = []
-            for chain in chains:
-                value, names, order = chain
-                axis, bit = order[0]
-                pos = names.index((axis, bit))
-                mine = (spots[axis] >> bit) & 1
-                send = lax.dynamic_index_in_dim(value, 1 - mine, pos, keepdims=False).astype(BF16)
-                keep = lax.dynamic_index_in_dim(value, mine, pos, keepdims=False)
-                sent.append((keep, swap(send, axis, 1 << bit)))
-                chain[1] = names[:pos] + names[pos + 1 :]
-                chain[2] = order[1:]
-            return sent
-
-        def settle(sent, pinned):
-            for chain, (keep, got) in zip(chains, sent):
-                chain[0] = keep + got.astype(F32)
-            out = lax.optimization_barrier((pinned,) + tuple(chain[0] for chain in chains))
-            for chain, value in zip(chains, out[1:]):
-                chain[0] = value
-            return out[0]
+        def split(chain):
+            value, _, names, order = chain
+            axis, bit = order[0]
+            pos = names.index((axis, bit))
+            mine = (spots[axis] >> bit) & 1
+            chain[0] = lax.dynamic_index_in_dim(value, mine, pos, keepdims=False)
+            chain[1] = lax.dynamic_index_in_dim(value, 1 - mine, pos, keepdims=False).astype(BF16)
+
+        def merge(chain):
+            _, _, names, order = chain
+            axis, bit = order[0]
+            got = swap(chain[1], axis, 1 << bit)
+            chain[0] = chain[0] + got.astype(F32)
+            chain[2] = [name for name in names if name != (axis, bit)]
+            chain[3] = order[1:]
+
+        def advance(after, before):
+            pinned = lax.optimization_barrier((after,) + tuple(chain[0] for chain in chains))
+            for chain, keep in zip(chains, pinned[1:]):
+                chain[0] = keep
+                merge(chain)
+                split(chain)
+            out = lax.optimization_barrier(
+                (before,) + tuple(chain[0] for chain in chains) + tuple(chain[1] for chain in chains)
+            )
+            for number, chain in enumerate(chains):
+                chain[0], chain[1] = out[1 + number], out[1 + len(chains) + number]
+            return pinned[0], out[0]
+
+        for chain in chains:
+            split(chain)
 
         half = max(seqs // 2, 1)
-        halves = [(first, half) for first in range(0, seqs, half)]
-        sent = stage()
-        shares, weight_grads = [], []
-        for number, (first, count) in enumerate(halves):
-            source = joint
-            if number:
-                source = settle(sent, joint)
-                sent = stage()
-            grad_joint = attend_backward(me_arr, source, grads, start, logs, first, count)
-            if number == 0:
-                grad_joint = settle(sent, grad_joint)
-                sent = stage()
+        pending, shares, weight_grads = [], [], []
+        source = joint
+        for first in range(0, seqs, half):
+            after = weight_grads[-1][1] if weight_grads else branch
+            _, (source, *held) = advance(after, (source,) + tuple(pending))
+            pending = []
+            grad_joint = attend_backward(me_arr, source, grads, start, logs, first, half)
+            if first:
+                grad_joint, _ = advance(grad_joint, start)
             share, weight_grad, norm_sums, bias_sums = unproject(grad_joint, tokens, params, joint_lo, first)
             weight_grads.append((weight_grad, norm_sums, bias_sums))
+            if held:
+                shares.append(held)
             known = {k: share[k] for k in range(n_ctx)}
-            for bit in ctx_bits:
+            for bit in ctx_bits[:-1]:
                 mask = 1 << bit
                 known = {
                     k: value.astype(F32) + swap(known[k | mask].astype(BF16), "ctx", mask).astype(F32)
                     for k, value in known.items()
                     if not k & mask
                 }
-            shares.append(known[0])
+            pending = [known[0], known[1 << ctx_bits[-1]].astype(BF16)]
+        shares.append(pending)
+        shares = [kept + swap(sent, "ctx", 1 << ctx_bits[-1]).astype(F32) for kept, sent in shares]
         weight_grad, norm_sums, bias_sums = [sum(items) for items in zip(*weight_grads)]
 
         plain, scale = norm_parts(tokens_in.astype(F32))
@@ -669,9 +683,12 @@
         sum_joint = jnp.stack([item[:part].reshape(part, 3, group) for item in reorder(arrived, me)], axis=2)
         sum_joint = sum_joint.reshape(part, 3 * width)
 
-        for chain, (keep, got) in zip(chains, sent):
-            chain[0] = keep + got.astype(F32)
-        sum_shrink, sum_expand, sum_output = [halve(value, names, order, spots) for value, names, order in chains]
+        for chain in chains:
+            merge(chain)
+            while chain[3]:
+                split(chain)
+                merge(chain)
+        sum_shrink, sum_expand, sum_output = [chain[0] for chain in chains]
         sum_shrink = sum_shrink.reshape(spans * part, width)
         sum_expand = sum_expand.reshape(part, spans, n_dev, part).transpose(0, 2, 1, 3).reshape(part, hidden)
 

time: 520 us -> 491 us (0.944); the launches traced: 511 us -> 489 us
  waiting for transfers between devices: 199 us -> 177 us
  matrix products: 17.4 us -> 29.3 us
  other arithmetic: 49.6 us -> 40.4 us
    ppermute x45, waiting for transfers between devices: 199 us -> 177 us  [swap(): lax.ppermute(value, axis, [(place, place ^ mask) for place in range(sizes...]
    dot_general x6, matrix products: 17.4 us -> 29.3 us  [dot(): lax.dot_general(left, right, (dims, ((), ())), preferred_element_type=F32)]
    dot_general x2 -> x0, local copies, waits for them, and re-layouts: 10.3 us -> none  [dot(): lax.dot_general(left, right, (dims, ((), ())), preferred_element_type=F32)]
    add x11 -> x16, other arithmetic: 19.1 us -> 12 us  [the longest x14 9.87 us: merge(): chain[0] = chain[0] + got.astype(F32)]
  transfers between devices with their start and end apart: 46 -> 46, of which waited for: 23 -> 19; matrix products, arithmetic and copies ran while one was open for 16% -> 21% of each run, Pallas kernels for 19% -> 19%
where the time goes in v3:
time: 491 us; the launch traced here: 489 us
  waiting for transfers between devices  177 us (36%)
  Pallas kernels  132 us (27%)
  local copies, waits for them, and re-layouts  47.9 us (10%)
  starting transfers between devices  47 us (10%)
  other arithmetic  40.4 us (8%)
  matrix products  29.3 us (6%)
  between operations  15.6 us (3%)
    ppermute x45, waiting for transfers between devices, swap(): lax.ppermute(value, axis, [(place, place ^ mask) for place in range(sizes...  177 us
    ppermute x45, starting transfers between devices, swap(): lax.ppermute(value, axis, [(place, place ^ mask) for place in range(sizes...  47 us
    pallas_call x1, Pallas kernels, layer(): pl.pallas_call(functools.partial(layer_kernel, n_ctx, spans), grid_spec=p...  38 us
    pallas_call x2, Pallas kernels, attend_backward(): pl.pallas_call(functools.partial(backward_kernel, n_blk, blk, heads), gri...  38 us
    dot_general x6, matrix products, dot(): lax.dot_general(left, right, (dims, ((), ())), preferred_element_type=F32)  29.3 us
    pallas_call x1, Pallas kernels, attend_forward(): pl.pallas_call(functools.partial(forward_kernel, n_blk, blk, heads), grid...  24.9 us
    pallas_call x2, Pallas kernels, unproject(): pl.pallas_call(functools.partial(unproject_kernel, n_blk), grid=(count,),...  20.9 us
    pallas_call x1, Pallas kernels, project(): pl.pallas_call(functools.partial(project_kernel, n_blk), grid=(seqs,), in...  10.4 us
  transfers between devices with their start and end apart: 46, of which 19 were waited for; matrix products, arithmetic and copies ran while one was open for 21% of the time, Pallas kernels for 19%

profile of v3, /device:TPU:0, one launch (start us, length us, event | category | flops | bytes accessed | tf_op | source)
XLA Modules:
  0.0 489.1 jit_solution(4221639506917861982)
XLA Ops:
  7.2 3.0 collective-permute-start.5
  17.2 1.3 collective-permute-start.2
  18.6 1.2 reshape.443
  20.0 1.3 reshape.444
  23.3 2.7 collective-permute-start.3
  26.6 7.6 %collective-permute-done.3 = bf16[4,25,576]{2,1,0:T(8,128)(2,1)S(1)} collective-permute-done((bf16[4,25,576]{2,1,0:T(8,128)(2,1)S(1)}, bf16[4,25,576]{2,1,0:T(8,128)(2,1)S(1)}, u32[]{:S(2)}, u32[]{:S(2)}) %collective-permute-start.3) | collective-permute-done | bytes 115232 | tf_op jit(solution)/shard_map/ppermute | solution.py:463
  34.9 46.0 %collective-permute-done.9.refs_2_.refs_3_ = bf16[4,256,768]{2,1,0:T(8,128)(2,1)} collective-permute-done((bf16[4,256,768]{2,1,0:T(8,128)(2,1)S(1)}, bf16[4,256,768]{2,1,0:T(8,128)(2,1)}, u32[]{:S(2)}, u32[]{:S(2)}) %collective-permute-start.9) | collective-permute-done | bytes 1572896 | tf_op jit(solution)/shard_map/ppermute | solution.py:463
  81.2 13.6 %collective-permute-done.7 = bf16[2,4,25,576]{3,2,1,0:T(8,128)(2,1)S(1)} collective-permute-done((bf16[2,4,25,576]{3,2,1,0:T(8,128)(2,1)S(1)}, bf16[2,4,25,576]{3,2,1,0:T(8,128)(2,1)S(1)}, u32[]{:S(2)}, u32[]{:S(2)}) %collective-permute-start.7) | collective-permute-done | bytes 230432 | tf_op jit(solution)/shard_map/ppermute | solution.py:463
  95.3 1.6 collective-permute-start.11
  96.9 19.7 %collective-permute-done.11 = bf16[2,2,4,25,576]{4,2,3,1,0:T(4,128)(2,1)S(1)} collective-permute-done((bf16[2,2,4,25,576]{4,2,3,1,0:T(4,128)(2,1)S(1)}, bf16[2,2,4,25,576]{4,2,3,1,0:T(4,128)(2,1)S(1)}, u32[]{:S(2)}, u32[]{:S(2)}) %collective-permute-start.11) | collective-permute-done | bytes 460832 | tf_op jit(solution)/shard_map/ppermute | solution.py:463
  121.9 10.4 %project.1.joint_ref = bf16[4,4,256,576]{3,2,1,0:T(8,128)(2,1)} custom-call(bf16[4,256,768]{2,1,0:T(8,128)(2,1)} %refs_1_.1, bf16[4,256,768]{2,1,0:T(8,128)(2,1)} %collective-permute-done.8.refs_1_.refs_2_, bf16[4,256,768]{2,1,0:T(8,128)(2,1)} %collective-permute-done.9.refs_2_.refs_3_, bf16[4,256,768]{2,1,0:T(8,128)(2,1)} %collective-permute-done.10.refs_3_.refs_4_, ...), custom_call_target="tpu_custom_call" | custom-call | flops 3623878656 | bytes 11010048 | tf_op jit(solution)/shard_map/project/pallas_call | solution.py:72
  132.3 24.9 %attend_forward.1 = (bf16[4,4,256,192]{3,2,1,0:T(8,128)(2,1)}, f32[4,3,1024]{2,1,0:T(4,128)}) custom-call(s32[1]{0:T(128)} %bitcast.me_ref, bf16[4,4,256,576]{3,2,1,0:T(8,128)(2,1)} %project.1.joint_ref, s32[4,1,1024]{2,1,0:T(1,128)} %compare_select_fusion.2.start_ref.refs_4_), custom_call_target="tpu_custom_call" | custom-call | flops 9663676416 | bytes 7077888 | tf_op jit(solution)/shard_map/attend_forward/pallas_call | solution.py:151
  157.3 2.9 fusion.52
  160.2 1.9 collective-permute-start.12
  162.3 12.5 %collective-permute-done.14.refs_3_ = bf16[4,256,192]{2,1,0:T(8,128)(2,1)} collective-permute-done((bf16[4,256,192]{2,1,0:T(8,128)(2,1)}, bf16[4,256,192]{2,1,0:T(8,128)(2,1)}, u32[]{:S(2)}, u32[]{:S(2)}) %collective-permute-start.14) | collective-permute-done | bytes 393248 | tf_op jit(solution)/shard_map/ppermute | solution.py:463
  174.8 8.4 %collective-permute-done.13.refs_2_ = bf16[4,256,192]{2,1,0:T(8,128)(2,1)} collective-permute-done((bf16[4,256,192]{2,1,0:T(8,128)(2,1)S(1)}, bf16[4,256,192]{2,1,0:T(8,128)(2,1)}, u32[]{:S(2)}, u32[]{:S(2)}) %collective-permute-start.13) | collective-permute-done | bytes 393248 | tf_op jit(solution)/shard_map/ppermute | solution.py:463
  183.2 38.0 %layer.1 = (bf16[4,256,768]{2,1,0:T(8,128)(2,1)}, f32[4,256,768]{2,1,0:T(8,128)}, bf16[4,256,768]{2,1,0:T(8,128)(2,1)}, bf16[768,1024]{1,0:T(8,128)(2,1)}, bf16[...) custom-call(s32[1]{0:T(128)} %bitcast.me_ref, ...), custom_call_target="tpu_custom_call" | custom-call | flops 21743271936 | bytes 34209792 | tf_op jit(solution)/shard_map/layer/pallas_call | solution.py:263
  221.3 2.6 slice_bitcast_fusion.4
  225.4 1.8 collective-permute-start.20
  227.7 1.6 convolution_bitcast_fusion
  229.3 1.6 convolution_bitcast_fusion.1
  230.9 1.6 convolution_bitcast_fusion.2
  233.3 1.4 slice-done
  235.8 5.1 %fusion.56 = f32[2,2,2,2,2,24,3072]{6,5,4,3,2,1,0:T(8,128)S(1)} fusion(bf16[2,2,2,2,2,24,1024]{6,5,4,3,2,1,0:T(8,128)(2,1)S(1)} %bitcast.280, bf16[1024,3072,1,1,1,1,1]{1,0,6,5,4,3,2:T(8,128)(2,1)S(1)} %bitcast.279), kind=kOutput, calls=%fused_computation.210 | convolution fusion | flops 4831838208 | bytes 17301504 | tf_op jit(solution)/shard_map/dot_general | solution.py:56
  242.3 19.0 %fusion.55 = f32[4,2,2,2,2,2,24,768]{7,6,5,4,3,2,1,0:T(8,128)S(1)} fusion(bf16[4,2,2,2,2,2,24,1024]{7,6,5,4,3,2,1,0:T(8,128)(2,1)} %bitcast.276, bf16[1024,768,1,1,1,1,1,1]{1,0,7,6,5,4,3,2:T(8,128)(2,1)S(1)} %bitcast.275), kind=kOutput, calls=%fused_computation.209 | convolution fusion | flops 4831838208 | bytes 17301504 | tf_op jit(solution)/shard_map/dot_general | solution.py:56
  264.9 1.2 fusion.17
  266.4 2.5 convert_add_fusion.1
  270.3 1.6 dynamic-slice_bitcast_fusion.2
  271.9 2.0 collective-permute-start.25
  273.9 18.8 %attend_backward.2.refs_0_ = bf16[4,2,256,576]{3,2,1,0:T(8,128)(2,1)} custom-call(s32[1]{0:T(128)} %bitcast.me_ref, bf16[4,4,256,576]{3,2,1,0:T(8,128)(2,1)} %project.1.joint_ref, bf16[4,256,192]{2,1,0:T(8,128)(2,1)} %get-tuple-element.189.refs_0_, bf16[4,256,192]{2,1,0:T(8,128)(2,1)} %copy-done.34, bf16[4,256,192]{2,1,0:T(8,128)(2,1)} %collective-permute-done.19.refs_2_, ...), custom_call_target="tpu_custom_call" | custom-call | flops 12079595520 | bytes 7077888 | tf_op jit(solution)/shard_map/attend_backward/pallas_call | solution.py:367
  292.7 10.4 %unproject.2 = (bf16[4,2,256,768]{3,2,1,0:T(8,128)(2,1)}, f32[768,576]{1,0:T(8,128)}, f32[2,768]{1,0:T(2,128)}, f32[1,576]{1,0:T(1,128)}) custom-call(bf16[4,2,256,576]{3,2,1,0:T(8,128)(2,1)} %attend_backward.2.refs_0_, bf16[4,256,768]{2,1,0:T(8,128)(2,1)} %refs_1_.1, bf16[4,256,768]{2,1,0:T(8,128)(2,1)} %collective-permute-done.8.refs_1_.refs_2_, ...), custom_call_target="tpu_custom_call" | custom-call | flops 3623878656 | bytes 8650752 | tf_op jit(solution)/shard_map/unproject/pallas_call | solution.py:429
  303.2 2.6 slice_bitcast_fusion.2
  308.7 2.0 collective-permute-start.23
  313.1 3.7 fusion.14
  316.9 1.6 convert_add_fusion.2
  319.5 17.5 %collective-permute-done.23 = bf16[4,2,2,2,24,768]{5,4,3,2,1,0:T(8,128)(2,1)S(1)} collective-permute-done((bf16[4,2,2,2,24,768]{5,4,3,2,1,0:T(8,128)(2,1)}, bf16[4,2,2,2,24,768]{5,4,3,2,1,0:T(8,128)(2,1)S(1)}, u32[]{:S(2)}, u32[]{:S(2)}) %collective-permute-start.23) | collective-permute-done | bytes 1179680 | tf_op jit(solution)/shard_map/ppermute | solution.py:463
  337.6 1.8 collective-permute-start.38
  339.4 19.2 %attend_backward.3.refs_0_ = bf16[4,2,256,576]{3,2,1,0:T(8,128)(2,1)} custom-call(s32[1]{0:T(128)} %bitcast.me_ref, bf16[4,4,256,576]{3,2,1,0:T(8,128)(2,1)} %project.1.joint_ref, bf16[4,256,192]{2,1,0:T(8,128)(2,1)} %get-tuple-element.189.refs_0_, bf16[4,256,192]{2,1,0:T(8,128)(2,1)} %copy-done.34, bf16[4,256,192]{2,1,0:T(8,128)(2,1)} %collective-permute-done.19.refs_2_, ...), custom_call_target="tpu_custom_call" | custom-call | flops 12079595520 | bytes 7077888 | tf_op jit(solution)/shard_map/attend_backward/pallas_call | solution.py:367
  358.6 10.5 %unproject.3 = (bf16[4,2,256,768]{3,2,1,0:T(8,128)(2,1)}, f32[768,576]{1,0:T(8,128)}, f32[2,768]{1,0:T(2,128)}, f32[1,576]{1,0:T(1,128)}) custom-call(bf16[4,2,256,576]{3,2,1,0:T(8,128)(2,1)} %attend_backward.3.refs_0_, bf16[4,256,768]{2,1,0:T(8,128)(2,1)} %refs_1_.1, bf16[4,256,768]{2,1,0:T(8,128)(2,1)} %collective-permute-done.8.refs_1_.refs_2_, ...), custom_call_target="tpu_custom_call" | custom-call | flops 3623878656 | bytes 8650752 | tf_op jit(solution)/shard_map/unproject/pallas_call | solution.py:429
  371.8 2.3 add.331
  376.2 1.7 collective-permute-start.37
  377.9 2.0 collective-permute-start.26
  382.1 7.5 %collective-permute-done.30 = bf16[2,2,4,25,576]{4,2,3,1,0:T(4,128)(2,1)S(1)} collective-permute-done((bf16[2,2,4,25,576]{4,2,3,1,0:T(4,128)(2,1)S(1)}, bf16[2,2,4,25,576]{4,2,3,1,0:T(4,128)(2,1)S(1)}, u32[]{:S(2)}, u32[]{:S(2)}) %collective-permute-start.30) | collective-permute-done | bytes 460832 | tf_op jit(solution)/shard_map/ppermute | solution.py:463
  389.7 10.4 %collective-permute-done.37 = bf16[2,2,24,3072]{3,2,1,0:T(8,128)(2,1)S(1)} collective-permute-done((bf16[2,2,24,3072]{3,2,1,0:T(8,128)(2,1)S(1)}, bf16[2,2,24,3072]{3,2,1,0:T(8,128)(2,1)S(1)}, u32[]{:S(2)}, u32[]{:S(2)}) %collective-permute-start.37) | collective-permute-done | bytes 589856 | tf_op jit(solution)/shard_map/ppermute | solution.py:463
  404.3 3.1 collective-permute-done.39
  408.3 6.1 %collective-permute-done.31 = bf16[2,4,25,576]{3,2,1,0:T(8,128)(2,1)S(1)} collective-permute-done((bf16[2,4,25,576]{3,2,1,0:T(8,128)(2,1)S(1)}, bf16[2,4,25,576]{3,2,1,0:T(8,128)(2,1)S(1)}, u32[]{:S(2)}, u32[]{:S(2)}) %collective-permute-start.31) | collective-permute-done | bytes 230432 | tf_op jit(solution)/shard_map/ppermute | solution.py:463
  414.4 5.3 %collective-permute-start.40 = (bf16[24,768]{1,0:T(8,128)(2,1)S(1)}, bf16[24,768]{1,0:T(8,128)(2,1)S(1)}, u32[]{:S(2)}, u32[]{:S(2)}) collective-permute-start(bf16[24,768]{1,0:T(8,128)(2,1)S(1)} %fusion.40), channel_id=1, source_target_pairs={{0,16},{4,20},{8,24},{12,28},{16,0},{20,4},{24,8},{28,12},{1,17},{... | collective-permute-start | bytes 110600 | tf_op jit(solution)/shard_map/ppermute | solution.py:463
  419.7 2.3 collective-permute-done.40
  422.0 3.0 collective-permute-start.43
  426.9 2.0 collective-permute-start.29
  429.1 10.8 %collective-permute-done.32 = bf16[4,25,576]{2,1,0:T(8,128)(2,1)S(1)} collective-permute-done((bf16[4,25,576]{2,1,0:T(8,128)(2,1)S(1)}, bf16[4,25,576]{2,1,0:T(8,128)(2,1)S(1)}, u32[]{:S(2)}, u32[]{:S(2)}) %collective-permute-start.32) | collective-permute-done | bytes 115232 | tf_op jit(solution)/shard_map/ppermute | solution.py:463
  441.3 1.7 collective-permute-start.35
  443.0 1.7 collective-permute-done.35
  444.7 2.0 collective-permute-start.34
  446.8 2.0 collective-permute-done.34
  451.1 2.1 multiply_subtract_fusion.2
  457.6 2.1 collective-permute-start.44
  459.7 5.9 %collective-permute-done.42 = bf16[24,3072]{1,0:T(8,128)(2,1)S(1)} collective-permute-done((bf16[24,3072]{1,0:T(8,128)(2,1)S(1)}, bf16[24,3072]{1,0:T(8,128)(2,1)S(1)}, u32[]{:S(2)}, u32[]{:S(2)}) %collective-permute-start.42) | collective-permute-done | bytes 147488 | tf_op jit(solution)/shard_map/ppermute | solution.py:463
  467.9 2.4 copy.158
  470.4 3.3 reshape.467
  473.6 2.1 multiply_subtract_fusion.1
  475.7 2.0 fusion.13
  477.8 1.2 fusion.11
  479.7 2.3 fusion.7
  (302 shorter events, 59.1 us)
Async XLA Ops:
  7.2 176.0 %all-gather.2.cloned.1.call-start = ((), (), s32[]{:S(2)}) async-start(), calls=%async_computation | async-start | bytes 10948608 | tf_op jit(solution)/shard_map/all_gather | solution.py:555
  7.2 14.0 %collective-permute-start.5 = (s32[4,256]{1,0:T(4,128)}, s32[4,256]{1,0:T(4,128)S(1)}, u32[]{:S(2)}, u32[]{:S(2)}) collective-permute-start(s32[4,256]{1,0:T(4,128)} %param.19), channel_id=1, source_target_pairs={{0,2},{1,3},{2,0},{3,1},{4,6},{5,7},{6,4},{7,5},{8,10},{9,11},{10,... | collective-permute-start | bytes 12296 | tf_op jit(solution)/shard_map/ppermute | solution.py:463
  10.2 12.6 %collective-permute-start.4 = (s32[4,256]{1,0:T(4,128)}, s32[4,256]{1,0:T(4,128)S(1)}, u32[]{:S(2)}, u32[]{:S(2)}) collective-permute-start(s32[4,256]{1,0:T(4,128)} %param.19), channel_id=1, source_target_pairs={{0,1},{1,0},{2,3},{3,2},{4,5},{5,4},{6,7},{7,6},{8,9},{9,8},{10,11... | collective-permute-start | bytes 12296 | tf_op jit(solution)/shard_map/ppermute | solution.py:463
  16.5 6.6 %collective-permute-start = (bf16[25,576]{1,0:T(8,128)(2,1)S(1)}, bf16[25,576]{1,0:T(8,128)(2,1)S(1)}, u32[]{:S(2)}, u32[]{:S(2)}) collective-permute-start(bf16[25,576]{1,0:T(8,128)(2,1)S(1)} %get-tuple-element.220), channel_id=1, source_target_pairs={{0,1},{1,0},{2,3},{3,2},{4,5},{5,4},{6,7},{7,6},{8,9},{9,8},{10,11... | collective-permute-start | bytes 86408 | tf_op jit(solution)/shard_map/ppermute | solution.py:463
  17.1 6.0 %collective-permute-start.1 = (bf16[25,576]{1,0:T(8,128)(2,1)S(1)}, bf16[25,576]{1,0:T(8,128)(2,1)S(1)}, u32[]{:S(2)}, u32[]{:S(2)}) collective-permute-start(bf16[25,576]{1,0:T(8,128)(2,1)S(1)} %get-tuple-element.221), channel_id=1, source_target_pairs={{0,2},{1,3},{2,0},{3,1},{4,6},{5,7},{6,4},{7,5},{8,10},{9,11},{10,... | collective-permute-start | bytes 86408 | tf_op jit(solution)/shard_map/ppermute | solution.py:463
  17.2 6.0 %collective-permute-start.2 = (bf16[25,576]{1,0:T(8,128)(2,1)S(1)}, bf16[25,576]{1,0:T(8,128)(2,1)S(1)}, u32[]{:S(2)}, u32[]{:S(2)}) collective-permute-start(bf16[25,576]{1,0:T(8,128)(2,1)S(1)} %get-tuple-element.222), channel_id=1, source_target_pairs={{0,3},{1,2},{2,1},{3,0},{4,7},{5,6},{6,5},{7,4},{8,11},{9,10},{10,... | collective-permute-start | bytes 86408 | tf_op jit(solution)/shard_map/ppermute | solution.py:463
  20.0 14.3 %copy-start = (bf16[4,256,768]{2,1,0:T(8,128)(2,1)S(1)}, bf16[4,256,768]{2,1,0:T(8,128)(2,1)}, u32[]{:S(2)}) copy-start(bf16[4,256,768]{2,1,0:T(8,128)(2,1)} %refs_1_.1) | copy-start | bytes 4718596
  21.3 1.6 collective-permute-start.6
  23.3 10.9 %collective-permute-start.3 = (bf16[4,25,576]{2,1,0:T(8,128)(2,1)S(1)}, bf16[4,25,576]{2,1,0:T(8,128)(2,1)S(1)}, u32[]{:S(2)}, u32[]{:S(2)}) collective-permute-start(bf16[4,25,576]{2,1,0:T(8,128)(2,1)S(1)} %get-tuple-element.205), channel_id=1, source_target_pairs={{0,16},{4,20},{8,24},{12,28},{16,0},{20,4},{24,8},{28,12},{1,17},{... | collective-permute-start | bytes 345608 | tf_op jit(solution)/shard_map/ppermute | solution.py:463
  34.3 46.6 %collective-permute-start.9 = (bf16[4,256,768]{2,1,0:T(8,128)(2,1)S(1)}, bf16[4,256,768]{2,1,0:T(8,128)(2,1)}, u32[]{:S(2)}, u32[]{:S(2)}) collective-permute-start(bf16[4,256,768]{2,1,0:T(8,128)(2,1)S(1)} %copy-done), channel_id=1, source_target_pairs={{0,2},{1,3},{2,0},{3,1},{4,6},{5,7},{6,4},{7,5},{8,10},{9,11},{10,... | collective-permute-start | bytes 4718600 | tf_op jit(solution)/shard_map/ppermute | solution.py:463
  34.9 60.1 %collective-permute-start.8 = (bf16[4,256,768]{2,1,0:T(8,128)(2,1)S(1)}, bf16[4,256,768]{2,1,0:T(8,128)(2,1)}, u32[]{:S(2)}, u32[]{:S(2)}) collective-permute-start(bf16[4,256,768]{2,1,0:T(8,128)(2,1)S(1)} %copy-done), channel_id=1, source_target_pairs={{0,1},{1,0},{2,3},{3,2},{4,5},{5,4},{6,7},{7,6},{8,9},{9,8},{10,11... | collective-permute-start | bytes 4718600 | tf_op jit(solution)/shard_map/ppermute | solution.py:463
  80.9 14.1 %collective-permute-start.10 = (bf16[4,256,768]{2,1,0:T(8,128)(2,1)}, bf16[4,256,768]{2,1,0:T(8,128)(2,1)}, u32[]{:S(2)}, u32[]{:S(2)}) collective-permute-start(bf16[4,256,768]{2,1,0:T(8,128)(2,1)} %collective-permute-done.9.refs_2_.refs_3_), channel_id=1, source_target_pairs={{0,1},{1,0},{2,3},{3,2},{4,5},{5,4},{6,7},{7,6},{8,9},{9,8},{10,11... | collective-permute-start | bytes 4718600 | tf_op jit(solution)/shard_map/ppermute | solution.py:463
  80.9 13.9 %collective-permute-start.7 = (bf16[2,4,25,576]{3,2,1,0:T(8,128)(2,1)S(1)}, bf16[2,4,25,576]{3,2,1,0:T(8,128)(2,1)S(1)}, u32[]{:S(2)}, u32[]{:S(2)}) collective-permute-start(bf16[2,4,25,576]{3,2,1,0:T(8,128)(2,1)S(1)} %maximum_select_fusion.2), channel_id=1, source_target_pairs={{0,8},{4,12},{8,0},{12,4},{16,24},{20,28},{24,16},{28,20},{1,9},{5... | collective-permute-start | bytes 691208 | tf_op jit(solution)/shard_map/ppermute | solution.py:463
  95.3 21.4 %collective-permute-start.11 = (bf16[2,2,4,25,576]{4,2,3,1,0:T(4,128)(2,1)S(1)}, bf16[2,2,4,25,576]{4,2,3,1,0:T(4,128)(2,1)S(1)}, u32[]{:S(2)}, u32[]{:S(2)}) collective-permute-start(bf16[2,2,4,25,576]{4,2,3,1,0:T(4,128)(2,1)S(1)} %copy.135), channel_id=1, source_target_pairs={{0,4},{4,0},{8,12},{12,8},{16,20},{20,16},{24,28},{28,24},{1,5},{5... | collective-permute-start | bytes 1382408 | tf_op jit(solution)/shard_map/ppermute | solution.py:463
  160.2 14.6 %collective-permute-start.14 = (bf16[4,256,192]{2,1,0:T(8,128)(2,1)}, bf16[4,256,192]{2,1,0:T(8,128)(2,1)}, u32[]{:S(2)}, u32[]{:S(2)}) collective-permute-start(bf16[4,256,192]{2,1,0:T(8,128)(2,1)} %get-tuple-element.193), channel_id=1, source_target_pairs={{0,3},{1,2},{2,1},{3,0},{4,7},{5,6},{6,5},{7,4},{8,11},{9,10},{10,... | collective-permute-start | bytes 1179656 | tf_op jit(solution)/shard_map/ppermute | solution.py:463
  160.2 23.0 %collective-permute-start.13 = (bf16[4,256,192]{2,1,0:T(8,128)(2,1)S(1)}, bf16[4,256,192]{2,1,0:T(8,128)(2,1)}, u32[]{:S(2)}, u32[]{:S(2)}) collective-permute-start(bf16[4,256,192]{2,1,0:T(8,128)(2,1)S(1)} %get-tuple-element.194), channel_id=1, source_target_pairs={{0,2},{1,3},{2,0},{3,1},{4,6},{5,7},{6,4},{7,5},{8,10},{9,11},{10,... | collective-permute-start | bytes 1179656 | tf_op jit(solution)/shard_map/ppermute | solution.py:463
  160.2 23.0 %collective-permute-start.12 = (bf16[4,256,192]{2,1,0:T(8,128)(2,1)S(1)}, bf16[4,256,192]{2,1,0:T(8,128)(2,1)}, u32[]{:S(2)}, u32[]{:S(2)}) collective-permute-start(bf16[4,256,192]{2,1,0:T(8,128)(2,1)S(1)} %get-tuple-element.195), channel_id=1, source_target_pairs={{0,1},{1,0},{2,3},{3,2},{4,5},{5,4},{6,7},{7,6},{8,9},{9,8},{10,11... | collective-permute-start | bytes 1179656 | tf_op jit(solution)/shard_map/ppermute | solution.py:463
  221.2 6.0 %copy-start.4 = (bf16[4,256,768]{2,1,0:T(8,128)(2,1)S(1)}, bf16[4,256,768]{2,1,0:T(8,128)(2,1)}, u32[]{:S(2)}) copy-start(bf16[4,256,768]{2,1,0:T(8,128)(2,1)} %get-tuple-element.106) | copy-start | bytes 4718596
  223.8 3.4 collective-permute-start.15
  225.4 48.5 %collective-permute-start.20 = (bf16[4,256,192]{2,1,0:T(8,128)(2,1)S(1)}, bf16[4,256,192]{2,1,0:T(8,128)(2,1)}, u32[]{:S(2)}, u32[]{:S(2)}) collective-permute-start(bf16[4,256,192]{2,1,0:T(8,128)(2,1)S(1)} %get-tuple-element.187), channel_id=1, source_target_pairs={{0,3},{1,2},{2,1},{3,0},{4,7},{5,6},{6,5},{7,4},{8,11},{9,10},{10,... | collective-permute-start | bytes 1179656 | tf_op jit(solution)/shard_map/ppermute | solution.py:463
  227.2 46.7 %collective-permute-start.19 = (bf16[4,256,192]{2,1,0:T(8,128)(2,1)S(1)}, bf16[4,256,192]{2,1,0:T(8,128)(2,1)}, u32[]{:S(2)}, u32[]{:S(2)}) collective-permute-start(bf16[4,256,192]{2,1,0:T(8,128)(2,1)S(1)} %get-tuple-element.188), channel_id=1, source_target_pairs={{0,2},{1,3},{2,0},{3,1},{4,6},{5,7},{6,4},{7,5},{8,10},{9,11},{10,... | collective-permute-start | bytes 1179656 | tf_op jit(solution)/shard_map/ppermute | solution.py:463
  233.0 30.0 %collective-permute-start.18 = (bf16[2,2,2,2,24,768]{5,4,3,2,1,0:T(8,128)(2,1)S(1)}, bf16[2,2,2,2,24,768]{5,4,3,2,1,0:T(8,128)(2,1)S(1)}, u32[]{:S(2)}, u32[]{:S(2)}) collective-permute-start(bf16[2,2,2,2,24,768]{5,4,3,2,1,0:T(8,128)(2,1)S(1)} %fusion.18), channel_id=1, source_target_pairs={{0,1},{1,0},{2,3},{3,2},{4,5},{5,4},{6,7},{7,6},{8,9},{9,8},{10,11... | collective-permute-start | bytes 1769480 | tf_op jit(solution)/shard_map/ppermute | solution.py:463
  241.2 22.7 %collective-permute-start.17 = (bf16[2,2,2,2,24,3072]{5,4,3,2,1,0:T(8,128)(2,1)S(1)}, bf16[2,2,2,2,24,3072]{5,4,3,2,1,0:T(8,128)(2,1)S(1)}, u32[]{:S(2)}, u32[]{:S(2)}) collective-permute-start(bf16[2,2,2,2,24,3072]{5,4,3,2,1,0:T(8,128)(2,1)S(1)} %fusion.10), channel_id=1, source_target_pairs={{0,1},{1,0},{2,3},{3,2},{4,5},{5,4},{6,7},{7,6},{8,9},{9,8},{10,11... | collective-permute-start | bytes 7077896 | tf_op jit(solution)/shard_map/ppermute | solution.py:463
  261.7 4.7 collective-permute-start.16
  271.9 38.8 %collective-permute-start.25 = (bf16[2,2,2,24,768]{4,3,2,1,0:T(8,128)(2,1)}, bf16[2,2,2,24,768]{4,3,2,1,0:T(8,128)(2,1)}, u32[]{:S(2)}, u32[]{:S(2)}) collective-permute-start(bf16[2,2,2,24,768]{4,3,2,1,0:T(8,128)(2,1)} %fusion.25), channel_id=1, source_target_pairs={{0,2},{1,3},{2,0},{3,1},{4,6},{5,7},{6,4},{7,5},{8,10},{9,11},{10,... | collective-permute-start | bytes 884744 | tf_op jit(solution)/shard_map/ppermute | solution.py:463
  273.9 43.0 %collective-permute-start.24 = (bf16[2,2,2,24,3072]{4,3,2,1,0:T(8,128)(2,1)}, bf16[2,2,2,24,3072]{4,3,2,1,0:T(8,128)(2,1)}, u32[]{:S(2)}, u32[]{:S(2)}) collective-permute-start(bf16[2,2,2,24,3072]{4,3,2,1,0:T(8,128)(2,1)} %fusion.17), channel_id=1, source_target_pairs={{0,2},{1,3},{2,0},{3,1},{4,6},{5,7},{6,4},{7,5},{8,10},{9,11},{10,... | collective-permute-start | bytes 3538952 | tf_op jit(solution)/shard_map/ppermute | solution.py:463
  305.8 7.4 %collective-permute-start.22 = (bf16[2,256,768]{2,1,0:T(8,128)(2,1)}, bf16[2,256,768]{2,1,0:T(8,128)(2,1)}, u32[]{:S(2)}, u32[]{:S(2)}) collective-permute-start(bf16[2,256,768]{2,1,0:T(8,128)(2,1)} %get-tuple-element.181), channel_id=1, source_target_pairs={{0,1},{1,0},{2,3},{3,2},{4,5},{5,4},{6,7},{7,6},{8,9},{9,8},{10,11... | collective-permute-start | bytes 2359304 | tf_op jit(solution)/shard_map/ppermute | solution.py:463
  305.8 7.4 %collective-permute-start.21 = (bf16[2,256,768]{2,1,0:T(8,128)(2,1)}, bf16[2,256,768]{2,1,0:T(8,128)(2,1)}, u32[]{:S(2)}, u32[]{:S(2)}) collective-permute-start(bf16[2,256,768]{2,1,0:T(8,128)(2,1)} %get-tuple-element.182), channel_id=1, source_target_pairs={{0,1},{1,0},{2,3},{3,2},{4,5},{5,4},{6,7},{7,6},{8,9},{9,8},{10,11... | collective-permute-start | bytes 2359304 | tf_op jit(solution)/shard_map/ppermute | solution.py:463
  308.7 28.4 %collective-permute-start.23 = (bf16[4,2,2,2,24,768]{5,4,3,2,1,0:T(8,128)(2,1)}, bf16[4,2,2,2,24,768]{5,4,3,2,1,0:T(8,128)(2,1)S(1)}, u32[]{:S(2)}, u32[]{:S(2)}) collective-permute-start(bf16[4,2,2,2,24,768]{5,4,3,2,1,0:T(8,128)(2,1)} %fusion.16), channel_id=1, source_target_pairs={{0,4},{4,0},{8,12},{12,8},{16,20},{20,16},{24,28},{28,24},{1,5},{5... | collective-permute-start | bytes 3538952 | tf_op jit(solution)/shard_map/ppermute | solution.py:463
  337.6 43.4 %collective-permute-start.38 = (bf16[2,2,24,768]{3,2,1,0:T(8,128)(2,1)}, bf16[2,2,24,768]{3,2,1,0:T(8,128)(2,1)}, u32[]{:S(2)}, u32[]{:S(2)}) collective-permute-start(bf16[2,2,24,768]{3,2,1,0:T(8,128)(2,1)} %fusion.31), channel_id=1, source_target_pairs={{0,4},{4,0},{8,12},{12,8},{16,20},{20,16},{24,28},{28,24},{1,5},{5... | collective-permute-start | bytes 442376 | tf_op jit(solution)/shard_map/ppermute | solution.py:463
  358.6 10.6 %copy-start.32 = (f32[1,576]{1,0:T(1,128)S(1)}, f32[1,576]{1,0:T(1,128)}, u32[]{:S(2)}) copy-start(f32[1,576]{1,0:T(1,128)} %get-tuple-element.138) | copy-start | bytes 6916
  358.6 11.3 %copy-start.30 = (f32[2,768]{1,0:T(2,128)S(1)}, f32[2,768]{1,0:T(2,128)}, u32[]{:S(2)}) copy-start(f32[2,768]{1,0:T(2,128)} %get-tuple-element.117) | copy-start | bytes 18436
  358.6 12.4 %copy-start.18 = (f32[3,8,4,24]{3,0,1,2:T(4,128)S(1)}, f32[3,8,4,24]{3,0,1,2:T(4,128)}, u32[]{:S(2)}) copy-start(f32[3,8,4,24]{3,0,1,2:T(4,128)} %copy.150) | copy-start | bytes 27652
  358.6 12.4 %copy-start.19 = (f32[4,8,4,24]{3,0,1,2:T(4,128)S(1)}, f32[4,8,4,24]{3,0,1,2:T(4,128)}, u32[]{:S(2)}) copy-start(f32[4,8,4,24]{3,0,1,2:T(4,128)} %copy.151) | copy-start | bytes 36868
  358.6 12.4 %copy-start.23 = (f32[1,8,4,24]{3,0,1,2:T(1,128)S(1)}, f32[1,8,4,24]{3,0,1,2:T(1,128)}, u32[]{:S(2)}) copy-start(f32[1,8,4,24]{3,0,1,2:T(1,128)} %copy.152) | copy-start | bytes 9220
  374.1 5.7 %copy-start.8 = (bf16[4,2,256,768]{3,2,1,0:T(8,128)(2,1)S(1)}, bf16[4,2,256,768]{3,2,1,0:T(8,128)(2,1)}, u32[]{:S(2)}) copy-start(bf16[4,2,256,768]{3,2,1,0:T(8,128)(2,1)} %get-tuple-element.134) | copy-start | bytes 9437188
  374.9 14.7 %collective-permute-start.30 = (bf16[2,2,4,25,576]{4,2,3,1,0:T(4,128)(2,1)S(1)}, bf16[2,2,4,25,576]{4,2,3,1,0:T(4,128)(2,1)S(1)}, u32[]{:S(2)}, u32[]{:S(2)}) collective-permute-start(bf16[2,2,4,25,576]{4,2,3,1,0:T(4,128)(2,1)S(1)} %fusion.21), channel_id=1, source_target_pairs={{0,4},{4,0},{8,12},{12,8},{16,20},{20,16},{24,28},{28,24},{1,5},{5... | collective-permute-start | bytes 1382408 | tf_op jit(solution)/shard_map/ppermute | solution.py:463
  375.2 25.8 %collective-permute-start.36 = (bf16[4,2,2,24,768]{4,3,2,1,0:T(8,128)(2,1)S(1)}, bf16[4,2,2,24,768]{4,3,2,1,0:T(8,128)(2,1)S(1)}, u32[]{:S(2)}, u32[]{:S(2)}) collective-permute-start(bf16[4,2,2,24,768]{4,3,2,1,0:T(8,128)(2,1)S(1)} %fusion.19), channel_id=1, source_target_pairs={{0,8},{4,12},{8,0},{12,4},{16,24},{20,28},{24,16},{28,20},{1,9},{5... | collective-permute-start | bytes 1769480 | tf_op jit(solution)/shard_map/ppermute | solution.py:463
  376.2 24.0 %collective-permute-start.37 = (bf16[2,2,24,3072]{3,2,1,0:T(8,128)(2,1)S(1)}, bf16[2,2,24,3072]{3,2,1,0:T(8,128)(2,1)S(1)}, u32[]{:S(2)}, u32[]{:S(2)}) collective-permute-start(bf16[2,2,24,3072]{3,2,1,0:T(8,128)(2,1)S(1)} %copy-done.14), channel_id=1, source_target_pairs={{0,4},{4,0},{8,12},{12,8},{16,20},{20,16},{24,28},{28,24},{1,5},{5... | collective-permute-start | bytes 1769480 | tf_op jit(solution)/shard_map/ppermute | solution.py:463
  377.9 49.1 %collective-permute-start.26 = (bf16[2,256,768]{2,1,0:T(8,128)(2,1)S(1)}, bf16[2,256,768]{2,1,0:T(8,128)(2,1)S(1)}, u32[]{:S(2)}, u32[]{:S(2)}) collective-permute-start(bf16[2,256,768]{2,1,0:T(8,128)(2,1)S(1)} %copy-done.13), channel_id=1, source_target_pairs={{0,2},{1,3},{2,0},{3,1},{4,6},{5,7},{6,4},{7,5},{8,10},{9,11},{10,... | collective-permute-start | bytes 2359304 | tf_op jit(solution)/shard_map/ppermute | solution.py:463
  381.0 94.7 %collective-permute-start.27 = (bf16[2,256,768]{2,1,0:T(8,128)(2,1)}, bf16[2,256,768]{2,1,0:T(8,128)(2,1)}, u32[]{:S(2)}, u32[]{:S(2)}) collective-permute-start(bf16[2,256,768]{2,1,0:T(8,128)(2,1)} %get-tuple-element.177), channel_id=1, source_target_pairs={{0,1},{1,0},{2,3},{3,2},{4,5},{5,4},{6,7},{7,6},{8,9},{9,8},{10,11... | collective-permute-start | bytes 2359304 | tf_op jit(solution)/shard_map/ppermute | solution.py:463
  389.6 36.2 %collective-permute-start.28 = (bf16[2,256,768]{2,1,0:T(8,128)(2,1)S(1)}, bf16[2,256,768]{2,1,0:T(8,128)(2,1)S(1)}, u32[]{:S(2)}, u32[]{:S(2)}) collective-permute-start(bf16[2,256,768]{2,1,0:T(8,128)(2,1)S(1)} %get-tuple-element.178), channel_id=1, source_target_pairs={{0,1},{1,0},{2,3},{3,2},{4,5},{5,4},{6,7},{7,6},{8,9},{9,8},{10,11... | collective-permute-start | bytes 2359304 | tf_op jit(solution)/shard_map/ppermute | solution.py:463
  401.2 23.8 %copy-start.15 = (f32[24,768]{1,0:T(8,128)S(1)}, f32[24,768]{1,0:T(8,128)}, u32[]{:S(2)}) copy-start(f32[24,768]{1,0:T(8,128)} %param.22) | copy-start | bytes 221188
  401.2 23.8 %copy-start.20 = (f32[24,768]{1,0:T(8,128)S(1)}, f32[24,768]{1,0:T(8,128)}, u32[]{:S(2)}) copy-start(f32[24,768]{1,0:T(8,128)} %param.26) | copy-start | bytes 221188
  401.3 23.8 %copy-start.21 = (f32[24,768]{1,0:T(8,128)S(1)}, f32[24,768]{1,0:T(8,128)}, u32[]{:S(2)}) copy-start(f32[24,768]{1,0:T(8,128)} %param.30) | copy-start | bytes 221188
  402.1 5.3 %collective-permute-start.39 = (bf16[2,24,768]{2,1,0:T(8,128)(2,1)S(1)}, bf16[2,24,768]{2,1,0:T(8,128)(2,1)S(1)}, u32[]{:S(2)}, u32[]{:S(2)}) collective-permute-start(bf16[2,24,768]{2,1,0:T(8,128)(2,1)S(1)} %fusion.35), channel_id=1, source_target_pairs={{0,8},{4,12},{8,0},{12,4},{16,24},{20,28},{24,16},{28,20},{1,9},{5... | collective-permute-start | bytes 221192 | tf_op jit(solution)/shard_map/ppermute | solution.py:463
  403.1 11.3 %collective-permute-start.31 = (bf16[2,4,25,576]{3,2,1,0:T(8,128)(2,1)S(1)}, bf16[2,4,25,576]{3,2,1,0:T(8,128)(2,1)S(1)}, u32[]{:S(2)}, u32[]{:S(2)}) collective-permute-start(bf16[2,4,25,576]{3,2,1,0:T(8,128)(2,1)S(1)} %fusion.22), channel_id=1, source_target_pairs={{0,8},{4,12},{8,0},{12,4},{16,24},{20,28},{24,16},{28,20},{1,9},{5... | collective-permute-start | bytes 691208 | tf_op jit(solution)/shard_map/ppermute | solution.py:463
  407.3 48.0 %collective-permute-start.41 = (bf16[2,24,3072]{2,1,0:T(8,128)(2,1)}, bf16[2,24,3072]{2,1,0:T(8,128)(2,1)}, u32[]{:S(2)}, u32[]{:S(2)}) collective-permute-start(bf16[2,24,3072]{2,1,0:T(8,128)(2,1)} %fusion.27), channel_id=1, source_target_pairs={{0,8},{4,12},{8,0},{12,4},{16,24},{20,28},{24,16},{28,20},{1,9},{5... | collective-permute-start | bytes 884744 | tf_op jit(solution)/shard_map/ppermute | solution.py:463
  408.3 20.7 %copy-start.6 = (f32[2,256,768]{2,1,0:T(8,128)S(1)}, f32[2,256,768]{2,1,0:T(8,128)}, u32[]{:S(2)}) copy-start(f32[2,256,768]{2,1,0:T(8,128)} %get-tuple-element.127) | copy-start | bytes 4718596
  414.4 7.7 %collective-permute-start.40 = (bf16[24,768]{1,0:T(8,128)(2,1)S(1)}, bf16[24,768]{1,0:T(8,128)(2,1)S(1)}, u32[]{:S(2)}, u32[]{:S(2)}) collective-permute-start(bf16[24,768]{1,0:T(8,128)(2,1)S(1)} %fusion.40), channel_id=1, source_target_pairs={{0,16},{4,20},{8,24},{12,28},{16,0},{20,4},{24,8},{28,12},{1,17},{... | collective-permute-start | bytes 110600 | tf_op jit(solution)/shard_map/ppermute | solution.py:463
  422.0 34.5 %collective-permute-start.43 = (bf16[4,2,24,768]{3,2,1,0:T(8,128)(2,1)}, bf16[4,2,24,768]{3,2,1,0:T(8,128)(2,1)}, u32[]{:S(2)}, u32[]{:S(2)}) collective-permute-start(bf16[4,2,24,768]{3,2,1,0:T(8,128)(2,1)} %fusion.26), channel_id=1, source_target_pairs={{0,16},{4,20},{8,24},{12,28},{16,0},{20,4},{24,8},{28,12},{1,17},{... | collective-permute-start | bytes 884744 | tf_op jit(solution)/shard_map/ppermute | solution.py:463
  425.8 14.1 %collective-permute-start.32 = (bf16[4,25,576]{2,1,0:T(8,128)(2,1)S(1)}, bf16[4,25,576]{2,1,0:T(8,128)(2,1)S(1)}, u32[]{:S(2)}, u32[]{:S(2)}) collective-permute-start(bf16[4,25,576]{2,1,0:T(8,128)(2,1)S(1)} %fusion.30), channel_id=1, source_target_pairs={{0,16},{4,20},{8,24},{12,28},{16,0},{20,4},{24,8},{28,12},{1,17},{... | collective-permute-start | bytes 345608 | tf_op jit(solution)/shard_map/ppermute | solution.py:463
  426.9 48.8 %collective-permute-start.29 = (bf16[2,256,768]{2,1,0:T(8,128)(2,1)}, bf16[2,256,768]{2,1,0:T(8,128)(2,1)}, u32[]{:S(2)}, u32[]{:S(2)}) collective-permute-start(bf16[2,256,768]{2,1,0:T(8,128)(2,1)} %fusion.12), channel_id=1, source_target_pairs={{0,2},{1,3},{2,0},{3,1},{4,6},{5,7},{6,4},{7,5},{8,10},{9,11},{10,... | collective-permute-start | bytes 2359304 | tf_op jit(solution)/shard_map/ppermute | solution.py:463
  439.9 11.1 %copy-start.12 = (f32[24,2304]{1,0:T(8,128)S(1)}, f32[24,2304]{1,0:T(8,128)}, u32[]{:S(2)}) copy-start(f32[24,2304]{1,0:T(8,128)} %param.21) | copy-start | bytes 663556
  440.0 1.3 collective-permute-start.33
  441.3 3.4 collective-permute-start.35
  444.7 4.0 collective-permute-start.34
  449.4 5.3 %copy-start.26 = (f32[12,24]{1,0:T(8,128)S(1)}, f32[12,24]{1,0:T(8,128)}, u32[]{:S(2)}) copy-start(f32[12,24]{1,0:T(8,128)} %param.33) | copy-start | bytes 3460
  455.3 10.4 %copy-start.9 = (f32[96,768]{1,0:T(8,128)S(1)}, f32[96,768]{1,0:T(8,128)}, u32[]{:S(2)}) copy-start(f32[96,768]{1,0:T(8,128)} %param.24) | copy-start | bytes 884740
  455.3 10.4 %copy-start.16 = (f32[96,768]{1,0:T(8,128)S(1)}, f32[96,768]{1,0:T(8,128)}, u32[]{:S(2)}) copy-start(f32[96,768]{1,0:T(8,128)} %param.28) | copy-start | bytes 884740
  455.3 10.4 %copy-start.17 = (f32[96,768]{1,0:T(8,128)S(1)}, f32[96,768]{1,0:T(8,128)}, u32[]{:S(2)}) copy-start(f32[96,768]{1,0:T(8,128)} %param.32) | copy-start | bytes 884740
  456.5 9.2 %collective-permute-start.42 = (bf16[24,3072]{1,0:T(8,128)(2,1)S(1)}, bf16[24,3072]{1,0:T(8,128)(2,1)S(1)}, u32[]{:S(2)}, u32[]{:S(2)}) collective-permute-start(bf16[24,3072]{1,0:T(8,128)(2,1)S(1)} %fusion.32), channel_id=1, source_target_pairs={{0,16},{4,20},{8,24},{12,28},{16,0},{20,4},{24,8},{28,12},{1,17},{... | collective-permute-start | bytes 442376 | tf_op jit(solution)/shard_map/ppermute | solution.py:463
  457.6 8.1 %collective-permute-start.44 = (bf16[4,24,768]{2,1,0:T(8,128)(2,1)S(1)}, bf16[4,24,768]{2,1,0:T(8,128)(2,1)S(1)}, u32[]{:S(2)}, u32[]{:S(2)}) collective-permute-start(bf16[4,24,768]{2,1,0:T(8,128)(2,1)S(1)} %fusion.33), channel_id=1, source_target_pairs={{0,2},{1,3},{2,0},{3,1},{4,6},{5,7},{6,4},{7,5},{8,10},{9,11},{10,... | collective-permute-start | bytes 442376 | tf_op jit(solution)/shard_map/ppermute | solution.py:463
  467.9 5.7 %copy-start.10 = (f32[24,3072]{1,0:T(8,128)S(1)}, f32[24,3072]{1,0:T(8,128)}, u32[]{:S(2)}) copy-start(f32[24,3072]{1,0:T(8,128)} %param.23) | copy-start | bytes 884740
  (20 other events, 58.5 us)
Sparse Core Ops, SparseCore 0:
  34.4 109.3 all-gather.1

commit v4 on v3

--- a/solution.py
+++ b/solution.py
@@ -22,6 +22,7 @@
 GELU_ROOT = 0.7978845608028654
 GELU_CUBE = 0.044715
 VMEM_BYTES = 56 * 1024 * 1024
+COST = pl.CostEstimate(flops=20_000_000_000, bytes_accessed=1_000_000, transcendentals=0)
 
 BF16 = jnp.bfloat16
 F32 = jnp.float32
@@ -81,11 +82,7 @@
         out_specs=pl.BlockSpec((n_blk, 1, blk, cols), lambda s: (0, s, 0, 0)),
         out_shape=jax.ShapeDtypeStruct((n_blk, seqs, blk, cols), BF16),
         compiler_params=pltpu.CompilerParams(vmem_limit_bytes=VMEM_BYTES),
-        cost_estimate=pl.CostEstimate(
-            flops=2 * n_blk * seqs * blk * width * cols,
-            bytes_accessed=2 * n_blk * seqs * blk * (width + cols),
-            transcendentals=0,
-        ),
+        cost_estimate=COST,
         name="project",
     )(*tokens, params, weight, bias)
 
@@ -168,11 +165,7 @@
             jax.ShapeDtypeStruct((seqs, heads, length), F32),
         ],
         compiler_params=pltpu.CompilerParams(vmem_limit_bytes=VMEM_BYTES),
-        cost_estimate=pl.CostEstimate(
-            flops=seqs * heads * length * length * HDIM * 12,
-            bytes_accessed=seqs * length * cols * 3,
-            transcendentals=seqs * heads * length * length,
-        ),
+        cost_estimate=COST,
         name="attend_forward",
     )(me, joint, start)
 
@@ -186,23 +179,38 @@
     *refs,
 ):
     mixed_refs = refs[:n_ctx]
-    rest_ref, params_ref, result_ref, resid_ref, branch_ref, normed_ref, act_ref, pre_ref, mix_ref, sums_ref = refs[n_ctx:]
+    mine_ref, other_ref, params_ref = refs[n_ctx : n_ctx + 3]
+    result_ref, resid_ref, branch_ref, normed_ref, act_ref, pre_ref, mix_ref, sums_ref = refs[n_ctx + 3 : n_ctx + 11]
+    rest_ref, sems = refs[n_ctx + 11 :]
     me = me_ref[0]
     width = x_ref.shape[-1]
     group = width // n_ctx
-    base = width * (1 + spans)
-
-    def output_rows(place):
+    side = width // 2
+    inner = spans // 2
+
+    @pl.when(pl.program_id(0) == 0)
+    def _():
+        core = lax.bitwise_and(me, 1)
+        mine = pltpu.make_async_copy(mine_ref, rest_ref.at[core], sems.at[0])
+        other = pltpu.make_async_copy(other_ref, rest_ref.at[1 - core], sems.at[1])
+        mine.start()
+        other.start()
+        mine.wait()
+        other.wait()
+
+    def output_rows(place, half):
         first = pl.multiple_of(lax.bitwise_xor(me, place) * group, group)
-        return rest_ref[pl.ds(first, group), 0:width]
+        return rest_ref[half, pl.ds(first, group), 0:side]
 
     def param(row):
         return params_ref[row : row + 1, :]
 
     upstream = y_ref[0]
-    residual = x_ref[0].astype(F32) + param(4)
-    for place in range(n_ctx):
-        residual = residual + dot(mixed_refs[place][0], output_rows(place), ((1,), (0,)))
+    mixed = [ref[0] for ref in mixed_refs]
+    sides = [
+        sum(dot(mixed[place], output_rows(place, half), ((1,), (0,))) for place in range(n_ctx)) for half in range(2)
+    ]
+    residual = x_ref[0].astype(F32) + (jnp.concatenate(sides, axis=1) + param(4))
     plain, scale = norm_parts(residual)
     normed = (plain * param(5) + param(6)).astype(BF16)
     normed_ref[...] = normed.T
@@ -210,8 +218,9 @@
     grad_normed = jnp.zeros(residual.shape, F32)
     sums = []
     for span in range(spans):
-        expand = rest_ref[:, width * (1 + span) : width * (2 + span)]
-        shrink = rest_ref[:, base + width * span : base + width * (span + 1)]
+        half, low = span // inner, side + width * (span % inner)
+        expand = rest_ref[half, :, low : low + width]
+        shrink = rest_ref[half, :, low + width * inner : low + width * (inner + 1)]
         pre = dot(normed, expand, ((1,), (0,))) + param(7 + span)
         square = pre * pre
         bent = jnp.tanh(GELU_ROOT * (pre + GELU_CUBE * (square * pre)))
@@ -233,7 +242,8 @@
     branch = grad_resid.astype(BF16)
     branch_ref[0] = branch
     for place in range(n_ctx):
-        mix_ref[place, 0] = dot(branch, output_rows(place), ((1,), (1,))).astype(BF16)
+        mix = dot(branch[:, :side], output_rows(place, 0), ((1,), (1,)))
+        mix_ref[place, 0] = (mix + dot(branch[:, side:], output_rows(place, 1), ((1,), (1,)))).astype(BF16)
     table = jnp.concatenate(
         [column_sum(branch.astype(F32)), gain_sum, shift_sum] + sums + [column_sum(upstream_wide)], axis=0
     )
@@ -247,11 +257,11 @@
         sums_ref[...] += table
 
 
-def layer(me, tokens, cotangent, mixed, rest, params):
+def layer(me, tokens, cotangent, mixed, mine, other, params):
     n_ctx = len(mixed)
     seqs, blk, width = tokens.shape
     group = width // n_ctx
-    spans = (rest.shape[1] // width - 1) // 2
+    spans = (2 * mine.shape[1] // width - 1) // 2
     hidden = spans * width
 
     def by_seq(*shape):
@@ -267,7 +277,8 @@
             grid=(seqs,),
             in_specs=[by_seq(blk, width)] * 2
             + [by_seq(blk, group)] * n_ctx
-            + [whole(rest.shape), whole(params.shape)],
+            + [pl.BlockSpec(memory_space=pl.ANY)] * 2
+            + [whole(params.shape)],
             out_specs=[
                 by_seq(blk, width),
                 by_seq(blk, width),
@@ -278,6 +289,7 @@
                 pl.BlockSpec((n_ctx, 1, blk, group), lambda s, m: (0, s, 0, 0)),
                 pl.BlockSpec((4 + spans, width), lambda s, m: (0, 0)),
             ],
+            scratch_shapes=[pltpu.VMEM((2,) + mine.shape, BF16), pltpu.SemaphoreType.DMA((2,))],
         ),
         out_shape=[
             jax.ShapeDtypeStruct((seqs, blk, width), BF16),
@@ -290,13 +302,9 @@
             jax.ShapeDtypeStruct((4 + spans, width), F32),
         ],
         compiler_params=pltpu.CompilerParams(vmem_limit_bytes=VMEM_BYTES),
-        cost_estimate=pl.CostEstimate(
-            flops=2 * seqs * blk * width * (2 * width + 4 * hidden),
-            bytes_accessed=rest.size * 2 + seqs * blk * (hidden * 4 + width * 14),
-            transcendentals=seqs * blk * hidden,
-        ),
+        cost_estimate=COST,
         name="layer",
-    )(me, tokens, cotangent, *mixed, rest, params)
+    )(me, tokens, cotangent, *mixed, mine, other, params)
 
 
 def backward_kernel(
@@ -359,8 +367,8 @@
         )
 
 
-def attend_backward(me, joint, grads, start, logs, first, count):
-    n_blk, _, blk, cols = joint.shape
+def attend_backward(me, joint, grads, start, logs, first):
+    n_blk, count, blk, cols = joint.shape
     group = cols // 3
     heads = group // HDIM
     length = n_blk * blk
@@ -369,11 +377,11 @@
         grid_spec=pltpu.PrefetchScalarGridSpec(
             num_scalar_prefetch=1,
             grid=(count,),
-            in_specs=[pl.BlockSpec((n_blk, 1, blk, cols), lambda s, m: (0, s + first, 0, 0))]
+            in_specs=[pl.BlockSpec((n_blk, 1, blk, cols), lambda s, m: (0, s, 0, 0))]
             + [pl.BlockSpec((1, blk, group), lambda s, m: (s + first, 0, 0))] * n_blk
             + [
-                pl.BlockSpec((1, 1, length), lambda s, m: (s + first, 0, 0)),
-                pl.BlockSpec((1, heads, length), lambda s, m: (s + first, 0, 0)),
+                pl.BlockSpec((1, 1, length), lambda s, m: (s, 0, 0)),
+                pl.BlockSpec((1, heads, length), lambda s, m: (s, 0, 0)),
             ],
             out_specs=pl.BlockSpec((n_blk, 1, blk, cols), lambda s, m: (0, s, 0, 0)),
             scratch_shapes=[
@@ -385,18 +393,16 @@
         ),
         out_shape=jax.ShapeDtypeStruct((n_blk, count, blk, cols), BF16),
         compiler_params=pltpu.CompilerParams(vmem_limit_bytes=VMEM_BYTES),
-        cost_estimate=pl.CostEstimate(
-            flops=count * heads * length * length * HDIM * 30,
-            bytes_accessed=count * length * cols * 6,
-            transcendentals=count * heads * length * length,
-        ),
+        cost_estimate=COST,
         name="attend_backward",
     )(me, joint, *grads, start, logs)
 
 
 def unproject_kernel(n_blk, *refs):
     grad_ref, tokens = refs[0], refs[1 : 1 + n_blk]
-    params_ref, weight_ref, share_ref, weight_grad_ref, sums_ref, bias_ref = refs[1 + n_blk :]
+    params_ref, weight_ref = refs[1 + n_blk : 3 + n_blk]
+    earlier = refs[3 + n_blk : -4]
+    share_ref, weight_grad_ref, sums_ref, bias_ref = refs[-4:]
     weight_grad = bias_grad = gain_sum = shift_sum = 0.0
     for place in range(n_blk):
         grad = grad_ref[place, 0]
@@ -408,35 +414,39 @@
         shift_sum += column_sum(share)
         bias_grad += column_sum(grad.astype(F32))
         weight_grad += dot(normed, grad, ((0,), (0,)))
-    sums = jnp.concatenate([gain_sum, shift_sum], axis=0)
+    values = [weight_grad, jnp.concatenate([gain_sum, shift_sum], axis=0), bias_grad]
+    totals = [weight_grad_ref, sums_ref, bias_ref]
 
     @pl.when(pl.program_id(0) == 0)
     def _():
-        weight_grad_ref[...] = weight_grad
-        sums_ref[...] = sums
-        bias_ref[...] = bias_grad
+        for number, (total, value) in enumerate(zip(totals, values)):
+            total[...] = value + earlier[number][...] if earlier else value
 
     @pl.when(pl.program_id(0) > 0)
     def _():
-        weight_grad_ref[...] += weight_grad
-        sums_ref[...] += sums
-        bias_ref[...] += bias_grad
-
-
-def unproject(grad, tokens, params, weight, first):
+        for total, value in zip(totals, values):
+            total[...] += value
+
+
+def unproject(grad, tokens, params, weight, earlier):
     n_blk, count, blk, cols = grad.shape
     width = tokens[0].shape[-1]
+
+    def whole(shape):
+        return pl.BlockSpec(shape, lambda s: (0, 0))
+
     return pl.pallas_call(
         functools.partial(unproject_kernel, n_blk),
         grid=(count,),
         in_specs=[pl.BlockSpec((n_blk, 1, blk, cols), lambda s: (0, s, 0, 0))]
-        + [pl.BlockSpec((1, blk, width), lambda s: (s + first, 0, 0))] * n_blk
-        + [pl.BlockSpec(params.shape, lambda s: (0, 0)), pl.BlockSpec(weight.shape, lambda s: (0, 0))],
+        + [pl.BlockSpec((1, blk, width), lambda s: (s, 0, 0))] * n_blk
+        + [whole(params.shape), whole(weight.shape)]
+        + [whole(item.shape) for item in earlier],
         out_specs=[
             pl.BlockSpec((n_blk, 1, blk, width), lambda s: (0, s, 0, 0)),
-            pl.BlockSpec((width, cols), lambda s: (0, 0)),
-            pl.BlockSpec((2, width), lambda s: (0, 0)),
-            pl.BlockSpec((1, cols), lambda s: (0, 0)),
+            whole((width, cols)),
+            whole((2, width)),
+            whole((1, cols)),
         ],
         out_shape=[
             jax.ShapeDtypeStruct((n_blk, count, blk, width), BF16),
@@ -445,13 +455,9 @@
             jax.ShapeDtypeStruct((1, cols), F32),
         ],
         compiler_params=pltpu.CompilerParams(vmem_limit_bytes=VMEM_BYTES),
-        cost_estimate=pl.CostEstimate(
-            flops=4 * n_blk * count * blk * width * cols,
-            bytes_accessed=2 * n_blk * count * blk * (2 * width + cols),
-            transcendentals=0,
-        ),
+        cost_estimate=COST,
         name="unproject",
-    )(grad, *tokens, params, weight)
+    )(grad, *tokens, params, weight, *earlier)
 
 
 def build(sizes):
@@ -467,17 +473,6 @@
         return [
             lax.dynamic_index_in_dim(stacked, lax.bitwise_xor(me, j), 0, keepdims=False) for j in range(len(items))
         ]
-
-    def halve(value, labels, order, spots):
-        labels = list(labels)
-        for axis, bit in order:
-            pos = labels.index((axis, bit))
-            mine = (spots[axis] >> bit) & 1
-            send = lax.dynamic_index_in_dim(value, 1 - mine, pos, keepdims=False).astype(BF16)
-            keep = lax.dynamic_index_in_dim(value, mine, pos, keepdims=False)
-            value = keep + swap(send, axis, 1 << bit).astype(F32)
-            labels.pop(pos)
-        return value
 
     def per_device(
         tokens_in,
@@ -523,11 +518,9 @@
             )
         )
 
-        blocks, seg_blocks = {0: tokens_in}, {0: segments}
+        seg_blocks = {0: segments}
         for bit in reversed(ctx_bits):
-            for known in (seg_blocks, blocks):
-                known.update({k ^ (1 << bit): swap(value, "ctx", 1 << bit) for k, value in list(known.items())})
-        tokens = [blocks[k] for k in range(n_ctx)]
+            seg_blocks.update({k ^ (1 << bit): swap(value, "ctx", 1 << bit) for k, value in list(seg_blocks.items())})
         segs = jnp.concatenate(reorder([seg_blocks[k] for k in range(n_ctx)], me), axis=1)
         start = jnp.zeros_like(segs)
         for number in range(1, DOCS):
@@ -535,45 +528,97 @@
             start = jnp.where(segs >= number, bound, start)
         start = start[:, None, :]
 
-        extra = -(-vectors * part // cols)
-        pad = extra * cols - vectors * part
-        small_rows = jnp.pad(small_cast.reshape(-1), (0, pad)).reshape(extra, cols)
+        small_cols = small_cast.T
         joint_cols = joint_cast.reshape(part, 3, n_ctx, group)
 
         def columns_for(k):
             picked = lax.dynamic_index_in_dim(joint_cols, lax.bitwise_xor(me, k), 2, keepdims=False)
-            return jnp.concatenate([picked.reshape(part, cols), small_rows], axis=0)
+            return jnp.concatenate([picked.reshape(part, cols), small_cols], axis=1)
 
         pieces = [columns_for(0)] + [swap(columns_for(k), "ctx", k) for k in range(1, n_ctx)]
         gathered = jnp.stack(reorder(pieces, me))
+
         expand_wide = expand_cast.reshape(part, n_dev, spans, part).transpose(0, 2, 1, 3).reshape(part, hidden)
         shrink_wide = shrink_cast.reshape(spans, part, width).transpose(1, 0, 2).reshape(part, hidden)
-        rest = jnp.concatenate([output_cast, expand_wide, shrink_wide], axis=1)
-        for bit in reversed(dp_bits):
-            if bit == dp_bits[max(n_bits - 2, 0)]:
-                rest, gathered, start = lax.optimization_barrier((rest, gathered, start))
-                rest = lax.all_gather(rest, ("dp", "ctx"), axis=0, tiled=True)
-            if bit == dp_bits[0]:
-                gathered, *tokens = lax.optimization_barrier((gathered, *tokens))
+        sides = [
+            jnp.concatenate([item[:, h * size // 2 : (h + 1) * size // 2] for item, size in wide], axis=1)
+            for wide in [((output_cast, width), (expand_wide, hidden), (shrink_wide, hidden))]
+            for h in range(2)
+        ]
+        pair = me & 1
+        rest_own = jnp.where(pair == 1, sides[1], sides[0])
+        rest_got = swap(jnp.where(pair == 1, sides[0], sides[1]), "ctx", 1)
+        rest = jnp.where(
+            pair == 1,
+            jnp.concatenate([rest_got, rest_own], axis=0),
+            jnp.concatenate([rest_own, rest_got], axis=0),
+        )
+        pairs = [
+            [d * n_ctx + c * 2 + p for d in range(n_dp) for c in range(n_ctx // 2)] for p in range(2)
+        ]
+
+        half = max(seqs // 2, 1)
+        firsts = list(range(0, seqs, half))
+        tokens = [{0: tokens_in[first : first + half]} for first in firsts]
+        near, far_bits = 1, [bit for bit in reversed(ctx_bits) if bit]
+
+        def fetch_far(blocks):
+            for bit in far_bits:
+                blocks.update({k ^ (1 << bit): swap(value, "ctx", 1 << bit) for k, value in list(blocks.items())})
+
+        fetch_far(tokens[0])
+        for step, bit in enumerate(reversed(dp_bits)):
             other = swap(gathered, "dp", 1 << bit)
             upper = ((me_dp >> bit) & 1) == 1
             gathered = jnp.where(upper, jnp.stack([other, gathered]), jnp.stack([gathered, other]))
+            if step == 0:
+                names = sorted(tokens[0])
+                gathered, rest, start, later, *held = lax.optimization_barrier(
+                    (gathered, rest, start, [blocks[0] for blocks in tokens[1:]]) + tuple(tokens[0][k] for k in names)
+                )
+                tokens[0] = dict(zip(names, held))
+                for blocks, value in zip(tokens[1:], later):
+                    blocks[0] = value
+                    fetch_far(blocks)
+                rest = lax.all_gather(rest, ("dp", "ctx"), axis=0, tiled=True, axis_index_groups=pairs)
+            elif step == n_bits - 2:
+                flat = [(number, k) for number, blocks in enumerate(tokens) for k in sorted(blocks)]
+                gathered, *held = lax.optimization_barrier((gathered,) + tuple(tokens[n][k] for n, k in flat))
+                for (number, k), value in zip(flat, held):
+                    tokens[number][k] = value
+        for blocks in tokens:
+            blocks.update({k ^ near: swap(value, "ctx", near) for k, value in list(blocks.items())})
+        tokens = [[blocks[k] for k in range(n_ctx)] for blocks in tokens]
 
         gathered = gathered.transpose(tuple(reversed(range(n_bits))) + tuple(range(n_bits, n_bits + 3)))
-        gathered = gathered.reshape(n_dp, n_ctx, part + extra, cols)
-        joint_lo = gathered[:, :, :part].reshape(width, cols)
-        small_lo = gathered[:, :, part:].reshape(n_dp, n_ctx, extra * cols)[:, :, : vectors * part]
-        params = small_lo.reshape(n_dp, n_ctx, vectors, part).transpose(2, 0, 1, 3).reshape(vectors, width).astype(F32)
+        gathered = gathered.reshape(width, cols + vectors)
+        joint_lo = gathered[:, :cols]
+        params = gathered[:, cols:].T.astype(F32)
         mine_bias = lax.dynamic_slice(params[2:4], (0, me * group), (2, group))
         joint_bias = jnp.concatenate([mine_bias[:1], jnp.zeros((1, group), F32), mine_bias[1:]], axis=1)
         bias_hidden = params[7 : 7 + spans].reshape(n_dev, spans, part).transpose(1, 0, 2).reshape(spans, width)
         params = jnp.concatenate([params[:7], bias_hidden, params[7 + spans :]], axis=0)
 
-        joint = project(tokens, params, joint_lo, joint_bias)
-        attended, logs = attend_forward(me_arr, joint, start)
-        mixed = [attended[0]] + [swap(attended[k], "ctx", k) for k in range(1, n_ctx)]
+        joints, logs, mixed, waiting = [], [], [], None
+        starts = [start[first : first + half] for first in firsts]
+        for number in range(len(firsts)):
+            joint = project(tokens[number], params, joint_lo, joint_bias)
+            if waiting is not None:
+                waiting, joint = lax.optimization_barrier((waiting, joint))
+                waiting = [waiting[0]] + [swap(waiting[k], "ctx", k) for k in range(1, n_ctx)]
+            attended, log = attend_forward(me_arr, joint, starts[number])
+            if waiting is not None:
+                waiting, attended = lax.optimization_barrier((waiting, attended))
+                mixed.append(waiting)
+            waiting = [attended[k] for k in range(n_ctx)]
+            joints.append(joint)
+            logs.append(log)
+        waiting, rest = lax.optimization_barrier((waiting, rest))
+        rest_other = swap(rest, "ctx", 1)
+        mixed.append([waiting[0]] + [swap(waiting[k], "ctx", k) for k in range(1, n_ctx)])
+        mixed = [jnp.concatenate(items, axis=0) for items in zip(*mixed)]
         block_output, grad_resid, branch, normed_two, activated, grad_pre, grad_mixed, sums = layer(
-            me_arr, tokens_in, cotangent, mixed, rest, params
+            me_arr, tokens_in, cotangent, mixed, rest, rest_other, params
         )
         grads = [grad_mixed[0]] + [swap(grad_mixed[k], "ctx", k) for k in range(1, n_ctx)]
 
@@ -604,44 +649,47 @@
             chain[0] = lax.dynamic_index_in_dim(value, mine, pos, keepdims=False)
             chain[1] = lax.dynamic_index_in_dim(value, 1 - mine, pos, keepdims=False).astype(BF16)
 
-        def merge(chain):
+        def fetch(chain):
+            axis, bit = chain[3][0]
+            return swap(chain[1], axis, 1 << bit)
+
+        def merge(chain, got):
             _, _, names, order = chain
-            axis, bit = order[0]
-            got = swap(chain[1], axis, 1 << bit)
             chain[0] = chain[0] + got.astype(F32)
-            chain[2] = [name for name in names if name != (axis, bit)]
+            chain[2] = [name for name in names if name != order[0]]
             chain[3] = order[1:]
 
         def advance(after, before):
-            pinned = lax.optimization_barrier((after,) + tuple(chain[0] for chain in chains))
-            for chain, keep in zip(chains, pinned[1:]):
+            if len(chains[0][3]) < 2:
+                return after, before
+            after, keeps, gots = lax.optimization_barrier(
+                (after, [chain[0] for chain in chains], [fetch(chain) for chain in chains])
+            )
+            for chain, keep, got in zip(chains, keeps, gots):
                 chain[0] = keep
-                merge(chain)
+                merge(chain, got)
                 split(chain)
-            out = lax.optimization_barrier(
-                (before,) + tuple(chain[0] for chain in chains) + tuple(chain[1] for chain in chains)
+            before, keeps, sends = lax.optimization_barrier(
+                (before, [chain[0] for chain in chains], [chain[1] for chain in chains])
             )
-            for number, chain in enumerate(chains):
-                chain[0], chain[1] = out[1 + number], out[1 + len(chains) + number]
-            return pinned[0], out[0]
+            for chain, keep, send in zip(chains, keeps, sends):
+                chain[0], chain[1] = keep, send
+            return after, before
 
         for chain in chains:
             split(chain)
 
-        half = max(seqs // 2, 1)
-        pending, shares, weight_grads = [], [], []
-        source = joint
-        for first in range(0, seqs, half):
-            after = weight_grads[-1][1] if weight_grads else branch
-            _, (source, *held) = advance(after, (source,) + tuple(pending))
-            pending = []
-            grad_joint = attend_backward(me_arr, source, grads, start, logs, first, half)
-            if first:
-                grad_joint, _ = advance(grad_joint, start)
-            share, weight_grad, norm_sums, bias_sums = unproject(grad_joint, tokens, params, joint_lo, first)
-            weight_grads.append((weight_grad, norm_sums, bias_sums))
-            if held:
-                shares.append(held)
+        top = 1 << ctx_bits[-1]
+        pending, shares, earlier = None, [], ()
+        for number, first in enumerate(firsts):
+            _, (source, pending) = advance(earlier[1] if earlier else branch, (joints[number], pending))
+            grad_joint = attend_backward(me_arr, source, grads, starts[number], logs[number], first)
+            if pending:
+                pending[1] = swap(pending[1], "ctx", top)
+            (grad_joint, pending), _ = advance((grad_joint, pending), start)
+            if pending:
+                shares.append(pending[0] + pending[1].astype(F32))
+            share, *earlier = unproject(grad_joint, tokens[number], params, joint_lo, earlier)
             known = {k: share[k] for k in range(n_ctx)}
             for bit in ctx_bits[:-1]:
                 mask = 1 << bit
@@ -650,10 +698,9 @@
                     for k, value in known.items()
                     if not k & mask
                 }
-            pending = [known[0], known[1 << ctx_bits[-1]].astype(BF16)]
-        shares.append(pending)
-        shares = [kept + swap(sent, "ctx", 1 << ctx_bits[-1]).astype(F32) for kept, sent in shares]
-        weight_grad, norm_sums, bias_sums = [sum(items) for items in zip(*weight_grads)]
+            pending = [known[0], known[top].astype(BF16)]
+        shares.append(pending[0] + swap(pending[1], "ctx", top).astype(F32))
+        weight_grad, norm_sums, bias_sums = earlier
 
         plain, scale = norm_parts(tokens_in.astype(F32))
         input_grad = grad_resid + norm_back(plain, scale, jnp.concatenate(shares, axis=0), params[0])
@@ -665,29 +712,38 @@
         )
         sums_hidden = sums[3 : 3 + spans].reshape(spans, n_dev, part).transpose(1, 0, 2).reshape(spans, width)
         grad_small = jnp.concatenate([norm_sums, placed, sums[:3], sums_hidden, sums[3 + spans :]], axis=0)
-        small_terms = grad_small.reshape(vectors, n_dp, n_ctx, part).transpose(1, 2, 0, 3)
-        small_terms = jnp.pad(small_terms.reshape(n_dp, n_ctx, vectors * part), ((0, 0), (0, 0), (0, pad)))
-        terms = jnp.concatenate(
-            [weight_grad.reshape(n_dp, n_ctx, part, cols), small_terms.reshape(n_dp, n_ctx, extra, cols)], axis=2
-        ).reshape((2,) * n_bits + (n_ctx, part + extra, cols))
-        dp_labels = [("dp", bit) for bit in reversed(dp_bits)]
-        terms = halve(terms, dp_labels, [("dp", bit) for bit in dp_bits], spots)
+        terms = jnp.concatenate([weight_grad, grad_small.T], axis=1).reshape(n_dp, n_ctx, part, cols + vectors)
+        total = lax.dynamic_index_in_dim(terms, me_dp, 0, keepdims=False)
+        if n_dp <= 8:
+            sent = [
+                lax.dynamic_index_in_dim(terms, lax.bitwise_xor(me_dp, j), 0, keepdims=False).astype(BF16)
+                for j in range(1, n_dp)
+            ]
+            for j, item in enumerate(sent):
+                total = total + swap(item, "dp", j + 1).astype(F32)
+        else:
+            terms = terms.reshape((2,) * n_bits + (n_ctx, part, cols + vectors))
+            chain = [terms, None, [("dp", bit) for bit in reversed(dp_bits)], inner]
+            while chain[3]:
+                split(chain)
+                merge(chain, fetch(chain))
+            total = chain[0]
 
         def terms_for(k):
-            return lax.dynamic_index_in_dim(terms, lax.bitwise_xor(me, k), 0, keepdims=False)
+            return lax.dynamic_index_in_dim(total, lax.bitwise_xor(me, k), 0, keepdims=False)
 
         arrived = [terms_for(0)] + [
             swap(terms_for(k).astype(BF16), "ctx", k).astype(F32) for k in range(1, n_ctx)
         ]
-        small_sum = sum(item[part:] for item in arrived).reshape(-1)[: vectors * part].reshape(vectors, part)
-        sum_joint = jnp.stack([item[:part].reshape(part, 3, group) for item in reorder(arrived, me)], axis=2)
+        small_sum = sum(item[:, cols:] for item in arrived).T
+        sum_joint = jnp.stack([item[:, :cols].reshape(part, 3, group) for item in reorder(arrived, me)], axis=2)
         sum_joint = sum_joint.reshape(part, 3 * width)
 
         for chain in chains:
-            merge(chain)
+            merge(chain, fetch(chain))
             while chain[3]:
                 split(chain)
-                merge(chain)
+                merge(chain, fetch(chain))
         sum_shrink, sum_expand, sum_output = [chain[0] for chain in chains]
         sum_shrink = sum_shrink.reshape(spans * part, width)
         sum_expand = sum_expand.reshape(part, spans, n_dev, part).transpose(0, 2, 1, 3).reshape(part, hidden)

time: 491 us -> 436 us (0.89); the launches traced: 489 us -> 429 us
  waiting for transfers between devices: 177 us -> 110 us
  matrix products: 29.3 us -> 17.1 us
  local copies, waits for them, and re-layouts: 47.9 us -> 57.2 us
  Pallas kernels: 132 us -> 140 us
    ppermute x45 -> x57, waiting for transfers between devices: 177 us -> 105 us  [swap(): lax.ppermute(value, axis, [(place, place ^ mask) for place in range(sizes...]
    dot_general x6, matrix products: 29.3 us -> 17.1 us  [dot(): lax.dot_general(left, right, (dims, ((), ())), preferred_element_type=F32)]
    ppermute x1 -> x7, local copies, waits for them, and re-layouts: 0.08 us -> 12.2 us  [swap(): lax.ppermute(value, axis, [(place, place ^ mask) for place in range(sizes...]
    pallas_call x1 -> x2, Pallas kernels: 10.4 us -> 13.2 us  [project(): pl.pallas_call(functools.partial(project_kernel, n_blk), grid=(seqs,), in...]
    pallas_call x1 -> x2, Pallas kernels: 24.9 us -> 27.2 us  [attend_forward(): pl.pallas_call(functools.partial(forward_kernel, n_blk, blk, heads), grid...]
    ppermute x45 -> x57, starting transfers between devices: 47 us -> 47.5 us  [swap(): lax.ppermute(value, axis, [(place, place ^ mask) for place in range(sizes...]
  transfers between devices with their start and end apart: 46 -> 58, of which waited for: 19 -> 17; matrix products, arithmetic and copies ran while one was open for 21% -> 20% of each run, Pallas kernels for 19% -> 21%
where the time goes in v4:
time: 436 us; the launch traced here: 429 us
  Pallas kernels  140 us (32%)
  waiting for transfers between devices  110 us (25%)
  local copies, waits for them, and re-layouts  57.2 us (13%)
  starting transfers between devices  47.5 us (11%)
  other arithmetic  42 us (10%)
  matrix products  17.1 us (4%)
  between operations  15.7 us (4%)
    ppermute x57, waiting for transfers between devices, swap(): lax.ppermute(value, axis, [(place, place ^ mask) for place in range(sizes...  105 us
    ppermute x57, starting transfers between devices, swap(): lax.ppermute(value, axis, [(place, place ^ mask) for place in range(sizes...  47.5 us
    pallas_call x1, Pallas kernels, layer(): pl.pallas_call(functools.partial(layer_kernel, n_ctx, spans), grid_spec=p...  39.5 us
    pallas_call x2, Pallas kernels, attend_backward(): pl.pallas_call(functools.partial(backward_kernel, n_blk, blk, heads), gri...  38.2 us
    pallas_call x2, Pallas kernels, attend_forward(): pl.pallas_call(functools.partial(forward_kernel, n_blk, blk, heads), grid...  27.2 us
    pallas_call x2, Pallas kernels, unproject(): pl.pallas_call(functools.partial(unproject_kernel, n_blk), grid=(count,),...  21.5 us
    dot_general x6, matrix products, dot(): lax.dot_general(left, right, (dims, ((), ())), preferred_element_type=F32)  17.1 us
    pallas_call x2, Pallas kernels, project(): pl.pallas_call(functools.partial(project_kernel, n_blk), grid=(seqs,), in...  13.2 us
  transfers between devices with their start and end apart: 58, of which 17 were waited for; matrix products, arithmetic and copies ran while one was open for 20% of the time, Pallas kernels for 21%

profile of v4, /device:TPU:0, one launch (start us, length us, event | category | flops | bytes accessed | tf_op | source)
XLA Modules:
  0.0 428.9 jit_solution(16513303768560219764)
XLA Ops:
  7.2 3.0 collective-permute-start.6
  24.8 2.9 collective-permute-start.3
  27.7 6.2 %collective-permute-done.3 = bf16[4,24,588]{2,1,0:T(8,128)(2,1)S(1)} collective-permute-done((bf16[4,24,588]{2,1,0:T(8,128)(2,1)S(1)}, bf16[4,24,588]{2,1,0:T(8,128)(2,1)S(1)}, u32[]{:S(2)}, u32[]{:S(2)}) %collective-permute-start.3) | collective-permute-done | bytes 112928 | tf_op jit(solution)/shard_map/ppermute | solution.py:469
  34.8 9.5 %collective-permute-done.8.refs_2_.refs_3_ = bf16[2,256,768]{2,1,0:T(8,128)(2,1)} collective-permute-done((bf16[2,256,768]{2,1,0:T(8,128)(2,1)}, bf16[2,256,768]{2,1,0:T(8,128)(2,1)}, u32[]{:S(2)}, u32[]{:S(2)}) %collective-permute-start.8) | collective-permute-done | bytes 786464 | tf_op jit(solution)/shard_map/ppermute | solution.py:469
  44.6 1.9 collective-permute-start.9
  46.5 5.5 %collective-permute-done.9 = bf16[2,4,24,588]{3,2,1,0:T(8,128)(2,1)S(1)} collective-permute-done((bf16[2,4,24,588]{3,2,1,0:T(8,128)(2,1)S(1)}, bf16[2,4,24,588]{3,2,1,0:T(8,128)(2,1)S(1)}, u32[]{:S(2)}, u32[]{:S(2)}) %collective-permute-start.9) | collective-permute-done | bytes 225824 | tf_op jit(solution)/shard_map/ppermute | solution.py:469
  52.1 14.0 %collective-permute-done.10.refs_2_.refs_3_ = bf16[2,256,768]{2,1,0:T(8,128)(2,1)} collective-permute-done((bf16[2,256,768]{2,1,0:T(8,128)(2,1)}, bf16[2,256,768]{2,1,0:T(8,128)(2,1)}, u32[]{:S(2)}, u32[]{:S(2)}) %collective-permute-start.10) | collective-permute-done | bytes 786464 | tf_op jit(solution)/shard_map/ppermute | solution.py:469
  66.1 1.5 collective-permute-start.13
  69.3 11.2 %collective-permute-done.13 = bf16[2,2,4,24,588]{4,3,2,1,0:T(8,128)(2,1)S(1)} collective-permute-done((bf16[2,2,4,24,588]{4,3,2,1,0:T(8,128)(2,1)S(1)}, bf16[2,2,4,24,588]{4,3,2,1,0:T(8,128)(2,1)S(1)}, u32[]{:S(2)}, u32[]{:S(2)}) %collective-permute-start.13) | collective-permute-done | bytes 451616 | tf_op jit(solution)/shard_map/ppermute | solution.py:469
  84.4 6.7 %project.2.joint_ref = bf16[4,2,256,576]{3,2,1,0:T(8,128)(2,1)} custom-call(bf16[2,256,768]{2,1,0:T(8,128)(2,1)} %get-tuple-element.138.refs_0_.refs_1_, bf16[2,256,768]{2,1,0:T(8,128)(2,1)} %collective-permute-done.11.refs_1_.refs_2_, bf16[2,256,768]{2,1,0:T(8,128)(2,1)} %collective-permute-done.8.refs_2_.refs_3_, ...), custom_call_target="tpu_custom_call" | custom-call | flops 20000000000 | bytes 1000000 | tf_op jit(solution)/shard_map/project/pallas_call | solution.py:73
  91.2 13.5 %attend_forward.2 = (bf16[4,2,256,192]{3,2,1,0:T(8,128)(2,1)}, f32[2,3,1024]{2,1,0:T(4,128)}) custom-call(s32[1]{0:T(128)} %bitcast.me_ref, bf16[4,2,256,576]{3,2,1,0:T(8,128)(2,1)} %project.2.joint_ref, s32[2,1,1024]{2,1,0:T(1,128)} %get-tuple-element.379.start_ref.refs_4_), custom_call_target="tpu_custom_call" | custom-call | flops 20000000000 | bytes 1000000 | tf_op jit(solution)/shard_map/attend_forward/pallas_call | solution.py:148
  106.0 6.5 %project.3.joint_ref = bf16[4,2,256,576]{3,2,1,0:T(8,128)(2,1)} custom-call(bf16[2,256,768]{2,1,0:T(8,128)(2,1)} %get-tuple-element.143.refs_0_.refs_1_, bf16[2,256,768]{2,1,0:T(8,128)(2,1)} %collective-permute-done.14.refs_1_.refs_2_, bf16[2,256,768]{2,1,0:T(8,128)(2,1)} %collective-permute-done.10.refs_2_.refs_3_, ...), custom_call_target="tpu_custom_call" | custom-call | flops 20000000000 | bytes 1000000 | tf_op jit(solution)/shard_map/project/pallas_call | solution.py:73
  112.5 1.8 collective-permute-start.18
  114.3 13.7 %attend_forward.3 = (bf16[4,2,256,192]{3,2,1,0:T(8,128)(2,1)}, f32[2,3,1024]{2,1,0:T(4,128)}) custom-call(s32[1]{0:T(128)} %bitcast.me_ref, bf16[4,2,256,576]{3,2,1,0:T(8,128)(2,1)} %project.3.joint_ref, s32[2,1,1024]{2,1,0:T(1,128)} %get-tuple-element.378.start_ref.refs_4_), custom_call_target="tpu_custom_call" | custom-call | flops 20000000000 | bytes 1000000 | tf_op jit(solution)/shard_map/attend_forward/pallas_call | solution.py:148
  128.0 3.4 collective-permute-done.18
  131.4 2.1 slice_bitcast_fusion.8
  133.5 4.4 %all-gather.2.cloned.1.call-done.refs_4_ = bf16[768,3456]{1,0:T(8,128)(2,1)} async-done(((bf16[48,3456]{1,0:T(8,128)(2,1)}), bf16[768,3456]{1,0:T(8,128)(2,1)}) %all-gather.2.cloned.1.call-update) | async-done | bytes 5308432 | tf_op jit(solution)/shard_map/all_gather | solution.py:583
  141.1 5.7 %collective-permute-done.21 = bf16[2,256,192]{2,1,0:T(8,128)(2,1)S(1)} collective-permute-done((bf16[2,256,192]{2,1,0:T(8,128)(2,1)S(1)}, bf16[2,256,192]{2,1,0:T(8,128)(2,1)S(1)}, u32[]{:S(2)}, u32[]{:S(2)}) %collective-permute-start.21) | collective-permute-done | bytes 196640 | tf_op jit(solution)/shard_map/ppermute | solution.py:469
  146.8 6.2 %collective-permute-done.20 = bf16[2,256,192]{2,1,0:T(8,128)(2,1)S(1)} collective-permute-done((bf16[2,256,192]{2,1,0:T(8,128)(2,1)S(1)}, bf16[2,256,192]{2,1,0:T(8,128)(2,1)S(1)}, u32[]{:S(2)}, u32[]{:S(2)}) %collective-permute-start.20) | collective-permute-done | bytes 196640 | tf_op jit(solution)/shard_map/ppermute | solution.py:469
  154.0 39.5 %layer.1 = (bf16[4,256,768]{2,1,0:T(8,128)(2,1)}, f32[4,256,768]{2,1,0:T(8,128)}, bf16[4,256,768]{2,1,0:T(8,128)(2,1)}, bf16[768,1024]{1,0:T(8,128)(2,1)}, bf16[...) custom-call(s32[1]{0:T(128)} %bitcast.me_ref, ...), custom_call_target="tpu_custom_call" | custom-call | flops 20000000000 | bytes 1000000 | tf_op jit(solution)/shard_map/layer/pallas_call | solution.py:273
  193.6 2.9 slice_bitcast_fusion.4
  200.0 7.4 %fusion.71 = f32[2,2,2,2,2,24,3072]{6,5,4,3,2,1,0:T(8,128)S(1)} fusion(bf16[2,2,2,2,2,24,1024]{6,5,4,3,2,1,0:T(8,128)(2,1)S(1)} %bitcast.295, bf16[1024,3072,1,1,1,1,1]{1,0,6,5,4,3,2:T(8,128)(2,1)} %bitcast.294), kind=kOutput, calls=%fused_computation.241 | convolution fusion | flops 4831838208 | bytes 17301504 | tf_op jit(solution)/shard_map/dot_general | solution.py:57
  208.8 7.7 %fusion.70 = f32[4,2,2,2,2,2,24,768]{7,6,5,4,3,2,1,0:T(8,128)S(1)} fusion(bf16[4,2,2,2,2,2,24,1024]{7,6,5,4,3,2,1,0:T(8,128)(2,1)} %bitcast.293, bf16[1024,768,1,1,1,1,1,1]{1,0,7,6,5,4,3,2:T(8,128)(2,1)S(1)} %bitcast.292), kind=kOutput, calls=%fused_computation.240 | convolution fusion | flops 4831838208 | bytes 17301504 | tf_op jit(solution)/shard_map/dot_general | solution.py:57
  228.8 19.0 %attend_backward.2.refs_0_ = bf16[4,2,256,576]{3,2,1,0:T(8,128)(2,1)} custom-call(s32[1]{0:T(128)} %bitcast.me_ref, bf16[4,2,256,576]{3,2,1,0:T(8,128)(2,1)} %project.2.joint_ref, bf16[4,256,192]{2,1,0:T(8,128)(2,1)} %get-tuple-element.328.refs_0_, bf16[4,256,192]{2,1,0:T(8,128)(2,1)} %copy-done.41, bf16[4,256,192]{2,1,0:T(8,128)(2,1)} %collective-permute-done.27.refs_2_, ...), custom_call_target="tpu_custom_call" | custom-call | flops 20000000000 | bytes 1000000 | tf_op jit(solution)/shard_map/attend_backward/pallas_call | solution.py:375
  247.8 13.2 %collective-permute-done.31 = bf16[2,2,2,24,768]{4,3,2,1,0:T(8,128)(2,1)S(1)} collective-permute-done((bf16[2,2,2,24,768]{4,3,2,1,0:T(8,128)(2,1)}, bf16[2,2,2,24,768]{4,3,2,1,0:T(8,128)(2,1)S(1)}, u32[]{:S(2)}, u32[]{:S(2)}) %collective-permute-start.31) | collective-permute-done | bytes 294944 | tf_op jit(solution)/shard_map/ppermute | solution.py:469
  262.7 1.5 convert_add_fusion.2
  264.4 1.6 convert_add_fusion.3
  266.2 1.3 collective-permute-start.34
  267.5 1.6 collective-permute-start.35
  269.5 10.4 %unproject.2 = (bf16[4,2,256,768]{3,2,1,0:T(8,128)(2,1)}, f32[768,576]{1,0:T(8,128)}, f32[2,768]{1,0:T(2,128)}, f32[1,576]{1,0:T(1,128)}) custom-call(bf16[4,2,256,576]{3,2,1,0:T(8,128)(2,1)} %attend_backward.2.refs_0_, bf16[2,256,768]{2,1,0:T(8,128)(2,1)} %get-tuple-element.138.refs_0_.refs_1_, ...), custom_call_target="tpu_custom_call" | custom-call | flops 20000000000 | bytes 1000000 | tf_op jit(solution)/shard_map/unproject/pallas_call | solution.py:438
  280.0 1.5 slice_bitcast_fusion.2
  282.0 2.7 collective-permute-done.36
  285.3 1.6 copy-done.4
  289.1 1.4 collective-permute-start.38
  292.6 19.2 %attend_backward.3.refs_0_ = bf16[4,2,256,576]{3,2,1,0:T(8,128)(2,1)} custom-call(s32[1]{0:T(128)} %bitcast.me_ref, bf16[4,2,256,576]{3,2,1,0:T(8,128)(2,1)} %project.3.joint_ref, bf16[4,256,192]{2,1,0:T(8,128)(2,1)} %get-tuple-element.328.refs_0_, bf16[4,256,192]{2,1,0:T(8,128)(2,1)} %copy-done.41, bf16[4,256,192]{2,1,0:T(8,128)(2,1)} %collective-permute-done.27.refs_2_, ...), custom_call_target="tpu_custom_call" | custom-call | flops 20000000000 | bytes 1000000 | tf_op jit(solution)/shard_map/attend_backward/pallas_call | solution.py:375
  316.3 11.1 %unproject.3 = (bf16[4,2,256,768]{3,2,1,0:T(8,128)(2,1)}, f32[768,576]{1,0:T(8,128)}, f32[2,768]{1,0:T(2,128)}, f32[1,576]{1,0:T(1,128)}) custom-call(bf16[4,2,256,576]{3,2,1,0:T(8,128)(2,1)} %attend_backward.3.refs_0_, bf16[2,256,768]{2,1,0:T(8,128)(2,1)} %get-tuple-element.143.refs_0_.refs_1_, ...), custom_call_target="tpu_custom_call" | custom-call | flops 20000000000 | bytes 1000000 | tf_op jit(solution)/shard_map/unproject/pallas_call | solution.py:438
  329.5 1.9 pad_maximum_fusion.2
  332.4 1.4 collective-permute-start.44
  333.7 1.4 collective-permute-start.45
  335.8 1.5 collective-permute-start.47
  337.3 1.4 collective-permute-start.54
  340.7 7.7 %collective-permute-done.54 = bf16[24,768]{1,0:T(8,128)(2,1)S(1)} collective-permute-done((bf16[24,768]{1,0:T(8,128)(2,1)}, bf16[24,768]{1,0:T(8,128)(2,1)S(1)}, u32[]{:S(2)}, u32[]{:S(2)}) %collective-permute-start.54) | collective-permute-done | bytes 36896 | tf_op jit(solution)/shard_map/ppermute | solution.py:469
  349.0 2.1 collective-permute-start.49
  351.0 2.3 collective-permute-start.50
  353.3 1.6 multiply_subtract_fusion.3
  356.1 2.0 copy.250
  358.1 1.4 collective-permute-start.56
  359.5 2.0 copy.251
  363.2 1.9 copy.253
  365.7 2.0 copy.254
  367.7 2.0 copy.255
  369.6 2.5 fusion.20
  374.7 5.0 %collective-permute-done.52 = bf16[24,588]{0,1:T(8,128)(2,1)S(1)} collective-permute-done((bf16[24,588]{0,1:T(8,128)(2,1)S(1)}, bf16[24,588]{0,1:T(8,128)(2,1)S(1)}, u32[]{:S(2)}, u32[]{:S(2)}) %collective-permute-start.52) | collective-permute-done | bytes 28256 | tf_op jit(solution)/shard_map/ppermute | solution.py:469
  380.8 4.8 %collective-permute-done.53 = bf16[24,588]{0,1:T(8,128)(2,1)} collective-permute-done((bf16[24,588]{0,1:T(8,128)(2,1)S(1)}, bf16[24,588]{0,1:T(8,128)(2,1)}, u32[]{:S(2)}, u32[]{:S(2)}) %collective-permute-start.53) | collective-permute-done | bytes 28256 | tf_op jit(solution)/shard_map/ppermute | solution.py:469
  385.6 1.7 fusion.64
  388.5 2.1 multiply_subtract_fusion.2
  390.5 1.3 multiply_subtract_fusion.4
  393.8 2.5 fusion.12
  399.6 2.4 copy.261
  402.0 3.3 reshape.415
  405.3 2.1 multiply_subtract_fusion.1
  407.4 8.4 %collective-permute-done.43 = bf16[2,256,768]{2,1,0:T(8,128)(2,1)} collective-permute-done((bf16[2,256,768]{2,1,0:T(8,128)(2,1)}, bf16[2,256,768]{2,1,0:T(8,128)(2,1)}, u32[]{:S(2)}, u32[]{:S(2)}) %collective-permute-start.43) | collective-permute-done | bytes 786464 | tf_op jit(solution)/shard_map/ppermute | solution.py:469
  415.8 1.9 fusion.13
  419.6 2.3 fusion.7
  (332 shorter events, 77.2 us)
Async XLA Ops:
  7.2 130.7 %all-gather.2.cloned.1.call-start = ((), (), s32[]{:S(2)}) async-start(), calls=%async_computation | async-start | bytes 5640192 | tf_op jit(solution)/shard_map/all_gather | solution.py:583
  7.2 14.7 %collective-permute-start.6 = (s32[4,256]{1,0:T(4,128)}, s32[4,256]{1,0:T(4,128)S(1)}, u32[]{:S(2)}, u32[]{:S(2)}) collective-permute-start(s32[4,256]{1,0:T(4,128)} %param.19), channel_id=1, source_target_pairs={{0,2},{1,3},{2,0},{3,1},{4,6},{5,7},{6,4},{7,5},{8,10},{9,11},{10,... | collective-permute-start | bytes 12296 | tf_op jit(solution)/shard_map/ppermute | solution.py:469
  10.2 13.8 %collective-permute-start.5 = (s32[4,256]{1,0:T(4,128)}, s32[4,256]{1,0:T(4,128)S(1)}, u32[]{:S(2)}, u32[]{:S(2)}) collective-permute-start(s32[4,256]{1,0:T(4,128)} %param.19), channel_id=1, source_target_pairs={{0,1},{1,0},{2,3},{3,2},{4,5},{5,4},{6,7},{7,6},{8,9},{9,8},{10,11... | collective-permute-start | bytes 12296 | tf_op jit(solution)/shard_map/ppermute | solution.py:469
  17.1 7.5 %collective-permute-start = (bf16[24,588]{1,0:T(8,128)(2,1)}, bf16[24,588]{1,0:T(8,128)(2,1)S(1)}, u32[]{:S(2)}, u32[]{:S(2)}) collective-permute-start(bf16[24,588]{1,0:T(8,128)(2,1)} %get-tuple-element.385), channel_id=1, source_target_pairs={{0,1},{1,0},{2,3},{3,2},{4,5},{5,4},{6,7},{7,6},{8,9},{9,8},{10,11... | collective-permute-start | bytes 84680 | tf_op jit(solution)/shard_map/ppermute | solution.py:469
  17.6 7.0 %collective-permute-start.1 = (bf16[24,588]{1,0:T(8,128)(2,1)S(1)}, bf16[24,588]{1,0:T(8,128)(2,1)S(1)}, u32[]{:S(2)}, u32[]{:S(2)}) collective-permute-start(bf16[24,588]{1,0:T(8,128)(2,1)S(1)} %get-tuple-element.386), channel_id=1, source_target_pairs={{0,2},{1,3},{2,0},{3,1},{4,6},{5,7},{6,4},{7,5},{8,10},{9,11},{10,... | collective-permute-start | bytes 84680 | tf_op jit(solution)/shard_map/ppermute | solution.py:469
  17.7 6.9 %collective-permute-start.2 = (bf16[24,588]{1,0:T(8,128)(2,1)S(1)}, bf16[24,588]{1,0:T(8,128)(2,1)S(1)}, u32[]{:S(2)}, u32[]{:S(2)}) collective-permute-start(bf16[24,588]{1,0:T(8,128)(2,1)S(1)} %get-tuple-element.387), channel_id=1, source_target_pairs={{0,3},{1,2},{2,1},{3,0},{4,7},{5,6},{6,5},{7,4},{8,11},{9,10},{10,... | collective-permute-start | bytes 84680 | tf_op jit(solution)/shard_map/ppermute | solution.py:469
  21.9 2.1 collective-permute-start.7
  24.0 10.0 %collective-permute-start.4 = (bf16[24,3456]{1,0:T(8,128)(2,1)S(1)}, bf16[24,3456]{1,0:T(8,128)(2,1)S(1)}, u32[]{:S(2)}, u32[]{:S(2)}) collective-permute-start(bf16[24,3456]{1,0:T(8,128)(2,1)S(1)} %get-tuple-element.354), channel_id=1, source_target_pairs={{0,1},{1,0},{2,3},{3,2},{4,5},{5,4},{6,7},{7,6},{8,9},{9,8},{10,11... | collective-permute-start | bytes 497672 | tf_op jit(solution)/shard_map/ppermute | solution.py:469
  24.0 20.3 %collective-permute-start.8 = (bf16[2,256,768]{2,1,0:T(8,128)(2,1)}, bf16[2,256,768]{2,1,0:T(8,128)(2,1)}, u32[]{:S(2)}, u32[]{:S(2)}) collective-permute-start(bf16[2,256,768]{2,1,0:T(8,128)(2,1)} %get-tuple-element.138.refs_0_.refs_1_), channel_id=1, source_target_pairs={{0,2},{1,3},{2,0},{3,1},{4,6},{5,7},{6,4},{7,5},{8,10},{9,11},{10,... | collective-permute-start | bytes 2359304 | tf_op jit(solution)/shard_map/ppermute | solution.py:469
  24.8 9.1 %collective-permute-start.3 = (bf16[4,24,588]{2,1,0:T(8,128)(2,1)S(1)}, bf16[4,24,588]{2,1,0:T(8,128)(2,1)S(1)}, u32[]{:S(2)}, u32[]{:S(2)}) collective-permute-start(bf16[4,24,588]{2,1,0:T(8,128)(2,1)S(1)} %get-tuple-element.370), channel_id=1, source_target_pairs={{0,16},{4,20},{8,24},{12,28},{16,0},{20,4},{24,8},{28,12},{1,17},{... | collective-permute-start | bytes 338696 | tf_op jit(solution)/shard_map/ppermute | solution.py:469
  44.3 21.8 %collective-permute-start.10 = (bf16[2,256,768]{2,1,0:T(8,128)(2,1)}, bf16[2,256,768]{2,1,0:T(8,128)(2,1)}, u32[]{:S(2)}, u32[]{:S(2)}) collective-permute-start(bf16[2,256,768]{2,1,0:T(8,128)(2,1)} %get-tuple-element.143.refs_0_.refs_1_), channel_id=1, source_target_pairs={{0,2},{1,3},{2,0},{3,1},{4,6},{5,7},{6,4},{7,5},{8,10},{9,11},{10,... | collective-permute-start | bytes 2359304 | tf_op jit(solution)/shard_map/ppermute | solution.py:469
  44.6 7.4 %collective-permute-start.9 = (bf16[2,4,24,588]{3,2,1,0:T(8,128)(2,1)S(1)}, bf16[2,4,24,588]{3,2,1,0:T(8,128)(2,1)S(1)}, u32[]{:S(2)}, u32[]{:S(2)}) collective-permute-start(bf16[2,4,24,588]{3,2,1,0:T(8,128)(2,1)S(1)} %maximum_select_fusion.3), channel_id=1, source_target_pairs={{0,8},{4,12},{8,0},{12,4},{16,24},{20,28},{24,16},{28,20},{1,9},{5... | collective-permute-start | bytes 677384 | tf_op jit(solution)/shard_map/ppermute | solution.py:469
  66.1 14.4 %collective-permute-start.13 = (bf16[2,2,4,24,588]{4,3,2,1,0:T(8,128)(2,1)S(1)}, bf16[2,2,4,24,588]{4,3,2,1,0:T(8,128)(2,1)S(1)}, u32[]{:S(2)}, u32[]{:S(2)}) collective-permute-start(bf16[2,2,4,24,588]{4,3,2,1,0:T(8,128)(2,1)S(1)} %maximum_select_fusion.1), channel_id=1, source_target_pairs={{0,4},{4,0},{8,12},{12,8},{16,20},{20,16},{24,28},{28,24},{1,5},{5... | collective-permute-start | bytes 1354760 | tf_op jit(solution)/shard_map/ppermute | solution.py:469
  68.3 37.7 %collective-permute-start.14 = (bf16[2,256,768]{2,1,0:T(8,128)(2,1)}, bf16[2,256,768]{2,1,0:T(8,128)(2,1)}, u32[]{:S(2)}, u32[]{:S(2)}) collective-permute-start(bf16[2,256,768]{2,1,0:T(8,128)(2,1)} %get-tuple-element.143.refs_0_.refs_1_), channel_id=1, source_target_pairs={{0,1},{1,0},{2,3},{3,2},{4,5},{5,4},{6,7},{7,6},{8,9},{9,8},{10,11... | collective-permute-start | bytes 2359304 | tf_op jit(solution)/shard_map/ppermute | solution.py:469
  68.3 37.7 %collective-permute-start.15 = (bf16[2,256,768]{2,1,0:T(8,128)(2,1)}, bf16[2,256,768]{2,1,0:T(8,128)(2,1)}, u32[]{:S(2)}, u32[]{:S(2)}) collective-permute-start(bf16[2,256,768]{2,1,0:T(8,128)(2,1)} %collective-permute-done.10.refs_2_.refs_3_), channel_id=1, source_target_pairs={{0,1},{1,0},{2,3},{3,2},{4,5},{5,4},{6,7},{7,6},{8,9},{9,8},{10,11... | collective-permute-start | bytes 2359304 | tf_op jit(solution)/shard_map/ppermute | solution.py:469
  68.8 15.6 %collective-permute-start.11 = (bf16[2,256,768]{2,1,0:T(8,128)(2,1)}, bf16[2,256,768]{2,1,0:T(8,128)(2,1)}, u32[]{:S(2)}, u32[]{:S(2)}) collective-permute-start(bf16[2,256,768]{2,1,0:T(8,128)(2,1)} %get-tuple-element.138.refs_0_.refs_1_), channel_id=1, source_target_pairs={{0,1},{1,0},{2,3},{3,2},{4,5},{5,4},{6,7},{7,6},{8,9},{9,8},{10,11... | collective-permute-start | bytes 2359304 | tf_op jit(solution)/shard_map/ppermute | solution.py:469
  68.8 15.6 %collective-permute-start.12 = (bf16[2,256,768]{2,1,0:T(8,128)(2,1)}, bf16[2,256,768]{2,1,0:T(8,128)(2,1)}, u32[]{:S(2)}, u32[]{:S(2)}) collective-permute-start(bf16[2,256,768]{2,1,0:T(8,128)(2,1)} %collective-permute-done.8.refs_2_.refs_3_), channel_id=1, source_target_pairs={{0,1},{1,0},{2,3},{3,2},{4,5},{5,4},{6,7},{7,6},{8,9},{9,8},{10,11... | collective-permute-start | bytes 2359304 | tf_op jit(solution)/shard_map/ppermute | solution.py:469
  112.5 15.6 %collective-permute-start.16 = (bf16[2,256,192]{2,1,0:T(8,128)(2,1)S(1)}, bf16[2,256,192]{2,1,0:T(8,128)(2,1)S(1)}, u32[]{:S(2)}, u32[]{:S(2)}) collective-permute-start(bf16[2,256,192]{2,1,0:T(8,128)(2,1)S(1)} %get-tuple-element.146), channel_id=1, source_target_pairs={{0,1},{1,0},{2,3},{3,2},{4,5},{5,4},{6,7},{7,6},{8,9},{9,8},{10,11... | collective-permute-start | bytes 589832 | tf_op jit(solution)/shard_map/ppermute | solution.py:469
  112.5 15.6 %collective-permute-start.17 = (bf16[2,256,192]{2,1,0:T(8,128)(2,1)S(1)}, bf16[2,256,192]{2,1,0:T(8,128)(2,1)S(1)}, u32[]{:S(2)}, u32[]{:S(2)}) collective-permute-start(bf16[2,256,192]{2,1,0:T(8,128)(2,1)S(1)} %get-tuple-element.147), channel_id=1, source_target_pairs={{0,2},{1,3},{2,0},{3,1},{4,6},{5,7},{6,4},{7,5},{8,10},{9,11},{10,... | collective-permute-start | bytes 589832 | tf_op jit(solution)/shard_map/ppermute | solution.py:469
  112.5 18.8 %collective-permute-start.18 = (bf16[2,256,192]{2,1,0:T(8,128)(2,1)S(1)}, bf16[2,256,192]{2,1,0:T(8,128)(2,1)S(1)}, u32[]{:S(2)}, u32[]{:S(2)}) collective-permute-start(bf16[2,256,192]{2,1,0:T(8,128)(2,1)S(1)} %get-tuple-element.148), channel_id=1, source_target_pairs={{0,3},{1,2},{2,1},{3,0},{4,7},{5,6},{6,5},{7,4},{8,11},{9,10},{10,... | collective-permute-start | bytes 589832 | tf_op jit(solution)/shard_map/ppermute | solution.py:469
  137.9 15.3 %collective-permute-start.22 = (bf16[768,3456]{1,0:T(8,128)(2,1)}, bf16[768,3456]{1,0:T(8,128)(2,1)}, u32[]{:S(2)}, u32[]{:S(2)}) collective-permute-start(bf16[768,3456]{1,0:T(8,128)(2,1)} %all-gather.2.cloned.1.call-done.refs_4_), channel_id=1, source_target_pairs={{0,1},{1,0},{2,3},{3,2},{4,5},{5,4},{6,7},{7,6},{8,9},{9,8},{10,11... | collective-permute-start | bytes 15925256 | tf_op jit(solution)/shard_map/ppermute | solution.py:469
  138.2 58.3 %copy-start.31 = (f32[4,256]{1,0:T(4,128)}, f32[4,256]{1,0:T(4,128)S(1)}, u32[]{:S(2)}) copy-start(f32[4,256]{1,0:T(4,128)S(1)} %broadcast_multiply_fusion.1) | copy-start | bytes 12292
  138.8 8.0 %collective-permute-start.21 = (bf16[2,256,192]{2,1,0:T(8,128)(2,1)S(1)}, bf16[2,256,192]{2,1,0:T(8,128)(2,1)S(1)}, u32[]{:S(2)}, u32[]{:S(2)}) collective-permute-start(bf16[2,256,192]{2,1,0:T(8,128)(2,1)S(1)} %copy-done.29), channel_id=1, source_target_pairs={{0,3},{1,2},{2,1},{3,0},{4,7},{5,6},{6,5},{7,4},{8,11},{9,10},{10,... | collective-permute-start | bytes 589832 | tf_op jit(solution)/shard_map/ppermute | solution.py:469
  139.9 13.2 %collective-permute-start.20 = (bf16[2,256,192]{2,1,0:T(8,128)(2,1)S(1)}, bf16[2,256,192]{2,1,0:T(8,128)(2,1)S(1)}, u32[]{:S(2)}, u32[]{:S(2)}) collective-permute-start(bf16[2,256,192]{2,1,0:T(8,128)(2,1)S(1)} %copy-done.28), channel_id=1, source_target_pairs={{0,2},{1,3},{2,0},{3,1},{4,6},{5,7},{6,4},{7,5},{8,10},{9,11},{10,... | collective-permute-start | bytes 589832 | tf_op jit(solution)/shard_map/ppermute | solution.py:469
  141.1 12.0 %collective-permute-start.19 = (bf16[2,256,192]{2,1,0:T(8,128)(2,1)S(1)}, bf16[2,256,192]{2,1,0:T(8,128)(2,1)S(1)}, u32[]{:S(2)}, u32[]{:S(2)}) collective-permute-start(bf16[2,256,192]{2,1,0:T(8,128)(2,1)S(1)} %copy-done.27), channel_id=1, source_target_pairs={{0,1},{1,0},{2,3},{3,2},{4,5},{5,4},{6,7},{7,6},{8,9},{9,8},{10,11... | collective-permute-start | bytes 589832 | tf_op jit(solution)/shard_map/ppermute | solution.py:469
  141.1 12.1 %copy-start.18 = (bf16[4,256,192]{2,1,0:T(8,128)(2,1)}, bf16[4,256,192]{2,1,0:T(8,128)(2,1)S(1)}, u32[]{:S(2)}) copy-start(bf16[4,256,192]{2,1,0:T(8,128)(2,1)S(1)} %constant_dynamic-update-slice_fusion.4.refs_0_) | copy-start | bytes 1179652
  196.5 3.4 collective-permute-start.23
  197.7 31.0 %collective-permute-start.27 = (bf16[4,256,192]{2,1,0:T(8,128)(2,1)}, bf16[4,256,192]{2,1,0:T(8,128)(2,1)}, u32[]{:S(2)}, u32[]{:S(2)}) collective-permute-start(bf16[4,256,192]{2,1,0:T(8,128)(2,1)} %get-tuple-element.327), channel_id=1, source_target_pairs={{0,2},{1,3},{2,0},{3,1},{4,6},{5,7},{6,4},{7,5},{8,10},{9,11},{10,... | collective-permute-start | bytes 1179656 | tf_op jit(solution)/shard_map/ppermute | solution.py:469
  198.7 30.1 %collective-permute-start.28 = (bf16[4,256,192]{2,1,0:T(8,128)(2,1)}, bf16[4,256,192]{2,1,0:T(8,128)(2,1)}, u32[]{:S(2)}, u32[]{:S(2)}) collective-permute-start(bf16[4,256,192]{2,1,0:T(8,128)(2,1)} %get-tuple-element.326), channel_id=1, source_target_pairs={{0,3},{1,2},{2,1},{3,0},{4,7},{5,6},{6,5},{7,4},{8,11},{9,10},{10,... | collective-permute-start | bytes 1179656 | tf_op jit(solution)/shard_map/ppermute | solution.py:469
  207.7 15.0 %collective-permute-start.25 = (bf16[2,2,2,2,24,3072]{5,4,3,2,1,0:T(8,128)(2,1)S(1)}, bf16[2,2,2,2,24,3072]{5,4,3,2,1,0:T(8,128)(2,1)S(1)}, u32[]{:S(2)}, u32[]{:S(2)}) collective-permute-start(bf16[2,2,2,2,24,3072]{5,4,3,2,1,0:T(8,128)(2,1)S(1)} %fusion.10), channel_id=1, source_target_pairs={{0,1},{1,0},{2,3},{3,2},{4,5},{5,4},{6,7},{7,6},{8,9},{9,8},{10,11... | collective-permute-start | bytes 7077896 | tf_op jit(solution)/shard_map/ppermute | solution.py:469
  216.9 5.9 %collective-permute-start.24 = (bf16[4,2,2,2,2,24,768]{6,5,4,3,2,1,0:T(8,128)(2,1)S(1)}, bf16[4,2,2,2,2,24,768]{6,5,4,3,2,1,0:T(8,128)(2,1)S(1)}, u32[]{:S(2)}, u32[]{:S(2)}) collective-permute-start(bf16[4,2,2,2,2,24,768]{6,5,4,3,2,1,0:T(8,128)(2,1)S(1)} %fusion.9), channel_id=1, source_target_pairs={{0,1},{1,0},{2,3},{3,2},{4,5},{5,4},{6,7},{7,6},{8,9},{9,8},{10,11... | collective-permute-start | bytes 7077896 | tf_op jit(solution)/shard_map/ppermute | solution.py:469
  220.7 2.1 collective-permute-start.26
  226.2 34.7 %collective-permute-start.29 = (bf16[4,2,2,2,24,768]{5,4,3,2,1,0:T(8,128)(2,1)S(1)}, bf16[4,2,2,2,24,768]{5,4,3,2,1,0:T(8,128)(2,1)}, u32[]{:S(2)}, u32[]{:S(2)}) collective-permute-start(bf16[4,2,2,2,24,768]{5,4,3,2,1,0:T(8,128)(2,1)S(1)} %fusion.21), channel_id=1, source_target_pairs={{0,4},{4,0},{8,12},{12,8},{16,20},{20,16},{24,28},{28,24},{1,5},{5... | collective-permute-start | bytes 3538952 | tf_op jit(solution)/shard_map/ppermute | solution.py:469
  226.7 34.9 %collective-permute-start.30 = (bf16[2,2,2,24,3072]{4,3,2,1,0:T(8,128)(2,1)S(1)}, bf16[2,2,2,24,3072]{4,3,2,1,0:T(8,128)(2,1)}, u32[]{:S(2)}, u32[]{:S(2)}) collective-permute-start(bf16[2,2,2,24,3072]{4,3,2,1,0:T(8,128)(2,1)S(1)} %fusion.22), channel_id=1, source_target_pairs={{0,2},{1,3},{2,0},{3,1},{4,6},{5,7},{6,4},{7,5},{8,10},{9,11},{10,... | collective-permute-start | bytes 3538952 | tf_op jit(solution)/shard_map/ppermute | solution.py:469
  227.6 33.3 %collective-permute-start.31 = (bf16[2,2,2,24,768]{4,3,2,1,0:T(8,128)(2,1)}, bf16[2,2,2,24,768]{4,3,2,1,0:T(8,128)(2,1)S(1)}, u32[]{:S(2)}, u32[]{:S(2)}) collective-permute-start(bf16[2,2,2,24,768]{4,3,2,1,0:T(8,128)(2,1)} %fusion.29), channel_id=1, source_target_pairs={{0,2},{1,3},{2,0},{3,1},{4,6},{5,7},{6,4},{7,5},{8,10},{9,11},{10,... | collective-permute-start | bytes 884744 | tf_op jit(solution)/shard_map/ppermute | solution.py:469
  266.2 18.6 %collective-permute-start.34 = (bf16[4,2,2,24,768]{4,3,2,1,0:T(8,128)(2,1)S(1)}, bf16[4,2,2,24,768]{4,3,2,1,0:T(8,128)(2,1)S(1)}, u32[]{:S(2)}, u32[]{:S(2)}) collective-permute-start(bf16[4,2,2,24,768]{4,3,2,1,0:T(8,128)(2,1)S(1)} %fusion.25), channel_id=1, source_target_pairs={{0,8},{4,12},{8,0},{12,4},{16,24},{20,28},{24,16},{28,20},{1,9},{5... | collective-permute-start | bytes 1769480 | tf_op jit(solution)/shard_map/ppermute | solution.py:469
  267.5 17.2 %collective-permute-start.35 = (bf16[2,2,24,3072]{3,2,1,0:T(8,128)(2,1)S(1)}, bf16[2,2,24,3072]{3,2,1,0:T(8,128)(2,1)S(1)}, u32[]{:S(2)}, u32[]{:S(2)}) collective-permute-start(bf16[2,2,24,3072]{3,2,1,0:T(8,128)(2,1)S(1)} %fusion.26), channel_id=1, source_target_pairs={{0,4},{4,0},{8,12},{12,8},{16,20},{20,16},{24,28},{28,24},{1,5},{5... | collective-permute-start | bytes 1769480 | tf_op jit(solution)/shard_map/ppermute | solution.py:469
  269.1 15.7 %collective-permute-start.36 = (bf16[2,2,24,768]{3,2,1,0:T(8,128)(2,1)S(1)}, bf16[2,2,24,768]{3,2,1,0:T(8,128)(2,1)S(1)}, u32[]{:S(2)}, u32[]{:S(2)}) collective-permute-start(bf16[2,2,24,768]{3,2,1,0:T(8,128)(2,1)S(1)} %fusion.37), channel_id=1, source_target_pairs={{0,4},{4,0},{8,12},{12,8},{16,20},{20,16},{24,28},{28,24},{1,5},{5... | collective-permute-start | bytes 442376 | tf_op jit(solution)/shard_map/ppermute | solution.py:469
  281.5 3.9 collective-permute-start.32
  281.5 3.8 collective-permute-start.33
  288.2 23.6 %collective-permute-start.37 = (bf16[2,256,768]{2,1,0:T(8,128)(2,1)}, bf16[2,256,768]{2,1,0:T(8,128)(2,1)S(1)}, u32[]{:S(2)}, u32[]{:S(2)}) collective-permute-start(bf16[2,256,768]{2,1,0:T(8,128)(2,1)} %get-tuple-element.212), channel_id=1, source_target_pairs={{0,2},{1,3},{2,0},{3,1},{4,6},{5,7},{6,4},{7,5},{8,10},{9,11},{10,... | collective-permute-start | bytes 2359304 | tf_op jit(solution)/shard_map/ppermute | solution.py:469
  289.1 22.7 %collective-permute-start.38 = (bf16[4,2,24,768]{3,2,1,0:T(8,128)(2,1)S(1)}, bf16[4,2,24,768]{3,2,1,0:T(8,128)(2,1)S(1)}, u32[]{:S(2)}, u32[]{:S(2)}) collective-permute-start(bf16[4,2,24,768]{3,2,1,0:T(8,128)(2,1)S(1)} %fusion.30), channel_id=1, source_target_pairs={{0,16},{4,20},{8,24},{12,28},{16,0},{20,4},{24,8},{28,12},{1,17},{... | collective-permute-start | bytes 884744 | tf_op jit(solution)/shard_map/ppermute | solution.py:469
  290.6 21.2 %collective-permute-start.39 = (bf16[2,24,3072]{2,1,0:T(8,128)(2,1)S(1)}, bf16[2,24,3072]{2,1,0:T(8,128)(2,1)S(1)}, u32[]{:S(2)}, u32[]{:S(2)}) collective-permute-start(bf16[2,24,3072]{2,1,0:T(8,128)(2,1)S(1)} %fusion.31), channel_id=1, source_target_pairs={{0,8},{4,12},{8,0},{12,4},{16,24},{20,28},{24,16},{28,20},{1,9},{5... | collective-permute-start | bytes 884744 | tf_op jit(solution)/shard_map/ppermute | solution.py:469
  291.7 20.1 %collective-permute-start.40 = (bf16[2,24,768]{2,1,0:T(8,128)(2,1)S(1)}, bf16[2,24,768]{2,1,0:T(8,128)(2,1)S(1)}, u32[]{:S(2)}, u32[]{:S(2)}) collective-permute-start(bf16[2,24,768]{2,1,0:T(8,128)(2,1)S(1)} %fusion.48), channel_id=1, source_target_pairs={{0,8},{4,12},{8,0},{12,4},{16,24},{20,28},{24,16},{28,20},{1,9},{5... | collective-permute-start | bytes 221192 | tf_op jit(solution)/shard_map/ppermute | solution.py:469
  332.4 16.6 %collective-permute-start.44 = (bf16[4,24,588]{2,1,0:T(8,128)(2,1)}, bf16[4,24,588]{2,1,0:T(8,128)(2,1)}, u32[]{:S(2)}, u32[]{:S(2)}) collective-permute-start(bf16[4,24,588]{2,1,0:T(8,128)(2,1)} %get-tuple-element.330), channel_id=1, source_target_pairs={{0,4},{4,0},{8,12},{12,8},{16,20},{20,16},{24,28},{28,24},{1,5},{5... | collective-permute-start | bytes 338696 | tf_op jit(solution)/shard_map/ppermute | solution.py:469
  333.7 17.3 %collective-permute-start.45 = (bf16[4,24,588]{2,1,0:T(8,128)(2,1)}, bf16[4,24,588]{2,1,0:T(8,128)(2,1)}, u32[]{:S(2)}, u32[]{:S(2)}) collective-permute-start(bf16[4,24,588]{2,1,0:T(8,128)(2,1)} %get-tuple-element.336), channel_id=1, source_target_pairs={{0,8},{4,12},{8,0},{12,4},{16,24},{20,28},{24,16},{28,20},{1,9},{5... | collective-permute-start | bytes 338696 | tf_op jit(solution)/shard_map/ppermute | solution.py:469
  335.1 23.0 %collective-permute-start.46 = (bf16[4,24,588]{2,1,0:T(8,128)(2,1)}, bf16[4,24,588]{2,1,0:T(8,128)(2,1)}, u32[]{:S(2)}, u32[]{:S(2)}) collective-permute-start(bf16[4,24,588]{2,1,0:T(8,128)(2,1)} %get-tuple-element.335), channel_id=1, source_target_pairs={{0,12},{4,8},{8,4},{12,0},{16,28},{20,24},{24,20},{28,16},{1,13},{... | collective-permute-start | bytes 338696 | tf_op jit(solution)/shard_map/ppermute | solution.py:469
  335.8 25.7 %collective-permute-start.47 = (bf16[4,24,588]{2,1,0:T(8,128)(2,1)}, bf16[4,24,588]{2,1,0:T(8,128)(2,1)S(1)}, u32[]{:S(2)}, u32[]{:S(2)}) collective-permute-start(bf16[4,24,588]{2,1,0:T(8,128)(2,1)} %get-tuple-element.334), channel_id=1, source_target_pairs={{0,16},{4,20},{8,24},{12,28},{16,0},{20,4},{24,8},{28,12},{1,17},{... | collective-permute-start | bytes 338696 | tf_op jit(solution)/shard_map/ppermute | solution.py:469
  337.3 11.0 %collective-permute-start.54 = (bf16[24,768]{1,0:T(8,128)(2,1)}, bf16[24,768]{1,0:T(8,128)(2,1)S(1)}, u32[]{:S(2)}, u32[]{:S(2)}) collective-permute-start(bf16[24,768]{1,0:T(8,128)(2,1)} %fusion.49), channel_id=1, source_target_pairs={{0,16},{4,20},{8,24},{12,28},{16,0},{20,4},{24,8},{28,12},{1,17},{... | collective-permute-start | bytes 110600 | tf_op jit(solution)/shard_map/ppermute | solution.py:469
  340.1 13.2 %copy-start.23 = (f32[24,768]{1,0:T(8,128)S(1)}, f32[24,768]{1,0:T(8,128)}, u32[]{:S(2)}) copy-start(f32[24,768]{1,0:T(8,128)} %param.22) | copy-start | bytes 221188
  340.1 13.2 %copy-start.30 = (f32[24,768]{1,0:T(8,128)S(1)}, f32[24,768]{1,0:T(8,128)}, u32[]{:S(2)}) copy-start(f32[24,768]{1,0:T(8,128)} %param.26) | copy-start | bytes 221188
  348.4 14.9 %collective-permute-start.48 = (bf16[4,24,588]{2,1,0:T(8,128)(2,1)}, bf16[4,24,588]{2,1,0:T(8,128)(2,1)}, u32[]{:S(2)}, u32[]{:S(2)}) collective-permute-start(bf16[4,24,588]{2,1,0:T(8,128)(2,1)} %get-tuple-element.333), channel_id=1, source_target_pairs={{0,20},{4,16},{8,28},{12,24},{16,4},{20,0},{24,12},{28,8},{1,21},{... | collective-permute-start | bytes 338696 | tf_op jit(solution)/shard_map/ppermute | solution.py:469
  349.0 16.2 %collective-permute-start.49 = (bf16[4,24,588]{2,1,0:T(8,128)(2,1)}, bf16[4,24,588]{2,1,0:T(8,128)(2,1)}, u32[]{:S(2)}, u32[]{:S(2)}) collective-permute-start(bf16[4,24,588]{2,1,0:T(8,128)(2,1)} %get-tuple-element.332), channel_id=1, source_target_pairs={{0,24},{4,28},{8,16},{12,20},{16,8},{20,12},{24,0},{28,4},{1,25},{... | collective-permute-start | bytes 338696 | tf_op jit(solution)/shard_map/ppermute | solution.py:469
  351.0 16.6 %collective-permute-start.50 = (bf16[4,24,588]{2,1,0:T(8,128)(2,1)}, bf16[4,24,588]{2,1,0:T(8,128)(2,1)}, u32[]{:S(2)}, u32[]{:S(2)}) collective-permute-start(bf16[4,24,588]{2,1,0:T(8,128)(2,1)} %get-tuple-element.331), channel_id=1, source_target_pairs={{0,28},{4,24},{8,20},{12,16},{16,12},{20,8},{24,4},{28,0},{1,29},{... | collective-permute-start | bytes 338696 | tf_op jit(solution)/shard_map/ppermute | solution.py:469
  358.1 33.8 %collective-permute-start.56 = (bf16[4,24,768]{2,1,0:T(8,128)(2,1)}, bf16[4,24,768]{2,1,0:T(8,128)(2,1)}, u32[]{:S(2)}, u32[]{:S(2)}) collective-permute-start(bf16[4,24,768]{2,1,0:T(8,128)(2,1)} %fusion.38), channel_id=1, source_target_pairs={{0,2},{1,3},{2,0},{3,1},{4,6},{5,7},{6,4},{7,5},{8,10},{9,11},{10,... | collective-permute-start | bytes 442376 | tf_op jit(solution)/shard_map/ppermute | solution.py:469
  361.5 31.3 %collective-permute-start.55 = (bf16[24,3072]{1,0:T(8,128)(2,1)}, bf16[24,3072]{1,0:T(8,128)(2,1)}, u32[]{:S(2)}, u32[]{:S(2)}) collective-permute-start(bf16[24,3072]{1,0:T(8,128)(2,1)} %fusion.39), channel_id=1, source_target_pairs={{0,16},{4,20},{8,24},{12,28},{16,0},{20,4},{24,8},{28,12},{1,17},{... | collective-permute-start | bytes 442376 | tf_op jit(solution)/shard_map/ppermute | solution.py:469
  363.2 30.6 %collective-permute-start.42 = (bf16[2,256,768]{2,1,0:T(8,128)(2,1)}, bf16[2,256,768]{2,1,0:T(8,128)(2,1)}, u32[]{:S(2)}, u32[]{:S(2)}) collective-permute-start(bf16[2,256,768]{2,1,0:T(8,128)(2,1)} %get-tuple-element.317), channel_id=1, source_target_pairs={{0,1},{1,0},{2,3},{3,2},{4,5},{5,4},{6,7},{7,6},{8,9},{9,8},{10,11... | collective-permute-start | bytes 2359304 | tf_op jit(solution)/shard_map/ppermute | solution.py:469
  365.2 42.2 %collective-permute-start.41 = (bf16[2,256,768]{2,1,0:T(8,128)(2,1)}, bf16[2,256,768]{2,1,0:T(8,128)(2,1)}, u32[]{:S(2)}, u32[]{:S(2)}) collective-permute-start(bf16[2,256,768]{2,1,0:T(8,128)(2,1)} %get-tuple-element.316), channel_id=1, source_target_pairs={{0,1},{1,0},{2,3},{3,2},{4,5},{5,4},{6,7},{7,6},{8,9},{9,8},{10,11... | collective-permute-start | bytes 2359304 | tf_op jit(solution)/shard_map/ppermute | solution.py:469
  372.3 1.4 collective-permute-start.51
  373.7 6.0 %collective-permute-start.52 = (bf16[24,588]{0,1:T(8,128)(2,1)S(1)}, bf16[24,588]{0,1:T(8,128)(2,1)S(1)}, u32[]{:S(2)}, u32[]{:S(2)}) collective-permute-start(bf16[24,588]{0,1:T(8,128)(2,1)S(1)} %get-tuple-element.341), channel_id=1, source_target_pairs={{0,2},{1,3},{2,0},{3,1},{4,6},{5,7},{6,4},{7,5},{8,10},{9,11},{10,... | collective-permute-start | bytes 84680 | tf_op jit(solution)/shard_map/ppermute | solution.py:469
  379.7 5.8 %collective-permute-start.53 = (bf16[24,588]{0,1:T(8,128)(2,1)S(1)}, bf16[24,588]{0,1:T(8,128)(2,1)}, u32[]{:S(2)}, u32[]{:S(2)}) collective-permute-start(bf16[24,588]{0,1:T(8,128)(2,1)S(1)} %get-tuple-element.340), channel_id=1, source_target_pairs={{0,3},{1,2},{2,1},{3,0},{4,7},{5,6},{6,5},{7,4},{8,11},{9,10},{10,... | collective-permute-start | bytes 84680 | tf_op jit(solution)/shard_map/ppermute | solution.py:469
  396.3 19.4 %collective-permute-start.43 = (bf16[2,256,768]{2,1,0:T(8,128)(2,1)}, bf16[2,256,768]{2,1,0:T(8,128)(2,1)}, u32[]{:S(2)}, u32[]{:S(2)}) collective-permute-start(bf16[2,256,768]{2,1,0:T(8,128)(2,1)} %fusion.12), channel_id=1, source_target_pairs={{0,2},{1,3},{2,0},{3,1},{4,6},{5,7},{6,4},{7,5},{8,10},{9,11},{10,... | collective-permute-start | bytes 2359304 | tf_op jit(solution)/shard_map/ppermute | solution.py:469
  407.4 10.3 %copy-start.33 = (f32[768]{0:T(1024)S(1)}, f32[768]{0:T(1024)}, u32[]{:S(2)}) copy-start(f32[768]{0:T(1024)} %get-tuple-element.350) | copy-start | bytes 9220
  407.4 10.3 %copy-start.34 = (f32[4,256]{1,0:T(4,128)S(1)}, f32[4,256]{1,0:T(4,128)}, u32[]{:S(2)}) copy-start(f32[4,256]{1,0:T(4,128)} %add_rsqrt_fusion) | copy-start | bytes 12292
  (37 other events, 154.6 us)
Sparse Core Ops, SparseCore 0:
  44.7 93.1 all-gather.1

commit v5 on v4

--- a/solution.py
+++ b/solution.py
@@ -106,7 +106,8 @@
     return n_blk * (n_blk + 1) // 2 * blk
 
 
-def forward_kernel(n_blk, blk, heads, me_ref, joint_ref, start_ref, out_ref, log_ref, joint, bias):
+def forward_kernel(n_blk, blk, heads, me_ref, joint_ref, start_ref, *refs):
+    out_refs, (log_ref, joint, bias, out) = refs[:n_blk], refs[n_blk:]
     me = me_ref[0]
     group = heads * HDIM
     for block in range(n_blk):
@@ -136,8 +137,10 @@
         mixed.append(dot(value, exponent.astype(BF16), ((0,), (0,))) * (1.0 / total))
         log_ref[0, head : head + 1, block * blk : (block + 1) * blk] = top + jnp.log(total)
         if head == heads - 1:
-            out_ref[lax.bitwise_xor(me, block), 0] = jnp.concatenate(mixed, axis=0).T.astype(BF16)
+            out[lax.bitwise_xor(me, block)] = jnp.concatenate(mixed, axis=0).T.astype(BF16)
             mixed = []
+    for place in range(n_blk):
+        out_refs[place][0] = out[place]
 
 
 def attend_forward(me, joint, start):
@@ -154,16 +157,16 @@
                 pl.BlockSpec((n_blk, 1, blk, cols), lambda s, m: (0, s, 0, 0)),
                 pl.BlockSpec((1, 1, length), lambda s, m: (s, 0, 0)),
             ],
-            out_specs=[
-                pl.BlockSpec((n_blk, 1, blk, group), lambda s, m: (0, s, 0, 0)),
-                pl.BlockSpec((1, heads, length), lambda s, m: (s, 0, 0)),
+            out_specs=[pl.BlockSpec((1, blk, group), lambda s, m: (s, 0, 0))] * n_blk
+            + [pl.BlockSpec((1, heads, length), lambda s, m: (s, 0, 0))],
+            scratch_shapes=[
+                pltpu.VMEM((length, cols), BF16),
+                pltpu.VMEM((bias_rows(n_blk, blk), blk), F32),
+                pltpu.VMEM((n_blk, blk, group), BF16),
             ],
-            scratch_shapes=[pltpu.VMEM((length, cols), BF16), pltpu.VMEM((bias_rows(n_blk, blk), blk), F32)],
         ),
-        out_shape=[
-            jax.ShapeDtypeStruct((n_blk, seqs, blk, group), BF16),
-            jax.ShapeDtypeStruct((seqs, heads, length), F32),
-        ],
+        out_shape=[jax.ShapeDtypeStruct((seqs, blk, group), BF16)] * n_blk
+        + [jax.ShapeDtypeStruct((seqs, heads, length), F32)],
         compiler_params=pltpu.CompilerParams(vmem_limit_bytes=VMEM_BYTES),
         cost_estimate=COST,
         name="attend_forward",
@@ -180,8 +183,9 @@
 ):
     mixed_refs = refs[:n_ctx]
     mine_ref, other_ref, params_ref = refs[n_ctx : n_ctx + 3]
-    result_ref, resid_ref, branch_ref, normed_ref, act_ref, pre_ref, mix_ref, sums_ref = refs[n_ctx + 3 : n_ctx + 11]
-    rest_ref, sems = refs[n_ctx + 11 :]
+    result_ref, resid_ref, branch_ref, normed_ref, act_ref, pre_ref = refs[n_ctx + 3 : n_ctx + 9]
+    mix_refs = refs[n_ctx + 9 : 2 * n_ctx + 9]
+    sums_ref, rest_ref, sems = refs[2 * n_ctx + 9 :]
     me = me_ref[0]
     width = x_ref.shape[-1]
     group = width // n_ctx
@@ -243,7 +247,7 @@
     branch_ref[0] = branch
     for place in range(n_ctx):
         mix = dot(branch[:, :side], output_rows(place, 0), ((1,), (1,)))
-        mix_ref[place, 0] = (mix + dot(branch[:, side:], output_rows(place, 1), ((1,), (1,)))).astype(BF16)
+        mix_refs[place][0] = (mix + dot(branch[:, side:], output_rows(place, 1), ((1,), (1,)))).astype(BF16)
     table = jnp.concatenate(
         [column_sum(branch.astype(F32)), gain_sum, shift_sum] + sums + [column_sum(upstream_wide)], axis=0
     )
@@ -286,9 +290,9 @@
                 pl.BlockSpec((width, blk), lambda s, m: (0, s)),
                 pl.BlockSpec((hidden, blk), lambda s, m: (0, s)),
                 by_seq(blk, hidden),
-                pl.BlockSpec((n_ctx, 1, blk, group), lambda s, m: (0, s, 0, 0)),
-                pl.BlockSpec((4 + spans, width), lambda s, m: (0, 0)),
-            ],
+            ]
+            + [by_seq(blk, group)] * n_ctx
+            + [pl.BlockSpec((4 + spans, width), lambda s, m: (0, 0))],
             scratch_shapes=[pltpu.VMEM((2,) + mine.shape, BF16), pltpu.SemaphoreType.DMA((2,))],
         ),
         out_shape=[
@@ -298,9 +302,9 @@
             jax.ShapeDtypeStruct((width, seqs * blk), BF16),
             jax.ShapeDtypeStruct((hidden, seqs * blk), BF16),
             jax.ShapeDtypeStruct((seqs, blk, hidden), BF16),
-            jax.ShapeDtypeStruct((n_ctx, seqs, blk, group), BF16),
-            jax.ShapeDtypeStruct((4 + spans, width), F32),
-        ],
+        ]
+        + [jax.ShapeDtypeStruct((seqs, blk, group), BF16)] * n_ctx
+        + [jax.ShapeDtypeStruct((4 + spans, width), F32)],
         compiler_params=pltpu.CompilerParams(vmem_limit_bytes=VMEM_BYTES),
         cost_estimate=COST,
         name="layer",
@@ -398,66 +402,101 @@
     )(me, joint, *grads, start, logs)
 
 
-def unproject_kernel(n_blk, *refs):
+def unproject_kernel(n_blk, me_ref, *refs):
     grad_ref, tokens = refs[0], refs[1 : 1 + n_blk]
-    params_ref, weight_ref = refs[1 + n_blk : 3 + n_blk]
-    earlier = refs[3 + n_blk : -4]
-    share_ref, weight_grad_ref, sums_ref, bias_ref = refs[-4:]
+    params_ref, weight_ref, earlier_ref, kept_ref, sent_ref, terms_ref = refs[1 + n_blk :]
+    cols = grad_ref.shape[-1]
+    group = cols // 3
+    vectors = params_ref.shape[0]
+    width = params_ref.shape[1]
     weight_grad = bias_grad = gain_sum = shift_sum = 0.0
     for place in range(n_blk):
         grad = grad_ref[place, 0]
         plain, _ = norm_parts(tokens[place][0].astype(F32))
         normed = (plain * params_ref[0:1, :] + params_ref[1:2, :]).astype(BF16)
         share = dot(grad, weight_ref[...], ((1,), (1,)))
-        share_ref[place, 0] = share.astype(BF16)
+        (sent_ref if place % 2 else kept_ref)[place // 2, 0] = share.astype(BF16)
         gain_sum += column_sum(share * plain)
         shift_sum += column_sum(share)
         bias_grad += column_sum(grad.astype(F32))
         weight_grad += dot(normed, grad, ((0,), (0,)))
-    values = [weight_grad, jnp.concatenate([gain_sum, shift_sum], axis=0), bias_grad]
-    totals = [weight_grad_ref, sums_ref, bias_ref]
+
+    def placed(values):
+        return jnp.concatenate([jnp.where(me_ref[0] == j, values, 0.0) for j in range(n_blk)], axis=1)
+
+    table = jnp.concatenate(
+        [gain_sum, shift_sum, placed(bias_grad[:, :group]), placed(bias_grad[:, 2 * group :])]
+        + [jnp.zeros((vectors - 4, width), F32)],
+        axis=0,
+    ).T
 
     @pl.when(pl.program_id(0) == 0)
     def _():
-        for number, (total, value) in enumerate(zip(totals, values)):
-            total[...] = value + earlier[number][...] if earlier else value
+        terms_ref[:, :cols] = weight_grad + earlier_ref[:, :cols]
+        terms_ref[:, cols:] = table + earlier_ref[:, cols:]
 
     @pl.when(pl.program_id(0) > 0)
     def _():
-        for total, value in zip(totals, values):
-            total[...] += value
-
-
-def unproject(grad, tokens, params, weight, earlier):
+        terms_ref[:, :cols] += weight_grad
+        terms_ref[:, cols:] += table
+
+
+def unproject(me, grad, tokens, params, weight, earlier):
     n_blk, count, blk, cols = grad.shape
     width = tokens[0].shape[-1]
 
     def whole(shape):
-        return pl.BlockSpec(shape, lambda s: (0, 0))
-
+        return pl.BlockSpec(shape, lambda s, m: (0, 0))
+
+    part = pl.BlockSpec((n_blk // 2, 1, blk, width), lambda s, m: (0, s, 0, 0))
     return pl.pallas_call(
         functools.partial(unproject_kernel, n_blk),
-        grid=(count,),
-        in_specs=[pl.BlockSpec((n_blk, 1, blk, cols), lambda s: (0, s, 0, 0))]
-        + [pl.BlockSpec((1, blk, width), lambda s: (s, 0, 0))] * n_blk
-        + [whole(params.shape), whole(weight.shape)]
-        + [whole(item.shape) for item in earlier],
-        out_specs=[
-            pl.BlockSpec((n_blk, 1, blk, width), lambda s: (0, s, 0, 0)),
-            whole((width, cols)),
-            whole((2, width)),
-            whole((1, cols)),
-        ],
-        out_shape=[
-            jax.ShapeDtypeStruct((n_blk, count, blk, width), BF16),
-            jax.ShapeDtypeStruct((width, cols), F32),
-            jax.ShapeDtypeStruct((2, width), F32),
-            jax.ShapeDtypeStruct((1, cols), F32),
-        ],
+        grid_spec=pltpu.PrefetchScalarGridSpec(
+            num_scalar_prefetch=1,
+            grid=(count,),
+            in_specs=[pl.BlockSpec((n_blk, 1, blk, cols), lambda s, m: (0, s, 0, 0))]
+            + [pl.BlockSpec((1, blk, width), lambda s, m: (s, 0, 0))] * n_blk
+            + [whole(params.shape), whole(weight.shape), whole(earlier.shape)],
+            out_specs=[part, part, whole(earlier.shape)],
+        ),
+        out_shape=[jax.ShapeDtypeStruct((n_blk // 2, count, blk, width), BF16)] * 2
+        + [jax.ShapeDtypeStruct(earlier.shape, F32)],
         compiler_params=pltpu.CompilerParams(vmem_limit_bytes=VMEM_BYTES),
         cost_estimate=COST,
         name="unproject",
-    )(grad, *tokens, params, weight, *earlier)
+    )(me, grad, *tokens, params, weight, earlier)
+
+
+def finish_kernel(n_ctx, me_ref, *refs):
+    pieces, refs = refs[:n_ctx], refs[n_ctx:]
+    states, outs, held = refs[:6], refs[6:12], refs[12]
+    for place in range(n_ctx):
+        held[place] = pieces[place][...].astype(F32)
+    vectors = states[3].shape[0]
+    cols = held.shape[-1] - vectors
+    group = cols // 3
+    groups = [held[lax.bitwise_xor(me_ref[0], j)] for j in range(n_ctx)]
+    gradient = jnp.concatenate(
+        [item[:, third * group : (third + 1) * group] for third in range(3) for item in groups], axis=1
+    )
+    small = sum(item[:, cols:] for item in groups).T
+    results = adam_step(states[0][...], gradient, states[1][...], states[2][...], RATE_MATRIX, WEIGHT_DECAY)
+    results += adam_step(states[3][...], small, states[4][...], states[5][...], RATE_VECTOR, 0.0)
+    for out, result in zip(outs, results):
+        out[...] = result
+
+
+def finish(me, pieces, states):
+    n_ctx = len(pieces)
+    return pl.pallas_call(
+        functools.partial(finish_kernel, n_ctx),
+        in_specs=[pl.BlockSpec(memory_space=pltpu.SMEM)] + [pl.BlockSpec(memory_space=pltpu.VMEM)] * (n_ctx + 6),
+        out_specs=[pl.BlockSpec(memory_space=pltpu.VMEM)] * 6,
+        out_shape=[jax.ShapeDtypeStruct(item.shape, F32) for item in states],
+        scratch_shapes=[pltpu.VMEM((n_ctx,) + pieces[0].shape, F32)],
+        compiler_params=pltpu.CompilerParams(vmem_limit_bytes=VMEM_BYTES),
+        name="finish",
+    )(me, *pieces, *states)
 
 
 def build(sizes):
@@ -508,14 +547,9 @@
         spots = {"dp": me_dp, "ctx": me}
         me_arr = me.astype(jnp.int32).reshape(1)
 
-        joint_cast, small_cast, output_cast, expand_cast, shrink_cast = lax.optimization_barrier(
-            (
-                joint_weight.astype(BF16),
-                small_params.astype(BF16),
-                output_weight.astype(BF16),
-                expand_weight.astype(BF16),
-                shrink_weight.astype(BF16),
-            )
+        joint_cast, small_cast = lax.optimization_barrier((joint_weight.astype(BF16), small_params.astype(BF16)))
+        output_cast, expand_cast, shrink_cast = lax.optimization_barrier(
+            (output_weight.astype(BF16), expand_weight.astype(BF16), shrink_weight.astype(BF16))
         )
 
         seg_blocks = {0: segments}
@@ -536,7 +570,6 @@
             return jnp.concatenate([picked.reshape(part, cols), small_cols], axis=1)
 
         pieces = [columns_for(0)] + [swap(columns_for(k), "ctx", k) for k in range(1, n_ctx)]
-        gathered = jnp.stack(reorder(pieces, me))
 
         expand_wide = expand_cast.reshape(part, n_dev, spans, part).transpose(0, 2, 1, 3).reshape(part, hidden)
         shrink_wide = shrink_cast.reshape(spans, part, width).transpose(1, 0, 2).reshape(part, hidden)
@@ -553,9 +586,9 @@
             jnp.concatenate([rest_got, rest_own], axis=0),
             jnp.concatenate([rest_own, rest_got], axis=0),
         )
-        pairs = [
+        rest = lax.all_gather(rest, ("dp", "ctx"), axis=0, tiled=True, axis_index_groups=[
             [d * n_ctx + c * 2 + p for d in range(n_dp) for c in range(n_ctx // 2)] for p in range(2)
-        ]
+        ])
 
         half = max(seqs // 2, 1)
         firsts = list(range(0, seqs, half))
@@ -567,21 +600,20 @@
                 blocks.update({k ^ (1 << bit): swap(value, "ctx", 1 << bit) for k, value in list(blocks.items())})
 
         fetch_far(tokens[0])
+        names = sorted(tokens[0])
+        pieces, start, later, held = lax.optimization_barrier(
+            (pieces, start, [blocks[0] for blocks in tokens[1:]], [tokens[0][k] for k in names])
+        )
+        tokens[0] = dict(zip(names, held))
+        for blocks, value in zip(tokens[1:], later):
+            blocks[0] = value
+            fetch_far(blocks)
+        gathered = jnp.stack(reorder(pieces, me))
         for step, bit in enumerate(reversed(dp_bits)):
             other = swap(gathered, "dp", 1 << bit)
             upper = ((me_dp >> bit) & 1) == 1
             gathered = jnp.where(upper, jnp.stack([other, gathered]), jnp.stack([gathered, other]))
-            if step == 0:
-                names = sorted(tokens[0])
-                gathered, rest, start, later, *held = lax.optimization_barrier(
-                    (gathered, rest, start, [blocks[0] for blocks in tokens[1:]]) + tuple(tokens[0][k] for k in names)
-                )
-                tokens[0] = dict(zip(names, held))
-                for blocks, value in zip(tokens[1:], later):
-                    blocks[0] = value
-                    fetch_far(blocks)
-                rest = lax.all_gather(rest, ("dp", "ctx"), axis=0, tiled=True, axis_index_groups=pairs)
-            elif step == n_bits - 2:
+            if step == max(n_bits - 2, 0):
                 flat = [(number, k) for number, blocks in enumerate(tokens) for k in sorted(blocks)]
                 gathered, *held = lax.optimization_barrier((gathered,) + tuple(tokens[n][k] for n, k in flat))
                 for (number, k), value in zip(flat, held):
@@ -606,18 +638,18 @@
             if waiting is not None:
                 waiting, joint = lax.optimization_barrier((waiting, joint))
                 waiting = [waiting[0]] + [swap(waiting[k], "ctx", k) for k in range(1, n_ctx)]
-            attended, log = attend_forward(me_arr, joint, starts[number])
+            *attended, log = attend_forward(me_arr, joint, starts[number])
             if waiting is not None:
                 waiting, attended = lax.optimization_barrier((waiting, attended))
                 mixed.append(waiting)
-            waiting = [attended[k] for k in range(n_ctx)]
+            waiting = attended
             joints.append(joint)
             logs.append(log)
         waiting, rest = lax.optimization_barrier((waiting, rest))
         rest_other = swap(rest, "ctx", 1)
         mixed.append([waiting[0]] + [swap(waiting[k], "ctx", k) for k in range(1, n_ctx)])
         mixed = [jnp.concatenate(items, axis=0) for items in zip(*mixed)]
-        block_output, grad_resid, branch, normed_two, activated, grad_pre, grad_mixed, sums = layer(
+        block_output, grad_resid, branch, normed_two, activated, grad_pre, *grad_mixed, sums = layer(
             me_arr, tokens_in, cotangent, mixed, rest, rest_other, params
         )
         grads = [grad_mixed[0]] + [swap(grad_mixed[k], "ctx", k) for k in range(1, n_ctx)]
@@ -626,19 +658,31 @@
             (activated, grad_pre, normed_two, branch, grads[1])
         )
         branch = branch.reshape(rows, width)
-        grad_shrink = dot(activated, cotangent.reshape(rows, width), ((1,), (0,)))
-        grad_expand = dot(normed_two, grad_pre.reshape(rows, hidden), ((1,), (0,)))
-        grad_output = [dot(item.reshape(rows, group), branch, ((0,), (0,))) for item in mixed]
-        grad_output = jnp.concatenate(reorder(grad_output, me), axis=0)
-
+        upstream = cotangent.reshape(rows, width)
+        grad_pre = grad_pre.reshape(rows, hidden)
         labels = [("dp", bit) for bit in reversed(dp_bits)] + [("ctx", bit) for bit in reversed(ctx_bits)]
         bit_dims = (2,) * len(labels)
         core, far = [("ctx", ctx_bits[0])], [("ctx", bit) for bit in ctx_bits[1:]]
-        inner = [("dp", bit) for bit in dp_bits]
+        low, high = [("dp", dp_bits[0])], [("dp", bit) for bit in dp_bits[1:]]
+        cut = (spans - 1) * width
+        grad_shrink = dot(activated[:cut], upstream, ((1,), (0,))).reshape((spans - 1,) + bit_dims + (part, width))
+        grad_expand = dot(normed_two, grad_pre[:, :cut], ((1,), (0,))).reshape(bit_dims + (part, cut))
+        grad_output = [dot(item.reshape(rows, group), branch, ((0,), (0,))) for item in mixed]
+        grad_output = jnp.concatenate(reorder(grad_output, me), axis=0)
+        grad_last = jnp.stack(
+            [
+                dot(activated[cut:], upstream, ((1,), (0,))),
+                dot(normed_two, grad_pre[:, cut:], ((1,), (0,))),
+                grad_output,
+            ]
+        ).reshape((3,) + bit_dims + (part, width))
+        grad_shrink, grad_expand, grad_last, grads = lax.optimization_barrier(
+            (grad_shrink, grad_expand, grad_last, grads)
+        )
         chains = [
-            [grad_shrink.reshape((spans,) + bit_dims + (part, width)), None, ["span"] + labels, core + inner + far],
-            [grad_expand.reshape(bit_dims + (part, hidden)), None, labels, core + far + inner],
-            [grad_output.reshape(bit_dims + (part, width)), None, labels, core + far + inner],
+            [grad_shrink, None, ["unit"] + labels, core + low + high + far],
+            [grad_expand, None, labels, core + far + low + high],
+            [grad_last, None, ["unit"] + labels, core + high[:1] + far + low + high[1:]],
         ]
 
         def split(chain):
@@ -679,78 +723,72 @@
         for chain in chains:
             split(chain)
 
-        top = 1 << ctx_bits[-1]
-        pending, shares, earlier = None, [], ()
+        sums_hidden = sums[3 : 3 + spans].reshape(spans, n_dev, part).transpose(1, 0, 2).reshape(spans, width)
+        table = jnp.concatenate([jnp.zeros((4, width), F32), sums[:3], sums_hidden, sums[3 + spans :]], axis=0)
+        terms = jnp.concatenate([jnp.zeros((width, cols), F32), table.T], axis=1)
+        pending, shares = None, []
         for number, first in enumerate(firsts):
-            _, (source, pending) = advance(earlier[1] if earlier else branch, (joints[number], pending))
+            _, (source, pending) = advance(terms if number else branch, (joints[number], pending))
             grad_joint = attend_backward(me_arr, source, grads, starts[number], logs[number], first)
             if pending:
-                pending[1] = swap(pending[1], "ctx", top)
+                pending[1] = [swap(value, "ctx", 1 << bit) for value, bit in zip(pending[1], ctx_bits[1:])]
             (grad_joint, pending), _ = advance((grad_joint, pending), start)
             if pending:
-                shares.append(pending[0] + pending[1].astype(F32))
-            share, *earlier = unproject(grad_joint, tokens[number], params, joint_lo, earlier)
-            known = {k: share[k] for k in range(n_ctx)}
-            for bit in ctx_bits[:-1]:
-                mask = 1 << bit
-                known = {
-                    k: value.astype(F32) + swap(known[k | mask].astype(BF16), "ctx", mask).astype(F32)
-                    for k, value in known.items()
-                    if not k & mask
-                }
-            pending = [known[0], known[top].astype(BF16)]
-        shares.append(pending[0] + swap(pending[1], "ctx", top).astype(F32))
-        weight_grad, norm_sums, bias_sums = earlier
-
-        plain, scale = norm_parts(tokens_in.astype(F32))
-        input_grad = grad_resid + norm_back(plain, scale, jnp.concatenate(shares, axis=0), params[0])
-
-        placed = lax.dynamic_update_slice(
-            jnp.zeros((2, width), F32),
-            jnp.concatenate([bias_sums[:, :group], bias_sums[:, 2 * group :]], axis=0),
-            (0, me * group),
-        )
-        sums_hidden = sums[3 : 3 + spans].reshape(spans, n_dev, part).transpose(1, 0, 2).reshape(spans, width)
-        grad_small = jnp.concatenate([norm_sums, placed, sums[:3], sums_hidden, sums[3 + spans :]], axis=0)
-        terms = jnp.concatenate([weight_grad, grad_small.T], axis=1).reshape(n_dp, n_ctx, part, cols + vectors)
-        total = lax.dynamic_index_in_dim(terms, me_dp, 0, keepdims=False)
+                shares.append(sum((value.astype(F32) for value in pending[1]), pending[0]))
+            kept, sent, terms = unproject(me_arr, grad_joint, tokens[number], params, joint_lo, terms)
+            if number < len(firsts) - 1:
+                joined = kept.astype(F32) + swap(sent, "ctx", 1).astype(F32)
+                pending = [joined[0], [joined[1 << (bit - 1)].astype(BF16) for bit in ctx_bits[1:]]]
+
+        terms = terms.reshape((2,) * n_bits + (n_ctx, part, cols + vectors))
+        chain = [terms, None, [("dp", bit) for bit in reversed(dp_bits)], low + high]
+        split(chain)
+        got, sent, kept = lax.optimization_barrier((fetch(chain), swap(sent, "ctx", 1), kept))
+        merge(chain, got)
+        joined = kept.astype(F32) + sent.astype(F32)
+        crossing = [swap(joined[1 << (bit - 1)].astype(BF16), "ctx", 1 << bit) for bit in ctx_bits[1:]]
         if n_dp <= 8:
+            items = chain[0].reshape(n_dp // 2, n_ctx, part, cols + vectors)
+            spot = me_dp >> 1
+            total = lax.dynamic_index_in_dim(items, spot, 0, keepdims=False)
             sent = [
-                lax.dynamic_index_in_dim(terms, lax.bitwise_xor(me_dp, j), 0, keepdims=False).astype(BF16)
-                for j in range(1, n_dp)
+                lax.dynamic_index_in_dim(items, lax.bitwise_xor(spot, j), 0, keepdims=False).astype(BF16)
+                for j in range(1, n_dp // 2)
             ]
-            for j, item in enumerate(sent):
-                total = total + swap(item, "dp", j + 1).astype(F32)
+            gots = [swap(item, "dp", 2 * (j + 1)) for j, item in enumerate(sent)]
+            total, gots, crossing = lax.optimization_barrier((total, gots, crossing))
+            total = sum((item.astype(F32) for item in gots), total)
         else:
-            terms = terms.reshape((2,) * n_bits + (n_ctx, part, cols + vectors))
-            chain = [terms, None, [("dp", bit) for bit in reversed(dp_bits)], inner]
             while chain[3]:
                 split(chain)
                 merge(chain, fetch(chain))
             total = chain[0]
+        shares.append(sum((value.astype(F32) for value in crossing), joined[0]))
 
         def terms_for(k):
             return lax.dynamic_index_in_dim(total, lax.bitwise_xor(me, k), 0, keepdims=False)
 
-        arrived = [terms_for(0)] + [
-            swap(terms_for(k).astype(BF16), "ctx", k).astype(F32) for k in range(1, n_ctx)
-        ]
-        small_sum = sum(item[:, cols:] for item in arrived).T
-        sum_joint = jnp.stack([item[:, :cols].reshape(part, 3, group) for item in reorder(arrived, me)], axis=2)
-        sum_joint = sum_joint.reshape(part, 3 * width)
+        sent = lax.optimization_barrier([terms_for(k).astype(BF16) for k in range(1, n_ctx)])
+        arrived = [terms_for(0)] + [swap(item, "ctx", k + 1) for k, item in enumerate(sent)]
+        new_joint, first_joint, second_joint, new_small, first_small, second_small = finish(
+            me_arr,
+            arrived,
+            (joint_weight, momentum_joint, variance_joint, small_params, momentum_small, variance_small),
+        )
+
+        plain, scale = norm_parts(tokens_in.astype(F32))
+        input_grad = grad_resid + norm_back(plain, scale, jnp.concatenate(shares, axis=0), params[0])
 
         for chain in chains:
             merge(chain, fetch(chain))
             while chain[3]:
                 split(chain)
                 merge(chain, fetch(chain))
-        sum_shrink, sum_expand, sum_output = [chain[0] for chain in chains]
-        sum_shrink = sum_shrink.reshape(spans * part, width)
+        last_shrink, last_expand, sum_output = chains[2][0]
+        sum_shrink = jnp.concatenate([chains[0][0].reshape(cut // n_dev, width), last_shrink], axis=0)
+        sum_expand = jnp.concatenate([chains[1][0], last_expand], axis=1)
         sum_expand = sum_expand.reshape(part, spans, n_dev, part).transpose(0, 2, 1, 3).reshape(part, hidden)
 
-        new_joint, first_joint, second_joint = adam_step(
-            joint_weight, sum_joint, momentum_joint, variance_joint, RATE_MATRIX, WEIGHT_DECAY
-        )
         new_output, first_output, second_output = adam_step(
             output_weight, sum_output, momentum_output, variance_output, RATE_MATRIX, WEIGHT_DECAY
         )
@@ -759,9 +797,6 @@
         )
         new_shrink, first_shrink, second_shrink = adam_step(
             shrink_weight, sum_shrink, momentum_shrink, variance_shrink, RATE_MATRIX, WEIGHT_DECAY
-        )
-        new_small, first_small, second_small = adam_step(
-            small_params, small_sum, momentum_small, variance_small, RATE_VECTOR, 0.0
         )
         return (
             block_output,

time: 436 us -> 382 us (0.88)
  waiting for transfers between devices: 110 us -> 76.9 us
  other arithmetic: 42 us -> 31.3 us
  starting transfers between devices: 47.5 us -> 40.5 us
  local copies, waits for them, and re-layouts: 57.2 us -> 50.8 us
    ppermute x57 -> x52, waiting for transfers between devices: 105 us -> 76.8 us  [swap(): lax.ppermute(value, axis, [(place, place ^ mask) for place in range(sizes...]
    ppermute x7 -> x0, local copies, waits for them, and re-layouts: 12.2 us -> none  [swap(): lax.ppermute(value, axis, [(place, place ^ mask) for place in range(sizes...]
    squeeze x5 -> x2, local copies, waits for them, and re-layouts: 8.99 us -> 0.12 us  [the longest x1 0.1 us: per_device(): joined[0]]
    ppermute x57 -> x52, starting transfers between devices: 47.5 us -> 40.4 us  [swap(): lax.ppermute(value, axis, [(place, place ^ mask) for place in range(sizes...]
    convert_element_type x5 -> x0, other arithmetic: 6.28 us -> none  [the longest x2 3.78 us: per_device(): pending = [known[0], known[top].astype(BF16)]]
    convert_element_type x15 -> x16, local copies, waits for them, and re-layouts: 4.03 us -> 9.66 us  [split(): lax.dynamic_index_in_dim(value, 1 - mine, pos, keepdims=False).astype(BF16)]
    all_gather x1, waiting for transfers between devices: 4.41 us -> 0.02 us  [per_device(): lax.all_gather(rest, ('dp', 'ctx'), axis=0, tiled=True, axis_index_groups...]
    add x14 -> x16, other arithmetic: 8.18 us -> 12.4 us  [merge(): chain[0] = chain[0] + got.astype(F32)]
  transfers between devices with their start and end apart: 58 -> 53, of which waited for: 17 -> 16; matrix products, arithmetic and copies ran while one was open for 20% -> 19% of each run, Pallas kernels for 21% -> 27%
where the time goes in v5:
time: 382 us; the launch traced here: 376 us
  Pallas kernels  144 us (38%)
  waiting for transfers between devices  76.9 us (20%)
  local copies, waits for them, and re-layouts  50.8 us (13%)
  starting transfers between devices  40.5 us (11%)
  other arithmetic  31.3 us (8%)
  matrix products  16.5 us (4%)
  between operations  16.1 us (4%)
    ppermute x52, waiting for transfers between devices, swap(): lax.ppermute(value, axis, [(place, place ^ mask) for place in range(sizes...  76.8 us
    ppermute x52, starting transfers between devices, swap(): lax.ppermute(value, axis, [(place, place ^ mask) for place in range(sizes...  40.4 us
    pallas_call x1, Pallas kernels, layer(): pl.pallas_call(functools.partial(layer_kernel, n_ctx, spans), grid_spec=p...  39.5 us
    pallas_call x2, Pallas kernels, attend_backward(): pl.pallas_call(functools.partial(backward_kernel, n_blk, blk, heads), gri...  37.7 us
    pallas_call x2, Pallas kernels, attend_forward(): pl.pallas_call(functools.partial(forward_kernel, n_blk, blk, heads), grid...  27.3 us
    pallas_call x2, Pallas kernels, unproject(): pl.pallas_call(functools.partial(unproject_kernel, n_blk), grid_spec=pltp...  23.1 us
    dot_general x8, matrix products, dot(): lax.dot_general(left, right, (dims, ((), ())), preferred_element_type=F32)  16.5 us
    pallas_call x2, Pallas kernels, project(): pl.pallas_call(functools.partial(project_kernel, n_blk), grid=(seqs,), in...  13.7 us
  transfers between devices with their start and end apart: 53, of which 16 were waited for; matrix products, arithmetic and copies ran while one was open for 19% of the time, Pallas kernels for 27%

profile of v5, /device:TPU:0, one launch (start us, length us, event | category | flops | bytes accessed | tf_op | source)
XLA Modules:
  0.0 375.7 jit_solution(12179070292836101383)
XLA Ops:
  7.3 3.0 collective-permute-start.4
  14.9 1.3 collective-permute-start.2
  17.2 1.2 reshape.464
  18.6 1.3 reshape.465
  24.1 18.9 %collective-permute-done.6.refs_2_.refs_3_ = bf16[2,256,768]{2,1,0:T(8,128)(2,1)S(1)} collective-permute-done((bf16[2,256,768]{2,1,0:T(8,128)(2,1)S(1)}, bf16[2,256,768]{2,1,0:T(8,128)(2,1)S(1)}, u32[]{:S(2)}, u32[]{:S(2)}) %collective-permute-start.6) | collective-permute-done | bytes 786464 | tf_op jit(solution)/shard_map/ppermute | solution.py:508
  44.0 2.7 collective-permute-start.7
  46.7 7.2 %collective-permute-done.7 = bf16[4,24,588]{2,1,0:T(8,128)(2,1)S(1)} collective-permute-done((bf16[4,24,588]{2,1,0:T(8,128)(2,1)S(1)}, bf16[4,24,588]{2,1,0:T(8,128)(2,1)S(1)}, u32[]{:S(2)}, u32[]{:S(2)}) %collective-permute-start.7) | collective-permute-done | bytes 112928 | tf_op jit(solution)/shard_map/ppermute | solution.py:508
  54.1 14.7 %collective-permute-done.8 = bf16[2,4,24,588]{3,2,1,0:T(8,128)(2,1)S(1)} collective-permute-done((bf16[2,4,24,588]{3,2,1,0:T(8,128)(2,1)S(1)}, bf16[2,4,24,588]{3,2,1,0:T(8,128)(2,1)S(1)}, u32[]{:S(2)}, u32[]{:S(2)}) %collective-permute-start.8) | collective-permute-done | bytes 225824 | tf_op jit(solution)/shard_map/ppermute | solution.py:508
  68.9 1.5 collective-permute-start.12
  72.1 6.1 %collective-permute-done.12 = bf16[2,2,4,24,588]{4,3,2,1,0:T(8,128)(2,1)S(1)} collective-permute-done((bf16[2,2,4,24,588]{4,3,2,1,0:T(8,128)(2,1)S(1)}, bf16[2,2,4,24,588]{4,3,2,1,0:T(8,128)(2,1)S(1)}, u32[]{:S(2)}, u32[]{:S(2)}) %collective-permute-start.12) | collective-permute-done | bytes 451616 | tf_op jit(solution)/shard_map/ppermute | solution.py:508
  82.2 7.1 %project.2.joint_ref = bf16[4,2,256,576]{3,2,1,0:T(8,128)(2,1)} custom-call(bf16[2,256,768]{2,1,0:T(8,128)(2,1)} %copy-done.22, bf16[2,256,768]{2,1,0:T(8,128)(2,1)} %collective-permute-done.10.refs_1_.refs_2_, bf16[2,256,768]{2,1,0:T(8,128)(2,1)} %copy-done.37, bf16[2,256,768]{2,1,0:T(8,128)(2,1)} %collective-permute-done.11.refs_3_.refs_4_, ...), custom_call_target="tpu_custom_call" | custom-call | flops 20000000000 | bytes 1000000 | tf_op jit(solution)/shard_map/project/pallas_call | solution.py:73
  89.3 13.6 %attend_forward.2 = (bf16[2,256,192]{2,1,0:T(8,128)(2,1)}, bf16[2,256,192]{2,1,0:T(8,128)(2,1)}, bf16[2,256,192]{2,1,0:T(8,128)(2,1)}, bf16[2,256,192]{2,1,0:T(8,128)(2,1)}, f32[2,3,1024]{2,1,0:T(4,128)}) custom-call(s32[1]{0:T(128)} %bitcast.me_ref, bf16[4,2,256,576]{3,2,1,0:T(8,128)(2,1)} %project.2.joint_ref, ...), custom_call_target="tpu_custom_call" | custom-call | flops 20000000000 | bytes 1000000 | tf_op jit(solution)/shard_map/attend_forward/pallas_call | solution.py:151
  103.0 6.5 %project.3.joint_ref = bf16[4,2,256,576]{3,2,1,0:T(8,128)(2,1)} custom-call(bf16[2,256,768]{2,1,0:T(8,128)(2,1)} %copy-done.21, bf16[2,256,768]{2,1,0:T(8,128)(2,1)} %collective-permute-done.13.refs_1_.refs_2_, bf16[2,256,768]{2,1,0:T(8,128)(2,1)} %collective-permute-done.9.refs_2_.refs_3_, bf16[2,256,768]{2,1,0:T(8,128)(2,1)} %collective-permute-done.14.refs_3_.refs_4_, ...), custom_call_target="tpu_custom_call" | custom-call | flops 20000000000 | bytes 1000000 | tf_op jit(solution)/shard_map/project/pallas_call | solution.py:73
  109.6 1.8 collective-permute-start.17
  111.4 13.7 %attend_forward.3 = (bf16[2,256,192]{2,1,0:T(8,128)(2,1)}, bf16[2,256,192]{2,1,0:T(8,128)(2,1)}, bf16[2,256,192]{2,1,0:T(8,128)(2,1)}, bf16[2,256,192]{2,1,0:T(8,128)(2,1)}, f32[2,3,1024]{2,1,0:T(4,128)}) custom-call(s32[1]{0:T(128)} %bitcast.me_ref, bf16[4,2,256,576]{3,2,1,0:T(8,128)(2,1)} %project.3.joint_ref, ...), custom_call_target="tpu_custom_call" | custom-call | flops 20000000000 | bytes 1000000 | tf_op jit(solution)/shard_map/attend_forward/pallas_call | solution.py:151
  125.9 1.7 collective-permute-start.20
  128.6 5.5 %collective-permute-done.21 = bf16[2,256,192]{2,1,0:T(8,128)(2,1)S(1)} collective-permute-done((bf16[2,256,192]{2,1,0:T(8,128)(2,1)}, bf16[2,256,192]{2,1,0:T(8,128)(2,1)S(1)}, u32[]{:S(2)}, u32[]{:S(2)}) %collective-permute-start.21) | collective-permute-done | bytes 196640 | tf_op jit(solution)/shard_map/ppermute | solution.py:508
  134.2 5.9 %collective-permute-done.20 = bf16[2,256,192]{2,1,0:T(8,128)(2,1)S(1)} collective-permute-done((bf16[2,256,192]{2,1,0:T(8,128)(2,1)}, bf16[2,256,192]{2,1,0:T(8,128)(2,1)S(1)}, u32[]{:S(2)}, u32[]{:S(2)}) %collective-permute-start.20) | collective-permute-done | bytes 196640 | tf_op jit(solution)/shard_map/ppermute | solution.py:508
  141.2 39.5 %layer.1 = (bf16[4,256,768]{2,1,0:T(8,128)(2,1)}, f32[4,256,768]{2,1,0:T(8,128)}, bf16[4,256,768]{2,1,0:T(8,128)(2,1)}, bf16[768,1024]{1,0:T(8,128)(2,1)}, bf16[...) custom-call(s32[1]{0:T(128)} %bitcast.me_ref, ...), custom_call_target="tpu_custom_call" | custom-call | flops 20000000000 | bytes 1000000 | tf_op jit(solution)/shard_map/layer/pallas_call | solution.py:277
  181.0 1.7 collective-permute-start.25
  182.9 2.3 convolution_bitcast_fusion.4
  186.8 1.4 copy-done.43
  188.2 2.9 fusion.16
  191.2 3.8 %fusion = f32[768,2304]{1,0:T(8,128)S(1)} fusion(bf16[768,1024]{1,0:T(8,128)(2,1)S(1)} %copy-done.44, bf16[1024,3072]{1,0:T(8,128)(2,1)S(1)} %bitcast.251), kind=kOutput, calls=%fused_computation.1 | convolution fusion | flops 3623878656 | bytes 13369344 | tf_op jit(solution)/shard_map/dot_general | solution.py:57
  196.1 2.4 copy-done.36
  198.5 1.4 convolution_bitcast_fusion
  199.9 4.5 %fusion.54 = f32[3,2,2,2,2,2,24,768]{7,6,5,4,3,2,1,0:T(8,128)S(1)} fusion(bf16[3,2,2,2,2,2,24,1024]{7,6,5,4,3,2,1,0:T(8,128)(2,1)S(1)} %bitcast.206, bf16[1024,768,1,1,1,1,1,1]{1,0,7,6,5,4,3,2:T(8,128)(2,1)S(1)} %bitcast.249), kind=kOutput, calls=%fused_computation.201 | convolution fusion | flops 3623878656 | bytes 13369344 | tf_op jit(solution)/shard_map/dot_general | solution.py:57
  207.9 2.1 fusion.12
  210.2 1.4 fusion.13
  214.3 2.7 concatenate.129.refs_7_
  217.0 2.5 dynamic-slice_bitcast_fusion
  219.4 2.3 dynamic-slice_bitcast_fusion.1
  222.1 2.0 convert_add_fusion
  224.3 1.9 convert_add_fusion.1
  227.4 2.0 convert_add_fusion.2
  231.9 18.9 %attend_backward.2.refs_0_ = bf16[4,2,256,576]{3,2,1,0:T(8,128)(2,1)} custom-call(s32[1]{0:T(128)} %bitcast.me_ref, bf16[4,2,256,576]{3,2,1,0:T(8,128)(2,1)} %project.2.joint_ref, bf16[4,256,192]{2,1,0:T(8,128)(2,1)} %get-tuple-element.234.refs_0_, bf16[4,256,192]{2,1,0:T(8,128)(2,1)} %copy-done.38, bf16[4,256,192]{2,1,0:T(8,128)(2,1)} %copy-done.39, ...), custom_call_target="tpu_custom_call" | custom-call | flops 20000000000 | bytes 1000000 | tf_op jit(solution)/shard_map/attend_backward/pallas_call | solution.py:379
  250.9 1.8 collective-permute-done.29
  253.6 1.4 convert_add_fusion.5
  255.1 1.3 convert_add_fusion.6
  256.6 1.4 convert_add_fusion.7
  259.0 1.7 collective-permute-start.35
  260.8 11.6 %unproject.2 = (bf16[2,2,256,768]{3,2,1,0:T(8,128)(2,1)}, bf16[2,2,256,768]{3,2,1,0:T(8,128)(2,1)}, f32[768,588]{1,0:T(8,128)}) custom-call(s32[1]{0:T(128)} %bitcast.me_ref, bf16[4,2,256,576]{3,2,1,0:T(8,128)(2,1)} %attend_backward.2.refs_0_, bf16[2,256,768]{2,1,0:T(8,128)(2,1)} %copy-done.22, bf16[2,256,768]{2,1,0:T(8,128)(2,1)} %collective-permute-done.10.refs_1_.refs_2_, ...), custom_call_target="tpu_custom_call" | custom-call | flops 20000000000 | bytes 1000000 | tf_op jit(solution)/shard_map/unproject/pallas_call | solution.py:452
  273.7 2.4 collective-permute-done.32
  277.8 3.7 collective-permute-start.37
  281.6 1.6 collective-permute-start.39
  283.2 18.8 %attend_backward.3.refs_0_ = bf16[4,2,256,576]{3,2,1,0:T(8,128)(2,1)} custom-call(s32[1]{0:T(128)} %bitcast.me_ref, bf16[4,2,256,576]{3,2,1,0:T(8,128)(2,1)} %project.3.joint_ref, bf16[4,256,192]{2,1,0:T(8,128)(2,1)} %get-tuple-element.234.refs_0_, bf16[4,256,192]{2,1,0:T(8,128)(2,1)} %copy-done.38, bf16[4,256,192]{2,1,0:T(8,128)(2,1)} %copy-done.39, ...), custom_call_target="tpu_custom_call" | custom-call | flops 20000000000 | bytes 1000000 | tf_op jit(solution)/shard_map/attend_backward/pallas_call | solution.py:379
  303.6 1.7 collective-permute-start.51
  305.8 2.4 collective-permute-start.50
  308.3 11.5 %unproject.3 = (bf16[2,2,256,768]{3,2,1,0:T(8,128)(2,1)}, bf16[2,2,256,768]{3,2,1,0:T(8,128)(2,1)}, f32[768,588]{1,0:T(8,128)}) custom-call(s32[1]{0:T(128)} %bitcast.me_ref, bf16[4,2,256,576]{3,2,1,0:T(8,128)(2,1)} %attend_backward.3.refs_0_, bf16[2,256,768]{2,1,0:T(8,128)(2,1)} %copy-done.21, bf16[2,256,768]{2,1,0:T(8,128)(2,1)} %collective-permute-done.13.refs_1_.refs_2_, ...), custom_call_target="tpu_custom_call" | custom-call | flops 20000000000 | bytes 1000000 | tf_op jit(solution)/shard_map/unproject/pallas_call | solution.py:452
  319.9 2.1 fusion.24
  323.3 2.3 reshape.476
  325.6 3.8 %copy.131 = f32[24,32,4,24]{3,2,1,0:T(4,128)} copy(f32[24,32,4,24]{3,1,2,0:T(8,128)} %bitcast.205) | data formatting | bytes 589824 | tf_op jit(solution)/shard_map/transpose | solution.py:790
  329.4 3.3 reshape.477
  332.7 2.3 multiply_subtract_fusion.1
  336.1 1.8 convert_add_fusion.3
  338.4 1.7 multiply_subtract_fusion.2
  342.4 1.9 collective-permute-start.42
  344.3 2.5 collective-permute-start.44
  346.8 1.3 collective-permute-done.42
  348.1 7.8 %collective-permute-done.43 = bf16[4,24,588]{2,1,0:T(8,128)(2,1)S(1)} collective-permute-done((bf16[4,24,588]{2,1,0:T(8,128)(2,1)S(1)}, bf16[4,24,588]{2,1,0:T(8,128)(2,1)S(1)}, u32[]{:S(2)}, u32[]{:S(2)}) %collective-permute-start.43) | collective-permute-done | bytes 112928 | tf_op jit(solution)/shard_map/ppermute | solution.py:508
  356.0 1.8 collective-permute-done.45
  358.3 1.5 collective-permute-start.48
  361.9 2.3 fusion.9
  366.0 2.3 finish.1
  (315 shorter events, 50.0 us)
Async XLA Ops:
  7.2 10.0 %copy-start.10 = (f32[96,768]{1,0:T(8,128)S(1)}, f32[96,768]{1,0:T(8,128)}, u32[]{:S(2)}) copy-start(f32[96,768]{1,0:T(8,128)} %param.24) | copy-start | bytes 884740
  7.2 10.0 %copy-start.23 = (f32[24,768]{1,0:T(8,128)S(1)}, f32[24,768]{1,0:T(8,128)}, u32[]{:S(2)}) copy-start(f32[24,768]{1,0:T(8,128)} %param.22) | copy-start | bytes 221188
  7.2 118.0 %all-gather.2.cloned.1.call-start = ((), (), s32[]{:S(2)}) async-start(), calls=%async_computation | async-start | bytes 5640192 | tf_op jit(solution)/shard_map/all_gather | solution.py:589
  7.3 12.9 %collective-permute-start.4 = (s32[4,256]{1,0:T(4,128)}, s32[4,256]{1,0:T(4,128)S(1)}, u32[]{:S(2)}, u32[]{:S(2)}) collective-permute-start(s32[4,256]{1,0:T(4,128)} %param.19), channel_id=1, source_target_pairs={{0,2},{1,3},{2,0},{3,1},{4,6},{5,7},{6,4},{7,5},{8,10},{9,11},{10,... | collective-permute-start | bytes 12296 | tf_op jit(solution)/shard_map/ppermute | solution.py:508
  10.3 10.8 %collective-permute-start.3 = (s32[4,256]{1,0:T(4,128)}, s32[4,256]{1,0:T(4,128)S(1)}, u32[]{:S(2)}, u32[]{:S(2)}) collective-permute-start(s32[4,256]{1,0:T(4,128)} %param.19), channel_id=1, source_target_pairs={{0,1},{1,0},{2,3},{3,2},{4,5},{5,4},{6,7},{7,6},{8,9},{9,8},{10,11... | collective-permute-start | bytes 12296 | tf_op jit(solution)/shard_map/ppermute | solution.py:508
  14.3 9.8 %collective-permute-start = (bf16[24,588]{1,0:T(8,128)(2,1)}, bf16[24,588]{1,0:T(8,128)(2,1)S(1)}, u32[]{:S(2)}, u32[]{:S(2)}) collective-permute-start(bf16[24,588]{1,0:T(8,128)(2,1)} %get-tuple-element.371), channel_id=1, source_target_pairs={{0,1},{1,0},{2,3},{3,2},{4,5},{5,4},{6,7},{7,6},{8,9},{9,8},{10,11... | collective-permute-start | bytes 84680 | tf_op jit(solution)/shard_map/ppermute | solution.py:508
  14.8 9.3 %collective-permute-start.1 = (bf16[24,588]{1,0:T(8,128)(2,1)S(1)}, bf16[24,588]{1,0:T(8,128)(2,1)S(1)}, u32[]{:S(2)}, u32[]{:S(2)}) collective-permute-start(bf16[24,588]{1,0:T(8,128)(2,1)S(1)} %get-tuple-element.372), channel_id=1, source_target_pairs={{0,2},{1,3},{2,0},{3,1},{4,6},{5,7},{6,4},{7,5},{8,10},{9,11},{10,... | collective-permute-start | bytes 84680 | tf_op jit(solution)/shard_map/ppermute | solution.py:508
  14.9 9.2 %collective-permute-start.2 = (bf16[24,588]{1,0:T(8,128)(2,1)S(1)}, bf16[24,588]{1,0:T(8,128)(2,1)S(1)}, u32[]{:S(2)}, u32[]{:S(2)}) collective-permute-start(bf16[24,588]{1,0:T(8,128)(2,1)S(1)} %get-tuple-element.370), channel_id=1, source_target_pairs={{0,3},{1,2},{2,1},{3,0},{4,7},{5,6},{6,5},{7,4},{8,11},{9,10},{10,... | collective-permute-start | bytes 84680 | tf_op jit(solution)/shard_map/ppermute | solution.py:508
  20.1 1.7 collective-permute-start.5
  21.1 57.4 %copy-start.21 = (bf16[2,256,768]{2,1,0:T(8,128)(2,1)}, bf16[2,256,768]{2,1,0:T(8,128)(2,1)S(1)}, u32[]{:S(2)}) copy-start(bf16[2,256,768]{2,1,0:T(8,128)(2,1)S(1)} %get-tuple-element.182.refs_0_.refs_1_) | copy-start | bytes 2359300
  21.1 57.4 %copy-start.22 = (bf16[2,256,768]{2,1,0:T(8,128)(2,1)}, bf16[2,256,768]{2,1,0:T(8,128)(2,1)S(1)}, u32[]{:S(2)}) copy-start(bf16[2,256,768]{2,1,0:T(8,128)(2,1)S(1)} %get-tuple-element.174.refs_0_.refs_1_) | copy-start | bytes 2359300
  21.1 21.9 %collective-permute-start.6 = (bf16[2,256,768]{2,1,0:T(8,128)(2,1)S(1)}, bf16[2,256,768]{2,1,0:T(8,128)(2,1)S(1)}, u32[]{:S(2)}, u32[]{:S(2)}) collective-permute-start(bf16[2,256,768]{2,1,0:T(8,128)(2,1)S(1)} %get-tuple-element.174.refs_0_.refs_1_), channel_id=1, source_target_pairs={{0,2},{1,3},{2,0},{3,1},{4,6},{5,7},{6,4},{7,5},{8,10},{9,11},{10,... | collective-permute-start | bytes 2359304 | tf_op jit(solution)/shard_map/ppermute | solution.py:508
  21.8 1.4 collective-permute-start.18
  43.0 25.9 %collective-permute-start.9 = (bf16[2,256,768]{2,1,0:T(8,128)(2,1)S(1)}, bf16[2,256,768]{2,1,0:T(8,128)(2,1)}, u32[]{:S(2)}, u32[]{:S(2)}) collective-permute-start(bf16[2,256,768]{2,1,0:T(8,128)(2,1)S(1)} %get-tuple-element.182.refs_0_.refs_1_), channel_id=1, source_target_pairs={{0,2},{1,3},{2,0},{3,1},{4,6},{5,7},{6,4},{7,5},{8,10},{9,11},{10,... | collective-permute-start | bytes 2359304 | tf_op jit(solution)/shard_map/ppermute | solution.py:508
  44.0 9.9 %collective-permute-start.7 = (bf16[4,24,588]{2,1,0:T(8,128)(2,1)S(1)}, bf16[4,24,588]{2,1,0:T(8,128)(2,1)S(1)}, u32[]{:S(2)}, u32[]{:S(2)}) collective-permute-start(bf16[4,24,588]{2,1,0:T(8,128)(2,1)S(1)} %get-tuple-element.357), channel_id=1, source_target_pairs={{0,16},{4,20},{8,24},{12,28},{16,0},{20,4},{24,8},{28,12},{1,17},{... | collective-permute-start | bytes 338696 | tf_op jit(solution)/shard_map/ppermute | solution.py:508
  53.9 14.8 %collective-permute-start.8 = (bf16[2,4,24,588]{3,2,1,0:T(8,128)(2,1)S(1)}, bf16[2,4,24,588]{3,2,1,0:T(8,128)(2,1)S(1)}, u32[]{:S(2)}, u32[]{:S(2)}) collective-permute-start(bf16[2,4,24,588]{3,2,1,0:T(8,128)(2,1)S(1)} %maximum_select_fusion.3), channel_id=1, source_target_pairs={{0,8},{4,12},{8,0},{12,4},{16,24},{20,28},{24,16},{28,20},{1,9},{5... | collective-permute-start | bytes 677384 | tf_op jit(solution)/shard_map/ppermute | solution.py:508
  68.9 9.3 %collective-permute-start.12 = (bf16[2,2,4,24,588]{4,3,2,1,0:T(8,128)(2,1)S(1)}, bf16[2,2,4,24,588]{4,3,2,1,0:T(8,128)(2,1)S(1)}, u32[]{:S(2)}, u32[]{:S(2)}) collective-permute-start(bf16[2,2,4,24,588]{4,3,2,1,0:T(8,128)(2,1)S(1)} %maximum_select_fusion.1), channel_id=1, source_target_pairs={{0,4},{4,0},{8,12},{12,8},{16,20},{20,16},{24,28},{28,24},{1,5},{5... | collective-permute-start | bytes 1354760 | tf_op jit(solution)/shard_map/ppermute | solution.py:508
  71.1 31.8 %collective-permute-start.13 = (bf16[2,256,768]{2,1,0:T(8,128)(2,1)S(1)}, bf16[2,256,768]{2,1,0:T(8,128)(2,1)}, u32[]{:S(2)}, u32[]{:S(2)}) collective-permute-start(bf16[2,256,768]{2,1,0:T(8,128)(2,1)S(1)} %get-tuple-element.182.refs_0_.refs_1_), channel_id=1, source_target_pairs={{0,1},{1,0},{2,3},{3,2},{4,5},{5,4},{6,7},{7,6},{8,9},{9,8},{10,11... | collective-permute-start | bytes 2359304 | tf_op jit(solution)/shard_map/ppermute | solution.py:508
  71.1 31.8 %collective-permute-start.14 = (bf16[2,256,768]{2,1,0:T(8,128)(2,1)}, bf16[2,256,768]{2,1,0:T(8,128)(2,1)}, u32[]{:S(2)}, u32[]{:S(2)}) collective-permute-start(bf16[2,256,768]{2,1,0:T(8,128)(2,1)} %collective-permute-done.9.refs_2_.refs_3_), channel_id=1, source_target_pairs={{0,1},{1,0},{2,3},{3,2},{4,5},{5,4},{6,7},{7,6},{8,9},{9,8},{10,11... | collective-permute-start | bytes 2359304 | tf_op jit(solution)/shard_map/ppermute | solution.py:508
  71.6 10.6 %collective-permute-start.10 = (bf16[2,256,768]{2,1,0:T(8,128)(2,1)S(1)}, bf16[2,256,768]{2,1,0:T(8,128)(2,1)}, u32[]{:S(2)}, u32[]{:S(2)}) collective-permute-start(bf16[2,256,768]{2,1,0:T(8,128)(2,1)S(1)} %get-tuple-element.174.refs_0_.refs_1_), channel_id=1, source_target_pairs={{0,1},{1,0},{2,3},{3,2},{4,5},{5,4},{6,7},{7,6},{8,9},{9,8},{10,11... | collective-permute-start | bytes 2359304 | tf_op jit(solution)/shard_map/ppermute | solution.py:508
  71.6 10.6 %collective-permute-start.11 = (bf16[2,256,768]{2,1,0:T(8,128)(2,1)}, bf16[2,256,768]{2,1,0:T(8,128)(2,1)}, u32[]{:S(2)}, u32[]{:S(2)}) collective-permute-start(bf16[2,256,768]{2,1,0:T(8,128)(2,1)} %copy-done.37), channel_id=1, source_target_pairs={{0,1},{1,0},{2,3},{3,2},{4,5},{5,4},{6,7},{7,6},{8,9},{9,8},{10,11... | collective-permute-start | bytes 2359304 | tf_op jit(solution)/shard_map/ppermute | solution.py:508
  102.9 6.7 %copy-start.40 = (bf16[2,256,192]{2,1,0:T(8,128)(2,1)S(1)}, bf16[2,256,192]{2,1,0:T(8,128)(2,1)}, u32[]{:S(2)}) copy-start(bf16[2,256,192]{2,1,0:T(8,128)(2,1)} %get-tuple-element.187) | copy-start | bytes 589828
  109.5 15.6 %collective-permute-start.15 = (bf16[2,256,192]{2,1,0:T(8,128)(2,1)S(1)}, bf16[2,256,192]{2,1,0:T(8,128)(2,1)S(1)}, u32[]{:S(2)}, u32[]{:S(2)}) collective-permute-start(bf16[2,256,192]{2,1,0:T(8,128)(2,1)S(1)} %copy-done.42), channel_id=1, source_target_pairs={{0,1},{1,0},{2,3},{3,2},{4,5},{5,4},{6,7},{7,6},{8,9},{9,8},{10,11... | collective-permute-start | bytes 589832 | tf_op jit(solution)/shard_map/ppermute | solution.py:508
  109.5 15.6 %collective-permute-start.16 = (bf16[2,256,192]{2,1,0:T(8,128)(2,1)S(1)}, bf16[2,256,192]{2,1,0:T(8,128)(2,1)S(1)}, u32[]{:S(2)}, u32[]{:S(2)}) collective-permute-start(bf16[2,256,192]{2,1,0:T(8,128)(2,1)S(1)} %copy-done.41), channel_id=1, source_target_pairs={{0,2},{1,3},{2,0},{3,1},{4,6},{5,7},{6,4},{7,5},{8,10},{9,11},{10,... | collective-permute-start | bytes 589832 | tf_op jit(solution)/shard_map/ppermute | solution.py:508
  109.6 15.5 %collective-permute-start.17 = (bf16[2,256,192]{2,1,0:T(8,128)(2,1)S(1)}, bf16[2,256,192]{2,1,0:T(8,128)(2,1)S(1)}, u32[]{:S(2)}, u32[]{:S(2)}) collective-permute-start(bf16[2,256,192]{2,1,0:T(8,128)(2,1)S(1)} %copy-done.40), channel_id=1, source_target_pairs={{0,3},{1,2},{2,1},{3,0},{4,7},{5,6},{6,5},{7,4},{8,11},{9,10},{10,... | collective-permute-start | bytes 589832 | tf_op jit(solution)/shard_map/ppermute | solution.py:508
  111.4 14.4 %copy-start.27 = (bf16[2,256,192]{2,1,0:T(8,128)(2,1)S(1)}, bf16[2,256,192]{2,1,0:T(8,128)(2,1)}, u32[]{:S(2)}) copy-start(bf16[2,256,192]{2,1,0:T(8,128)(2,1)} %get-tuple-element.193) | copy-start | bytes 589828
  125.2 15.0 %collective-permute-start.22 = (bf16[768,3456]{1,0:T(8,128)(2,1)}, bf16[768,3456]{1,0:T(8,128)(2,1)}, u32[]{:S(2)}, u32[]{:S(2)}) collective-permute-start(bf16[768,3456]{1,0:T(8,128)(2,1)} %all-gather.2.cloned.1.call-done.refs_4_), channel_id=1, source_target_pairs={{0,1},{1,0},{2,3},{3,2},{4,5},{5,4},{6,7},{7,6},{8,9},{9,8},{10,11... | collective-permute-start | bytes 15925256 | tf_op jit(solution)/shard_map/ppermute | solution.py:508
  125.6 8.5 %collective-permute-start.21 = (bf16[2,256,192]{2,1,0:T(8,128)(2,1)}, bf16[2,256,192]{2,1,0:T(8,128)(2,1)S(1)}, u32[]{:S(2)}, u32[]{:S(2)}) collective-permute-start(bf16[2,256,192]{2,1,0:T(8,128)(2,1)} %get-tuple-element.207), channel_id=1, source_target_pairs={{0,3},{1,2},{2,1},{3,0},{4,7},{5,6},{6,5},{7,4},{8,11},{9,10},{10,... | collective-permute-start | bytes 589832 | tf_op jit(solution)/shard_map/ppermute | solution.py:508
  125.9 14.3 %collective-permute-start.20 = (bf16[2,256,192]{2,1,0:T(8,128)(2,1)}, bf16[2,256,192]{2,1,0:T(8,128)(2,1)S(1)}, u32[]{:S(2)}, u32[]{:S(2)}) collective-permute-start(bf16[2,256,192]{2,1,0:T(8,128)(2,1)} %get-tuple-element.205), channel_id=1, source_target_pairs={{0,2},{1,3},{2,0},{3,1},{4,6},{5,7},{6,4},{7,5},{8,10},{9,11},{10,... | collective-permute-start | bytes 589832 | tf_op jit(solution)/shard_map/ppermute | solution.py:508
  127.6 12.6 %collective-permute-start.19 = (bf16[2,256,192]{2,1,0:T(8,128)(2,1)}, bf16[2,256,192]{2,1,0:T(8,128)(2,1)S(1)}, u32[]{:S(2)}, u32[]{:S(2)}) collective-permute-start(bf16[2,256,192]{2,1,0:T(8,128)(2,1)} %get-tuple-element.203), channel_id=1, source_target_pairs={{0,1},{1,0},{2,3},{3,2},{4,5},{5,4},{6,7},{7,6},{8,9},{9,8},{10,11... | collective-permute-start | bytes 589832 | tf_op jit(solution)/shard_map/ppermute | solution.py:508
  128.6 11.6 %copy-start.18 = (bf16[4,256,192]{2,1,0:T(8,128)(2,1)}, bf16[4,256,192]{2,1,0:T(8,128)(2,1)S(1)}, u32[]{:S(2)}) copy-start(bf16[4,256,192]{2,1,0:T(8,128)(2,1)S(1)} %constant_dynamic-update-slice_fusion.4.refs_0_) | copy-start | bytes 1179652
  180.7 2.2 collective-permute-start.23
  180.8 24.6 %collective-permute-start.24 = (bf16[4,256,192]{2,1,0:T(8,128)(2,1)}, bf16[4,256,192]{2,1,0:T(8,128)(2,1)S(1)}, u32[]{:S(2)}, u32[]{:S(2)}) collective-permute-start(bf16[4,256,192]{2,1,0:T(8,128)(2,1)} %get-tuple-element.222), channel_id=1, source_target_pairs={{0,2},{1,3},{2,0},{3,1},{4,6},{5,7},{6,4},{7,5},{8,10},{9,11},{10,... | collective-permute-start | bytes 1179656 | tf_op jit(solution)/shard_map/ppermute | solution.py:508
  181.0 25.2 %collective-permute-start.25 = (bf16[4,256,192]{2,1,0:T(8,128)(2,1)}, bf16[4,256,192]{2,1,0:T(8,128)(2,1)}, u32[]{:S(2)}, u32[]{:S(2)}) collective-permute-start(bf16[4,256,192]{2,1,0:T(8,128)(2,1)} %get-tuple-element.223), channel_id=1, source_target_pairs={{0,3},{1,2},{2,1},{3,0},{4,7},{5,6},{6,5},{7,4},{8,11},{9,10},{10,... | collective-permute-start | bytes 1179656 | tf_op jit(solution)/shard_map/ppermute | solution.py:508
  188.2 6.8 %slice-start = ((s8[6291456]{0:T(1024)(128)(4,1)}), s8[4194304]{0:T(1024)(128)(4,1)S(1)}, s32[]{:S(2)}) async-start(s8[6291456]{0:T(1024)(128)(4,1)} %bitcast.203), calls=%async_computation.1 | async-start | bytes 8388608
  195.0 12.9 %copy-start.4 = (f32[768,2304]{1,0:T(8,128)}, f32[768,2304]{1,0:T(8,128)S(1)}, u32[]{:S(2)}) copy-start(f32[768,2304]{1,0:T(8,128)S(1)} %fusion) | copy-start | bytes 21233668
  207.7 14.3 %collective-permute-start.26 = (bf16[3,2,2,2,2,24,768]{6,5,4,3,2,1,0:T(8,128)(2,1)S(1)}, bf16[3,2,2,2,2,24,768]{6,5,4,3,2,1,0:T(8,128)(2,1)}, u32[]{:S(2)}, u32[]{:S(2)}) collective-permute-start(bf16[3,2,2,2,2,24,768]{6,5,4,3,2,1,0:T(8,128)(2,1)S(1)} %fusion.11), channel_id=1, source_target_pairs={{0,1},{1,0},{2,3},{3,2},{4,5},{5,4},{6,7},{7,6},{8,9},{9,8},{10,11... | collective-permute-start | bytes 5308424 | tf_op jit(solution)/shard_map/ppermute | solution.py:508
  210.0 12.0 %collective-permute-start.27 = (bf16[2,2,2,2,24,2304]{5,4,0,1,2,3:T(8,128)(2,1)}, bf16[2,2,2,2,24,2304]{5,4,0,1,2,3:T(8,128)(2,1)}, u32[]{:S(2)}, u32[]{:S(2)}) collective-permute-start(bf16[2,2,2,2,24,2304]{5,4,0,1,2,3:T(8,128)(2,1)} %fusion.12), channel_id=1, source_target_pairs={{0,1},{1,0},{2,3},{3,2},{4,5},{5,4},{6,7},{7,6},{8,9},{9,8},{10,11... | collective-permute-start | bytes 5308424 | tf_op jit(solution)/shard_map/ppermute | solution.py:508
  211.7 10.4 %collective-permute-start.28 = (bf16[3,2,2,2,2,24,768]{6,5,4,3,2,1,0:T(8,128)(2,1)}, bf16[3,2,2,2,2,24,768]{6,5,4,3,2,1,0:T(8,128)(2,1)}, u32[]{:S(2)}, u32[]{:S(2)}) collective-permute-start(bf16[3,2,2,2,2,24,768]{6,5,4,3,2,1,0:T(8,128)(2,1)} %fusion.13), channel_id=1, source_target_pairs={{0,1},{1,0},{2,3},{3,2},{4,5},{5,4},{6,7},{7,6},{8,9},{9,8},{10,11... | collective-permute-start | bytes 5308424 | tf_op jit(solution)/shard_map/ppermute | solution.py:508
  214.3 7.4 %slice-start.2 = ((s8[7077888]{0:T(1024)(128)(4,1)}), s8[4194304]{0:T(1024)(128)(4,1)S(1)}, s32[]{:S(2)}) async-start(s8[7077888]{0:T(1024)(128)(4,1)} %bitcast.208), calls=%async_computation.3 | async-start | bytes 8388608
  230.6 22.1 %collective-permute-start.29 = (bf16[3,2,2,2,24,768]{5,4,3,2,1,0:T(8,128)(2,1)}, bf16[3,2,2,2,24,768]{5,4,3,2,1,0:T(8,128)(2,1)}, u32[]{:S(2)}, u32[]{:S(2)}) collective-permute-start(bf16[3,2,2,2,24,768]{5,4,3,2,1,0:T(8,128)(2,1)} %fusion.19), channel_id=1, source_target_pairs={{0,4},{4,0},{8,12},{12,8},{16,20},{20,16},{24,28},{28,24},{1,5},{5... | collective-permute-start | bytes 2654216 | tf_op jit(solution)/shard_map/ppermute | solution.py:508
  231.8 21.8 %collective-permute-start.30 = (bf16[2,2,2,24,2304]{4,3,0,1,2:T(8,128)(2,1)}, bf16[2,2,2,24,2304]{4,3,0,1,2:T(8,128)(2,1)}, u32[]{:S(2)}, u32[]{:S(2)}) collective-permute-start(bf16[2,2,2,24,2304]{4,3,0,1,2:T(8,128)(2,1)} %fusion.20), channel_id=1, source_target_pairs={{0,2},{1,3},{2,0},{3,1},{4,6},{5,7},{6,4},{7,5},{8,10},{9,11},{10,... | collective-permute-start | bytes 2654216 | tf_op jit(solution)/shard_map/ppermute | solution.py:508
  231.9 21.7 %collective-permute-start.31 = (bf16[3,2,2,2,24,768]{5,4,3,2,1,0:T(8,128)(2,1)S(1)}, bf16[3,2,2,2,24,768]{5,4,3,2,1,0:T(8,128)(2,1)}, u32[]{:S(2)}, u32[]{:S(2)}) collective-permute-start(bf16[3,2,2,2,24,768]{5,4,3,2,1,0:T(8,128)(2,1)S(1)} %fusion.21), channel_id=1, source_target_pairs={{0,8},{4,12},{8,0},{12,4},{16,24},{20,28},{24,16},{28,20},{1,9},{5... | collective-permute-start | bytes 2654216 | tf_op jit(solution)/shard_map/ppermute | solution.py:508
  258.1 14.4 %collective-permute-start.33 = (bf16[3,2,2,24,768]{4,3,2,1,0:T(8,128)(2,1)S(1)}, bf16[3,2,2,24,768]{4,3,2,1,0:T(8,128)(2,1)S(1)}, u32[]{:S(2)}, u32[]{:S(2)}) collective-permute-start(bf16[3,2,2,24,768]{4,3,2,1,0:T(8,128)(2,1)S(1)} %fusion.25), channel_id=1, source_target_pairs={{0,8},{4,12},{8,0},{12,4},{16,24},{20,28},{24,16},{28,20},{1,9},{5... | collective-permute-start | bytes 1327112 | tf_op jit(solution)/shard_map/ppermute | solution.py:508
  258.2 14.2 %collective-permute-start.34 = (bf16[2,2,24,2304]{3,2,0,1:T(8,128)(2,1)S(1)}, bf16[2,2,24,2304]{3,2,0,1:T(8,128)(2,1)S(1)}, u32[]{:S(2)}, u32[]{:S(2)}) collective-permute-start(bf16[2,2,24,2304]{3,2,0,1:T(8,128)(2,1)S(1)} %fusion.26), channel_id=1, source_target_pairs={{0,4},{4,0},{8,12},{12,8},{16,20},{20,16},{24,28},{28,24},{1,5},{5... | collective-permute-start | bytes 1327112 | tf_op jit(solution)/shard_map/ppermute | solution.py:508
  259.0 13.4 %collective-permute-start.35 = (bf16[3,2,2,24,768]{4,3,2,1,0:T(8,128)(2,1)S(1)}, bf16[3,2,2,24,768]{4,3,2,1,0:T(8,128)(2,1)S(1)}, u32[]{:S(2)}, u32[]{:S(2)}) collective-permute-start(bf16[3,2,2,24,768]{4,3,2,1,0:T(8,128)(2,1)S(1)} %fusion.27), channel_id=1, source_target_pairs={{0,2},{1,3},{2,0},{3,1},{4,6},{5,7},{6,4},{7,5},{8,10},{9,11},{10,... | collective-permute-start | bytes 1327112 | tf_op jit(solution)/shard_map/ppermute | solution.py:508
  272.4 3.7 collective-permute-start.32
  277.5 24.5 %collective-permute-start.36 = (bf16[2,256,768]{2,1,0:T(8,128)(2,1)}, bf16[2,256,768]{2,1,0:T(8,128)(2,1)S(1)}, u32[]{:S(2)}, u32[]{:S(2)}) collective-permute-start(bf16[2,256,768]{2,1,0:T(8,128)(2,1)} %fusion.22), channel_id=1, source_target_pairs={{0,2},{1,3},{2,0},{3,1},{4,6},{5,7},{6,4},{7,5},{8,10},{9,11},{10,... | collective-permute-start | bytes 2359304 | tf_op jit(solution)/shard_map/ppermute | solution.py:508
  277.8 24.2 %collective-permute-start.37 = (bf16[3,2,24,768]{3,2,1,0:T(8,128)(2,1)S(1)}, bf16[3,2,24,768]{3,2,1,0:T(8,128)(2,1)S(1)}, u32[]{:S(2)}, u32[]{:S(2)}) collective-permute-start(bf16[3,2,24,768]{3,2,1,0:T(8,128)(2,1)S(1)} %fusion.30), channel_id=1, source_target_pairs={{0,16},{4,20},{8,24},{12,28},{16,0},{20,4},{24,8},{28,12},{1,17},{... | collective-permute-start | bytes 663560 | tf_op jit(solution)/shard_map/ppermute | solution.py:508
  281.5 20.5 %collective-permute-start.38 = (bf16[2,24,2304]{2,1,0:T(8,128)(2,1)}, bf16[2,24,2304]{2,1,0:T(8,128)(2,1)S(1)}, u32[]{:S(2)}, u32[]{:S(2)}) collective-permute-start(bf16[2,24,2304]{2,1,0:T(8,128)(2,1)} %fusion.31), channel_id=1, source_target_pairs={{0,8},{4,12},{8,0},{12,4},{16,24},{20,28},{24,16},{28,20},{1,9},{5... | collective-permute-start | bytes 663560 | tf_op jit(solution)/shard_map/ppermute | solution.py:508
  281.6 20.4 %collective-permute-start.39 = (bf16[3,2,24,768]{3,2,1,0:T(8,128)(2,1)S(1)}, bf16[3,2,24,768]{3,2,1,0:T(8,128)(2,1)S(1)}, u32[]{:S(2)}, u32[]{:S(2)}) collective-permute-start(bf16[3,2,24,768]{3,2,1,0:T(8,128)(2,1)S(1)} %fusion.32), channel_id=1, source_target_pairs={{0,4},{4,0},{8,12},{12,8},{16,20},{20,16},{24,28},{28,24},{1,5},{5... | collective-permute-start | bytes 663560 | tf_op jit(solution)/shard_map/ppermute | solution.py:508
  303.6 31.3 %collective-permute-start.51 = (bf16[3,24,768]{2,1,0:T(8,128)(2,1)}, bf16[3,24,768]{2,1,0:T(8,128)(2,1)}, u32[]{:S(2)}, u32[]{:S(2)}) collective-permute-start(bf16[3,24,768]{2,1,0:T(8,128)(2,1)} %fusion.36), channel_id=1, source_target_pairs={{0,2},{1,3},{2,0},{3,1},{4,6},{5,7},{6,4},{7,5},{8,10},{9,11},{10,... | collective-permute-start | bytes 331784 | tf_op jit(solution)/shard_map/ppermute | solution.py:508
  305.4 17.2 %collective-permute-start.49 = (bf16[3,24,768]{2,1,0:T(8,128)(2,1)S(1)}, bf16[3,24,768]{2,1,0:T(8,128)(2,1)S(1)}, u32[]{:S(2)}, u32[]{:S(2)}) collective-permute-start(bf16[3,24,768]{2,1,0:T(8,128)(2,1)S(1)} %fusion.38), channel_id=1, source_target_pairs={{0,16},{4,20},{8,24},{12,28},{16,0},{20,4},{24,8},{28,12},{1,17},{... | collective-permute-start | bytes 331784 | tf_op jit(solution)/shard_map/ppermute | solution.py:508
  305.8 16.7 %collective-permute-start.50 = (bf16[24,2304]{1,0:T(8,128)(2,1)S(1)}, bf16[24,2304]{1,0:T(8,128)(2,1)S(1)}, u32[]{:S(2)}, u32[]{:S(2)}) collective-permute-start(bf16[24,2304]{1,0:T(8,128)(2,1)S(1)} %fusion.37), channel_id=1, source_target_pairs={{0,16},{4,20},{8,24},{12,28},{16,0},{20,4},{24,8},{28,12},{1,17},{... | collective-permute-start | bytes 331784 | tf_op jit(solution)/shard_map/ppermute | solution.py:508
  319.8 16.2 %collective-permute-start.41 = (bf16[2,2,256,768]{3,2,1,0:T(8,128)(2,1)}, bf16[2,2,256,768]{3,2,1,0:T(8,128)(2,1)}, u32[]{:S(2)}, u32[]{:S(2)}) collective-permute-start(bf16[2,2,256,768]{3,2,1,0:T(8,128)(2,1)} %get-tuple-element.282), channel_id=1, source_target_pairs={{0,1},{1,0},{2,3},{3,2},{4,5},{5,4},{6,7},{7,6},{8,9},{9,8},{10,11... | collective-permute-start | bytes 4718600 | tf_op jit(solution)/shard_map/ppermute | solution.py:508
  321.9 14.1 %collective-permute-start.40 = (bf16[2,2,4,24,588]{4,3,2,1,0:T(8,128)(2,1)}, bf16[2,2,4,24,588]{4,3,2,1,0:T(8,128)(2,1)}, u32[]{:S(2)}, u32[]{:S(2)}) collective-permute-start(bf16[2,2,4,24,588]{4,3,2,1,0:T(8,128)(2,1)} %fusion.24), channel_id=1, source_target_pairs={{0,4},{4,0},{8,12},{12,8},{16,20},{20,16},{24,28},{28,24},{1,5},{5... | collective-permute-start | bytes 1354760 | tf_op jit(solution)/shard_map/ppermute | solution.py:508
  338.0 19.7 %collective-permute-start.45 = (bf16[2,256,768]{2,1,0:T(8,128)(2,1)S(1)}, bf16[2,256,768]{2,1,0:T(8,128)(2,1)S(1)}, u32[]{:S(2)}, u32[]{:S(2)}) collective-permute-start(bf16[2,256,768]{2,1,0:T(8,128)(2,1)S(1)} %fusion.23), channel_id=1, source_target_pairs={{0,2},{1,3},{2,0},{3,1},{4,6},{5,7},{6,4},{7,5},{8,10},{9,11},{10,... | collective-permute-start | bytes 2359304 | tf_op jit(solution)/shard_map/ppermute | solution.py:508
  342.4 5.8 %collective-permute-start.42 = (bf16[4,24,588]{2,1,0:T(8,128)(2,1)S(1)}, bf16[4,24,588]{2,1,0:T(8,128)(2,1)S(1)}, u32[]{:S(2)}, u32[]{:S(2)}) collective-permute-start(bf16[4,24,588]{2,1,0:T(8,128)(2,1)S(1)} %get-tuple-element.339), channel_id=1, source_target_pairs={{0,8},{4,12},{8,0},{12,4},{16,24},{20,28},{24,16},{28,20},{1,9},{5... | collective-permute-start | bytes 338696 | tf_op jit(solution)/shard_map/ppermute | solution.py:508
  344.3 11.7 %collective-permute-start.43 = (bf16[4,24,588]{2,1,0:T(8,128)(2,1)S(1)}, bf16[4,24,588]{2,1,0:T(8,128)(2,1)S(1)}, u32[]{:S(2)}, u32[]{:S(2)}) collective-permute-start(bf16[4,24,588]{2,1,0:T(8,128)(2,1)S(1)} %get-tuple-element.338), channel_id=1, source_target_pairs={{0,16},{4,20},{8,24},{12,28},{16,0},{20,4},{24,8},{28,12},{1,17},{... | collective-permute-start | bytes 338696 | tf_op jit(solution)/shard_map/ppermute | solution.py:508
  344.3 11.7 %collective-permute-start.44 = (bf16[4,24,588]{2,1,0:T(8,128)(2,1)S(1)}, bf16[4,24,588]{2,1,0:T(8,128)(2,1)S(1)}, u32[]{:S(2)}, u32[]{:S(2)}) collective-permute-start(bf16[4,24,588]{2,1,0:T(8,128)(2,1)S(1)} %get-tuple-element.337), channel_id=1, source_target_pairs={{0,24},{4,28},{8,16},{12,20},{16,8},{20,12},{24,0},{28,4},{1,25},{... | collective-permute-start | bytes 338696 | tf_op jit(solution)/shard_map/ppermute | solution.py:508
  346.8 13.1 %copy-start.30 = (f32[768]{0:T(1024)S(1)}, f32[768]{0:T(1024)}, u32[]{:S(2)}) copy-start(f32[768]{0:T(1024)} %get-tuple-element.340) | copy-start | bytes 9220
  357.8 7.0 %collective-permute-start.46 = (bf16[24,588]{1,0:T(8,128)(2,1)S(1)}, bf16[24,588]{1,0:T(8,128)(2,1)S(1)}, u32[]{:S(2)}, u32[]{:S(2)}) collective-permute-start(bf16[24,588]{1,0:T(8,128)(2,1)S(1)} %get-tuple-element.292), channel_id=1, source_target_pairs={{0,1},{1,0},{2,3},{3,2},{4,5},{5,4},{6,7},{7,6},{8,9},{9,8},{10,11... | collective-permute-start | bytes 84680 | tf_op jit(solution)/shard_map/ppermute | solution.py:508
  357.9 6.9 %collective-permute-start.47 = (bf16[24,588]{1,0:T(8,128)(2,1)S(1)}, bf16[24,588]{1,0:T(8,128)(2,1)S(1)}, u32[]{:S(2)}, u32[]{:S(2)}) collective-permute-start(bf16[24,588]{1,0:T(8,128)(2,1)S(1)} %get-tuple-element.293), channel_id=1, source_target_pairs={{0,2},{1,3},{2,0},{3,1},{4,6},{5,7},{6,4},{7,5},{8,10},{9,11},{10,... | collective-permute-start | bytes 84680 | tf_op jit(solution)/shard_map/ppermute | solution.py:508
  358.3 6.6 %collective-permute-start.48 = (bf16[24,588]{1,0:T(8,128)(2,1)S(1)}, bf16[24,588]{1,0:T(8,128)(2,1)S(1)}, u32[]{:S(2)}, u32[]{:S(2)}) collective-permute-start(bf16[24,588]{1,0:T(8,128)(2,1)S(1)} %get-tuple-element.294), channel_id=1, source_target_pairs={{0,3},{1,2},{2,1},{3,0},{4,7},{5,6},{6,5},{7,4},{8,11},{9,10},{10,... | collective-permute-start | bytes 84680 | tf_op jit(solution)/shard_map/ppermute | solution.py:508
  (38 other events, 107.8 us)
Sparse Core Ops, SparseCore 0:
  24.1 94.4 all-gather.1

commit v6 on v5

--- a/solution.py
+++ b/solution.py
@@ -58,10 +58,11 @@
 
 
 def project_kernel(n_blk, *refs):
-    tokens, (params_ref, weight_ref, bias_ref, joint_ref) = refs[:n_blk], refs[n_blk:]
+    tokens, (params_ref, weight_ref, bias_ref, joint_ref, normed_ref) = refs[:n_blk], refs[n_blk:]
     for place in range(n_blk):
         plain, _ = norm_parts(tokens[place][0].astype(F32))
         normed = (plain * params_ref[0:1, :] + params_ref[1:2, :]).astype(BF16)
+        normed_ref[place, 0] = normed
         joint = dot(normed, weight_ref[...], ((1,), (0,))) + bias_ref[...]
         joint_ref[place, 0] = joint.astype(BF16)
 
@@ -79,8 +80,8 @@
             pl.BlockSpec(weight.shape, lambda s: (0, 0)),
             pl.BlockSpec(bias.shape, lambda s: (0, 0)),
         ],
-        out_specs=pl.BlockSpec((n_blk, 1, blk, cols), lambda s: (0, s, 0, 0)),
-        out_shape=jax.ShapeDtypeStruct((n_blk, seqs, blk, cols), BF16),
+        out_specs=[pl.BlockSpec((n_blk, 1, blk, size), lambda s: (0, s, 0, 0)) for size in (cols, width)],
+        out_shape=[jax.ShapeDtypeStruct((n_blk, seqs, blk, size), BF16) for size in (cols, width)],
         compiler_params=pltpu.CompilerParams(vmem_limit_bytes=VMEM_BYTES),
         cost_estimate=COST,
         name="project",
@@ -402,69 +403,178 @@
     )(me, joint, *grads, start, logs)
 
 
-def unproject_kernel(n_blk, me_ref, *refs):
-    grad_ref, tokens = refs[0], refs[1 : 1 + n_blk]
-    params_ref, weight_ref, earlier_ref, kept_ref, sent_ref, terms_ref = refs[1 + n_blk :]
-    cols = grad_ref.shape[-1]
+def unproject_kernel(n_blk, last, me_ref, grad_ref, normed_ref, params_ref, weight_ref, earlier_ref, earlier_bias_ref, *outs):
+    kept_ref, sent_ref, terms_ref, bias_ref = outs
+    blk, cols = grad_ref.shape[2:]
     group = cols // 3
-    vectors = params_ref.shape[0]
-    width = params_ref.shape[1]
-    weight_grad = bias_grad = gain_sum = shift_sum = 0.0
+    vectors, width = params_ref.shape
+    grad = grad_ref[...].reshape(n_blk * blk, cols)
+    share = dot(grad, weight_ref[...], ((1,), (1,))).astype(BF16)
     for place in range(n_blk):
-        grad = grad_ref[place, 0]
-        plain, _ = norm_parts(tokens[place][0].astype(F32))
-        normed = (plain * params_ref[0:1, :] + params_ref[1:2, :]).astype(BF16)
-        share = dot(grad, weight_ref[...], ((1,), (1,)))
-        (sent_ref if place % 2 else kept_ref)[place // 2, 0] = share.astype(BF16)
-        gain_sum += column_sum(share * plain)
-        shift_sum += column_sum(share)
-        bias_grad += column_sum(grad.astype(F32))
-        weight_grad += dot(normed, grad, ((0,), (0,)))
-
-    def placed(values):
-        return jnp.concatenate([jnp.where(me_ref[0] == j, values, 0.0) for j in range(n_blk)], axis=1)
-
-    table = jnp.concatenate(
-        [gain_sum, shift_sum, placed(bias_grad[:, :group]), placed(bias_grad[:, 2 * group :])]
-        + [jnp.zeros((vectors - 4, width), F32)],
-        axis=0,
-    ).T
+        (sent_ref if place % 2 else kept_ref)[place // 2, 0] = share[place * blk : (place + 1) * blk]
+    weight_grad = dot(normed_ref[...].reshape(n_blk * blk, width), grad, ((0,), (0,)))
+    bias_grad = column_sum(grad.astype(F32))
 
     @pl.when(pl.program_id(0) == 0)
     def _():
         terms_ref[:, :cols] = weight_grad + earlier_ref[:, :cols]
-        terms_ref[:, cols:] = table + earlier_ref[:, cols:]
+        terms_ref[:, cols:] = earlier_ref[:, cols:]
+        bias_ref[...] = bias_grad + earlier_bias_ref[...]
 
     @pl.when(pl.program_id(0) > 0)
     def _():
         terms_ref[:, :cols] += weight_grad
-        terms_ref[:, cols:] += table
-
-
-def unproject(me, grad, tokens, params, weight, earlier):
+        bias_ref[...] += bias_grad
+
+    if not last:
+        return
+
+    @pl.when(pl.program_id(0) == pl.num_programs(0) - 1)
+    def _():
+        weight = weight_ref[...].astype(F32)
+        bias = bias_ref[...]
+        columns = params_ref[...].T
+        shift_sum = jnp.sum(weight * bias, axis=1, keepdims=True)
+        gain_sum = jnp.sum(weight * terms_ref[:, :cols], axis=1, keepdims=True)
+        gain_sum = (gain_sum - columns[:, 1:2] * shift_sum) / columns[:, 0:1]
+
+        def placed(values):
+            return jnp.concatenate([jnp.where(me_ref[0] == j, values, 0.0) for j in range(n_blk)], axis=1)
+
+        table = jnp.concatenate(
+            [placed(bias[:, :group]), placed(bias[:, 2 * group :]), jnp.zeros((vectors - 4, width), F32)], axis=0
+        ).T
+        terms_ref[:, cols:] += jnp.concatenate([gain_sum, shift_sum, table], axis=1)
+
+
+def unproject(me, grad, normed, params, weight, earlier, bias, last):
     n_blk, count, blk, cols = grad.shape
-    width = tokens[0].shape[-1]
+    width = normed.shape[-1]
 
     def whole(shape):
         return pl.BlockSpec(shape, lambda s, m: (0, 0))
 
-    part = pl.BlockSpec((n_blk // 2, 1, blk, width), lambda s, m: (0, s, 0, 0))
+    def by_seq(parts, size):
+        return pl.BlockSpec((parts, 1, blk, size), lambda s, m: (0, s, 0, 0))
+
     return pl.pallas_call(
-        functools.partial(unproject_kernel, n_blk),
+        functools.partial(unproject_kernel, n_blk, last),
         grid_spec=pltpu.PrefetchScalarGridSpec(
             num_scalar_prefetch=1,
             grid=(count,),
-            in_specs=[pl.BlockSpec((n_blk, 1, blk, cols), lambda s, m: (0, s, 0, 0))]
-            + [pl.BlockSpec((1, blk, width), lambda s, m: (s, 0, 0))] * n_blk
-            + [whole(params.shape), whole(weight.shape), whole(earlier.shape)],
-            out_specs=[part, part, whole(earlier.shape)],
+            in_specs=[by_seq(n_blk, cols), by_seq(n_blk, width)]
+            + [whole(params.shape), whole(weight.shape), whole(earlier.shape), whole(bias.shape)],
+            out_specs=[by_seq(n_blk // 2, width)] * 2 + [whole(earlier.shape), whole(bias.shape)],
         ),
         out_shape=[jax.ShapeDtypeStruct((n_blk // 2, count, blk, width), BF16)] * 2
-        + [jax.ShapeDtypeStruct(earlier.shape, F32)],
+        + [jax.ShapeDtypeStruct(earlier.shape, F32), jax.ShapeDtypeStruct(bias.shape, F32)],
         compiler_params=pltpu.CompilerParams(vmem_limit_bytes=VMEM_BYTES),
         cost_estimate=COST,
         name="unproject",
-    )(me, grad, *tokens, params, weight, earlier)
+    )(me, grad, normed, params, weight, earlier, bias)
+
+
+def weigh_kernel(n_ctx, last, me_ref, act_ref, pre_ref, normed_ref, up_ref, branch_ref, *refs):
+    mixed_refs, outs, total = refs[:n_ctx], refs[n_ctx : n_ctx + 6], refs[-1]
+    step = pl.program_id(0)
+    me = me_ref[0]
+    core = lax.bitwise_and(me, 1)
+    per_group = total.shape[0] // n_ctx
+
+    @pl.when((step < last) | (step == 2 * last))
+    def _():
+        total[...] = dot(act_ref[...], up_ref[...], ((1,), (0,))).reshape(total.shape)
+
+    @pl.when(((step >= last) & (step < 2 * last)) | (step == 2 * last + 1))
+    def _():
+        total[...] = dot(normed_ref[...], pre_ref[...], ((1,), (0,))).reshape(total.shape)
+
+    @pl.when(step == 2 * last + 2)
+    def _():
+        for place in range(n_ctx):
+            value = dot(mixed_refs[place][...], branch_ref[...], ((0,), (0,)))
+            total[pl.ds(lax.bitwise_xor(me, place) * per_group, per_group)] = value.reshape(
+                (per_group,) + total.shape[1:]
+            )
+
+    bounds = (0, last, 2 * last, 2 * last + 3)
+    for number in range(3):
+        keep_ref, send_ref = outs[2 * number : 2 * number + 2]
+
+        @pl.when((step >= bounds[number]) & (step < bounds[number + 1]))
+        def _():
+            keep_ref[0] = total[:, core]
+            send_ref[0] = total[:, 1 - core].astype(BF16)
+
+
+def weigh(me, activated, grad_pre, normed, upstream, branch, mixed, part):
+    hidden, rows = activated.shape
+    width = normed.shape[0]
+    n_ctx = len(mixed)
+    last = hidden // width - 1
+    pairs = width // (2 * part)
+
+    def whole(shape):
+        return pl.BlockSpec(shape, lambda s, m: (0, 0), pipeline_mode=pl.Buffered(1))
+
+    def units(count, begin):
+        return pl.BlockSpec(
+            (1, pairs, part, width), lambda s, m: (jnp.clip(s - begin, 0, count - 1), 0, 0, 0)
+        )
+
+    counts = ((last, 0), (last, last), (3, 2 * last))
+    return pl.pallas_call(
+        functools.partial(weigh_kernel, n_ctx, last),
+        grid_spec=pltpu.PrefetchScalarGridSpec(
+            num_scalar_prefetch=1,
+            grid=(2 * last + 3,),
+            in_specs=[
+                pl.BlockSpec((width, rows), lambda s, m: (jnp.where(s < 2 * last, jnp.minimum(s, last - 1), last), 0)),
+                pl.BlockSpec((rows, width), lambda s, m: (0, jnp.clip(s - last, 0, last))),
+                whole(normed.shape),
+                whole(upstream.shape),
+                whole(branch.shape),
+            ]
+            + [whole(item.shape) for item in mixed],
+            out_specs=[units(*item) for item in counts for _ in range(2)],
+            scratch_shapes=[pltpu.VMEM((pairs, 2, part, width), F32)],
+        ),
+        out_shape=[
+            jax.ShapeDtypeStruct((count, pairs, part, width), dtype) for count, _ in counts for dtype in (F32, BF16)
+        ],
+        compiler_params=pltpu.CompilerParams(vmem_limit_bytes=VMEM_BYTES),
+        cost_estimate=COST,
+        name="weigh",
+    )(me, activated, grad_pre, normed, upstream, branch, *mixed)
+
+
+def update_kernel(n_dev, *refs):
+    sums = [refs[c][...] + refs[3 + c][...].astype(F32) for c in range(3)]
+    states, outs = refs[6:15], refs[15:]
+    spans = sums[0].shape[0] + 1
+    part = sums[0].shape[1]
+    shrink = jnp.concatenate([sums[0][i] for i in range(spans - 1)] + [sums[2][0]], axis=0)
+    units = [sums[1][i] for i in range(spans - 1)] + [sums[2][1]]
+    expand = jnp.concatenate(
+        [units[span][:, place * part : (place + 1) * part] for place in range(n_dev) for span in range(spans)], axis=1
+    )
+    for number, gradient in enumerate((sums[2][2], expand, shrink)):
+        weight, first, second = [ref[...] for ref in states[3 * number : 3 * number + 3]]
+        results = adam_step(weight, gradient, first, second, RATE_MATRIX, WEIGHT_DECAY)
+        for out, result in zip(outs[3 * number : 3 * number + 3], results):
+            out[...] = result
+
+
+def update(keeps, gots, states, n_dev):
+    vmem = pl.BlockSpec(memory_space=pltpu.VMEM)
+    return pl.pallas_call(
+        functools.partial(update_kernel, n_dev),
+        in_specs=[vmem] * 15,
+        out_specs=[vmem] * 9,
+        out_shape=[jax.ShapeDtypeStruct(item.shape, F32) for item in states],
+        compiler_params=pltpu.CompilerParams(vmem_limit_bytes=VMEM_BYTES),
+        name="update",
+    )(*keeps, *gots, *states)
 
 
 def finish_kernel(n_ctx, me_ref, *refs):
@@ -592,29 +702,35 @@
 
         half = max(seqs // 2, 1)
         firsts = list(range(0, seqs, half))
-        tokens = [{0: tokens_in[first : first + half]} for first in firsts]
         near, far_bits = 1, [bit for bit in reversed(ctx_bits) if bit]
 
         def fetch_far(blocks):
             for bit in far_bits:
                 blocks.update({k ^ (1 << bit): swap(value, "ctx", 1 << bit) for k, value in list(blocks.items())})
 
-        fetch_far(tokens[0])
-        names = sorted(tokens[0])
+        names = range(0, n_ctx, 2)
+        ahead = {0: tokens_in[:1]}
+        fetch_far(ahead)
         pieces, start, later, held = lax.optimization_barrier(
-            (pieces, start, [blocks[0] for blocks in tokens[1:]], [tokens[0][k] for k in names])
-        )
-        tokens[0] = dict(zip(names, held))
-        for blocks, value in zip(tokens[1:], later):
-            blocks[0] = value
-            fetch_far(blocks)
+            (pieces, start, [tokens_in[1:half], tokens_in[half:]], [ahead[k] for k in names])
+        )
+        others = [{0: later[0]}, {0: later[1]}]
+        for blocks in others:
+            if blocks[0].shape[0]:
+                fetch_far(blocks)
+        first_half = {k: item for k, item in zip(names, held)}
+        if half > 1:
+            first_half = {k: jnp.concatenate([first_half[k], others[0][k]], axis=0) for k in names}
+        tokens = [first_half, others[1]]
+        for blocks, first in zip(tokens, firsts):
+            blocks[0] = tokens_in[first : first + half]
         gathered = jnp.stack(reorder(pieces, me))
         for step, bit in enumerate(reversed(dp_bits)):
             other = swap(gathered, "dp", 1 << bit)
             upper = ((me_dp >> bit) & 1) == 1
             gathered = jnp.where(upper, jnp.stack([other, gathered]), jnp.stack([gathered, other]))
             if step == max(n_bits - 2, 0):
-                flat = [(number, k) for number, blocks in enumerate(tokens) for k in sorted(blocks)]
+                flat = [(number, k) for number, blocks in enumerate(tokens) for k in sorted(blocks) if k]
                 gathered, *held = lax.optimization_barrier((gathered,) + tuple(tokens[n][k] for n, k in flat))
                 for (number, k), value in zip(flat, held):
                     tokens[number][k] = value
@@ -631,10 +747,11 @@
         bias_hidden = params[7 : 7 + spans].reshape(n_dev, spans, part).transpose(1, 0, 2).reshape(spans, width)
         params = jnp.concatenate([params[:7], bias_hidden, params[7 + spans :]], axis=0)
 
-        joints, logs, mixed, waiting = [], [], [], None
+        joints, normeds, logs, mixed, waiting = [], [], [], [], None
         starts = [start[first : first + half] for first in firsts]
         for number in range(len(firsts)):
-            joint = project(tokens[number], params, joint_lo, joint_bias)
+            joint, normed = project(tokens[number], params, joint_lo, joint_bias)
+            normeds.append(normed)
             if waiting is not None:
                 waiting, joint = lax.optimization_barrier((waiting, joint))
                 waiting = [waiting[0]] + [swap(waiting[k], "ctx", k) for k in range(1, n_ctx)]
@@ -664,26 +781,27 @@
         bit_dims = (2,) * len(labels)
         core, far = [("ctx", ctx_bits[0])], [("ctx", bit) for bit in ctx_bits[1:]]
         low, high = [("dp", dp_bits[0])], [("dp", bit) for bit in dp_bits[1:]]
-        cut = (spans - 1) * width
-        grad_shrink = dot(activated[:cut], upstream, ((1,), (0,))).reshape((spans - 1,) + bit_dims + (part, width))
-        grad_expand = dot(normed_two, grad_pre[:, :cut], ((1,), (0,))).reshape(bit_dims + (part, cut))
-        grad_output = [dot(item.reshape(rows, group), branch, ((0,), (0,))) for item in mixed]
-        grad_output = jnp.concatenate(reorder(grad_output, me), axis=0)
-        grad_last = jnp.stack(
-            [
-                dot(activated[cut:], upstream, ((1,), (0,))),
-                dot(normed_two, grad_pre[:, cut:], ((1,), (0,))),
-                grad_output,
+        mixed = [item.reshape(rows, group) for item in mixed]
+        orders = [core + low + high + far, core + far + low + high, core + high[:1] + far + low + high[1:]]
+        if part % 8 == 0:
+            halves = weigh(me_arr, activated, grad_pre, normed_two, upstream, branch, mixed, part)
+            halves, grads = lax.optimization_barrier((halves, grads))
+            names = ["unit"] + [label for label in labels if label not in core]
+            halves = [item.reshape(item.shape[:1] + bit_dims[1:] + (part, width)) for item in halves]
+            chains = [[halves[2 * c], halves[2 * c + 1], names, orders[c]] for c in range(3)]
+        else:
+            grad_shrink = dot(activated, upstream, ((1,), (0,))).reshape(spans, width, width)
+            grad_expand = dot(normed_two, grad_pre, ((1,), (0,))).reshape(width, spans, width).transpose(1, 0, 2)
+            grad_output = jnp.concatenate(reorder([dot(item, branch, ((0,), (0,))) for item in mixed], me), axis=0)
+            units = [
+                grad_shrink[:-1],
+                grad_expand[:-1],
+                jnp.stack([grad_shrink[-1], grad_expand[-1], grad_output]),
             ]
-        ).reshape((3,) + bit_dims + (part, width))
-        grad_shrink, grad_expand, grad_last, grads = lax.optimization_barrier(
-            (grad_shrink, grad_expand, grad_last, grads)
-        )
-        chains = [
-            [grad_shrink, None, ["unit"] + labels, core + low + high + far],
-            [grad_expand, None, labels, core + far + low + high],
-            [grad_last, None, ["unit"] + labels, core + high[:1] + far + low + high[1:]],
-        ]
+            chains = [
+                [item.reshape(item.shape[:1] + bit_dims + (part, width)), None, ["unit"] + labels, order]
+                for item, order in zip(units, orders)
+            ]
 
         def split(chain):
             value, _, names, order = chain
@@ -720,13 +838,15 @@
                 chain[0], chain[1] = keep, send
             return after, before
 
-        for chain in chains:
-            split(chain)
+        if part % 8:
+            for chain in chains:
+                split(chain)
 
         sums_hidden = sums[3 : 3 + spans].reshape(spans, n_dev, part).transpose(1, 0, 2).reshape(spans, width)
         table = jnp.concatenate([jnp.zeros((4, width), F32), sums[:3], sums_hidden, sums[3 + spans :]], axis=0)
         terms = jnp.concatenate([jnp.zeros((width, cols), F32), table.T], axis=1)
         pending, shares = None, []
+        bias_sums = jnp.zeros((1, cols), F32)
         for number, first in enumerate(firsts):
             _, (source, pending) = advance(terms if number else branch, (joints[number], pending))
             grad_joint = attend_backward(me_arr, source, grads, starts[number], logs[number], first)
@@ -735,7 +855,9 @@
             (grad_joint, pending), _ = advance((grad_joint, pending), start)
             if pending:
                 shares.append(sum((value.astype(F32) for value in pending[1]), pending[0]))
-            kept, sent, terms = unproject(me_arr, grad_joint, tokens[number], params, joint_lo, terms)
+            kept, sent, terms, bias_sums = unproject(
+                me_arr, grad_joint, normeds[number], params, joint_lo, terms, bias_sums, number == len(firsts) - 1
+            )
             if number < len(firsts) - 1:
                 joined = kept.astype(F32) + swap(sent, "ctx", 1).astype(F32)
                 pending = [joined[0], [joined[1 << (bit - 1)].astype(BF16) for bit in ctx_bits[1:]]]
@@ -779,25 +901,31 @@
         plain, scale = norm_parts(tokens_in.astype(F32))
         input_grad = grad_resid + norm_back(plain, scale, jnp.concatenate(shares, axis=0), params[0])
 
-        for chain in chains:
-            merge(chain, fetch(chain))
-            while chain[3]:
+        while len(chains[0][3]) > 1:
+            for chain in chains:
+                merge(chain, fetch(chain))
                 split(chain)
+        states = (
+            (output_weight, momentum_output, variance_output)
+            + (expand_weight, momentum_expand, variance_expand)
+            + (shrink_weight, momentum_shrink, variance_shrink)
+        )
+        if part % 8 == 0:
+            updated = update([chain[0] for chain in chains], [fetch(chain) for chain in chains], states, n_dev)
+        else:
+            for chain in chains:
                 merge(chain, fetch(chain))
-        last_shrink, last_expand, sum_output = chains[2][0]
-        sum_shrink = jnp.concatenate([chains[0][0].reshape(cut // n_dev, width), last_shrink], axis=0)
-        sum_expand = jnp.concatenate([chains[1][0], last_expand], axis=1)
-        sum_expand = sum_expand.reshape(part, spans, n_dev, part).transpose(0, 2, 1, 3).reshape(part, hidden)
-
-        new_output, first_output, second_output = adam_step(
-            output_weight, sum_output, momentum_output, variance_output, RATE_MATRIX, WEIGHT_DECAY
-        )
-        new_expand, first_expand, second_expand = adam_step(
-            expand_weight, sum_expand, momentum_expand, variance_expand, RATE_MATRIX, WEIGHT_DECAY
-        )
-        new_shrink, first_shrink, second_shrink = adam_step(
-            shrink_weight, sum_shrink, momentum_shrink, variance_shrink, RATE_MATRIX, WEIGHT_DECAY
-        )
+            last_shrink, last_expand, sum_output = chains[2][0]
+            sum_shrink = jnp.concatenate([*chains[0][0], last_shrink], axis=0)
+            sum_expand = jnp.stack([*chains[1][0], last_expand], axis=1)
+            sum_expand = sum_expand.reshape(part, spans, n_dev, part).transpose(0, 2, 1, 3).reshape(part, hidden)
+            updated = []
+            for number, gradient in enumerate((sum_output, sum_expand, sum_shrink)):
+                weight, first, second = states[3 * number : 3 * number + 3]
+                updated += adam_step(weight, gradient, first, second, RATE_MATRIX, WEIGHT_DECAY)
+        new_output, first_output, second_output = updated[:3]
+        new_expand, first_expand, second_expand = updated[3:6]
+        new_shrink, first_shrink, second_shrink = updated[6:]
         return (
             block_output,
             input_grad,

time: 382 us -> 383 us (level)
  Pallas kernels: 144 us -> 170 us
  matrix products: 16.5 us -> 0 us
  local copies, waits for them, and re-layouts: 50.8 us -> 39.7 us
  starting transfers between devices: 40.5 us -> 46.9 us
  waiting for transfers between devices: 76.9 us -> 71.6 us
    pallas_call x2 -> x4, Pallas kernels: 23.1 us -> 48.5 us  [the longest x2 22.5 us: unproject(): pl.pallas_call(functools.partial(unproject_kernel, n_blk, last), grid_spe...]
    dot_general x8 -> x0, matrix products: 16.5 us -> none  [dot(): lax.dot_general(left, right, (dims, ((), ())), preferred_element_type=F32)]
    ppermute x52 -> x53, starting transfers between devices: 40.4 us -> 46.9 us  [swap(): lax.ppermute(value, axis, [(place, place ^ mask) for place in range(sizes...]
    ppermute x52 -> x53, waiting for transfers between devices: 76.8 us -> 71.6 us  [swap(): lax.ppermute(value, axis, [(place, place ^ mask) for place in range(sizes...]
    sub x3 -> x0, other arithmetic: 5.08 us -> none  [adam_step(): weight - rate * (first_hat / (jnp.sqrt(second_hat) + ADAM_EPSILON) + deca...]
    convert_element_type x16 -> x13, local copies, waits for them, and re-layouts: 9.66 us -> 6.01 us  [split(): lax.dynamic_index_in_dim(value, 1 - mine, pos, keepdims=False).astype(BF16)]
    add x16 -> x13, other arithmetic: 12.4 us -> 15.7 us  [merge(): chain[0] = chain[0] + got.astype(F32)]
    unnamed x105 -> x89, local copies, waits for them, and re-layouts: 10.1 us -> 8.16 us
  transfers between devices with their start and end apart: 53 -> 54, of which waited for: 16 -> 16; matrix products, arithmetic and copies ran while one was open for 19% -> 11% of each run, Pallas kernels for 27% -> 31%
where the time goes in v6:
time: 383 us; the launch traced here: 375 us
  Pallas kernels  170 us (44%)
  waiting for transfers between devices  71.6 us (19%)
  starting transfers between devices  46.9 us (12%)
  local copies, waits for them, and re-layouts  39.7 us (10%)
  other arithmetic  31.3 us (8%)
  between operations  15.8 us (4%)
    ppermute x53, waiting for transfers between devices, swap(): lax.ppermute(value, axis, [(place, place ^ mask) for place in range(sizes...  71.6 us
    ppermute x53, starting transfers between devices, swap(): lax.ppermute(value, axis, [(place, place ^ mask) for place in range(sizes...  46.9 us
    pallas_call x1, Pallas kernels, layer(): pl.pallas_call(functools.partial(layer_kernel, n_ctx, spans), grid_spec=p...  39.8 us
    pallas_call x2, Pallas kernels, attend_backward(): pl.pallas_call(functools.partial(backward_kernel, n_blk, blk, heads), gri...  37.7 us
    pallas_call x2, Pallas kernels, attend_forward(): pl.pallas_call(functools.partial(forward_kernel, n_blk, blk, heads), grid...  27.2 us
    pallas_call x2, Pallas kernels, unproject(): pl.pallas_call(functools.partial(unproject_kernel, n_blk, last), grid_spe...  22.5 us
    pallas_call x1, Pallas kernels, weigh(): pl.pallas_call(functools.partial(weigh_kernel, n_ctx, last), grid_spec=pl...  22.4 us
    add x13, other arithmetic, merge(): chain[0] = chain[0] + got.astype(F32)  15.7 us
  transfers between devices with their start and end apart: 54, of which 16 were waited for; matrix products, arithmetic and copies ran while one was open for 11% of the time, Pallas kernels for 31%

profile of v6, /device:TPU:0, one launch (start us, length us, event | category | flops | bytes accessed | tf_op | source)
XLA Modules:
  0.0 375.4 jit_solution(2359521856541804582)
XLA Ops:
  7.2 3.0 collective-permute-start.5
  14.9 1.3 collective-permute-start.3
  18.2 1.2 reshape.462
  19.6 1.3 reshape.463
  25.9 8.1 %collective-permute-done.7 = bf16[1,256,768]{2,1,0:T(8,128)(2,1)S(1)} collective-permute-done((bf16[1,256,768]{2,1,0:T(8,128)(2,1)S(1)}, bf16[1,256,768]{2,1,0:T(8,128)(2,1)S(1)}, u32[]{:S(2)}, u32[]{:S(2)}) %collective-permute-start.7) | collective-permute-done | bytes 393248 | tf_op jit(solution)/shard_map/ppermute | solution.py:618
  35.3 2.8 collective-permute-start.8
  38.1 1.5 collective-permute-start.10
  39.6 8.4 %collective-permute-done.8 = bf16[4,24,588]{2,1,0:T(8,128)(2,1)S(1)} collective-permute-done((bf16[4,24,588]{2,1,0:T(8,128)(2,1)S(1)}, bf16[4,24,588]{2,1,0:T(8,128)(2,1)S(1)}, u32[]{:S(2)}, u32[]{:S(2)}) %collective-permute-start.8) | collective-permute-done | bytes 112928 | tf_op jit(solution)/shard_map/ppermute | solution.py:618
  48.9 6.6 %collective-permute-done.9 = bf16[2,4,24,588]{3,2,1,0:T(8,128)(2,1)S(1)} collective-permute-done((bf16[2,4,24,588]{3,2,1,0:T(8,128)(2,1)S(1)}, bf16[2,4,24,588]{3,2,1,0:T(8,128)(2,1)S(1)}, u32[]{:S(2)}, u32[]{:S(2)}) %collective-permute-start.9) | collective-permute-done | bytes 225824 | tf_op jit(solution)/shard_map/ppermute | solution.py:618
  55.6 13.3 %collective-permute-done.10 = bf16[1,256,768]{2,1,0:T(8,128)(2,1)S(1)} collective-permute-done((bf16[1,256,768]{2,1,0:T(8,128)(2,1)S(1)}, bf16[1,256,768]{2,1,0:T(8,128)(2,1)S(1)}, u32[]{:S(2)}, u32[]{:S(2)}) %collective-permute-start.10) | collective-permute-done | bytes 393248 | tf_op jit(solution)/shard_map/ppermute | solution.py:618
  69.0 1.6 collective-permute-start.13
  72.9 5.0 %collective-permute-done.13 = bf16[2,2,4,24,588]{4,3,2,1,0:T(8,128)(2,1)S(1)} collective-permute-done((bf16[2,2,4,24,588]{4,3,2,1,0:T(8,128)(2,1)S(1)}, bf16[2,2,4,24,588]{4,3,2,1,0:T(8,128)(2,1)S(1)}, u32[]{:S(2)}, u32[]{:S(2)}) %collective-permute-start.13) | collective-permute-done | bytes 451616 | tf_op jit(solution)/shard_map/ppermute | solution.py:618
  81.8 7.3 %project.2 = (bf16[4,2,256,576]{3,2,1,0:T(8,128)(2,1)}, bf16[4,2,256,768]{3,2,1,0:T(8,128)(2,1)}) custom-call(bf16[2,256,768]{2,1,0:T(8,128)(2,1)} %get-tuple-element.367.refs_0_, bf16[2,256,768]{2,1,0:T(8,128)(2,1)} %collective-permute-done.refs_1_, bf16[2,256,768]{2,1,0:T(8,128)(2,1)} %copy-done.16, bf16[2,256,768]{2,1,0:T(8,128)(2,1)} %collective-permute-done.12.refs_3_, ...), custom_call_target="tpu_custom_call" | custom-call | flops 20000000000 | bytes 1000000 | tf_op jit(solution)/shard_map/project/pallas_call | solution.py:74
  89.1 13.6 %attend_forward.2 = (bf16[2,256,192]{2,1,0:T(8,128)(2,1)}, bf16[2,256,192]{2,1,0:T(8,128)(2,1)}, bf16[2,256,192]{2,1,0:T(8,128)(2,1)}, bf16[2,256,192]{2,1,0:T(8,128)(2,1)}, f32[2,3,1024]{2,1,0:T(4,128)}) custom-call(s32[1]{0:T(128)} %bitcast.me_ref, bf16[4,2,256,576]{3,2,1,0:T(8,128)(2,1)} %get-tuple-element.263.joint_ref, ...), custom_call_target="tpu_custom_call" | custom-call | flops 20000000000 | bytes 1000000 | tf_op jit(solution)/shard_map/attend_forward/pallas_call | solution.py:152
  102.8 7.2 %project.3 = (bf16[4,2,256,576]{3,2,1,0:T(8,128)(2,1)}, bf16[4,2,256,768]{3,2,1,0:T(8,128)(2,1)}) custom-call(bf16[2,256,768]{2,1,0:T(8,128)(2,1)} %copy-done.17, bf16[2,256,768]{2,1,0:T(8,128)(2,1)} %collective-permute-done.14.refs_1_, bf16[2,256,768]{2,1,0:T(8,128)(2,1)} %collective-permute-done.11.refs_2_, ...), custom_call_target="tpu_custom_call" | custom-call | flops 20000000000 | bytes 1000000 | tf_op jit(solution)/shard_map/project/pallas_call | solution.py:74
  112.0 13.6 %attend_forward.3 = (bf16[2,256,192]{2,1,0:T(8,128)(2,1)}, bf16[2,256,192]{2,1,0:T(8,128)(2,1)}, bf16[2,256,192]{2,1,0:T(8,128)(2,1)}, bf16[2,256,192]{2,1,0:T(8,128)(2,1)}, f32[2,3,1024]{2,1,0:T(4,128)}) custom-call(s32[1]{0:T(128)} %bitcast.me_ref, bf16[4,2,256,576]{3,2,1,0:T(8,128)(2,1)} %get-tuple-element.299.joint_ref, ...), custom_call_target="tpu_custom_call" | custom-call | flops 20000000000 | bytes 1000000 | tf_op jit(solution)/shard_map/attend_forward/pallas_call | solution.py:152
  126.7 1.3 collective-permute-start.21
  129.1 5.5 %collective-permute-done.22 = bf16[2,256,192]{2,1,0:T(8,128)(2,1)S(1)} collective-permute-done((bf16[2,256,192]{2,1,0:T(8,128)(2,1)}, bf16[2,256,192]{2,1,0:T(8,128)(2,1)S(1)}, u32[]{:S(2)}, u32[]{:S(2)}) %collective-permute-start.22) | collective-permute-done | bytes 196640 | tf_op jit(solution)/shard_map/ppermute | solution.py:618
  134.7 5.9 %collective-permute-done.21 = bf16[2,256,192]{2,1,0:T(8,128)(2,1)S(1)} collective-permute-done((bf16[2,256,192]{2,1,0:T(8,128)(2,1)}, bf16[2,256,192]{2,1,0:T(8,128)(2,1)S(1)}, u32[]{:S(2)}, u32[]{:S(2)}) %collective-permute-start.21) | collective-permute-done | bytes 196640 | tf_op jit(solution)/shard_map/ppermute | solution.py:618
  141.6 39.8 %layer.1 = (bf16[4,256,768]{2,1,0:T(8,128)(2,1)}, f32[4,256,768]{2,1,0:T(8,128)}, bf16[4,256,768]{2,1,0:T(8,128)(2,1)}, bf16[768,1024]{1,0:T(8,128)(2,1)}, bf16[...) custom-call(s32[1]{0:T(128)} %bitcast.me_ref, ...), custom_call_target="tpu_custom_call" | custom-call | flops 20000000000 | bytes 1000000 | tf_op jit(solution)/shard_map/layer/pallas_call | solution.py:278
  182.3 1.0 collective-permute-start.26
  183.7 22.4 %weigh.1 = (f32[3,16,24,768]{3,2,1,0:T(8,128)}, bf16[3,16,24,768]{3,2,1,0:T(8,128)(2,1)}, f32[3,16,24,768]{3,2,1,0:T(8,128)}, bf16[3,16,24,768]{3,2,1,0:T(8,128)...) custom-call(s32[1]{0:T(128)} %bitcast.me_ref, bf16[3072,1024]{1,0:T(8,128)(2,1)} %get-tuple-element.238.act_ref, ...), custom_call_target="tpu_custom_call" | custom-call | flops 20000000000 | bytes 1000000 | tf_op jit(solution)/shard_map/weigh/pallas_call | solution.py:526
  206.8 1.8 copy.115
  208.9 1.4 copy.116
  210.7 1.4 copy.117
  214.5 2.5 concatenate.122.earlier_ref
  217.8 3.0 copy_add_fusion
  221.1 1.8 copy-done.5
  222.8 1.9 copy_add_fusion.1
  225.9 1.2 copy-done.4
  227.1 1.9 copy_add_fusion.2
  229.1 1.0 fusion.12
  230.1 1.6 collective-permute-start.30
  232.2 1.7 collective-permute-start.32
  233.9 19.0 %attend_backward.2.grad_ref = bf16[4,2,256,576]{3,2,1,0:T(8,128)(2,1)} custom-call(s32[1]{0:T(128)} %bitcast.me_ref, bf16[4,2,256,576]{3,2,1,0:T(8,128)(2,1)} %get-tuple-element.263.joint_ref, bf16[4,256,192]{2,1,0:T(8,128)(2,1)} %get-tuple-element.264.refs_0_, bf16[4,256,192]{2,1,0:T(8,128)(2,1)} %collective-permute-done.24.refs_1_, ...), custom_call_target="tpu_custom_call" | custom-call | flops 20000000000 | bytes 1000000 | tf_op jit(solution)/shard_map/attend_backward/pallas_call | solution.py:380
  253.5 1.3 convert_add_fusion.2
  256.7 1.3 convert_add_fusion.3
  259.8 1.3 convert_add_fusion.4
  263.0 1.7 collective-permute-start.34
  265.1 1.5 collective-permute-start.36
  267.2 10.4 %unproject.2 = (bf16[2,2,256,768]{3,2,1,0:T(8,128)(2,1)}, bf16[2,2,256,768]{3,2,1,0:T(8,128)(2,1)}, f32[768,588]{1,0:T(8,128)}, f32[1,576]{1,0:T(1,128)}) custom-call(s32[1]{0:T(128)} %bitcast.me_ref, bf16[4,2,256,576]{3,2,1,0:T(8,128)(2,1)} %attend_backward.2.grad_ref, bf16[4,2,256,768]{3,2,1,0:T(8,128)(2,1)} %get-tuple-element.276.normed_ref, ...), custom_call_target="tpu_custom_call" | custom-call | flops 20000000000 | bytes 1000000 | tf_op jit(solution)/shard_map/unproject/pallas_call | solution.py:460
  277.8 1.2 convert_add_fusion.6
  279.1 1.1 convert_add_fusion.7
  280.2 1.2 convert_add_fusion.8
  281.7 1.7 convert_add_fusion.1
  284.2 2.8 collective-permute-start.38
  287.3 1.6 collective-permute-start.40
  288.9 18.8 %attend_backward.3.grad_ref = bf16[4,2,256,576]{3,2,1,0:T(8,128)(2,1)} custom-call(s32[1]{0:T(128)} %bitcast.me_ref, bf16[4,2,256,576]{3,2,1,0:T(8,128)(2,1)} %get-tuple-element.299.joint_ref, bf16[4,256,192]{2,1,0:T(8,128)(2,1)} %get-tuple-element.264.refs_0_, bf16[4,256,192]{2,1,0:T(8,128)(2,1)} %collective-permute-done.24.refs_1_, ...), custom_call_target="tpu_custom_call" | custom-call | flops 20000000000 | bytes 1000000 | tf_op jit(solution)/shard_map/attend_backward/pallas_call | solution.py:380
  307.7 12.0 %unproject.3 = (bf16[2,2,256,768]{3,2,1,0:T(8,128)(2,1)}, bf16[2,2,256,768]{3,2,1,0:T(8,128)(2,1)}, f32[768,588]{1,0:T(8,128)}, f32[1,576]{1,0:T(1,128)}) custom-call(s32[1]{0:T(128)} %bitcast.me_ref, bf16[4,2,256,576]{3,2,1,0:T(8,128)(2,1)} %attend_backward.3.grad_ref, bf16[4,2,256,768]{3,2,1,0:T(8,128)(2,1)} %get-tuple-element.312.normed_ref, ...), custom_call_target="tpu_custom_call" | custom-call | flops 20000000000 | bytes 1000000 | tf_op jit(solution)/shard_map/unproject/pallas_call | solution.py:460
  319.9 1.3 fusion.17
  324.0 1.5 collective-permute-start.50
  325.7 2.7 collective-permute-start.52
  328.4 6.5 %collective-permute-done.41 = bf16[2,2,4,24,588]{4,3,2,1,0:T(8,128)(2,1)} collective-permute-done((bf16[2,2,4,24,588]{4,3,2,1,0:T(8,128)(2,1)S(1)}, bf16[2,2,4,24,588]{4,3,2,1,0:T(8,128)(2,1)}, u32[]{:S(2)}, u32[]{:S(2)}) %collective-permute-start.41) | collective-permute-done | bytes 451616 | tf_op jit(solution)/shard_map/ppermute | solution.py:618
  335.4 1.6 collective-permute-start.46
  338.5 3.7 update.1
  342.2 1.3 bitcast_add_fusion
  343.5 1.7 collective-permute-start.43
  345.4 2.6 collective-permute-start.45
  349.0 7.3 %collective-permute-done.44 = bf16[4,24,588]{2,1,0:T(8,128)(2,1)S(1)} collective-permute-done((bf16[4,24,588]{2,1,0:T(8,128)(2,1)S(1)}, bf16[4,24,588]{2,1,0:T(8,128)(2,1)S(1)}, u32[]{:S(2)}, u32[]{:S(2)}) %collective-permute-start.44) | collective-permute-done | bytes 112928 | tf_op jit(solution)/shard_map/ppermute | solution.py:618
  356.5 1.1 collective-permute-start.48
  358.4 1.3 fusion.10
  359.7 1.1 fusion.9
  361.6 2.3 fusion.7
  365.8 2.3 finish.1
  (276 shorter events, 51.4 us)
Async XLA Ops:
  7.2 11.0 %copy-start.21 = (f32[24,768]{1,0:T(8,128)S(1)}, f32[24,768]{1,0:T(8,128)}, u32[]{:S(2)}) copy-start(f32[24,768]{1,0:T(8,128)} %refs_6_.3) | copy-start | bytes 221188
  7.2 118.4 %all-gather.2.cloned.1.call-start = ((), (), s32[]{:S(2)}) async-start(), calls=%async_computation | async-start | bytes 5640192 | tf_op jit(solution)/shard_map/all_gather | solution.py:699
  7.2 14.8 %collective-permute-start.5 = (s32[4,256]{1,0:T(4,128)}, s32[4,256]{1,0:T(4,128)S(1)}, u32[]{:S(2)}, u32[]{:S(2)}) collective-permute-start(s32[4,256]{1,0:T(4,128)} %param.19), channel_id=1, source_target_pairs={{0,2},{1,3},{2,0},{3,1},{4,6},{5,7},{6,4},{7,5},{8,10},{9,11},{10,... | collective-permute-start | bytes 12296 | tf_op jit(solution)/shard_map/ppermute | solution.py:618
  10.2 12.7 %collective-permute-start.4 = (s32[4,256]{1,0:T(4,128)}, s32[4,256]{1,0:T(4,128)S(1)}, u32[]{:S(2)}, u32[]{:S(2)}) collective-permute-start(s32[4,256]{1,0:T(4,128)} %param.19), channel_id=1, source_target_pairs={{0,1},{1,0},{2,3},{3,2},{4,5},{5,4},{6,7},{7,6},{8,9},{9,8},{10,11... | collective-permute-start | bytes 12296 | tf_op jit(solution)/shard_map/ppermute | solution.py:618
  14.3 11.6 %collective-permute-start.1 = (bf16[24,588]{1,0:T(8,128)(2,1)}, bf16[24,588]{1,0:T(8,128)(2,1)}, u32[]{:S(2)}, u32[]{:S(2)}) collective-permute-start(bf16[24,588]{1,0:T(8,128)(2,1)} %get-tuple-element.400), channel_id=1, source_target_pairs={{0,1},{1,0},{2,3},{3,2},{4,5},{5,4},{6,7},{7,6},{8,9},{9,8},{10,11... | collective-permute-start | bytes 84680 | tf_op jit(solution)/shard_map/ppermute | solution.py:618
  14.8 11.1 %collective-permute-start.2 = (bf16[24,588]{1,0:T(8,128)(2,1)}, bf16[24,588]{1,0:T(8,128)(2,1)}, u32[]{:S(2)}, u32[]{:S(2)}) collective-permute-start(bf16[24,588]{1,0:T(8,128)(2,1)} %get-tuple-element.401), channel_id=1, source_target_pairs={{0,2},{1,3},{2,0},{3,1},{4,6},{5,7},{6,4},{7,5},{8,10},{9,11},{10,... | collective-permute-start | bytes 84680 | tf_op jit(solution)/shard_map/ppermute | solution.py:618
  14.9 11.0 %collective-permute-start.3 = (bf16[24,588]{1,0:T(8,128)(2,1)}, bf16[24,588]{1,0:T(8,128)(2,1)}, u32[]{:S(2)}, u32[]{:S(2)}) collective-permute-start(bf16[24,588]{1,0:T(8,128)(2,1)} %get-tuple-element.399), channel_id=1, source_target_pairs={{0,3},{1,2},{2,1},{3,0},{4,7},{5,6},{6,5},{7,4},{8,11},{9,10},{10,... | collective-permute-start | bytes 84680 | tf_op jit(solution)/shard_map/ppermute | solution.py:618
  22.1 48.5 %copy-start.17 = (bf16[2,256,768]{2,1,0:T(8,128)(2,1)}, bf16[2,256,768]{2,1,0:T(8,128)(2,1)S(1)}, u32[]{:S(2)}) copy-start(bf16[2,256,768]{2,1,0:T(8,128)(2,1)S(1)} %get-tuple-element.194.refs_0_) | copy-start | bytes 2359300
  22.1 1.6 collective-permute-start.6
  22.9 11.1 %collective-permute-start.7 = (bf16[1,256,768]{2,1,0:T(8,128)(2,1)S(1)}, bf16[1,256,768]{2,1,0:T(8,128)(2,1)S(1)}, u32[]{:S(2)}, u32[]{:S(2)}) collective-permute-start(bf16[1,256,768]{2,1,0:T(8,128)(2,1)S(1)} %get-tuple-element.364), channel_id=1, source_target_pairs={{0,2},{1,3},{2,0},{3,1},{4,6},{5,7},{6,4},{7,5},{8,10},{9,11},{10,... | collective-permute-start | bytes 1179656 | tf_op jit(solution)/shard_map/ppermute | solution.py:618
  23.7 1.4 collective-permute-start.19
  34.0 34.9 %collective-permute-start.11 = (bf16[2,256,768]{2,1,0:T(8,128)(2,1)S(1)}, bf16[2,256,768]{2,1,0:T(8,128)(2,1)}, u32[]{:S(2)}, u32[]{:S(2)}) collective-permute-start(bf16[2,256,768]{2,1,0:T(8,128)(2,1)S(1)} %get-tuple-element.194.refs_0_), channel_id=1, source_target_pairs={{0,2},{1,3},{2,0},{3,1},{4,6},{5,7},{6,4},{7,5},{8,10},{9,11},{10,... | collective-permute-start | bytes 2359304 | tf_op jit(solution)/shard_map/ppermute | solution.py:618
  35.3 12.7 %collective-permute-start.8 = (bf16[4,24,588]{2,1,0:T(8,128)(2,1)S(1)}, bf16[4,24,588]{2,1,0:T(8,128)(2,1)S(1)}, u32[]{:S(2)}, u32[]{:S(2)}) collective-permute-start(bf16[4,24,588]{2,1,0:T(8,128)(2,1)S(1)} %get-tuple-element.386), channel_id=1, source_target_pairs={{0,16},{4,20},{8,24},{12,28},{16,0},{20,4},{24,8},{28,12},{1,17},{... | collective-permute-start | bytes 338696 | tf_op jit(solution)/shard_map/ppermute | solution.py:618
  38.1 30.7 %collective-permute-start.10 = (bf16[1,256,768]{2,1,0:T(8,128)(2,1)S(1)}, bf16[1,256,768]{2,1,0:T(8,128)(2,1)S(1)}, u32[]{:S(2)}, u32[]{:S(2)}) collective-permute-start(bf16[1,256,768]{2,1,0:T(8,128)(2,1)S(1)} %get-tuple-element.193), channel_id=1, source_target_pairs={{0,2},{1,3},{2,0},{3,1},{4,6},{5,7},{6,4},{7,5},{8,10},{9,11},{10,... | collective-permute-start | bytes 1179656 | tf_op jit(solution)/shard_map/ppermute | solution.py:618
  48.1 7.4 %collective-permute-start.9 = (bf16[2,4,24,588]{3,2,1,0:T(8,128)(2,1)S(1)}, bf16[2,4,24,588]{3,2,1,0:T(8,128)(2,1)S(1)}, u32[]{:S(2)}, u32[]{:S(2)}) collective-permute-start(bf16[2,4,24,588]{3,2,1,0:T(8,128)(2,1)S(1)} %maximum_select_fusion.3), channel_id=1, source_target_pairs={{0,8},{4,12},{8,0},{12,4},{16,24},{20,28},{24,16},{28,20},{1,9},{5... | collective-permute-start | bytes 677384 | tf_op jit(solution)/shard_map/ppermute | solution.py:618
  68.9 9.6 %copy-start.16 = (bf16[2,256,768]{2,1,0:T(8,128)(2,1)}, bf16[2,256,768]{2,1,0:T(8,128)(2,1)S(1)}, u32[]{:S(2)}) copy-start(bf16[2,256,768]{2,1,0:T(8,128)(2,1)S(1)} %pad_maximum_fusion.refs_2_) | copy-start | bytes 2359300
  69.0 8.9 %collective-permute-start.13 = (bf16[2,2,4,24,588]{4,3,2,1,0:T(8,128)(2,1)S(1)}, bf16[2,2,4,24,588]{4,3,2,1,0:T(8,128)(2,1)S(1)}, u32[]{:S(2)}, u32[]{:S(2)}) collective-permute-start(bf16[2,2,4,24,588]{4,3,2,1,0:T(8,128)(2,1)S(1)} %maximum_select_fusion.1), channel_id=1, source_target_pairs={{0,4},{4,0},{8,12},{12,8},{16,20},{20,16},{24,28},{28,24},{1,5},{5... | collective-permute-start | bytes 1354760 | tf_op jit(solution)/shard_map/ppermute | solution.py:618
  70.6 32.1 %collective-permute-start.14 = (bf16[2,256,768]{2,1,0:T(8,128)(2,1)S(1)}, bf16[2,256,768]{2,1,0:T(8,128)(2,1)}, u32[]{:S(2)}, u32[]{:S(2)}) collective-permute-start(bf16[2,256,768]{2,1,0:T(8,128)(2,1)S(1)} %get-tuple-element.194.refs_0_), channel_id=1, source_target_pairs={{0,1},{1,0},{2,3},{3,2},{4,5},{5,4},{6,7},{7,6},{8,9},{9,8},{10,11... | collective-permute-start | bytes 2359304 | tf_op jit(solution)/shard_map/ppermute | solution.py:618
  70.6 11.2 %collective-permute-start = (bf16[2,256,768]{2,1,0:T(8,128)(2,1)}, bf16[2,256,768]{2,1,0:T(8,128)(2,1)}, u32[]{:S(2)}, u32[]{:S(2)}) collective-permute-start(bf16[2,256,768]{2,1,0:T(8,128)(2,1)} %get-tuple-element.367.refs_0_), channel_id=1, source_target_pairs={{0,1},{1,0},{2,3},{3,2},{4,5},{5,4},{6,7},{7,6},{8,9},{9,8},{10,11... | collective-permute-start | bytes 2359304 | tf_op jit(solution)/shard_map/ppermute | solution.py:618
  72.4 30.4 %collective-permute-start.15 = (bf16[2,256,768]{2,1,0:T(8,128)(2,1)}, bf16[2,256,768]{2,1,0:T(8,128)(2,1)}, u32[]{:S(2)}, u32[]{:S(2)}) collective-permute-start(bf16[2,256,768]{2,1,0:T(8,128)(2,1)} %collective-permute-done.11.refs_2_), channel_id=1, source_target_pairs={{0,1},{1,0},{2,3},{3,2},{4,5},{5,4},{6,7},{7,6},{8,9},{9,8},{10,11... | collective-permute-start | bytes 2359304 | tf_op jit(solution)/shard_map/ppermute | solution.py:618
  72.4 9.4 %collective-permute-start.12 = (bf16[2,256,768]{2,1,0:T(8,128)(2,1)S(1)}, bf16[2,256,768]{2,1,0:T(8,128)(2,1)}, u32[]{:S(2)}, u32[]{:S(2)}) collective-permute-start(bf16[2,256,768]{2,1,0:T(8,128)(2,1)S(1)} %pad_maximum_fusion.refs_2_), channel_id=1, source_target_pairs={{0,1},{1,0},{2,3},{3,2},{4,5},{5,4},{6,7},{7,6},{8,9},{9,8},{10,11... | collective-permute-start | bytes 2359304 | tf_op jit(solution)/shard_map/ppermute | solution.py:618
  110.0 15.6 %collective-permute-start.16 = (bf16[2,256,192]{2,1,0:T(8,128)(2,1)S(1)}, bf16[2,256,192]{2,1,0:T(8,128)(2,1)S(1)}, u32[]{:S(2)}, u32[]{:S(2)}) collective-permute-start(bf16[2,256,192]{2,1,0:T(8,128)(2,1)S(1)} %copy-done.40), channel_id=1, source_target_pairs={{0,1},{1,0},{2,3},{3,2},{4,5},{5,4},{6,7},{7,6},{8,9},{9,8},{10,11... | collective-permute-start | bytes 589832 | tf_op jit(solution)/shard_map/ppermute | solution.py:618
  110.1 15.5 %collective-permute-start.17 = (bf16[2,256,192]{2,1,0:T(8,128)(2,1)S(1)}, bf16[2,256,192]{2,1,0:T(8,128)(2,1)S(1)}, u32[]{:S(2)}, u32[]{:S(2)}) collective-permute-start(bf16[2,256,192]{2,1,0:T(8,128)(2,1)S(1)} %copy-done.39), channel_id=1, source_target_pairs={{0,2},{1,3},{2,0},{3,1},{4,6},{5,7},{6,4},{7,5},{8,10},{9,11},{10,... | collective-permute-start | bytes 589832 | tf_op jit(solution)/shard_map/ppermute | solution.py:618
  111.0 14.6 %collective-permute-start.18 = (bf16[2,256,192]{2,1,0:T(8,128)(2,1)S(1)}, bf16[2,256,192]{2,1,0:T(8,128)(2,1)S(1)}, u32[]{:S(2)}, u32[]{:S(2)}) collective-permute-start(bf16[2,256,192]{2,1,0:T(8,128)(2,1)S(1)} %copy-done.38), channel_id=1, source_target_pairs={{0,3},{1,2},{2,1},{3,0},{4,7},{5,6},{6,5},{7,4},{8,11},{9,10},{10,... | collective-permute-start | bytes 589832 | tf_op jit(solution)/shard_map/ppermute | solution.py:618
  112.0 14.7 %copy-start.22 = (bf16[2,256,192]{2,1,0:T(8,128)(2,1)S(1)}, bf16[2,256,192]{2,1,0:T(8,128)(2,1)}, u32[]{:S(2)}) copy-start(bf16[2,256,192]{2,1,0:T(8,128)(2,1)} %get-tuple-element.214) | copy-start | bytes 589828
  125.6 15.0 %collective-permute-start.23 = (bf16[768,3456]{1,0:T(8,128)(2,1)}, bf16[768,3456]{1,0:T(8,128)(2,1)}, u32[]{:S(2)}, u32[]{:S(2)}) collective-permute-start(bf16[768,3456]{1,0:T(8,128)(2,1)} %all-gather.2.cloned.1.call-done.refs_4_), channel_id=1, source_target_pairs={{0,1},{1,0},{2,3},{3,2},{4,5},{5,4},{6,7},{7,6},{8,9},{9,8},{10,11... | collective-permute-start | bytes 15925256 | tf_op jit(solution)/shard_map/ppermute | solution.py:618
  126.1 8.5 %collective-permute-start.22 = (bf16[2,256,192]{2,1,0:T(8,128)(2,1)}, bf16[2,256,192]{2,1,0:T(8,128)(2,1)S(1)}, u32[]{:S(2)}, u32[]{:S(2)}) collective-permute-start(bf16[2,256,192]{2,1,0:T(8,128)(2,1)} %get-tuple-element.228), channel_id=1, source_target_pairs={{0,3},{1,2},{2,1},{3,0},{4,7},{5,6},{6,5},{7,4},{8,11},{9,10},{10,... | collective-permute-start | bytes 589832 | tf_op jit(solution)/shard_map/ppermute | solution.py:618
  126.7 13.9 %collective-permute-start.21 = (bf16[2,256,192]{2,1,0:T(8,128)(2,1)}, bf16[2,256,192]{2,1,0:T(8,128)(2,1)S(1)}, u32[]{:S(2)}, u32[]{:S(2)}) collective-permute-start(bf16[2,256,192]{2,1,0:T(8,128)(2,1)} %get-tuple-element.226), channel_id=1, source_target_pairs={{0,2},{1,3},{2,0},{3,1},{4,6},{5,7},{6,4},{7,5},{8,10},{9,11},{10,... | collective-permute-start | bytes 589832 | tf_op jit(solution)/shard_map/ppermute | solution.py:618
  128.1 12.6 %collective-permute-start.20 = (bf16[2,256,192]{2,1,0:T(8,128)(2,1)}, bf16[2,256,192]{2,1,0:T(8,128)(2,1)S(1)}, u32[]{:S(2)}, u32[]{:S(2)}) collective-permute-start(bf16[2,256,192]{2,1,0:T(8,128)(2,1)} %get-tuple-element.224), channel_id=1, source_target_pairs={{0,1},{1,0},{2,3},{3,2},{4,5},{5,4},{6,7},{7,6},{8,9},{9,8},{10,11... | collective-permute-start | bytes 589832 | tf_op jit(solution)/shard_map/ppermute | solution.py:618
  129.1 11.6 %copy-start.26 = (bf16[4,256,192]{2,1,0:T(8,128)(2,1)}, bf16[4,256,192]{2,1,0:T(8,128)(2,1)S(1)}, u32[]{:S(2)}) copy-start(bf16[4,256,192]{2,1,0:T(8,128)(2,1)S(1)} %constant_dynamic-update-slice_fusion.4.refs_0_) | copy-start | bytes 1179652
  181.4 2.3 collective-permute-start.24
  181.5 24.7 %collective-permute-start.25 = (bf16[4,256,192]{2,1,0:T(8,128)(2,1)}, bf16[4,256,192]{2,1,0:T(8,128)(2,1)S(1)}, u32[]{:S(2)}, u32[]{:S(2)}) collective-permute-start(bf16[4,256,192]{2,1,0:T(8,128)(2,1)} %get-tuple-element.249), channel_id=1, source_target_pairs={{0,2},{1,3},{2,0},{3,1},{4,6},{5,7},{6,4},{7,5},{8,10},{9,11},{10,... | collective-permute-start | bytes 1179656 | tf_op jit(solution)/shard_map/ppermute | solution.py:618
  182.3 24.5 %collective-permute-start.26 = (bf16[4,256,192]{2,1,0:T(8,128)(2,1)}, bf16[4,256,192]{2,1,0:T(8,128)(2,1)S(1)}, u32[]{:S(2)}, u32[]{:S(2)}) collective-permute-start(bf16[4,256,192]{2,1,0:T(8,128)(2,1)} %get-tuple-element.250), channel_id=1, source_target_pairs={{0,3},{1,2},{2,1},{3,0},{4,7},{5,6},{6,5},{7,4},{8,11},{9,10},{10,... | collective-permute-start | bytes 1179656 | tf_op jit(solution)/shard_map/ppermute | solution.py:618
  208.7 8.3 %collective-permute-start.27 = (bf16[3,2,2,2,2,24,768]{6,5,0,4,1,2,3:T(8,128)(2,1)S(1)}, bf16[3,2,2,2,2,24,768]{6,5,0,4,1,2,3:T(8,128)(2,1)}, u32[]{:S(2)}, u32[]{:S(2)}) collective-permute-start(bf16[3,2,2,2,2,24,768]{6,5,0,4,1,2,3:T(8,128)(2,1)S(1)} %copy.115), channel_id=1, source_target_pairs={{0,1},{1,0},{2,3},{3,2},{4,5},{5,4},{6,7},{7,6},{8,9},{9,8},{10,11... | collective-permute-start | bytes 5308424 | tf_op jit(solution)/shard_map/ppermute | solution.py:618
  210.4 6.6 %collective-permute-start.28 = (bf16[3,2,2,2,2,24,768]{6,5,0,1,2,3,4:T(8,128)(2,1)}, bf16[3,2,2,2,2,24,768]{6,5,0,1,2,3,4:T(8,128)(2,1)}, u32[]{:S(2)}, u32[]{:S(2)}) collective-permute-start(bf16[3,2,2,2,2,24,768]{6,5,0,1,2,3,4:T(8,128)(2,1)} %copy.116), channel_id=1, source_target_pairs={{0,1},{1,0},{2,3},{3,2},{4,5},{5,4},{6,7},{7,6},{8,9},{9,8},{10,11... | collective-permute-start | bytes 5308424 | tf_op jit(solution)/shard_map/ppermute | solution.py:618
  212.0 5.8 %collective-permute-start.29 = (bf16[3,2,2,2,2,24,768]{6,5,0,1,3,4,2:T(8,128)(2,1)}, bf16[3,2,2,2,2,24,768]{6,5,0,1,3,4,2:T(8,128)(2,1)}, u32[]{:S(2)}, u32[]{:S(2)}) collective-permute-start(bf16[3,2,2,2,2,24,768]{6,5,0,1,3,4,2:T(8,128)(2,1)} %copy.117), channel_id=1, source_target_pairs={{0,1},{1,0},{2,3},{3,2},{4,5},{5,4},{6,7},{7,6},{8,9},{9,8},{10,11... | collective-permute-start | bytes 5308424 | tf_op jit(solution)/shard_map/ppermute | solution.py:618
  230.1 22.7 %collective-permute-start.30 = (bf16[3,2,2,2,24,768]{5,4,0,3,1,2:T(8,128)(2,1)}, bf16[3,2,2,2,24,768]{5,4,0,3,1,2:T(8,128)(2,1)}, u32[]{:S(2)}, u32[]{:S(2)}) collective-permute-start(bf16[3,2,2,2,24,768]{5,4,0,3,1,2:T(8,128)(2,1)} %fusion.12), channel_id=1, source_target_pairs={{0,4},{4,0},{8,12},{12,8},{16,20},{20,16},{24,28},{28,24},{1,5},{5... | collective-permute-start | bytes 2654216 | tf_op jit(solution)/shard_map/ppermute | solution.py:618
  231.7 21.8 %collective-permute-start.31 = (bf16[3,2,2,2,24,768]{5,4,0,1,2,3:T(8,128)(2,1)}, bf16[3,2,2,2,24,768]{5,4,0,1,2,3:T(8,128)(2,1)}, u32[]{:S(2)}, u32[]{:S(2)}) collective-permute-start(bf16[3,2,2,2,24,768]{5,4,0,1,2,3:T(8,128)(2,1)} %fusion.13), channel_id=1, source_target_pairs={{0,2},{1,3},{2,0},{3,1},{4,6},{5,7},{6,4},{7,5},{8,10},{9,11},{10,... | collective-permute-start | bytes 2654216 | tf_op jit(solution)/shard_map/ppermute | solution.py:618
  232.2 21.3 %collective-permute-start.32 = (bf16[3,2,2,2,24,768]{5,4,0,1,2,3:T(8,128)(2,1)S(1)}, bf16[3,2,2,2,24,768]{5,4,0,1,2,3:T(8,128)(2,1)}, u32[]{:S(2)}, u32[]{:S(2)}) collective-permute-start(bf16[3,2,2,2,24,768]{5,4,0,1,2,3:T(8,128)(2,1)S(1)} %fusion.14), channel_id=1, source_target_pairs={{0,8},{4,12},{8,0},{12,4},{16,24},{20,28},{24,16},{28,20},{1,9},{5... | collective-permute-start | bytes 2654216 | tf_op jit(solution)/shard_map/ppermute | solution.py:618
  263.0 14.8 %collective-permute-start.34 = (bf16[3,2,2,24,768]{4,3,0,2,1:T(8,128)(2,1)}, bf16[3,2,2,24,768]{4,3,0,2,1:T(8,128)(2,1)}, u32[]{:S(2)}, u32[]{:S(2)}) collective-permute-start(bf16[3,2,2,24,768]{4,3,0,2,1:T(8,128)(2,1)} %fusion.18), channel_id=1, source_target_pairs={{0,8},{4,12},{8,0},{12,4},{16,24},{20,28},{24,16},{28,20},{1,9},{5... | collective-permute-start | bytes 1327112 | tf_op jit(solution)/shard_map/ppermute | solution.py:618
  264.7 13.1 %collective-permute-start.35 = (bf16[3,2,2,24,768]{4,3,0,1,2:T(8,128)(2,1)}, bf16[3,2,2,24,768]{4,3,0,1,2:T(8,128)(2,1)}, u32[]{:S(2)}, u32[]{:S(2)}) collective-permute-start(bf16[3,2,2,24,768]{4,3,0,1,2:T(8,128)(2,1)} %fusion.19), channel_id=1, source_target_pairs={{0,4},{4,0},{8,12},{12,8},{16,20},{20,16},{24,28},{28,24},{1,5},{5... | collective-permute-start | bytes 1327112 | tf_op jit(solution)/shard_map/ppermute | solution.py:618
  265.1 12.7 %collective-permute-start.36 = (bf16[3,2,2,24,768]{4,3,0,1,2:T(8,128)(2,1)}, bf16[3,2,2,24,768]{4,3,0,1,2:T(8,128)(2,1)}, u32[]{:S(2)}, u32[]{:S(2)}) collective-permute-start(bf16[3,2,2,24,768]{4,3,0,1,2:T(8,128)(2,1)} %fusion.20), channel_id=1, source_target_pairs={{0,2},{1,3},{2,0},{3,1},{4,6},{5,7},{6,4},{7,5},{8,10},{9,11},{10,... | collective-permute-start | bytes 1327112 | tf_op jit(solution)/shard_map/ppermute | solution.py:618
  267.2 10.6 %copy-start.6 = (f32[3,2,2,24,768]{4,3,0,1,2:T(8,128)S(1)}, f32[3,2,2,24,768]{4,3,0,1,2:T(8,128)}, u32[]{:S(2)}) copy-start(f32[3,2,2,24,768]{4,3,0,1,2:T(8,128)} %dynamic-slice_bitcast_fusion.3) | copy-start | bytes 2654212
  277.6 4.0 %collective-permute-start.33 = (bf16[2,2,256,768]{3,2,1,0:T(8,128)(2,1)}, bf16[2,2,256,768]{3,2,1,0:T(8,128)(2,1)}, u32[]{:S(2)}, u32[]{:S(2)}) collective-permute-start(bf16[2,2,256,768]{3,2,1,0:T(8,128)(2,1)} %get-tuple-element.279), channel_id=1, source_target_pairs={{0,1},{1,0},{2,3},{3,2},{4,5},{5,4},{6,7},{7,6},{8,9},{9,8},{10,11... | collective-permute-start | bytes 4718600 | tf_op jit(solution)/shard_map/ppermute | solution.py:618
  283.7 24.0 %collective-permute-start.37 = (bf16[2,256,768]{2,1,0:T(8,128)(2,1)S(1)}, bf16[2,256,768]{2,1,0:T(8,128)(2,1)S(1)}, u32[]{:S(2)}, u32[]{:S(2)}) collective-permute-start(bf16[2,256,768]{2,1,0:T(8,128)(2,1)S(1)} %fusion.15), channel_id=1, source_target_pairs={{0,2},{1,3},{2,0},{3,1},{4,6},{5,7},{6,4},{7,5},{8,10},{9,11},{10,... | collective-permute-start | bytes 2359304 | tf_op jit(solution)/shard_map/ppermute | solution.py:618
  284.2 23.5 %collective-permute-start.38 = (bf16[3,2,24,768]{3,2,0,1:T(8,128)(2,1)S(1)}, bf16[3,2,24,768]{3,2,0,1:T(8,128)(2,1)S(1)}, u32[]{:S(2)}, u32[]{:S(2)}) collective-permute-start(bf16[3,2,24,768]{3,2,0,1:T(8,128)(2,1)S(1)} %fusion.21), channel_id=1, source_target_pairs={{0,16},{4,20},{8,24},{12,28},{16,0},{20,4},{24,8},{28,12},{1,17},{... | collective-permute-start | bytes 663560 | tf_op jit(solution)/shard_map/ppermute | solution.py:618
  287.0 20.7 %collective-permute-start.39 = (bf16[3,2,24,768]{3,2,0,1:T(8,128)(2,1)S(1)}, bf16[3,2,24,768]{3,2,0,1:T(8,128)(2,1)S(1)}, u32[]{:S(2)}, u32[]{:S(2)}) collective-permute-start(bf16[3,2,24,768]{3,2,0,1:T(8,128)(2,1)S(1)} %fusion.22), channel_id=1, source_target_pairs={{0,8},{4,12},{8,0},{12,4},{16,24},{20,28},{24,16},{28,20},{1,9},{5... | collective-permute-start | bytes 663560 | tf_op jit(solution)/shard_map/ppermute | solution.py:618
  287.3 20.4 %collective-permute-start.40 = (bf16[3,2,24,768]{3,2,0,1:T(8,128)(2,1)S(1)}, bf16[3,2,24,768]{3,2,0,1:T(8,128)(2,1)S(1)}, u32[]{:S(2)}, u32[]{:S(2)}) collective-permute-start(bf16[3,2,24,768]{3,2,0,1:T(8,128)(2,1)S(1)} %fusion.23), channel_id=1, source_target_pairs={{0,4},{4,0},{8,12},{12,8},{16,20},{20,16},{24,28},{28,24},{1,5},{5... | collective-permute-start | bytes 663560 | tf_op jit(solution)/shard_map/ppermute | solution.py:618
  307.7 12.1 %copy-start.18 = (bf16[2,256,768]{2,1,0:T(8,128)(2,1)}, bf16[2,256,768]{2,1,0:T(8,128)(2,1)S(1)}, u32[]{:S(2)}) copy-start(bf16[2,256,768]{2,1,0:T(8,128)(2,1)S(1)} %collective-permute-done.37) | copy-start | bytes 2359300
  319.8 15.1 %collective-permute-start.42 = (bf16[2,2,256,768]{3,2,1,0:T(8,128)(2,1)}, bf16[2,2,256,768]{3,2,1,0:T(8,128)(2,1)S(1)}, u32[]{:S(2)}, u32[]{:S(2)}) collective-permute-start(bf16[2,2,256,768]{3,2,1,0:T(8,128)(2,1)} %get-tuple-element.315), channel_id=1, source_target_pairs={{0,1},{1,0},{2,3},{3,2},{4,5},{5,4},{6,7},{7,6},{8,9},{9,8},{10,11... | collective-permute-start | bytes 4718600 | tf_op jit(solution)/shard_map/ppermute | solution.py:618
  321.1 13.8 %copy-start.13 = (bf16[2,2,256,768]{3,2,1,0:T(8,128)(2,1)S(1)}, bf16[2,2,256,768]{3,2,1,0:T(8,128)(2,1)}, u32[]{:S(2)}) copy-start(bf16[2,2,256,768]{3,2,1,0:T(8,128)(2,1)} %get-tuple-element.317) | copy-start | bytes 4718596
  321.1 13.8 %collective-permute-start.41 = (bf16[2,2,4,24,588]{4,3,2,1,0:T(8,128)(2,1)S(1)}, bf16[2,2,4,24,588]{4,3,2,1,0:T(8,128)(2,1)}, u32[]{:S(2)}, u32[]{:S(2)}) collective-permute-start(bf16[2,2,4,24,588]{4,3,2,1,0:T(8,128)(2,1)S(1)} %fusion.17), channel_id=1, source_target_pairs={{0,4},{4,0},{8,12},{12,8},{16,20},{20,16},{24,28},{28,24},{1,5},{5... | collective-permute-start | bytes 1354760 | tf_op jit(solution)/shard_map/ppermute | solution.py:618
  324.0 13.2 %collective-permute-start.50 = (bf16[3,24,768]{2,1,0:T(8,128)(2,1)S(1)}, bf16[3,24,768]{2,1,0:T(8,128)(2,1)S(1)}, u32[]{:S(2)}, u32[]{:S(2)}) collective-permute-start(bf16[3,24,768]{2,1,0:T(8,128)(2,1)S(1)} %fusion.27), channel_id=1, source_target_pairs={{0,2},{1,3},{2,0},{3,1},{4,6},{5,7},{6,4},{7,5},{8,10},{9,11},{10,... | collective-permute-start | bytes 331784 | tf_op jit(solution)/shard_map/ppermute | solution.py:618
  325.5 11.7 %collective-permute-start.51 = (bf16[3,24,768]{2,1,0:T(8,128)(2,1)S(1)}, bf16[3,24,768]{2,1,0:T(8,128)(2,1)S(1)}, u32[]{:S(2)}, u32[]{:S(2)}) collective-permute-start(bf16[3,24,768]{2,1,0:T(8,128)(2,1)S(1)} %fusion.28), channel_id=1, source_target_pairs={{0,16},{4,20},{8,24},{12,28},{16,0},{20,4},{24,8},{28,12},{1,17},{... | collective-permute-start | bytes 331784 | tf_op jit(solution)/shard_map/ppermute | solution.py:618
  325.7 12.8 %collective-permute-start.52 = (bf16[3,24,768]{2,1,0:T(8,128)(2,1)S(1)}, bf16[3,24,768]{2,1,0:T(8,128)(2,1)}, u32[]{:S(2)}, u32[]{:S(2)}) collective-permute-start(bf16[3,24,768]{2,1,0:T(8,128)(2,1)S(1)} %fusion.29), channel_id=1, source_target_pairs={{0,16},{4,20},{8,24},{12,28},{16,0},{20,4},{24,8},{28,12},{1,17},{... | collective-permute-start | bytes 331784 | tf_op jit(solution)/shard_map/ppermute | solution.py:618
  335.4 21.0 %collective-permute-start.46 = (bf16[2,256,768]{2,1,0:T(8,128)(2,1)S(1)}, bf16[2,256,768]{2,1,0:T(8,128)(2,1)S(1)}, u32[]{:S(2)}, u32[]{:S(2)}) collective-permute-start(bf16[2,256,768]{2,1,0:T(8,128)(2,1)S(1)} %fusion.16), channel_id=1, source_target_pairs={{0,2},{1,3},{2,0},{3,1},{4,6},{5,7},{6,4},{7,5},{8,10},{9,11},{10,... | collective-permute-start | bytes 2359304 | tf_op jit(solution)/shard_map/ppermute | solution.py:618
  342.2 16.2 %copy-start.3 = (f32[2,2,256,768]{3,2,1,0:T(8,128)S(1)}, f32[2,2,256,768]{3,2,1,0:T(8,128)}, u32[]{:S(2)}) copy-start(f32[2,2,256,768]{3,2,1,0:T(8,128)} %copy-done.2) | copy-start | bytes 9437188
  343.5 5.5 %collective-permute-start.43 = (bf16[4,24,588]{2,1,0:T(8,128)(2,1)S(1)}, bf16[4,24,588]{2,1,0:T(8,128)(2,1)S(1)}, u32[]{:S(2)}, u32[]{:S(2)}) collective-permute-start(bf16[4,24,588]{2,1,0:T(8,128)(2,1)S(1)} %get-tuple-element.370), channel_id=1, source_target_pairs={{0,8},{4,12},{8,0},{12,4},{16,24},{20,28},{24,16},{28,20},{1,9},{5... | collective-permute-start | bytes 338696 | tf_op jit(solution)/shard_map/ppermute | solution.py:618
  345.2 11.1 %collective-permute-start.44 = (bf16[4,24,588]{2,1,0:T(8,128)(2,1)S(1)}, bf16[4,24,588]{2,1,0:T(8,128)(2,1)S(1)}, u32[]{:S(2)}, u32[]{:S(2)}) collective-permute-start(bf16[4,24,588]{2,1,0:T(8,128)(2,1)S(1)} %get-tuple-element.369), channel_id=1, source_target_pairs={{0,16},{4,20},{8,24},{12,28},{16,0},{20,4},{24,8},{28,12},{1,17},{... | collective-permute-start | bytes 338696 | tf_op jit(solution)/shard_map/ppermute | solution.py:618
  345.4 14.3 %copy-start.29 = (f32[768]{0:T(1024)S(1)}, f32[768]{0:T(1024)}, u32[]{:S(2)}) copy-start(f32[768]{0:T(1024)} %get-tuple-element.371) | copy-start | bytes 9220
  345.4 10.9 %collective-permute-start.45 = (bf16[4,24,588]{2,1,0:T(8,128)(2,1)S(1)}, bf16[4,24,588]{2,1,0:T(8,128)(2,1)S(1)}, u32[]{:S(2)}, u32[]{:S(2)}) collective-permute-start(bf16[4,24,588]{2,1,0:T(8,128)(2,1)S(1)} %get-tuple-element.368), channel_id=1, source_target_pairs={{0,24},{4,28},{8,16},{12,20},{16,8},{20,12},{24,0},{28,4},{1,25},{... | collective-permute-start | bytes 338696 | tf_op jit(solution)/shard_map/ppermute | solution.py:618
  356.5 8.1 %collective-permute-start.47 = (bf16[24,588]{1,0:T(8,128)(2,1)S(1)}, bf16[24,588]{1,0:T(8,128)(2,1)S(1)}, u32[]{:S(2)}, u32[]{:S(2)}) collective-permute-start(bf16[24,588]{1,0:T(8,128)(2,1)S(1)} %get-tuple-element.325), channel_id=1, source_target_pairs={{0,1},{1,0},{2,3},{3,2},{4,5},{5,4},{6,7},{7,6},{8,9},{9,8},{10,11... | collective-permute-start | bytes 84680 | tf_op jit(solution)/shard_map/ppermute | solution.py:618
  356.5 8.0 %collective-permute-start.48 = (bf16[24,588]{1,0:T(8,128)(2,1)S(1)}, bf16[24,588]{1,0:T(8,128)(2,1)S(1)}, u32[]{:S(2)}, u32[]{:S(2)}) collective-permute-start(bf16[24,588]{1,0:T(8,128)(2,1)S(1)} %get-tuple-element.326), channel_id=1, source_target_pairs={{0,2},{1,3},{2,0},{3,1},{4,6},{5,7},{6,4},{7,5},{8,10},{9,11},{10,... | collective-permute-start | bytes 84680 | tf_op jit(solution)/shard_map/ppermute | solution.py:618
  357.6 7.0 %collective-permute-start.49 = (bf16[24,588]{1,0:T(8,128)(2,1)S(1)}, bf16[24,588]{1,0:T(8,128)(2,1)S(1)}, u32[]{:S(2)}, u32[]{:S(2)}) collective-permute-start(bf16[24,588]{1,0:T(8,128)(2,1)S(1)} %get-tuple-element.327), channel_id=1, source_target_pairs={{0,3},{1,2},{2,1},{3,0},{4,7},{5,6},{6,5},{7,4},{8,11},{9,10},{10,... | collective-permute-start | bytes 84680 | tf_op jit(solution)/shard_map/ppermute | solution.py:618
  (31 other events, 85.0 us)
Sparse Core Ops, SparseCore 0:
  26.0 94.2 all-gather.1

commit v7 on v6

--- a/solution.py
+++ b/solution.py
@@ -403,34 +403,30 @@
     )(me, joint, *grads, start, logs)
 
 
-def unproject_kernel(n_blk, last, me_ref, grad_ref, normed_ref, params_ref, weight_ref, earlier_ref, earlier_bias_ref, *outs):
-    kept_ref, sent_ref, terms_ref, bias_ref = outs
+def collect_kernel(n_blk, first, last, me_ref, grad_ref, normed_ref, params_ref, weight_ref, table_ref, *refs):
+    terms_ref, bias_ref = refs[-2:]
     blk, cols = grad_ref.shape[2:]
     group = cols // 3
     vectors, width = params_ref.shape
     grad = grad_ref[...].reshape(n_blk * blk, cols)
-    share = dot(grad, weight_ref[...], ((1,), (1,))).astype(BF16)
-    for place in range(n_blk):
-        (sent_ref if place % 2 else kept_ref)[place // 2, 0] = share[place * blk : (place + 1) * blk]
     weight_grad = dot(normed_ref[...].reshape(n_blk * blk, width), grad, ((0,), (0,)))
     bias_grad = column_sum(grad.astype(F32))
 
     @pl.when(pl.program_id(0) == 0)
     def _():
-        terms_ref[:, :cols] = weight_grad + earlier_ref[:, :cols]
-        terms_ref[:, cols:] = earlier_ref[:, cols:]
-        bias_ref[...] = bias_grad + earlier_bias_ref[...]
+        terms_ref[:, :cols] = weight_grad if first else weight_grad + refs[0][:, :cols]
+        bias_ref[...] = bias_grad if first else bias_grad + refs[1][...]
 
     @pl.when(pl.program_id(0) > 0)
     def _():
         terms_ref[:, :cols] += weight_grad
         bias_ref[...] += bias_grad
 
-    if not last:
-        return
-
     @pl.when(pl.program_id(0) == pl.num_programs(0) - 1)
     def _():
+        if not last:
+            terms_ref[:, cols:] = jnp.zeros((width, vectors), F32)
+            return
         weight = weight_ref[...].astype(F32)
         bias = bias_ref[...]
         columns = params_ref[...].T
@@ -441,37 +437,60 @@
         def placed(values):
             return jnp.concatenate([jnp.where(me_ref[0] == j, values, 0.0) for j in range(n_blk)], axis=1)
 
-        table = jnp.concatenate(
-            [placed(bias[:, :group]), placed(bias[:, 2 * group :]), jnp.zeros((vectors - 4, width), F32)], axis=0
-        ).T
-        terms_ref[:, cols:] += jnp.concatenate([gain_sum, shift_sum, table], axis=1)
-
-
-def unproject(me, grad, normed, params, weight, earlier, bias, last):
+        table = jnp.concatenate([placed(bias[:, :group]), placed(bias[:, 2 * group :]), table_ref[...]], axis=0).T
+        terms_ref[:, cols:] = jnp.concatenate([gain_sum, shift_sum, table], axis=1)
+
+
+def collect(me, grad, normed, params, weight, table, earlier, last):
     n_blk, count, blk, cols = grad.shape
-    width = normed.shape[-1]
+    vectors, width = params.shape
 
     def whole(shape):
         return pl.BlockSpec(shape, lambda s, m: (0, 0))
 
-    def by_seq(parts, size):
-        return pl.BlockSpec((parts, 1, blk, size), lambda s, m: (0, s, 0, 0))
-
+    def by_seq(size):
+        return pl.BlockSpec((n_blk, 1, blk, size), lambda s, m: (0, s, 0, 0))
+
+    shapes = [(width, cols + vectors), (1, cols)]
     return pl.pallas_call(
-        functools.partial(unproject_kernel, n_blk, last),
+        functools.partial(collect_kernel, n_blk, not earlier, last),
         grid_spec=pltpu.PrefetchScalarGridSpec(
             num_scalar_prefetch=1,
             grid=(count,),
-            in_specs=[by_seq(n_blk, cols), by_seq(n_blk, width)]
-            + [whole(params.shape), whole(weight.shape), whole(earlier.shape), whole(bias.shape)],
-            out_specs=[by_seq(n_blk // 2, width)] * 2 + [whole(earlier.shape), whole(bias.shape)],
+            in_specs=[by_seq(cols), by_seq(width)]
+            + [whole(item.shape) for item in (params, weight, table, *earlier)],
+            out_specs=[whole(shape) for shape in shapes],
         ),
-        out_shape=[jax.ShapeDtypeStruct((n_blk // 2, count, blk, width), BF16)] * 2
-        + [jax.ShapeDtypeStruct(earlier.shape, F32), jax.ShapeDtypeStruct(bias.shape, F32)],
+        out_shape=[jax.ShapeDtypeStruct(shape, F32) for shape in shapes],
+        compiler_params=pltpu.CompilerParams(vmem_limit_bytes=VMEM_BYTES),
+        cost_estimate=COST,
+        name="collect",
+    )(me, grad, normed, params, weight, table, *earlier)
+
+
+def unproject_kernel(n_blk, grad_ref, weight_ref, kept_ref, sent_ref):
+    for place in range(n_blk):
+        share = dot(grad_ref[place, 0], weight_ref[...], ((1,), (1,))).astype(BF16)
+        (sent_ref if place % 2 else kept_ref)[place // 2, 0] = share
+
+
+def unproject(grad, weight):
+    n_blk, count, blk, cols = grad.shape
+    width = weight.shape[0]
+    out = pl.BlockSpec((n_blk // 2, 1, blk, width), lambda s: (0, s, 0, 0))
+    return pl.pallas_call(
+        functools.partial(unproject_kernel, n_blk),
+        grid=(count,),
+        in_specs=[
+            pl.BlockSpec((n_blk, 1, blk, cols), lambda s: (0, s, 0, 0)),
+            pl.BlockSpec(weight.shape, lambda s: (0, 0)),
+        ],
+        out_specs=[out, out],
+        out_shape=[jax.ShapeDtypeStruct((n_blk // 2, count, blk, width), BF16)] * 2,
         compiler_params=pltpu.CompilerParams(vmem_limit_bytes=VMEM_BYTES),
         cost_estimate=COST,
         name="unproject",
-    )(me, grad, normed, params, weight, earlier, bias)
+    )(grad, weight)
 
 
 def weigh_kernel(n_ctx, last, me_ref, act_ref, pre_ref, normed_ref, up_ref, branch_ref, *refs):
@@ -503,7 +522,7 @@
 
         @pl.when((step >= bounds[number]) & (step < bounds[number + 1]))
         def _():
-            keep_ref[0] = total[:, core]
+            keep_ref[0] = total[:, core].astype(BF16)
             send_ref[0] = total[:, 1 - core].astype(BF16)
 
 
@@ -540,7 +559,7 @@
             scratch_shapes=[pltpu.VMEM((pairs, 2, part, width), F32)],
         ),
         out_shape=[
-            jax.ShapeDtypeStruct((count, pairs, part, width), dtype) for count, _ in counts for dtype in (F32, BF16)
+            jax.ShapeDtypeStruct((count, pairs, part, width), dtype) for count, _ in counts for dtype in (BF16, BF16)
         ],
         compiler_params=pltpu.CompilerParams(vmem_limit_bytes=VMEM_BYTES),
         cost_estimate=COST,
@@ -817,7 +836,7 @@
 
         def merge(chain, got):
             _, _, names, order = chain
-            chain[0] = chain[0] + got.astype(F32)
+            chain[0] = chain[0].astype(F32) + got.astype(F32)
             chain[2] = [name for name in names if name != order[0]]
             chain[3] = order[1:]
 
@@ -843,32 +862,60 @@
                 split(chain)
 
         sums_hidden = sums[3 : 3 + spans].reshape(spans, n_dev, part).transpose(1, 0, 2).reshape(spans, width)
-        table = jnp.concatenate([jnp.zeros((4, width), F32), sums[:3], sums_hidden, sums[3 + spans :]], axis=0)
-        terms = jnp.concatenate([jnp.zeros((width, cols), F32), table.T], axis=1)
+        table = jnp.concatenate([sums[:3], sums_hidden, sums[3 + spans :]], axis=0)
         pending, shares = None, []
-        bias_sums = jnp.zeros((1, cols), F32)
+        earlier, after = (), branch
         for number, first in enumerate(firsts):
-            _, (source, pending) = advance(terms if number else branch, (joints[number], pending))
+            _, (source, pending) = advance(after, (joints[number], pending))
             grad_joint = attend_backward(me_arr, source, grads, starts[number], logs[number], first)
             if pending:
                 pending[1] = [swap(value, "ctx", 1 << bit) for value, bit in zip(pending[1], ctx_bits[1:])]
             (grad_joint, pending), _ = advance((grad_joint, pending), start)
             if pending:
                 shares.append(sum((value.astype(F32) for value in pending[1]), pending[0]))
-            kept, sent, terms, bias_sums = unproject(
-                me_arr, grad_joint, normeds[number], params, joint_lo, terms, bias_sums, number == len(firsts) - 1
+            earlier = collect(
+                me_arr, grad_joint, normeds[number], params, joint_lo, table, earlier, number == len(firsts) - 1
             )
+            if number == len(firsts) - 1:
+                grad_joint, earlier = lax.optimization_barrier((grad_joint, earlier))
+            kept, sent = unproject(grad_joint, joint_lo)
+            after = (earlier, kept)
             if number < len(firsts) - 1:
                 joined = kept.astype(F32) + swap(sent, "ctx", 1).astype(F32)
                 pending = [joined[0], [joined[1 << (bit - 1)].astype(BF16) for bit in ctx_bits[1:]]]
 
-        terms = terms.reshape((2,) * n_bits + (n_ctx, part, cols + vectors))
+        terms = earlier[0].reshape((2,) * n_bits + (n_ctx, part, cols + vectors))
         chain = [terms, None, [("dp", bit) for bit in reversed(dp_bits)], low + high]
         split(chain)
         got, sent, kept = lax.optimization_barrier((fetch(chain), swap(sent, "ctx", 1), kept))
         merge(chain, got)
         joined = kept.astype(F32) + sent.astype(F32)
         crossing = [swap(joined[1 << (bit - 1)].astype(BF16), "ctx", 1 << bit) for bit in ctx_bits[1:]]
+        while len(chains[0][3]) > 1:
+            for item in chains:
+                merge(item, fetch(item))
+                split(item)
+        chain[0], keeps = lax.optimization_barrier((chain[0], [item[0] for item in chains]))
+        for item, keep in zip(chains, keeps):
+            item[0] = keep
+        states = (
+            (output_weight, momentum_output, variance_output)
+            + (expand_weight, momentum_expand, variance_expand)
+            + (shrink_weight, momentum_shrink, variance_shrink)
+        )
+        if part % 8 == 0:
+            updated = update([item[0] for item in chains], [fetch(item) for item in chains], states, n_dev)
+        else:
+            for item in chains:
+                merge(item, fetch(item))
+            last_shrink, last_expand, sum_output = chains[2][0]
+            sum_shrink = jnp.concatenate([*chains[0][0], last_shrink], axis=0)
+            sum_expand = jnp.stack([*chains[1][0], last_expand], axis=1)
+            sum_expand = sum_expand.reshape(part, spans, n_dev, part).transpose(0, 2, 1, 3).reshape(part, hidden)
+            updated = []
+            for number, gradient in enumerate((sum_output, sum_expand, sum_shrink)):
+                weight, first, second = states[3 * number : 3 * number + 3]
+                updated += adam_step(weight, gradient, first, second, RATE_MATRIX, WEIGHT_DECAY)
         if n_dp <= 8:
             items = chain[0].reshape(n_dp // 2, n_ctx, part, cols + vectors)
             spot = me_dp >> 1
@@ -878,7 +925,7 @@
                 for j in range(1, n_dp // 2)
             ]
             gots = [swap(item, "dp", 2 * (j + 1)) for j, item in enumerate(sent)]
-            total, gots, crossing = lax.optimization_barrier((total, gots, crossing))
+            total, gots, crossing, updated = lax.optimization_barrier((total, gots, crossing, updated))
             total = sum((item.astype(F32) for item in gots), total)
         else:
             while chain[3]:
@@ -901,28 +948,6 @@
         plain, scale = norm_parts(tokens_in.astype(F32))
         input_grad = grad_resid + norm_back(plain, scale, jnp.concatenate(shares, axis=0), params[0])
 
-        while len(chains[0][3]) > 1:
-            for chain in chains:
-                merge(chain, fetch(chain))
-                split(chain)
-        states = (
-            (output_weight, momentum_output, variance_output)
-            + (expand_weight, momentum_expand, variance_expand)
-            + (shrink_weight, momentum_shrink, variance_shrink)
-        )
-        if part % 8 == 0:
-            updated = update([chain[0] for chain in chains], [fetch(chain) for chain in chains], states, n_dev)
-        else:
-            for chain in chains:
-                merge(chain, fetch(chain))
-            last_shrink, last_expand, sum_output = chains[2][0]
-            sum_shrink = jnp.concatenate([*chains[0][0], last_shrink], axis=0)
-            sum_expand = jnp.stack([*chains[1][0], last_expand], axis=1)
-            sum_expand = sum_expand.reshape(part, spans, n_dev, part).transpose(0, 2, 1, 3).reshape(part, hidden)
-            updated = []
-            for number, gradient in enumerate((sum_output, sum_expand, sum_shrink)):
-                weight, first, second = states[3 * number : 3 * number + 3]
-                updated += adam_step(weight, gradient, first, second, RATE_MATRIX, WEIGHT_DECAY)
         new_output, first_output, second_output = updated[:3]
         new_expand, first_expand, second_expand = updated[3:6]
         new_shrink, first_shrink, second_shrink = updated[6:]

time: 383 us -> 373 us (0.974)
  local copies, waits for them, and re-layouts: 39.7 us -> 27.3 us
  other arithmetic: 31.3 us -> 23.8 us
  waiting for transfers between devices: 71.6 us -> 76.8 us
  Pallas kernels: 170 us -> 174 us
    add x13, other arithmetic: 15.7 us -> 10.3 us  [merge(): chain[0] = chain[0].astype(F32) + got.astype(F32)]
    convert_element_type x13, local copies, waits for them, and re-layouts: 6.01 us -> 0.68 us  [split(): lax.dynamic_index_in_dim(value, 1 - mine, pos, keepdims=False).astype(BF16)]
    ppermute x53, waiting for transfers between devices: 71.6 us -> 76.8 us  [swap(): lax.ppermute(value, axis, [(place, place ^ mask) for place in range(sizes...]
    pallas_call x2 -> x4, Pallas kernels: 22.5 us -> 27.1 us  [the longest x2 15.4 us: collect(): pl.pallas_call(functools.partial(collect_kernel, n_blk, not earlier, last...]
    unnamed x89 -> x93, local copies, waits for them, and re-layouts: 8.16 us -> 7.48 us
  transfers between devices with their start and end apart: 54 -> 54, of which waited for: 16 -> 18; matrix products, arithmetic and copies ran while one was open for 11% -> 8% of each run, Pallas kernels for 31% -> 32%
where the time goes in v7:
time: 373 us; the launch traced here: 366 us
  Pallas kernels  174 us (47%)
  waiting for transfers between devices  76.8 us (21%)
  starting transfers between devices  48.6 us (13%)
  local copies, waits for them, and re-layouts  27.3 us (7%)
  other arithmetic  23.8 us (6%)
  between operations  15.8 us (4%)
    ppermute x53, waiting for transfers between devices, swap(): lax.ppermute(value, axis, [(place, place ^ mask) for place in range(sizes...  76.8 us
    ppermute x53, starting transfers between devices, swap(): lax.ppermute(value, axis, [(place, place ^ mask) for place in range(sizes...  48.6 us
    pallas_call x1, Pallas kernels, layer(): pl.pallas_call(functools.partial(layer_kernel, n_ctx, spans), grid_spec=p...  39.8 us
    pallas_call x2, Pallas kernels, attend_backward(): pl.pallas_call(functools.partial(backward_kernel, n_blk, blk, heads), gri...  37.7 us
    pallas_call x2, Pallas kernels, attend_forward(): pl.pallas_call(functools.partial(forward_kernel, n_blk, blk, heads), grid...  27.2 us
    pallas_call x1, Pallas kernels, weigh(): pl.pallas_call(functools.partial(weigh_kernel, n_ctx, last), grid_spec=pl...  21.2 us
    pallas_call x2, Pallas kernels, collect(): pl.pallas_call(functools.partial(collect_kernel, n_blk, not earlier, last...  15.4 us
    pallas_call x2, Pallas kernels, project(): pl.pallas_call(functools.partial(project_kernel, n_blk), grid=(seqs,), in...  14.6 us
  transfers between devices with their start and end apart: 54, of which 18 were waited for; matrix products, arithmetic and copies ran while one was open for 8% of the time, Pallas kernels for 32%

profile of v7, /device:TPU:0, one launch (start us, length us, event | category | flops | bytes accessed | tf_op | source)
XLA Modules:
  0.0 365.9 jit_solution(9774306627955564203)
XLA Ops:
  7.3 3.0 collective-permute-start.5
  12.2 1.0 dynamic-slice_reduce_fusion
  14.9 1.3 collective-permute-start.3
  17.2 1.2 reshape.462
  18.6 1.3 reshape.463
  24.9 8.1 %collective-permute-done.7 = bf16[1,256,768]{2,1,0:T(8,128)(2,1)S(1)} collective-permute-done((bf16[1,256,768]{2,1,0:T(8,128)(2,1)S(1)}, bf16[1,256,768]{2,1,0:T(8,128)(2,1)S(1)}, u32[]{:S(2)}, u32[]{:S(2)}) %collective-permute-start.7) | collective-permute-done | bytes 393248 | tf_op jit(solution)/shard_map/ppermute | solution.py:637
  33.6 2.8 collective-permute-start.8
  36.4 1.5 collective-permute-start.10
  37.8 7.5 %collective-permute-done.8 = bf16[4,24,588]{2,1,0:T(8,128)(2,1)S(1)} collective-permute-done((bf16[4,24,588]{2,1,0:T(8,128)(2,1)S(1)}, bf16[4,24,588]{2,1,0:T(8,128)(2,1)S(1)}, u32[]{:S(2)}, u32[]{:S(2)}) %collective-permute-start.8) | collective-permute-done | bytes 112928 | tf_op jit(solution)/shard_map/ppermute | solution.py:637
  45.4 2.4 collective-permute-start.9
  47.8 6.4 %collective-permute-done.9 = bf16[2,4,24,588]{3,2,1,0:T(8,128)(2,1)S(1)} collective-permute-done((bf16[2,4,24,588]{3,2,1,0:T(8,128)(2,1)S(1)}, bf16[2,4,24,588]{3,2,1,0:T(8,128)(2,1)S(1)}, u32[]{:S(2)}, u32[]{:S(2)}) %collective-permute-start.9) | collective-permute-done | bytes 225824 | tf_op jit(solution)/shard_map/ppermute | solution.py:637
  54.3 13.6 %collective-permute-done.10 = bf16[1,256,768]{2,1,0:T(8,128)(2,1)S(1)} collective-permute-done((bf16[1,256,768]{2,1,0:T(8,128)(2,1)S(1)}, bf16[1,256,768]{2,1,0:T(8,128)(2,1)S(1)}, u32[]{:S(2)}, u32[]{:S(2)}) %collective-permute-start.10) | collective-permute-done | bytes 393248 | tf_op jit(solution)/shard_map/ppermute | solution.py:637
  68.1 1.6 collective-permute-start.13
  71.4 5.6 %collective-permute-done.13 = bf16[2,2,4,24,588]{4,3,2,1,0:T(8,128)(2,1)S(1)} collective-permute-done((bf16[2,2,4,24,588]{4,3,2,1,0:T(8,128)(2,1)S(1)}, bf16[2,2,4,24,588]{4,3,2,1,0:T(8,128)(2,1)S(1)}, u32[]{:S(2)}, u32[]{:S(2)}) %collective-permute-start.13) | collective-permute-done | bytes 451616 | tf_op jit(solution)/shard_map/ppermute | solution.py:637
  80.9 7.3 %project.2 = (bf16[4,2,256,576]{3,2,1,0:T(8,128)(2,1)}, bf16[4,2,256,768]{3,2,1,0:T(8,128)(2,1)}) custom-call(bf16[2,256,768]{2,1,0:T(8,128)(2,1)} %get-tuple-element.397.refs_0_, bf16[2,256,768]{2,1,0:T(8,128)(2,1)} %collective-permute-done.refs_1_, bf16[2,256,768]{2,1,0:T(8,128)(2,1)} %copy-done.14, bf16[2,256,768]{2,1,0:T(8,128)(2,1)} %collective-permute-done.12.refs_3_, ...), custom_call_target="tpu_custom_call" | custom-call | flops 20000000000 | bytes 1000000 | tf_op jit(solution)/shard_map/project/pallas_call | solution.py:74
  88.2 13.6 %attend_forward.2 = (bf16[2,256,192]{2,1,0:T(8,128)(2,1)}, bf16[2,256,192]{2,1,0:T(8,128)(2,1)}, bf16[2,256,192]{2,1,0:T(8,128)(2,1)}, bf16[2,256,192]{2,1,0:T(8,128)(2,1)}, f32[2,3,1024]{2,1,0:T(4,128)}) custom-call(s32[1]{0:T(128)} %bitcast.me_ref, bf16[4,2,256,576]{3,2,1,0:T(8,128)(2,1)} %get-tuple-element.278.joint_ref, ...), custom_call_target="tpu_custom_call" | custom-call | flops 20000000000 | bytes 1000000 | tf_op jit(solution)/shard_map/attend_forward/pallas_call | solution.py:152
  101.8 7.2 %project.3 = (bf16[4,2,256,576]{3,2,1,0:T(8,128)(2,1)}, bf16[4,2,256,768]{3,2,1,0:T(8,128)(2,1)}) custom-call(bf16[2,256,768]{2,1,0:T(8,128)(2,1)} %copy-done.15, bf16[2,256,768]{2,1,0:T(8,128)(2,1)} %collective-permute-done.14.refs_1_, bf16[2,256,768]{2,1,0:T(8,128)(2,1)} %collective-permute-done.11.refs_2_, ...), custom_call_target="tpu_custom_call" | custom-call | flops 20000000000 | bytes 1000000 | tf_op jit(solution)/shard_map/project/pallas_call | solution.py:74
  111.0 13.6 %attend_forward.3 = (bf16[2,256,192]{2,1,0:T(8,128)(2,1)}, bf16[2,256,192]{2,1,0:T(8,128)(2,1)}, bf16[2,256,192]{2,1,0:T(8,128)(2,1)}, bf16[2,256,192]{2,1,0:T(8,128)(2,1)}, f32[2,3,1024]{2,1,0:T(4,128)}) custom-call(s32[1]{0:T(128)} %bitcast.me_ref, bf16[4,2,256,576]{3,2,1,0:T(8,128)(2,1)} %get-tuple-element.315.joint_ref, ...), custom_call_target="tpu_custom_call" | custom-call | flops 20000000000 | bytes 1000000 | tf_op jit(solution)/shard_map/attend_forward/pallas_call | solution.py:152
  125.8 1.3 collective-permute-start.21
  127.3 6.5 %collective-permute-done.22 = bf16[2,256,192]{2,1,0:T(8,128)(2,1)S(1)} collective-permute-done((bf16[2,256,192]{2,1,0:T(8,128)(2,1)}, bf16[2,256,192]{2,1,0:T(8,128)(2,1)S(1)}, u32[]{:S(2)}, u32[]{:S(2)}) %collective-permute-start.22) | collective-permute-done | bytes 196640 | tf_op jit(solution)/shard_map/ppermute | solution.py:637
  133.8 5.9 %collective-permute-done.21 = bf16[2,256,192]{2,1,0:T(8,128)(2,1)S(1)} collective-permute-done((bf16[2,256,192]{2,1,0:T(8,128)(2,1)S(1)}, bf16[2,256,192]{2,1,0:T(8,128)(2,1)S(1)}, u32[]{:S(2)}, u32[]{:S(2)}) %collective-permute-start.21) | collective-permute-done | bytes 196640 | tf_op jit(solution)/shard_map/ppermute | solution.py:637
  140.7 39.8 %layer.1 = (bf16[4,256,768]{2,1,0:T(8,128)(2,1)}, f32[4,256,768]{2,1,0:T(8,128)}, bf16[4,256,768]{2,1,0:T(8,128)(2,1)}, bf16[768,1024]{1,0:T(8,128)(2,1)}, bf16[...) custom-call(s32[1]{0:T(128)} %bitcast.me_ref, ...), custom_call_target="tpu_custom_call" | custom-call | flops 20000000000 | bytes 1000000 | tf_op jit(solution)/shard_map/layer/pallas_call | solution.py:278
  181.4 1.0 collective-permute-start.26
  182.8 21.2 %weigh.1 = (bf16[3,16,24,768]{3,2,1,0:T(8,128)(2,1)}, bf16[3,16,24,768]{3,2,1,0:T(8,128)(2,1)}, bf16[3,16,24,768]{3,2,1,0:T(8,128)(2,1)}, bf16[3,16,24,768]{3,2,...) custom-call(s32[1]{0:T(128)} %bitcast.me_ref, ...), custom_call_target="tpu_custom_call" | custom-call | flops 20000000000 | bytes 1000000 | tf_op jit(solution)/shard_map/weigh/pallas_call | solution.py:545
  204.0 1.9 collective-permute-done.26.refs_3_
  205.9 3.0 copy.110
  209.2 1.3 copy.111
  210.8 1.4 copy.112
  215.5 2.5 collective-permute-done.29
  218.0 1.9 convert_add_fusion
  220.2 1.2 copy-done.5
  221.4 1.9 convert_add_fusion.1
  223.6 1.2 copy-done.4
  224.8 2.0 convert_add_fusion.2
  227.0 1.6 collective-permute-start.30
  229.1 1.7 collective-permute-start.32
  230.8 19.0 %attend_backward.2.grad_ref = bf16[4,2,256,576]{3,2,1,0:T(8,128)(2,1)} custom-call(s32[1]{0:T(128)} %bitcast.me_ref, bf16[4,2,256,576]{3,2,1,0:T(8,128)(2,1)} %get-tuple-element.278.joint_ref, bf16[4,256,192]{2,1,0:T(8,128)(2,1)} %get-tuple-element.279.refs_0_, bf16[4,256,192]{2,1,0:T(8,128)(2,1)} %collective-permute-done.24.refs_1_, ...), custom_call_target="tpu_custom_call" | custom-call | flops 20000000000 | bytes 1000000 | tf_op jit(solution)/shard_map/attend_backward/pallas_call | solution.py:380
  250.5 1.3 convert_add_fusion.5
  252.0 1.3 convert_add_fusion.6
  253.5 1.3 convert_add_fusion.7
  255.0 1.7 collective-permute-start.34
  257.1 1.5 collective-permute-start.36
  258.7 5.7 %unproject.2 = (bf16[2,2,256,768]{3,2,1,0:T(8,128)(2,1)}, bf16[2,2,256,768]{3,2,1,0:T(8,128)(2,1)}) custom-call(bf16[4,2,256,576]{3,2,1,0:T(8,128)(2,1)} %attend_backward.2.grad_ref, bf16[768,576]{1,0:T(8,128)(2,1)} %bitcast.150), custom_call_target="tpu_custom_call" | custom-call | flops 20000000000 | bytes 1000000 | tf_op jit(solution)/shard_map/unproject/pallas_call | solution.py:481
  264.3 6.6 %collect.2 = (f32[768,588]{1,0:T(8,128)}, f32[1,576]{1,0:T(1,128)}) custom-call(s32[1]{0:T(128)} %bitcast.me_ref, bf16[4,2,256,576]{3,2,1,0:T(8,128)(2,1)} %attend_backward.2.grad_ref, bf16[4,2,256,768]{3,2,1,0:T(8,128)(2,1)} %get-tuple-element.293.normed_ref, f32[12,768]{1,0:T(8,128)} %pad_maximum_fusion.9.refs_4_.refs_6_.params_ref, ...), custom_call_target="tpu_custom_call" | custom-call | flops 20000000000 | bytes 1000000 | tf_op jit(solution)/shard_map/collect/pallas_call | solution.py:455
  271.5 1.2 copy-done.10
  273.8 2.8 collective-permute-start.38
  277.0 1.6 collective-permute-start.40
  278.5 18.8 %attend_backward.3.grad_ref = bf16[4,2,256,576]{3,2,1,0:T(8,128)(2,1)} custom-call(s32[1]{0:T(128)} %bitcast.me_ref, bf16[4,2,256,576]{3,2,1,0:T(8,128)(2,1)} %get-tuple-element.315.joint_ref, bf16[4,256,192]{2,1,0:T(8,128)(2,1)} %get-tuple-element.279.refs_0_, bf16[4,256,192]{2,1,0:T(8,128)(2,1)} %collective-permute-done.24.refs_1_, ...), custom_call_target="tpu_custom_call" | custom-call | flops 20000000000 | bytes 1000000 | tf_op jit(solution)/shard_map/attend_backward/pallas_call | solution.py:380
  297.4 8.8 %collect.3 = (f32[768,588]{1,0:T(8,128)}, f32[1,576]{1,0:T(1,128)}) custom-call(s32[1]{0:T(128)} %bitcast.me_ref, bf16[4,2,256,576]{3,2,1,0:T(8,128)(2,1)} %attend_backward.3.grad_ref, bf16[4,2,256,768]{3,2,1,0:T(8,128)(2,1)} %get-tuple-element.328.normed_ref, f32[12,768]{1,0:T(8,128)} %pad_maximum_fusion.9.refs_4_.refs_6_.params_ref, ...), custom_call_target="tpu_custom_call" | custom-call | flops 20000000000 | bytes 1000000 | tf_op jit(solution)/shard_map/collect/pallas_call | solution.py:455
  306.2 6.0 %unproject.3 = (bf16[2,2,256,768]{3,2,1,0:T(8,128)(2,1)}, bf16[2,2,256,768]{3,2,1,0:T(8,128)(2,1)}) custom-call(bf16[4,2,256,576]{3,2,1,0:T(8,128)(2,1)} %attend_backward.3.grad_ref, bf16[768,576]{1,0:T(8,128)(2,1)} %bitcast.153), custom_call_target="tpu_custom_call" | custom-call | flops 20000000000 | bytes 1000000 | tf_op jit(solution)/shard_map/unproject/pallas_call | solution.py:481
  315.2 1.5 collective-permute-start.47
  316.9 2.7 collective-permute-start.49
  319.7 6.4 %collective-permute-done.41 = bf16[2,2,4,24,588]{4,3,2,1,0:T(8,128)(2,1)S(1)} collective-permute-done((bf16[2,2,4,24,588]{4,3,2,1,0:T(8,128)(2,1)S(1)}, bf16[2,2,4,24,588]{4,3,2,1,0:T(8,128)(2,1)S(1)}, u32[]{:S(2)}, u32[]{:S(2)}) %collective-permute-start.41) | collective-permute-done | bytes 451616 | tf_op jit(solution)/shard_map/ppermute | solution.py:637
  327.4 1.5 collective-permute-start.46
  329.2 1.8 collective-permute-start.43
  331.1 2.6 collective-permute-start.45
  333.7 3.7 %update.1 = (f32[24,768]{1,0:T(8,128)}, f32[24,768]{1,0:T(8,128)}, f32[24,768]{1,0:T(8,128)}, f32[24,3072]{1,0:T(8,128)}, f32[24,3072]{1,0:T(8,128)}, /*index=5*...) custom-call(f32[3,24,768]{2,1,0:T(8,128)} %dynamic-slice_bitcast_fusion.12.refs_0_, ...), custom_call_target="tpu_custom_call" | custom-call | tf_op jit(solution)/shard_map/update/pallas_call | solution.py:589
  337.4 4.4 %collective-permute-done.44 = bf16[4,24,588]{2,1,0:T(8,128)(2,1)S(1)} collective-permute-done((bf16[4,24,588]{2,1,0:T(8,128)(2,1)S(1)}, bf16[4,24,588]{2,1,0:T(8,128)(2,1)S(1)}, u32[]{:S(2)}, u32[]{:S(2)}) %collective-permute-start.44) | collective-permute-done | bytes 112928 | tf_op jit(solution)/shard_map/ppermute | solution.py:637
  341.9 5.0 %collective-permute-done.46 = bf16[2,256,768]{2,1,0:T(8,128)(2,1)} collective-permute-done((bf16[2,256,768]{2,1,0:T(8,128)(2,1)}, bf16[2,256,768]{2,1,0:T(8,128)(2,1)}, u32[]{:S(2)}, u32[]{:S(2)}) %collective-permute-start.46) | collective-permute-done | bytes 786464 | tf_op jit(solution)/shard_map/ppermute | solution.py:637
  347.0 1.6 collective-permute-start.51
  348.9 1.3 fusion.10
  350.2 1.2 fusion.9
  352.1 2.3 fusion.7
  356.3 2.3 finish.1
  (277 shorter events, 37.9 us)
Async XLA Ops:
  7.2 10.0 %copy-start.12 = (f32[96,768]{1,0:T(8,128)S(1)}, f32[96,768]{1,0:T(8,128)}, u32[]{:S(2)}) copy-start(f32[96,768]{1,0:T(8,128)} %refs_12_.1) | copy-start | bytes 884740
  7.2 10.0 %copy-start.18 = (f32[24,768]{1,0:T(8,128)S(1)}, f32[24,768]{1,0:T(8,128)}, u32[]{:S(2)}) copy-start(f32[24,768]{1,0:T(8,128)} %refs_6_.2) | copy-start | bytes 221188
  7.2 117.5 %all-gather.2.cloned.1.call-start = ((), (), s32[]{:S(2)}) async-start(), calls=%async_computation | async-start | bytes 5640192 | tf_op jit(solution)/shard_map/all_gather | solution.py:718
  7.3 13.8 %collective-permute-start.5 = (s32[4,256]{1,0:T(4,128)}, s32[4,256]{1,0:T(4,128)S(1)}, u32[]{:S(2)}, u32[]{:S(2)}) collective-permute-start(s32[4,256]{1,0:T(4,128)} %param.19), channel_id=1, source_target_pairs={{0,2},{1,3},{2,0},{3,1},{4,6},{5,7},{6,4},{7,5},{8,10},{9,11},{10,... | collective-permute-start | bytes 12296 | tf_op jit(solution)/shard_map/ppermute | solution.py:637
  10.3 11.7 %collective-permute-start.4 = (s32[4,256]{1,0:T(4,128)}, s32[4,256]{1,0:T(4,128)S(1)}, u32[]{:S(2)}, u32[]{:S(2)}) collective-permute-start(s32[4,256]{1,0:T(4,128)} %param.19), channel_id=1, source_target_pairs={{0,1},{1,0},{2,3},{3,2},{4,5},{5,4},{6,7},{7,6},{8,9},{9,8},{10,11... | collective-permute-start | bytes 12296 | tf_op jit(solution)/shard_map/ppermute | solution.py:637
  14.3 10.6 %collective-permute-start.1 = (bf16[24,588]{1,0:T(8,128)(2,1)}, bf16[24,588]{1,0:T(8,128)(2,1)S(1)}, u32[]{:S(2)}, u32[]{:S(2)}) collective-permute-start(bf16[24,588]{1,0:T(8,128)(2,1)} %get-tuple-element.430), channel_id=1, source_target_pairs={{0,1},{1,0},{2,3},{3,2},{4,5},{5,4},{6,7},{7,6},{8,9},{9,8},{10,11... | collective-permute-start | bytes 84680 | tf_op jit(solution)/shard_map/ppermute | solution.py:637
  14.8 10.1 %collective-permute-start.2 = (bf16[24,588]{1,0:T(8,128)(2,1)S(1)}, bf16[24,588]{1,0:T(8,128)(2,1)S(1)}, u32[]{:S(2)}, u32[]{:S(2)}) collective-permute-start(bf16[24,588]{1,0:T(8,128)(2,1)S(1)} %get-tuple-element.431), channel_id=1, source_target_pairs={{0,2},{1,3},{2,0},{3,1},{4,6},{5,7},{6,4},{7,5},{8,10},{9,11},{10,... | collective-permute-start | bytes 84680 | tf_op jit(solution)/shard_map/ppermute | solution.py:637
  14.9 10.1 %collective-permute-start.3 = (bf16[24,588]{1,0:T(8,128)(2,1)S(1)}, bf16[24,588]{1,0:T(8,128)(2,1)S(1)}, u32[]{:S(2)}, u32[]{:S(2)}) collective-permute-start(bf16[24,588]{1,0:T(8,128)(2,1)S(1)} %get-tuple-element.429), channel_id=1, source_target_pairs={{0,3},{1,2},{2,1},{3,0},{4,7},{5,6},{6,5},{7,4},{8,11},{9,10},{10,... | collective-permute-start | bytes 84680 | tf_op jit(solution)/shard_map/ppermute | solution.py:637
  21.1 48.6 %copy-start.15 = (bf16[2,256,768]{2,1,0:T(8,128)(2,1)}, bf16[2,256,768]{2,1,0:T(8,128)(2,1)S(1)}, u32[]{:S(2)}) copy-start(bf16[2,256,768]{2,1,0:T(8,128)(2,1)S(1)} %get-tuple-element.209.refs_0_) | copy-start | bytes 2359300
  21.1 1.6 collective-permute-start.6
  22.0 11.1 %collective-permute-start.7 = (bf16[1,256,768]{2,1,0:T(8,128)(2,1)S(1)}, bf16[1,256,768]{2,1,0:T(8,128)(2,1)S(1)}, u32[]{:S(2)}, u32[]{:S(2)}) collective-permute-start(bf16[1,256,768]{2,1,0:T(8,128)(2,1)S(1)} %get-tuple-element.394), channel_id=1, source_target_pairs={{0,2},{1,3},{2,0},{3,1},{4,6},{5,7},{6,4},{7,5},{8,10},{9,11},{10,... | collective-permute-start | bytes 1179656 | tf_op jit(solution)/shard_map/ppermute | solution.py:637
  22.7 1.4 collective-permute-start.19
  33.1 35.0 %collective-permute-start.11 = (bf16[2,256,768]{2,1,0:T(8,128)(2,1)S(1)}, bf16[2,256,768]{2,1,0:T(8,128)(2,1)}, u32[]{:S(2)}, u32[]{:S(2)}) collective-permute-start(bf16[2,256,768]{2,1,0:T(8,128)(2,1)S(1)} %get-tuple-element.209.refs_0_), channel_id=1, source_target_pairs={{0,2},{1,3},{2,0},{3,1},{4,6},{5,7},{6,4},{7,5},{8,10},{9,11},{10,... | collective-permute-start | bytes 2359304 | tf_op jit(solution)/shard_map/ppermute | solution.py:637
  33.6 11.8 %collective-permute-start.8 = (bf16[4,24,588]{2,1,0:T(8,128)(2,1)S(1)}, bf16[4,24,588]{2,1,0:T(8,128)(2,1)S(1)}, u32[]{:S(2)}, u32[]{:S(2)}) collective-permute-start(bf16[4,24,588]{2,1,0:T(8,128)(2,1)S(1)} %get-tuple-element.416), channel_id=1, source_target_pairs={{0,16},{4,20},{8,24},{12,28},{16,0},{20,4},{24,8},{28,12},{1,17},{... | collective-permute-start | bytes 338696 | tf_op jit(solution)/shard_map/ppermute | solution.py:637
  36.4 31.6 %collective-permute-start.10 = (bf16[1,256,768]{2,1,0:T(8,128)(2,1)S(1)}, bf16[1,256,768]{2,1,0:T(8,128)(2,1)S(1)}, u32[]{:S(2)}, u32[]{:S(2)}) collective-permute-start(bf16[1,256,768]{2,1,0:T(8,128)(2,1)S(1)} %get-tuple-element.208), channel_id=1, source_target_pairs={{0,2},{1,3},{2,0},{3,1},{4,6},{5,7},{6,4},{7,5},{8,10},{9,11},{10,... | collective-permute-start | bytes 1179656 | tf_op jit(solution)/shard_map/ppermute | solution.py:637
  45.4 8.8 %collective-permute-start.9 = (bf16[2,4,24,588]{3,2,1,0:T(8,128)(2,1)S(1)}, bf16[2,4,24,588]{3,2,1,0:T(8,128)(2,1)S(1)}, u32[]{:S(2)}, u32[]{:S(2)}) collective-permute-start(bf16[2,4,24,588]{3,2,1,0:T(8,128)(2,1)S(1)} %maximum_select_fusion.3), channel_id=1, source_target_pairs={{0,8},{4,12},{8,0},{12,4},{16,24},{20,28},{24,16},{28,20},{1,9},{5... | collective-permute-start | bytes 677384 | tf_op jit(solution)/shard_map/ppermute | solution.py:637
  68.0 9.3 %copy-start.14 = (bf16[2,256,768]{2,1,0:T(8,128)(2,1)}, bf16[2,256,768]{2,1,0:T(8,128)(2,1)S(1)}, u32[]{:S(2)}) copy-start(bf16[2,256,768]{2,1,0:T(8,128)(2,1)S(1)} %pad_maximum_fusion.refs_2_) | copy-start | bytes 2359300
  68.1 8.9 %collective-permute-start.13 = (bf16[2,2,4,24,588]{4,3,2,1,0:T(8,128)(2,1)S(1)}, bf16[2,2,4,24,588]{4,3,2,1,0:T(8,128)(2,1)S(1)}, u32[]{:S(2)}, u32[]{:S(2)}) collective-permute-start(bf16[2,2,4,24,588]{4,3,2,1,0:T(8,128)(2,1)S(1)} %maximum_select_fusion.1), channel_id=1, source_target_pairs={{0,4},{4,0},{8,12},{12,8},{16,20},{20,16},{24,28},{28,24},{1,5},{5... | collective-permute-start | bytes 1354760 | tf_op jit(solution)/shard_map/ppermute | solution.py:637
  69.7 32.1 %collective-permute-start.14 = (bf16[2,256,768]{2,1,0:T(8,128)(2,1)S(1)}, bf16[2,256,768]{2,1,0:T(8,128)(2,1)}, u32[]{:S(2)}, u32[]{:S(2)}) collective-permute-start(bf16[2,256,768]{2,1,0:T(8,128)(2,1)S(1)} %get-tuple-element.209.refs_0_), channel_id=1, source_target_pairs={{0,1},{1,0},{2,3},{3,2},{4,5},{5,4},{6,7},{7,6},{8,9},{9,8},{10,11... | collective-permute-start | bytes 2359304 | tf_op jit(solution)/shard_map/ppermute | solution.py:637
  69.7 11.2 %collective-permute-start = (bf16[2,256,768]{2,1,0:T(8,128)(2,1)}, bf16[2,256,768]{2,1,0:T(8,128)(2,1)}, u32[]{:S(2)}, u32[]{:S(2)}) collective-permute-start(bf16[2,256,768]{2,1,0:T(8,128)(2,1)} %get-tuple-element.397.refs_0_), channel_id=1, source_target_pairs={{0,1},{1,0},{2,3},{3,2},{4,5},{5,4},{6,7},{7,6},{8,9},{9,8},{10,11... | collective-permute-start | bytes 2359304 | tf_op jit(solution)/shard_map/ppermute | solution.py:637
  70.9 31.0 %collective-permute-start.15 = (bf16[2,256,768]{2,1,0:T(8,128)(2,1)}, bf16[2,256,768]{2,1,0:T(8,128)(2,1)}, u32[]{:S(2)}, u32[]{:S(2)}) collective-permute-start(bf16[2,256,768]{2,1,0:T(8,128)(2,1)} %collective-permute-done.11.refs_2_), channel_id=1, source_target_pairs={{0,1},{1,0},{2,3},{3,2},{4,5},{5,4},{6,7},{7,6},{8,9},{9,8},{10,11... | collective-permute-start | bytes 2359304 | tf_op jit(solution)/shard_map/ppermute | solution.py:637
  70.9 10.0 %collective-permute-start.12 = (bf16[2,256,768]{2,1,0:T(8,128)(2,1)S(1)}, bf16[2,256,768]{2,1,0:T(8,128)(2,1)}, u32[]{:S(2)}, u32[]{:S(2)}) collective-permute-start(bf16[2,256,768]{2,1,0:T(8,128)(2,1)S(1)} %pad_maximum_fusion.refs_2_), channel_id=1, source_target_pairs={{0,1},{1,0},{2,3},{3,2},{4,5},{5,4},{6,7},{7,6},{8,9},{9,8},{10,11... | collective-permute-start | bytes 2359304 | tf_op jit(solution)/shard_map/ppermute | solution.py:637
  101.8 7.4 %copy-start.41 = (bf16[2,256,192]{2,1,0:T(8,128)(2,1)S(1)}, bf16[2,256,192]{2,1,0:T(8,128)(2,1)}, u32[]{:S(2)}) copy-start(bf16[2,256,192]{2,1,0:T(8,128)(2,1)} %get-tuple-element.222) | copy-start | bytes 589828
  101.8 8.2 %copy-start.40 = (bf16[2,256,192]{2,1,0:T(8,128)(2,1)S(1)}, bf16[2,256,192]{2,1,0:T(8,128)(2,1)}, u32[]{:S(2)}) copy-start(bf16[2,256,192]{2,1,0:T(8,128)(2,1)} %get-tuple-element.223) | copy-start | bytes 589828
  109.1 15.6 %collective-permute-start.16 = (bf16[2,256,192]{2,1,0:T(8,128)(2,1)S(1)}, bf16[2,256,192]{2,1,0:T(8,128)(2,1)S(1)}, u32[]{:S(2)}, u32[]{:S(2)}) collective-permute-start(bf16[2,256,192]{2,1,0:T(8,128)(2,1)S(1)} %copy-done.42), channel_id=1, source_target_pairs={{0,1},{1,0},{2,3},{3,2},{4,5},{5,4},{6,7},{7,6},{8,9},{9,8},{10,11... | collective-permute-start | bytes 589832 | tf_op jit(solution)/shard_map/ppermute | solution.py:637
  109.2 15.5 %collective-permute-start.17 = (bf16[2,256,192]{2,1,0:T(8,128)(2,1)S(1)}, bf16[2,256,192]{2,1,0:T(8,128)(2,1)S(1)}, u32[]{:S(2)}, u32[]{:S(2)}) collective-permute-start(bf16[2,256,192]{2,1,0:T(8,128)(2,1)S(1)} %copy-done.41), channel_id=1, source_target_pairs={{0,2},{1,3},{2,0},{3,1},{4,6},{5,7},{6,4},{7,5},{8,10},{9,11},{10,... | collective-permute-start | bytes 589832 | tf_op jit(solution)/shard_map/ppermute | solution.py:637
  110.0 14.7 %collective-permute-start.18 = (bf16[2,256,192]{2,1,0:T(8,128)(2,1)S(1)}, bf16[2,256,192]{2,1,0:T(8,128)(2,1)S(1)}, u32[]{:S(2)}, u32[]{:S(2)}) collective-permute-start(bf16[2,256,192]{2,1,0:T(8,128)(2,1)S(1)} %copy-done.40), channel_id=1, source_target_pairs={{0,3},{1,2},{2,1},{3,0},{4,7},{5,6},{6,5},{7,4},{8,11},{9,10},{10,... | collective-permute-start | bytes 589832 | tf_op jit(solution)/shard_map/ppermute | solution.py:637
  111.0 14.8 %copy-start.20 = (bf16[2,256,192]{2,1,0:T(8,128)(2,1)S(1)}, bf16[2,256,192]{2,1,0:T(8,128)(2,1)}, u32[]{:S(2)}) copy-start(bf16[2,256,192]{2,1,0:T(8,128)(2,1)} %get-tuple-element.229) | copy-start | bytes 589828
  124.7 15.0 %collective-permute-start.23 = (bf16[768,3456]{1,0:T(8,128)(2,1)}, bf16[768,3456]{1,0:T(8,128)(2,1)}, u32[]{:S(2)}, u32[]{:S(2)}) collective-permute-start(bf16[768,3456]{1,0:T(8,128)(2,1)} %all-gather.2.cloned.1.call-done.refs_4_), channel_id=1, source_target_pairs={{0,1},{1,0},{2,3},{3,2},{4,5},{5,4},{6,7},{7,6},{8,9},{9,8},{10,11... | collective-permute-start | bytes 15925256 | tf_op jit(solution)/shard_map/ppermute | solution.py:637
  125.2 8.5 %collective-permute-start.22 = (bf16[2,256,192]{2,1,0:T(8,128)(2,1)}, bf16[2,256,192]{2,1,0:T(8,128)(2,1)S(1)}, u32[]{:S(2)}, u32[]{:S(2)}) collective-permute-start(bf16[2,256,192]{2,1,0:T(8,128)(2,1)} %get-tuple-element.243), channel_id=1, source_target_pairs={{0,3},{1,2},{2,1},{3,0},{4,7},{5,6},{6,5},{7,4},{8,11},{9,10},{10,... | collective-permute-start | bytes 589832 | tf_op jit(solution)/shard_map/ppermute | solution.py:637
  125.8 13.8 %collective-permute-start.21 = (bf16[2,256,192]{2,1,0:T(8,128)(2,1)S(1)}, bf16[2,256,192]{2,1,0:T(8,128)(2,1)S(1)}, u32[]{:S(2)}, u32[]{:S(2)}) collective-permute-start(bf16[2,256,192]{2,1,0:T(8,128)(2,1)S(1)} %copy-done.39), channel_id=1, source_target_pairs={{0,2},{1,3},{2,0},{3,1},{4,6},{5,7},{6,4},{7,5},{8,10},{9,11},{10,... | collective-permute-start | bytes 589832 | tf_op jit(solution)/shard_map/ppermute | solution.py:637
  127.2 12.6 %collective-permute-start.20 = (bf16[2,256,192]{2,1,0:T(8,128)(2,1)S(1)}, bf16[2,256,192]{2,1,0:T(8,128)(2,1)S(1)}, u32[]{:S(2)}, u32[]{:S(2)}) collective-permute-start(bf16[2,256,192]{2,1,0:T(8,128)(2,1)S(1)} %copy-done.38), channel_id=1, source_target_pairs={{0,1},{1,0},{2,3},{3,2},{4,5},{5,4},{6,7},{7,6},{8,9},{9,8},{10,11... | collective-permute-start | bytes 589832 | tf_op jit(solution)/shard_map/ppermute | solution.py:637
  127.3 12.5 %copy-start.24 = (bf16[4,256,192]{2,1,0:T(8,128)(2,1)}, bf16[4,256,192]{2,1,0:T(8,128)(2,1)S(1)}, u32[]{:S(2)}) copy-start(bf16[4,256,192]{2,1,0:T(8,128)(2,1)S(1)} %constant_dynamic-update-slice_fusion.4.refs_0_) | copy-start | bytes 1179652
  180.5 2.3 collective-permute-start.24
  180.6 23.4 %collective-permute-start.25 = (bf16[4,256,192]{2,1,0:T(8,128)(2,1)}, bf16[4,256,192]{2,1,0:T(8,128)(2,1)S(1)}, u32[]{:S(2)}, u32[]{:S(2)}) collective-permute-start(bf16[4,256,192]{2,1,0:T(8,128)(2,1)} %get-tuple-element.264), channel_id=1, source_target_pairs={{0,2},{1,3},{2,0},{3,1},{4,6},{5,7},{6,4},{7,5},{8,10},{9,11},{10,... | collective-permute-start | bytes 1179656 | tf_op jit(solution)/shard_map/ppermute | solution.py:637
  181.4 24.5 %collective-permute-start.26 = (bf16[4,256,192]{2,1,0:T(8,128)(2,1)}, bf16[4,256,192]{2,1,0:T(8,128)(2,1)S(1)}, u32[]{:S(2)}, u32[]{:S(2)}) collective-permute-start(bf16[4,256,192]{2,1,0:T(8,128)(2,1)} %get-tuple-element.265), channel_id=1, source_target_pairs={{0,3},{1,2},{2,1},{3,0},{4,7},{5,6},{6,5},{7,4},{8,11},{9,10},{10,... | collective-permute-start | bytes 1179656 | tf_op jit(solution)/shard_map/ppermute | solution.py:637
  208.9 6.0 %collective-permute-start.27 = (bf16[3,2,2,2,2,24,768]{6,5,0,4,1,2,3:T(8,128)(2,1)}, bf16[3,2,2,2,2,24,768]{6,5,0,4,1,2,3:T(8,128)(2,1)}, u32[]{:S(2)}, u32[]{:S(2)}) collective-permute-start(bf16[3,2,2,2,2,24,768]{6,5,0,4,1,2,3:T(8,128)(2,1)} %copy.110), channel_id=1, source_target_pairs={{0,1},{1,0},{2,3},{3,2},{4,5},{5,4},{6,7},{7,6},{8,9},{9,8},{10,11... | collective-permute-start | bytes 5308424 | tf_op jit(solution)/shard_map/ppermute | solution.py:637
  210.5 4.9 %collective-permute-start.28 = (bf16[3,2,2,2,2,24,768]{6,5,0,1,2,3,4:T(8,128)(2,1)}, bf16[3,2,2,2,2,24,768]{6,5,0,1,2,3,4:T(8,128)(2,1)}, u32[]{:S(2)}, u32[]{:S(2)}) collective-permute-start(bf16[3,2,2,2,2,24,768]{6,5,0,1,2,3,4:T(8,128)(2,1)} %copy.111), channel_id=1, source_target_pairs={{0,1},{1,0},{2,3},{3,2},{4,5},{5,4},{6,7},{7,6},{8,9},{9,8},{10,11... | collective-permute-start | bytes 5308424 | tf_op jit(solution)/shard_map/ppermute | solution.py:637
  212.2 5.8 %collective-permute-start.29 = (bf16[3,2,2,2,2,24,768]{6,5,0,1,3,4,2:T(8,128)(2,1)}, bf16[3,2,2,2,2,24,768]{6,5,0,1,3,4,2:T(8,128)(2,1)}, u32[]{:S(2)}, u32[]{:S(2)}) collective-permute-start(bf16[3,2,2,2,2,24,768]{6,5,0,1,3,4,2:T(8,128)(2,1)} %copy.112), channel_id=1, source_target_pairs={{0,1},{1,0},{2,3},{3,2},{4,5},{5,4},{6,7},{7,6},{8,9},{9,8},{10,11... | collective-permute-start | bytes 5308424 | tf_op jit(solution)/shard_map/ppermute | solution.py:637
  227.0 22.7 %collective-permute-start.30 = (bf16[3,2,2,2,24,768]{5,4,0,3,1,2:T(8,128)(2,1)S(1)}, bf16[3,2,2,2,24,768]{5,4,0,3,1,2:T(8,128)(2,1)}, u32[]{:S(2)}, u32[]{:S(2)}) collective-permute-start(bf16[3,2,2,2,24,768]{5,4,0,3,1,2:T(8,128)(2,1)S(1)} %fusion.12), channel_id=1, source_target_pairs={{0,4},{4,0},{8,12},{12,8},{16,20},{20,16},{24,28},{28,24},{1,5},{5... | collective-permute-start | bytes 2654216 | tf_op jit(solution)/shard_map/ppermute | solution.py:637
  228.6 21.7 %collective-permute-start.31 = (bf16[3,2,2,2,24,768]{5,4,0,1,2,3:T(8,128)(2,1)S(1)}, bf16[3,2,2,2,24,768]{5,4,0,1,2,3:T(8,128)(2,1)}, u32[]{:S(2)}, u32[]{:S(2)}) collective-permute-start(bf16[3,2,2,2,24,768]{5,4,0,1,2,3:T(8,128)(2,1)S(1)} %fusion.13), channel_id=1, source_target_pairs={{0,2},{1,3},{2,0},{3,1},{4,6},{5,7},{6,4},{7,5},{8,10},{9,11},{10,... | collective-permute-start | bytes 2654216 | tf_op jit(solution)/shard_map/ppermute | solution.py:637
  229.1 21.4 %collective-permute-start.32 = (bf16[3,2,2,2,24,768]{5,4,0,1,2,3:T(8,128)(2,1)S(1)}, bf16[3,2,2,2,24,768]{5,4,0,1,2,3:T(8,128)(2,1)}, u32[]{:S(2)}, u32[]{:S(2)}) collective-permute-start(bf16[3,2,2,2,24,768]{5,4,0,1,2,3:T(8,128)(2,1)S(1)} %fusion.14), channel_id=1, source_target_pairs={{0,8},{4,12},{8,0},{12,4},{16,24},{20,28},{24,16},{28,20},{1,9},{5... | collective-permute-start | bytes 2654216 | tf_op jit(solution)/shard_map/ppermute | solution.py:637
  255.0 16.0 %collective-permute-start.34 = (bf16[3,2,2,24,768]{4,3,0,2,1:T(8,128)(2,1)S(1)}, bf16[3,2,2,24,768]{4,3,0,2,1:T(8,128)(2,1)S(1)}, u32[]{:S(2)}, u32[]{:S(2)}) collective-permute-start(bf16[3,2,2,24,768]{4,3,0,2,1:T(8,128)(2,1)S(1)} %fusion.18), channel_id=1, source_target_pairs={{0,8},{4,12},{8,0},{12,4},{16,24},{20,28},{24,16},{28,20},{1,9},{5... | collective-permute-start | bytes 1327112 | tf_op jit(solution)/shard_map/ppermute | solution.py:637
  256.7 14.3 %collective-permute-start.35 = (bf16[3,2,2,24,768]{4,3,0,1,2:T(8,128)(2,1)S(1)}, bf16[3,2,2,24,768]{4,3,0,1,2:T(8,128)(2,1)S(1)}, u32[]{:S(2)}, u32[]{:S(2)}) collective-permute-start(bf16[3,2,2,24,768]{4,3,0,1,2:T(8,128)(2,1)S(1)} %fusion.19), channel_id=1, source_target_pairs={{0,4},{4,0},{8,12},{12,8},{16,20},{20,16},{24,28},{28,24},{1,5},{5... | collective-permute-start | bytes 1327112 | tf_op jit(solution)/shard_map/ppermute | solution.py:637
  257.1 13.9 %collective-permute-start.36 = (bf16[3,2,2,24,768]{4,3,0,1,2:T(8,128)(2,1)S(1)}, bf16[3,2,2,24,768]{4,3,0,1,2:T(8,128)(2,1)S(1)}, u32[]{:S(2)}, u32[]{:S(2)}) collective-permute-start(bf16[3,2,2,24,768]{4,3,0,1,2:T(8,128)(2,1)S(1)} %fusion.20), channel_id=1, source_target_pairs={{0,2},{1,3},{2,0},{3,1},{4,6},{5,7},{6,4},{7,5},{8,10},{9,11},{10,... | collective-permute-start | bytes 1327112 | tf_op jit(solution)/shard_map/ppermute | solution.py:637
  264.3 7.2 %collective-permute-start.33 = (bf16[2,2,256,768]{3,2,1,0:T(8,128)(2,1)}, bf16[2,2,256,768]{3,2,1,0:T(8,128)(2,1)S(1)}, u32[]{:S(2)}, u32[]{:S(2)}) collective-permute-start(bf16[2,2,256,768]{3,2,1,0:T(8,128)(2,1)} %get-tuple-element.292), channel_id=1, source_target_pairs={{0,1},{1,0},{2,3},{3,2},{4,5},{5,4},{6,7},{7,6},{8,9},{9,8},{10,11... | collective-permute-start | bytes 4718600 | tf_op jit(solution)/shard_map/ppermute | solution.py:637
  273.3 24.1 %collective-permute-start.37 = (bf16[2,256,768]{2,1,0:T(8,128)(2,1)S(1)}, bf16[2,256,768]{2,1,0:T(8,128)(2,1)S(1)}, u32[]{:S(2)}, u32[]{:S(2)}) collective-permute-start(bf16[2,256,768]{2,1,0:T(8,128)(2,1)S(1)} %fusion.15), channel_id=1, source_target_pairs={{0,2},{1,3},{2,0},{3,1},{4,6},{5,7},{6,4},{7,5},{8,10},{9,11},{10,... | collective-permute-start | bytes 2359304 | tf_op jit(solution)/shard_map/ppermute | solution.py:637
  273.8 23.5 %collective-permute-start.38 = (bf16[3,2,24,768]{3,2,0,1:T(8,128)(2,1)S(1)}, bf16[3,2,24,768]{3,2,0,1:T(8,128)(2,1)S(1)}, u32[]{:S(2)}, u32[]{:S(2)}) collective-permute-start(bf16[3,2,24,768]{3,2,0,1:T(8,128)(2,1)S(1)} %fusion.21), channel_id=1, source_target_pairs={{0,16},{4,20},{8,24},{12,28},{16,0},{20,4},{24,8},{28,12},{1,17},{... | collective-permute-start | bytes 663560 | tf_op jit(solution)/shard_map/ppermute | solution.py:637
  276.6 20.7 %collective-permute-start.39 = (bf16[3,2,24,768]{3,2,0,1:T(8,128)(2,1)S(1)}, bf16[3,2,24,768]{3,2,0,1:T(8,128)(2,1)S(1)}, u32[]{:S(2)}, u32[]{:S(2)}) collective-permute-start(bf16[3,2,24,768]{3,2,0,1:T(8,128)(2,1)S(1)} %fusion.22), channel_id=1, source_target_pairs={{0,8},{4,12},{8,0},{12,4},{16,24},{20,28},{24,16},{28,20},{1,9},{5... | collective-permute-start | bytes 663560 | tf_op jit(solution)/shard_map/ppermute | solution.py:637
  277.0 20.3 %collective-permute-start.40 = (bf16[3,2,24,768]{3,2,0,1:T(8,128)(2,1)S(1)}, bf16[3,2,24,768]{3,2,0,1:T(8,128)(2,1)S(1)}, u32[]{:S(2)}, u32[]{:S(2)}) collective-permute-start(bf16[3,2,24,768]{3,2,0,1:T(8,128)(2,1)S(1)} %fusion.23), channel_id=1, source_target_pairs={{0,4},{4,0},{8,12},{12,8},{16,20},{20,16},{24,28},{28,24},{1,5},{5... | collective-permute-start | bytes 663560 | tf_op jit(solution)/shard_map/ppermute | solution.py:637
  297.4 8.8 %copy-start.16 = (bf16[2,256,768]{2,1,0:T(8,128)(2,1)}, bf16[2,256,768]{2,1,0:T(8,128)(2,1)S(1)}, u32[]{:S(2)}) copy-start(bf16[2,256,768]{2,1,0:T(8,128)(2,1)S(1)} %collective-permute-done.37) | copy-start | bytes 2359300
  312.2 13.8 %collective-permute-start.42 = (bf16[2,2,256,768]{3,2,1,0:T(8,128)(2,1)}, bf16[2,2,256,768]{3,2,1,0:T(8,128)(2,1)S(1)}, u32[]{:S(2)}, u32[]{:S(2)}) collective-permute-start(bf16[2,2,256,768]{3,2,1,0:T(8,128)(2,1)} %get-tuple-element.332), channel_id=1, source_target_pairs={{0,1},{1,0},{2,3},{3,2},{4,5},{5,4},{6,7},{7,6},{8,9},{9,8},{10,11... | collective-permute-start | bytes 4718600 | tf_op jit(solution)/shard_map/ppermute | solution.py:637
  312.4 13.7 %collective-permute-start.41 = (bf16[2,2,4,24,588]{4,3,2,1,0:T(8,128)(2,1)S(1)}, bf16[2,2,4,24,588]{4,3,2,1,0:T(8,128)(2,1)S(1)}, u32[]{:S(2)}, u32[]{:S(2)}) collective-permute-start(bf16[2,2,4,24,588]{4,3,2,1,0:T(8,128)(2,1)S(1)} %fusion.17), channel_id=1, source_target_pairs={{0,4},{4,0},{8,12},{12,8},{16,20},{20,16},{24,28},{28,24},{1,5},{5... | collective-permute-start | bytes 1354760 | tf_op jit(solution)/shard_map/ppermute | solution.py:637
  313.0 13.1 %copy-start.9 = (bf16[2,2,256,768]{3,2,1,0:T(8,128)(2,1)S(1)}, bf16[2,2,256,768]{3,2,1,0:T(8,128)(2,1)}, u32[]{:S(2)}) copy-start(bf16[2,2,256,768]{3,2,1,0:T(8,128)(2,1)} %get-tuple-element.334) | copy-start | bytes 4718596
  315.2 15.8 %collective-permute-start.47 = (bf16[3,24,768]{2,1,0:T(8,128)(2,1)S(1)}, bf16[3,24,768]{2,1,0:T(8,128)(2,1)S(1)}, u32[]{:S(2)}, u32[]{:S(2)}) collective-permute-start(bf16[3,24,768]{2,1,0:T(8,128)(2,1)S(1)} %fusion.27), channel_id=1, source_target_pairs={{0,2},{1,3},{2,0},{3,1},{4,6},{5,7},{6,4},{7,5},{8,10},{9,11},{10,... | collective-permute-start | bytes 331784 | tf_op jit(solution)/shard_map/ppermute | solution.py:637
  316.8 14.4 %collective-permute-start.48 = (bf16[3,24,768]{2,1,0:T(8,128)(2,1)S(1)}, bf16[3,24,768]{2,1,0:T(8,128)(2,1)S(1)}, u32[]{:S(2)}, u32[]{:S(2)}) collective-permute-start(bf16[3,24,768]{2,1,0:T(8,128)(2,1)S(1)} %fusion.28), channel_id=1, source_target_pairs={{0,16},{4,20},{8,24},{12,28},{16,0},{20,4},{24,8},{28,12},{1,17},{... | collective-permute-start | bytes 331784 | tf_op jit(solution)/shard_map/ppermute | solution.py:637
  316.9 16.8 %collective-permute-start.49 = (bf16[3,24,768]{2,1,0:T(8,128)(2,1)S(1)}, bf16[3,24,768]{2,1,0:T(8,128)(2,1)}, u32[]{:S(2)}, u32[]{:S(2)}) collective-permute-start(bf16[3,24,768]{2,1,0:T(8,128)(2,1)S(1)} %fusion.29), channel_id=1, source_target_pairs={{0,16},{4,20},{8,24},{12,28},{16,0},{20,4},{24,8},{28,12},{1,17},{... | collective-permute-start | bytes 331784 | tf_op jit(solution)/shard_map/ppermute | solution.py:637
  327.4 19.5 %collective-permute-start.46 = (bf16[2,256,768]{2,1,0:T(8,128)(2,1)}, bf16[2,256,768]{2,1,0:T(8,128)(2,1)}, u32[]{:S(2)}, u32[]{:S(2)}) collective-permute-start(bf16[2,256,768]{2,1,0:T(8,128)(2,1)} %fusion.16), channel_id=1, source_target_pairs={{0,2},{1,3},{2,0},{3,1},{4,6},{5,7},{6,4},{7,5},{8,10},{9,11},{10,... | collective-permute-start | bytes 2359304 | tf_op jit(solution)/shard_map/ppermute | solution.py:637
  329.2 8.2 %collective-permute-start.43 = (bf16[4,24,588]{2,1,0:T(8,128)(2,1)S(1)}, bf16[4,24,588]{2,1,0:T(8,128)(2,1)S(1)}, u32[]{:S(2)}, u32[]{:S(2)}) collective-permute-start(bf16[4,24,588]{2,1,0:T(8,128)(2,1)S(1)} %get-tuple-element.400), channel_id=1, source_target_pairs={{0,8},{4,12},{8,0},{12,4},{16,24},{20,28},{24,16},{28,20},{1,9},{5... | collective-permute-start | bytes 338696 | tf_op jit(solution)/shard_map/ppermute | solution.py:637
  331.0 10.8 %collective-permute-start.44 = (bf16[4,24,588]{2,1,0:T(8,128)(2,1)S(1)}, bf16[4,24,588]{2,1,0:T(8,128)(2,1)S(1)}, u32[]{:S(2)}, u32[]{:S(2)}) collective-permute-start(bf16[4,24,588]{2,1,0:T(8,128)(2,1)S(1)} %get-tuple-element.399), channel_id=1, source_target_pairs={{0,16},{4,20},{8,24},{12,28},{16,0},{20,4},{24,8},{28,12},{1,17},{... | collective-permute-start | bytes 338696 | tf_op jit(solution)/shard_map/ppermute | solution.py:637
  331.1 10.7 %collective-permute-start.45 = (bf16[4,24,588]{2,1,0:T(8,128)(2,1)S(1)}, bf16[4,24,588]{2,1,0:T(8,128)(2,1)S(1)}, u32[]{:S(2)}, u32[]{:S(2)}) collective-permute-start(bf16[4,24,588]{2,1,0:T(8,128)(2,1)S(1)} %get-tuple-element.398), channel_id=1, source_target_pairs={{0,24},{4,28},{8,16},{12,20},{16,8},{20,12},{24,0},{28,4},{1,25},{... | collective-permute-start | bytes 338696 | tf_op jit(solution)/shard_map/ppermute | solution.py:637
  346.9 8.1 %collective-permute-start.50 = (bf16[24,588]{1,0:T(8,128)(2,1)S(1)}, bf16[24,588]{1,0:T(8,128)(2,1)S(1)}, u32[]{:S(2)}, u32[]{:S(2)}) collective-permute-start(bf16[24,588]{1,0:T(8,128)(2,1)S(1)} %get-tuple-element.367), channel_id=1, source_target_pairs={{0,1},{1,0},{2,3},{3,2},{4,5},{5,4},{6,7},{7,6},{8,9},{9,8},{10,11... | collective-permute-start | bytes 84680 | tf_op jit(solution)/shard_map/ppermute | solution.py:637
  347.0 8.0 %collective-permute-start.51 = (bf16[24,588]{1,0:T(8,128)(2,1)S(1)}, bf16[24,588]{1,0:T(8,128)(2,1)S(1)}, u32[]{:S(2)}, u32[]{:S(2)}) collective-permute-start(bf16[24,588]{1,0:T(8,128)(2,1)S(1)} %get-tuple-element.368), channel_id=1, source_target_pairs={{0,2},{1,3},{2,0},{3,1},{4,6},{5,7},{6,4},{7,5},{8,10},{9,11},{10,... | collective-permute-start | bytes 84680 | tf_op jit(solution)/shard_map/ppermute | solution.py:637
  348.6 6.5 %collective-permute-start.52 = (bf16[24,588]{1,0:T(8,128)(2,1)S(1)}, bf16[24,588]{1,0:T(8,128)(2,1)S(1)}, u32[]{:S(2)}, u32[]{:S(2)}) collective-permute-start(bf16[24,588]{1,0:T(8,128)(2,1)S(1)} %get-tuple-element.369), channel_id=1, source_target_pairs={{0,3},{1,2},{2,1},{3,0},{4,7},{5,6},{6,5},{7,4},{8,11},{9,10},{10,... | collective-permute-start | bytes 84680 | tf_op jit(solution)/shard_map/ppermute | solution.py:637
  (33 other events, 92.1 us)
Sparse Core Ops, SparseCore 0:
  25.0 94.2 all-gather.1

commit v8 on v7

--- a/solution.py
+++ b/solution.py
@@ -193,15 +193,26 @@
     side = width // 2
     inner = spans // 2
 
+    core = lax.bitwise_and(me, 1)
+    cuts = (0, side, side + width * inner, side + 2 * width * inner)
+
+    def arrivals(sections):
+        return [
+            pltpu.make_async_copy(
+                source.at[:, cuts[section] : cuts[section + 1]],
+                rest_ref.at[half, :, cuts[section] : cuts[section + 1]],
+                sems.at[number, section],
+            )
+            for section in sections
+            for number, (source, half) in enumerate(((mine_ref, core), (other_ref, 1 - core)))
+        ]
+
     @pl.when(pl.program_id(0) == 0)
     def _():
-        core = lax.bitwise_and(me, 1)
-        mine = pltpu.make_async_copy(mine_ref, rest_ref.at[core], sems.at[0])
-        other = pltpu.make_async_copy(other_ref, rest_ref.at[1 - core], sems.at[1])
-        mine.start()
-        other.start()
-        mine.wait()
-        other.wait()
+        for copy in arrivals((0, 1, 2)):
+            copy.start()
+        for copy in arrivals((0,)):
+            copy.wait()
 
     def output_rows(place, half):
         first = pl.multiple_of(lax.bitwise_xor(me, place) * group, group)
@@ -221,6 +232,12 @@
     normed_ref[...] = normed.T
     result = residual + param(7 + spans)
     grad_normed = jnp.zeros(residual.shape, F32)
+
+    @pl.when(pl.program_id(0) == 0)
+    def _():
+        for copy in arrivals((1, 2)):
+            copy.wait()
+
     sums = []
     for span in range(spans):
         half, low = span // inner, side + width * (span % inner)
@@ -294,7 +311,7 @@
             ]
             + [by_seq(blk, group)] * n_ctx
             + [pl.BlockSpec((4 + spans, width), lambda s, m: (0, 0))],
-            scratch_shapes=[pltpu.VMEM((2,) + mine.shape, BF16), pltpu.SemaphoreType.DMA((2,))],
+            scratch_shapes=[pltpu.VMEM((2,) + mine.shape, BF16), pltpu.SemaphoreType.DMA((2, 3))],
         ),
         out_shape=[
             jax.ShapeDtypeStruct((seqs, blk, width), BF16),
@@ -468,22 +485,29 @@
     )(me, grad, normed, params, weight, table, *earlier)
 
 
-def unproject_kernel(n_blk, grad_ref, weight_ref, kept_ref, sent_ref):
-    for place in range(n_blk):
-        share = dot(grad_ref[place, 0], weight_ref[...], ((1,), (1,))).astype(BF16)
-        (sent_ref if place % 2 else kept_ref)[place // 2, 0] = share
+def unproject_kernel(grad_ref, weight_ref, kept_ref, sent_ref):
+    share = dot(grad_ref[0, 0], weight_ref[...], ((1,), (1,))).astype(BF16)
+    odd = pl.program_id(1) % 2
+
+    @pl.when(odd == 0)
+    def _():
+        kept_ref[0, 0] = share
+
+    @pl.when(odd == 1)
+    def _():
+        sent_ref[0, 0] = share
 
 
 def unproject(grad, weight):
     n_blk, count, blk, cols = grad.shape
     width = weight.shape[0]
-    out = pl.BlockSpec((n_blk // 2, 1, blk, width), lambda s: (0, s, 0, 0))
+    out = pl.BlockSpec((1, 1, blk, width), lambda s, k: (k // 2, s, 0, 0))
     return pl.pallas_call(
-        functools.partial(unproject_kernel, n_blk),
-        grid=(count,),
+        unproject_kernel,
+        grid=(count, n_blk),
         in_specs=[
-            pl.BlockSpec((n_blk, 1, blk, cols), lambda s: (0, s, 0, 0)),
-            pl.BlockSpec(weight.shape, lambda s: (0, 0)),
+            pl.BlockSpec((1, 1, blk, cols), lambda s, k: (k, s, 0, 0)),
+            pl.BlockSpec(weight.shape, lambda s, k: (0, 0)),
         ],
         out_specs=[out, out],
         out_shape=[jax.ShapeDtypeStruct((n_blk // 2, count, blk, width), BF16)] * 2,

time: 373 us -> 379 us (1.016)
  Pallas kernels: 174 us -> 180 us
    pallas_call x2, Pallas kernels: 11.7 us -> 17.8 us  [unproject(): pl.pallas_call(unproject_kernel, grid=(count, n_blk), in_specs=[pl.BlockS...]
where the time goes in v8:
time: 379 us; the launch traced here: 372 us
  Pallas kernels  180 us (47%)
  waiting for transfers between devices  76.9 us (20%)
  starting transfers between devices  48.6 us (13%)
  local copies, waits for them, and re-layouts  27.3 us (7%)
  other arithmetic  23.8 us (6%)
  between operations  15.8 us (4%)
    ppermute x53, waiting for transfers between devices, swap(): lax.ppermute(value, axis, [(place, place ^ mask) for place in range(sizes...  76.8 us
    ppermute x53, starting transfers between devices, swap(): lax.ppermute(value, axis, [(place, place ^ mask) for place in range(sizes...  48.5 us
    pallas_call x1, Pallas kernels, layer(): pl.pallas_call(functools.partial(layer_kernel, n_ctx, spans), grid_spec=p...  39.5 us
    pallas_call x2, Pallas kernels, attend_backward(): pl.pallas_call(functools.partial(backward_kernel, n_blk, blk, heads), gri...  38 us
    pallas_call x2, Pallas kernels, attend_forward(): pl.pallas_call(functools.partial(forward_kernel, n_blk, blk, heads), grid...  27.2 us
    pallas_call x1, Pallas kernels, weigh(): pl.pallas_call(functools.partial(weigh_kernel, n_ctx, last), grid_spec=pl...  21.2 us
    pallas_call x2, Pallas kernels, unproject(): pl.pallas_call(unproject_kernel, grid=(count, n_blk), in_specs=[pl.BlockS...  17.8 us
    pallas_call x2, Pallas kernels, collect(): pl.pallas_call(functools.partial(collect_kernel, n_blk, not earlier, last...  15.4 us
  transfers between devices with their start and end apart: 54, of which 18 were waited for; matrix products, arithmetic and copies ran while one was open for 8% of the time, Pallas kernels for 32%

profile of v8, /device:TPU:0, one launch (start us, length us, event | category | flops | bytes accessed | tf_op | source)
XLA Modules:
  0.0 371.9 jit_solution(4082804476777889122)
XLA Ops:
  7.3 3.0 collective-permute-start.5
  12.2 1.0 dynamic-slice_reduce_fusion
  14.9 1.3 collective-permute-start.3
  17.2 1.2 reshape.462
  18.6 1.3 reshape.463
  24.9 8.1 %collective-permute-done.7 = bf16[1,256,768]{2,1,0:T(8,128)(2,1)S(1)} collective-permute-done((bf16[1,256,768]{2,1,0:T(8,128)(2,1)S(1)}, bf16[1,256,768]{2,1,0:T(8,128)(2,1)S(1)}, u32[]{:S(2)}, u32[]{:S(2)}) %collective-permute-start.7) | collective-permute-done | bytes 393248 | tf_op jit(solution)/shard_map/ppermute | solution.py:661
  33.6 2.8 collective-permute-start.8
  36.4 1.5 collective-permute-start.10
  37.8 7.5 %collective-permute-done.8 = bf16[4,24,588]{2,1,0:T(8,128)(2,1)S(1)} collective-permute-done((bf16[4,24,588]{2,1,0:T(8,128)(2,1)S(1)}, bf16[4,24,588]{2,1,0:T(8,128)(2,1)S(1)}, u32[]{:S(2)}, u32[]{:S(2)}) %collective-permute-start.8) | collective-permute-done | bytes 112928 | tf_op jit(solution)/shard_map/ppermute | solution.py:661
  45.4 2.4 collective-permute-start.9
  47.8 6.4 %collective-permute-done.9 = bf16[2,4,24,588]{3,2,1,0:T(8,128)(2,1)S(1)} collective-permute-done((bf16[2,4,24,588]{3,2,1,0:T(8,128)(2,1)S(1)}, bf16[2,4,24,588]{3,2,1,0:T(8,128)(2,1)S(1)}, u32[]{:S(2)}, u32[]{:S(2)}) %collective-permute-start.9) | collective-permute-done | bytes 225824 | tf_op jit(solution)/shard_map/ppermute | solution.py:661
  54.3 13.6 %collective-permute-done.10 = bf16[1,256,768]{2,1,0:T(8,128)(2,1)S(1)} collective-permute-done((bf16[1,256,768]{2,1,0:T(8,128)(2,1)S(1)}, bf16[1,256,768]{2,1,0:T(8,128)(2,1)S(1)}, u32[]{:S(2)}, u32[]{:S(2)}) %collective-permute-start.10) | collective-permute-done | bytes 393248 | tf_op jit(solution)/shard_map/ppermute | solution.py:661
  68.1 1.6 collective-permute-start.13
  71.4 5.6 %collective-permute-done.13 = bf16[2,2,4,24,588]{4,3,2,1,0:T(8,128)(2,1)S(1)} collective-permute-done((bf16[2,2,4,24,588]{4,3,2,1,0:T(8,128)(2,1)S(1)}, bf16[2,2,4,24,588]{4,3,2,1,0:T(8,128)(2,1)S(1)}, u32[]{:S(2)}, u32[]{:S(2)}) %collective-permute-start.13) | collective-permute-done | bytes 451616 | tf_op jit(solution)/shard_map/ppermute | solution.py:661
  80.9 7.3 %project.2 = (bf16[4,2,256,576]{3,2,1,0:T(8,128)(2,1)}, bf16[4,2,256,768]{3,2,1,0:T(8,128)(2,1)}) custom-call(bf16[2,256,768]{2,1,0:T(8,128)(2,1)} %get-tuple-element.397.refs_0_, bf16[2,256,768]{2,1,0:T(8,128)(2,1)} %collective-permute-done.refs_1_, bf16[2,256,768]{2,1,0:T(8,128)(2,1)} %copy-done.14, bf16[2,256,768]{2,1,0:T(8,128)(2,1)} %collective-permute-done.12.refs_3_, ...), custom_call_target="tpu_custom_call" | custom-call | flops 20000000000 | bytes 1000000 | tf_op jit(solution)/shard_map/project/pallas_call | solution.py:74
  88.2 13.6 %attend_forward.2 = (bf16[2,256,192]{2,1,0:T(8,128)(2,1)}, bf16[2,256,192]{2,1,0:T(8,128)(2,1)}, bf16[2,256,192]{2,1,0:T(8,128)(2,1)}, bf16[2,256,192]{2,1,0:T(8,128)(2,1)}, f32[2,3,1024]{2,1,0:T(4,128)}) custom-call(s32[1]{0:T(128)} %bitcast.me_ref, bf16[4,2,256,576]{3,2,1,0:T(8,128)(2,1)} %get-tuple-element.278.joint_ref, ...), custom_call_target="tpu_custom_call" | custom-call | flops 20000000000 | bytes 1000000 | tf_op jit(solution)/shard_map/attend_forward/pallas_call | solution.py:152
  101.8 7.2 %project.3 = (bf16[4,2,256,576]{3,2,1,0:T(8,128)(2,1)}, bf16[4,2,256,768]{3,2,1,0:T(8,128)(2,1)}) custom-call(bf16[2,256,768]{2,1,0:T(8,128)(2,1)} %copy-done.15, bf16[2,256,768]{2,1,0:T(8,128)(2,1)} %collective-permute-done.14.refs_1_, bf16[2,256,768]{2,1,0:T(8,128)(2,1)} %collective-permute-done.11.refs_2_, ...), custom_call_target="tpu_custom_call" | custom-call | flops 20000000000 | bytes 1000000 | tf_op jit(solution)/shard_map/project/pallas_call | solution.py:74
  111.0 13.6 %attend_forward.3 = (bf16[2,256,192]{2,1,0:T(8,128)(2,1)}, bf16[2,256,192]{2,1,0:T(8,128)(2,1)}, bf16[2,256,192]{2,1,0:T(8,128)(2,1)}, bf16[2,256,192]{2,1,0:T(8,128)(2,1)}, f32[2,3,1024]{2,1,0:T(4,128)}) custom-call(s32[1]{0:T(128)} %bitcast.me_ref, bf16[4,2,256,576]{3,2,1,0:T(8,128)(2,1)} %get-tuple-element.315.joint_ref, ...), custom_call_target="tpu_custom_call" | custom-call | flops 20000000000 | bytes 1000000 | tf_op jit(solution)/shard_map/attend_forward/pallas_call | solution.py:152
  125.8 1.3 collective-permute-start.21
  127.3 6.5 %collective-permute-done.22 = bf16[2,256,192]{2,1,0:T(8,128)(2,1)S(1)} collective-permute-done((bf16[2,256,192]{2,1,0:T(8,128)(2,1)}, bf16[2,256,192]{2,1,0:T(8,128)(2,1)S(1)}, u32[]{:S(2)}, u32[]{:S(2)}) %collective-permute-start.22) | collective-permute-done | bytes 196640 | tf_op jit(solution)/shard_map/ppermute | solution.py:661
  133.8 5.9 %collective-permute-done.21 = bf16[2,256,192]{2,1,0:T(8,128)(2,1)S(1)} collective-permute-done((bf16[2,256,192]{2,1,0:T(8,128)(2,1)S(1)}, bf16[2,256,192]{2,1,0:T(8,128)(2,1)S(1)}, u32[]{:S(2)}, u32[]{:S(2)}) %collective-permute-start.21) | collective-permute-done | bytes 196640 | tf_op jit(solution)/shard_map/ppermute | solution.py:661
  140.7 39.5 %layer.1 = (bf16[4,256,768]{2,1,0:T(8,128)(2,1)}, f32[4,256,768]{2,1,0:T(8,128)}, bf16[4,256,768]{2,1,0:T(8,128)(2,1)}, bf16[768,1024]{1,0:T(8,128)(2,1)}, bf16[...) custom-call(s32[1]{0:T(128)} %bitcast.me_ref, ...), custom_call_target="tpu_custom_call" | custom-call | flops 20000000000 | bytes 1000000 | tf_op jit(solution)/shard_map/layer/pallas_call | solution.py:295
  181.2 1.0 collective-permute-start.26
  182.6 21.2 %weigh.1 = (bf16[3,16,24,768]{3,2,1,0:T(8,128)(2,1)}, bf16[3,16,24,768]{3,2,1,0:T(8,128)(2,1)}, bf16[3,16,24,768]{3,2,1,0:T(8,128)(2,1)}, bf16[3,16,24,768]{3,2,...) custom-call(s32[1]{0:T(128)} %bitcast.me_ref, ...), custom_call_target="tpu_custom_call" | custom-call | flops 20000000000 | bytes 1000000 | tf_op jit(solution)/shard_map/weigh/pallas_call | solution.py:569
  203.8 1.9 collective-permute-done.26.refs_3_
  205.7 3.0 copy.110
  209.0 1.3 copy.111
  210.5 1.4 copy.112
  215.2 2.5 collective-permute-done.29
  217.8 1.9 convert_add_fusion
  219.9 1.2 copy-done.5
  221.2 1.9 convert_add_fusion.1
  223.3 1.2 copy-done.4
  224.6 2.0 convert_add_fusion.2
  226.8 1.6 collective-permute-start.30
  228.9 1.7 collective-permute-start.32
  230.6 19.0 %attend_backward.2.grad_ref = bf16[4,2,256,576]{3,2,1,0:T(8,128)(2,1)} custom-call(s32[1]{0:T(128)} %bitcast.me_ref, bf16[4,2,256,576]{3,2,1,0:T(8,128)(2,1)} %get-tuple-element.278.joint_ref, bf16[4,256,192]{2,1,0:T(8,128)(2,1)} %get-tuple-element.279.refs_0_, bf16[4,256,192]{2,1,0:T(8,128)(2,1)} %collective-permute-done.24.refs_1_, ...), custom_call_target="tpu_custom_call" | custom-call | flops 20000000000 | bytes 1000000 | tf_op jit(solution)/shard_map/attend_backward/pallas_call | solution.py:397
  250.3 1.3 convert_add_fusion.5
  251.8 1.3 convert_add_fusion.6
  253.3 1.3 convert_add_fusion.7
  254.7 1.7 collective-permute-start.34
  256.9 1.5 collective-permute-start.36
  258.4 8.8 %unproject.2 = (bf16[2,2,256,768]{3,2,1,0:T(8,128)(2,1)}, bf16[2,2,256,768]{3,2,1,0:T(8,128)(2,1)}) custom-call(bf16[4,2,256,576]{3,2,1,0:T(8,128)(2,1)} %attend_backward.2.grad_ref, bf16[768,576]{1,0:T(8,128)(2,1)} %bitcast.150), custom_call_target="tpu_custom_call" | custom-call | flops 20000000000 | bytes 1000000 | tf_op jit(solution)/shard_map/unproject/pallas_call | solution.py:505
  267.3 6.6 %collect.2 = (f32[768,588]{1,0:T(8,128)}, f32[1,576]{1,0:T(1,128)}) custom-call(s32[1]{0:T(128)} %bitcast.me_ref, bf16[4,2,256,576]{3,2,1,0:T(8,128)(2,1)} %attend_backward.2.grad_ref, bf16[4,2,256,768]{3,2,1,0:T(8,128)(2,1)} %get-tuple-element.293.normed_ref, f32[12,768]{1,0:T(8,128)} %pad_maximum_fusion.9.refs_4_.refs_6_.params_ref, ...), custom_call_target="tpu_custom_call" | custom-call | flops 20000000000 | bytes 1000000 | tf_op jit(solution)/shard_map/collect/pallas_call | solution.py:472
  274.5 1.2 copy-done.10
  276.8 2.8 collective-permute-start.38
  279.9 1.6 collective-permute-start.40
  281.5 19.0 %attend_backward.3.grad_ref = bf16[4,2,256,576]{3,2,1,0:T(8,128)(2,1)} custom-call(s32[1]{0:T(128)} %bitcast.me_ref, bf16[4,2,256,576]{3,2,1,0:T(8,128)(2,1)} %get-tuple-element.315.joint_ref, bf16[4,256,192]{2,1,0:T(8,128)(2,1)} %get-tuple-element.279.refs_0_, bf16[4,256,192]{2,1,0:T(8,128)(2,1)} %collective-permute-done.24.refs_1_, ...), custom_call_target="tpu_custom_call" | custom-call | flops 20000000000 | bytes 1000000 | tf_op jit(solution)/shard_map/attend_backward/pallas_call | solution.py:397
  300.6 8.8 %collect.3 = (f32[768,588]{1,0:T(8,128)}, f32[1,576]{1,0:T(1,128)}) custom-call(s32[1]{0:T(128)} %bitcast.me_ref, bf16[4,2,256,576]{3,2,1,0:T(8,128)(2,1)} %attend_backward.3.grad_ref, bf16[4,2,256,768]{3,2,1,0:T(8,128)(2,1)} %get-tuple-element.328.normed_ref, f32[12,768]{1,0:T(8,128)} %pad_maximum_fusion.9.refs_4_.refs_6_.params_ref, ...), custom_call_target="tpu_custom_call" | custom-call | flops 20000000000 | bytes 1000000 | tf_op jit(solution)/shard_map/collect/pallas_call | solution.py:472
  309.4 8.9 %unproject.3 = (bf16[2,2,256,768]{3,2,1,0:T(8,128)(2,1)}, bf16[2,2,256,768]{3,2,1,0:T(8,128)(2,1)}) custom-call(bf16[4,2,256,576]{3,2,1,0:T(8,128)(2,1)} %attend_backward.3.grad_ref, bf16[768,576]{1,0:T(8,128)(2,1)} %bitcast.153), custom_call_target="tpu_custom_call" | custom-call | flops 20000000000 | bytes 1000000 | tf_op jit(solution)/shard_map/unproject/pallas_call | solution.py:505
  321.3 1.5 collective-permute-start.47
  322.9 2.7 collective-permute-start.49
  325.7 6.4 %collective-permute-done.41 = bf16[2,2,4,24,588]{4,3,2,1,0:T(8,128)(2,1)S(1)} collective-permute-done((bf16[2,2,4,24,588]{4,3,2,1,0:T(8,128)(2,1)S(1)}, bf16[2,2,4,24,588]{4,3,2,1,0:T(8,128)(2,1)S(1)}, u32[]{:S(2)}, u32[]{:S(2)}) %collective-permute-start.41) | collective-permute-done | bytes 451616 | tf_op jit(solution)/shard_map/ppermute | solution.py:661
  333.4 1.5 collective-permute-start.46
  335.3 1.7 collective-permute-start.43
  337.2 2.6 collective-permute-start.45
  339.7 3.7 update.1
  343.5 4.4 %collective-permute-done.44 = bf16[4,24,588]{2,1,0:T(8,128)(2,1)S(1)} collective-permute-done((bf16[4,24,588]{2,1,0:T(8,128)(2,1)S(1)}, bf16[4,24,588]{2,1,0:T(8,128)(2,1)S(1)}, u32[]{:S(2)}, u32[]{:S(2)}) %collective-permute-start.44) | collective-permute-done | bytes 112928 | tf_op jit(solution)/shard_map/ppermute | solution.py:661
  347.9 5.0 %collective-permute-done.46 = bf16[2,256,768]{2,1,0:T(8,128)(2,1)} collective-permute-done((bf16[2,256,768]{2,1,0:T(8,128)(2,1)}, bf16[2,256,768]{2,1,0:T(8,128)(2,1)}, u32[]{:S(2)}, u32[]{:S(2)}) %collective-permute-start.46) | collective-permute-done | bytes 786464 | tf_op jit(solution)/shard_map/ppermute | solution.py:661
  353.1 1.6 collective-permute-start.51
  354.9 1.3 fusion.10
  356.3 1.2 fusion.9
  358.2 2.3 fusion.7
  362.3 2.3 finish.1
  (277 shorter events, 37.9 us)
Async XLA Ops:
  7.2 10.0 %copy-start.12 = (f32[96,768]{1,0:T(8,128)S(1)}, f32[96,768]{1,0:T(8,128)}, u32[]{:S(2)}) copy-start(f32[96,768]{1,0:T(8,128)} %refs_12_.1) | copy-start | bytes 884740
  7.2 10.0 %copy-start.18 = (f32[24,768]{1,0:T(8,128)S(1)}, f32[24,768]{1,0:T(8,128)}, u32[]{:S(2)}) copy-start(f32[24,768]{1,0:T(8,128)} %refs_6_.2) | copy-start | bytes 221188
  7.2 117.5 %all-gather.2.cloned.1.call-start = ((), (), s32[]{:S(2)}) async-start(), calls=%async_computation | async-start | bytes 5640192 | tf_op jit(solution)/shard_map/all_gather | solution.py:742
  7.3 13.8 %collective-permute-start.5 = (s32[4,256]{1,0:T(4,128)}, s32[4,256]{1,0:T(4,128)S(1)}, u32[]{:S(2)}, u32[]{:S(2)}) collective-permute-start(s32[4,256]{1,0:T(4,128)} %param.19), channel_id=1, source_target_pairs={{0,2},{1,3},{2,0},{3,1},{4,6},{5,7},{6,4},{7,5},{8,10},{9,11},{10,... | collective-permute-start | bytes 12296 | tf_op jit(solution)/shard_map/ppermute | solution.py:661
  10.3 11.7 %collective-permute-start.4 = (s32[4,256]{1,0:T(4,128)}, s32[4,256]{1,0:T(4,128)S(1)}, u32[]{:S(2)}, u32[]{:S(2)}) collective-permute-start(s32[4,256]{1,0:T(4,128)} %param.19), channel_id=1, source_target_pairs={{0,1},{1,0},{2,3},{3,2},{4,5},{5,4},{6,7},{7,6},{8,9},{9,8},{10,11... | collective-permute-start | bytes 12296 | tf_op jit(solution)/shard_map/ppermute | solution.py:661
  14.3 10.6 %collective-permute-start.1 = (bf16[24,588]{1,0:T(8,128)(2,1)}, bf16[24,588]{1,0:T(8,128)(2,1)S(1)}, u32[]{:S(2)}, u32[]{:S(2)}) collective-permute-start(bf16[24,588]{1,0:T(8,128)(2,1)} %get-tuple-element.430), channel_id=1, source_target_pairs={{0,1},{1,0},{2,3},{3,2},{4,5},{5,4},{6,7},{7,6},{8,9},{9,8},{10,11... | collective-permute-start | bytes 84680 | tf_op jit(solution)/shard_map/ppermute | solution.py:661
  14.8 10.1 %collective-permute-start.2 = (bf16[24,588]{1,0:T(8,128)(2,1)S(1)}, bf16[24,588]{1,0:T(8,128)(2,1)S(1)}, u32[]{:S(2)}, u32[]{:S(2)}) collective-permute-start(bf16[24,588]{1,0:T(8,128)(2,1)S(1)} %get-tuple-element.431), channel_id=1, source_target_pairs={{0,2},{1,3},{2,0},{3,1},{4,6},{5,7},{6,4},{7,5},{8,10},{9,11},{10,... | collective-permute-start | bytes 84680 | tf_op jit(solution)/shard_map/ppermute | solution.py:661
  14.9 10.1 %collective-permute-start.3 = (bf16[24,588]{1,0:T(8,128)(2,1)S(1)}, bf16[24,588]{1,0:T(8,128)(2,1)S(1)}, u32[]{:S(2)}, u32[]{:S(2)}) collective-permute-start(bf16[24,588]{1,0:T(8,128)(2,1)S(1)} %get-tuple-element.429), channel_id=1, source_target_pairs={{0,3},{1,2},{2,1},{3,0},{4,7},{5,6},{6,5},{7,4},{8,11},{9,10},{10,... | collective-permute-start | bytes 84680 | tf_op jit(solution)/shard_map/ppermute | solution.py:661
  21.1 48.6 %copy-start.15 = (bf16[2,256,768]{2,1,0:T(8,128)(2,1)}, bf16[2,256,768]{2,1,0:T(8,128)(2,1)S(1)}, u32[]{:S(2)}) copy-start(bf16[2,256,768]{2,1,0:T(8,128)(2,1)S(1)} %get-tuple-element.209.refs_0_) | copy-start | bytes 2359300
  21.1 1.6 collective-permute-start.6
  22.0 11.1 %collective-permute-start.7 = (bf16[1,256,768]{2,1,0:T(8,128)(2,1)S(1)}, bf16[1,256,768]{2,1,0:T(8,128)(2,1)S(1)}, u32[]{:S(2)}, u32[]{:S(2)}) collective-permute-start(bf16[1,256,768]{2,1,0:T(8,128)(2,1)S(1)} %get-tuple-element.394), channel_id=1, source_target_pairs={{0,2},{1,3},{2,0},{3,1},{4,6},{5,7},{6,4},{7,5},{8,10},{9,11},{10,... | collective-permute-start | bytes 1179656 | tf_op jit(solution)/shard_map/ppermute | solution.py:661
  22.7 1.4 collective-permute-start.19
  33.1 35.0 %collective-permute-start.11 = (bf16[2,256,768]{2,1,0:T(8,128)(2,1)S(1)}, bf16[2,256,768]{2,1,0:T(8,128)(2,1)}, u32[]{:S(2)}, u32[]{:S(2)}) collective-permute-start(bf16[2,256,768]{2,1,0:T(8,128)(2,1)S(1)} %get-tuple-element.209.refs_0_), channel_id=1, source_target_pairs={{0,2},{1,3},{2,0},{3,1},{4,6},{5,7},{6,4},{7,5},{8,10},{9,11},{10,... | collective-permute-start | bytes 2359304 | tf_op jit(solution)/shard_map/ppermute | solution.py:661
  33.6 11.8 %collective-permute-start.8 = (bf16[4,24,588]{2,1,0:T(8,128)(2,1)S(1)}, bf16[4,24,588]{2,1,0:T(8,128)(2,1)S(1)}, u32[]{:S(2)}, u32[]{:S(2)}) collective-permute-start(bf16[4,24,588]{2,1,0:T(8,128)(2,1)S(1)} %get-tuple-element.416), channel_id=1, source_target_pairs={{0,16},{4,20},{8,24},{12,28},{16,0},{20,4},{24,8},{28,12},{1,17},{... | collective-permute-start | bytes 338696 | tf_op jit(solution)/shard_map/ppermute | solution.py:661
  36.4 31.6 %collective-permute-start.10 = (bf16[1,256,768]{2,1,0:T(8,128)(2,1)S(1)}, bf16[1,256,768]{2,1,0:T(8,128)(2,1)S(1)}, u32[]{:S(2)}, u32[]{:S(2)}) collective-permute-start(bf16[1,256,768]{2,1,0:T(8,128)(2,1)S(1)} %get-tuple-element.208), channel_id=1, source_target_pairs={{0,2},{1,3},{2,0},{3,1},{4,6},{5,7},{6,4},{7,5},{8,10},{9,11},{10,... | collective-permute-start | bytes 1179656 | tf_op jit(solution)/shard_map/ppermute | solution.py:661
  45.4 8.8 %collective-permute-start.9 = (bf16[2,4,24,588]{3,2,1,0:T(8,128)(2,1)S(1)}, bf16[2,4,24,588]{3,2,1,0:T(8,128)(2,1)S(1)}, u32[]{:S(2)}, u32[]{:S(2)}) collective-permute-start(bf16[2,4,24,588]{3,2,1,0:T(8,128)(2,1)S(1)} %maximum_select_fusion.3), channel_id=1, source_target_pairs={{0,8},{4,12},{8,0},{12,4},{16,24},{20,28},{24,16},{28,20},{1,9},{5... | collective-permute-start | bytes 677384 | tf_op jit(solution)/shard_map/ppermute | solution.py:661
  68.0 9.3 %copy-start.14 = (bf16[2,256,768]{2,1,0:T(8,128)(2,1)}, bf16[2,256,768]{2,1,0:T(8,128)(2,1)S(1)}, u32[]{:S(2)}) copy-start(bf16[2,256,768]{2,1,0:T(8,128)(2,1)S(1)} %pad_maximum_fusion.refs_2_) | copy-start | bytes 2359300
  68.1 8.9 %collective-permute-start.13 = (bf16[2,2,4,24,588]{4,3,2,1,0:T(8,128)(2,1)S(1)}, bf16[2,2,4,24,588]{4,3,2,1,0:T(8,128)(2,1)S(1)}, u32[]{:S(2)}, u32[]{:S(2)}) collective-permute-start(bf16[2,2,4,24,588]{4,3,2,1,0:T(8,128)(2,1)S(1)} %maximum_select_fusion.1), channel_id=1, source_target_pairs={{0,4},{4,0},{8,12},{12,8},{16,20},{20,16},{24,28},{28,24},{1,5},{5... | collective-permute-start | bytes 1354760 | tf_op jit(solution)/shard_map/ppermute | solution.py:661
  69.7 32.1 %collective-permute-start.14 = (bf16[2,256,768]{2,1,0:T(8,128)(2,1)S(1)}, bf16[2,256,768]{2,1,0:T(8,128)(2,1)}, u32[]{:S(2)}, u32[]{:S(2)}) collective-permute-start(bf16[2,256,768]{2,1,0:T(8,128)(2,1)S(1)} %get-tuple-element.209.refs_0_), channel_id=1, source_target_pairs={{0,1},{1,0},{2,3},{3,2},{4,5},{5,4},{6,7},{7,6},{8,9},{9,8},{10,11... | collective-permute-start | bytes 2359304 | tf_op jit(solution)/shard_map/ppermute | solution.py:661
  69.7 11.2 %collective-permute-start = (bf16[2,256,768]{2,1,0:T(8,128)(2,1)}, bf16[2,256,768]{2,1,0:T(8,128)(2,1)}, u32[]{:S(2)}, u32[]{:S(2)}) collective-permute-start(bf16[2,256,768]{2,1,0:T(8,128)(2,1)} %get-tuple-element.397.refs_0_), channel_id=1, source_target_pairs={{0,1},{1,0},{2,3},{3,2},{4,5},{5,4},{6,7},{7,6},{8,9},{9,8},{10,11... | collective-permute-start | bytes 2359304 | tf_op jit(solution)/shard_map/ppermute | solution.py:661
  70.9 31.0 %collective-permute-start.15 = (bf16[2,256,768]{2,1,0:T(8,128)(2,1)}, bf16[2,256,768]{2,1,0:T(8,128)(2,1)}, u32[]{:S(2)}, u32[]{:S(2)}) collective-permute-start(bf16[2,256,768]{2,1,0:T(8,128)(2,1)} %collective-permute-done.11.refs_2_), channel_id=1, source_target_pairs={{0,1},{1,0},{2,3},{3,2},{4,5},{5,4},{6,7},{7,6},{8,9},{9,8},{10,11... | collective-permute-start | bytes 2359304 | tf_op jit(solution)/shard_map/ppermute | solution.py:661
  70.9 10.0 %collective-permute-start.12 = (bf16[2,256,768]{2,1,0:T(8,128)(2,1)S(1)}, bf16[2,256,768]{2,1,0:T(8,128)(2,1)}, u32[]{:S(2)}, u32[]{:S(2)}) collective-permute-start(bf16[2,256,768]{2,1,0:T(8,128)(2,1)S(1)} %pad_maximum_fusion.refs_2_), channel_id=1, source_target_pairs={{0,1},{1,0},{2,3},{3,2},{4,5},{5,4},{6,7},{7,6},{8,9},{9,8},{10,11... | collective-permute-start | bytes 2359304 | tf_op jit(solution)/shard_map/ppermute | solution.py:661
  101.8 8.2 %copy-start.40 = (bf16[2,256,192]{2,1,0:T(8,128)(2,1)S(1)}, bf16[2,256,192]{2,1,0:T(8,128)(2,1)}, u32[]{:S(2)}) copy-start(bf16[2,256,192]{2,1,0:T(8,128)(2,1)} %get-tuple-element.223) | copy-start | bytes 589828
  109.1 15.6 %collective-permute-start.16 = (bf16[2,256,192]{2,1,0:T(8,128)(2,1)S(1)}, bf16[2,256,192]{2,1,0:T(8,128)(2,1)S(1)}, u32[]{:S(2)}, u32[]{:S(2)}) collective-permute-start(bf16[2,256,192]{2,1,0:T(8,128)(2,1)S(1)} %copy-done.42), channel_id=1, source_target_pairs={{0,1},{1,0},{2,3},{3,2},{4,5},{5,4},{6,7},{7,6},{8,9},{9,8},{10,11... | collective-permute-start | bytes 589832 | tf_op jit(solution)/shard_map/ppermute | solution.py:661
  109.2 15.5 %collective-permute-start.17 = (bf16[2,256,192]{2,1,0:T(8,128)(2,1)S(1)}, bf16[2,256,192]{2,1,0:T(8,128)(2,1)S(1)}, u32[]{:S(2)}, u32[]{:S(2)}) collective-permute-start(bf16[2,256,192]{2,1,0:T(8,128)(2,1)S(1)} %copy-done.41), channel_id=1, source_target_pairs={{0,2},{1,3},{2,0},{3,1},{4,6},{5,7},{6,4},{7,5},{8,10},{9,11},{10,... | collective-permute-start | bytes 589832 | tf_op jit(solution)/shard_map/ppermute | solution.py:661
  110.0 14.7 %collective-permute-start.18 = (bf16[2,256,192]{2,1,0:T(8,128)(2,1)S(1)}, bf16[2,256,192]{2,1,0:T(8,128)(2,1)S(1)}, u32[]{:S(2)}, u32[]{:S(2)}) collective-permute-start(bf16[2,256,192]{2,1,0:T(8,128)(2,1)S(1)} %copy-done.40), channel_id=1, source_target_pairs={{0,3},{1,2},{2,1},{3,0},{4,7},{5,6},{6,5},{7,4},{8,11},{9,10},{10,... | collective-permute-start | bytes 589832 | tf_op jit(solution)/shard_map/ppermute | solution.py:661
  111.0 14.8 %copy-start.20 = (bf16[2,256,192]{2,1,0:T(8,128)(2,1)S(1)}, bf16[2,256,192]{2,1,0:T(8,128)(2,1)}, u32[]{:S(2)}) copy-start(bf16[2,256,192]{2,1,0:T(8,128)(2,1)} %get-tuple-element.229) | copy-start | bytes 589828
  124.7 15.0 %collective-permute-start.23 = (bf16[768,3456]{1,0:T(8,128)(2,1)}, bf16[768,3456]{1,0:T(8,128)(2,1)}, u32[]{:S(2)}, u32[]{:S(2)}) collective-permute-start(bf16[768,3456]{1,0:T(8,128)(2,1)} %all-gather.2.cloned.1.call-done.refs_4_), channel_id=1, source_target_pairs={{0,1},{1,0},{2,3},{3,2},{4,5},{5,4},{6,7},{7,6},{8,9},{9,8},{10,11... | collective-permute-start | bytes 15925256 | tf_op jit(solution)/shard_map/ppermute | solution.py:661
  125.2 8.5 %collective-permute-start.22 = (bf16[2,256,192]{2,1,0:T(8,128)(2,1)}, bf16[2,256,192]{2,1,0:T(8,128)(2,1)S(1)}, u32[]{:S(2)}, u32[]{:S(2)}) collective-permute-start(bf16[2,256,192]{2,1,0:T(8,128)(2,1)} %get-tuple-element.243), channel_id=1, source_target_pairs={{0,3},{1,2},{2,1},{3,0},{4,7},{5,6},{6,5},{7,4},{8,11},{9,10},{10,... | collective-permute-start | bytes 589832 | tf_op jit(solution)/shard_map/ppermute | solution.py:661
  125.8 13.8 %collective-permute-start.21 = (bf16[2,256,192]{2,1,0:T(8,128)(2,1)S(1)}, bf16[2,256,192]{2,1,0:T(8,128)(2,1)S(1)}, u32[]{:S(2)}, u32[]{:S(2)}) collective-permute-start(bf16[2,256,192]{2,1,0:T(8,128)(2,1)S(1)} %copy-done.39), channel_id=1, source_target_pairs={{0,2},{1,3},{2,0},{3,1},{4,6},{5,7},{6,4},{7,5},{8,10},{9,11},{10,... | collective-permute-start | bytes 589832 | tf_op jit(solution)/shard_map/ppermute | solution.py:661
  127.2 12.6 %collective-permute-start.20 = (bf16[2,256,192]{2,1,0:T(8,128)(2,1)S(1)}, bf16[2,256,192]{2,1,0:T(8,128)(2,1)S(1)}, u32[]{:S(2)}, u32[]{:S(2)}) collective-permute-start(bf16[2,256,192]{2,1,0:T(8,128)(2,1)S(1)} %copy-done.38), channel_id=1, source_target_pairs={{0,1},{1,0},{2,3},{3,2},{4,5},{5,4},{6,7},{7,6},{8,9},{9,8},{10,11... | collective-permute-start | bytes 589832 | tf_op jit(solution)/shard_map/ppermute | solution.py:661
  127.3 12.5 %copy-start.24 = (bf16[4,256,192]{2,1,0:T(8,128)(2,1)}, bf16[4,256,192]{2,1,0:T(8,128)(2,1)S(1)}, u32[]{:S(2)}) copy-start(bf16[4,256,192]{2,1,0:T(8,128)(2,1)S(1)} %constant_dynamic-update-slice_fusion.4.refs_0_) | copy-start | bytes 1179652
  180.3 2.3 collective-permute-start.24
  180.3 23.4 %collective-permute-start.25 = (bf16[4,256,192]{2,1,0:T(8,128)(2,1)}, bf16[4,256,192]{2,1,0:T(8,128)(2,1)S(1)}, u32[]{:S(2)}, u32[]{:S(2)}) collective-permute-start(bf16[4,256,192]{2,1,0:T(8,128)(2,1)} %get-tuple-element.264), channel_id=1, source_target_pairs={{0,2},{1,3},{2,0},{3,1},{4,6},{5,7},{6,4},{7,5},{8,10},{9,11},{10,... | collective-permute-start | bytes 1179656 | tf_op jit(solution)/shard_map/ppermute | solution.py:661
  181.2 24.5 %collective-permute-start.26 = (bf16[4,256,192]{2,1,0:T(8,128)(2,1)}, bf16[4,256,192]{2,1,0:T(8,128)(2,1)S(1)}, u32[]{:S(2)}, u32[]{:S(2)}) collective-permute-start(bf16[4,256,192]{2,1,0:T(8,128)(2,1)} %get-tuple-element.265), channel_id=1, source_target_pairs={{0,3},{1,2},{2,1},{3,0},{4,7},{5,6},{6,5},{7,4},{8,11},{9,10},{10,... | collective-permute-start | bytes 1179656 | tf_op jit(solution)/shard_map/ppermute | solution.py:661
  208.7 6.0 %collective-permute-start.27 = (bf16[3,2,2,2,2,24,768]{6,5,0,4,1,2,3:T(8,128)(2,1)}, bf16[3,2,2,2,2,24,768]{6,5,0,4,1,2,3:T(8,128)(2,1)}, u32[]{:S(2)}, u32[]{:S(2)}) collective-permute-start(bf16[3,2,2,2,2,24,768]{6,5,0,4,1,2,3:T(8,128)(2,1)} %copy.110), channel_id=1, source_target_pairs={{0,1},{1,0},{2,3},{3,2},{4,5},{5,4},{6,7},{7,6},{8,9},{9,8},{10,11... | collective-permute-start | bytes 5308424 | tf_op jit(solution)/shard_map/ppermute | solution.py:661
  210.3 4.9 %collective-permute-start.28 = (bf16[3,2,2,2,2,24,768]{6,5,0,1,2,3,4:T(8,128)(2,1)}, bf16[3,2,2,2,2,24,768]{6,5,0,1,2,3,4:T(8,128)(2,1)}, u32[]{:S(2)}, u32[]{:S(2)}) collective-permute-start(bf16[3,2,2,2,2,24,768]{6,5,0,1,2,3,4:T(8,128)(2,1)} %copy.111), channel_id=1, source_target_pairs={{0,1},{1,0},{2,3},{3,2},{4,5},{5,4},{6,7},{7,6},{8,9},{9,8},{10,11... | collective-permute-start | bytes 5308424 | tf_op jit(solution)/shard_map/ppermute | solution.py:661
  211.9 5.8 %collective-permute-start.29 = (bf16[3,2,2,2,2,24,768]{6,5,0,1,3,4,2:T(8,128)(2,1)}, bf16[3,2,2,2,2,24,768]{6,5,0,1,3,4,2:T(8,128)(2,1)}, u32[]{:S(2)}, u32[]{:S(2)}) collective-permute-start(bf16[3,2,2,2,2,24,768]{6,5,0,1,3,4,2:T(8,128)(2,1)} %copy.112), channel_id=1, source_target_pairs={{0,1},{1,0},{2,3},{3,2},{4,5},{5,4},{6,7},{7,6},{8,9},{9,8},{10,11... | collective-permute-start | bytes 5308424 | tf_op jit(solution)/shard_map/ppermute | solution.py:661
  226.8 22.8 %collective-permute-start.30 = (bf16[3,2,2,2,24,768]{5,4,0,3,1,2:T(8,128)(2,1)S(1)}, bf16[3,2,2,2,24,768]{5,4,0,3,1,2:T(8,128)(2,1)}, u32[]{:S(2)}, u32[]{:S(2)}) collective-permute-start(bf16[3,2,2,2,24,768]{5,4,0,3,1,2:T(8,128)(2,1)S(1)} %fusion.12), channel_id=1, source_target_pairs={{0,4},{4,0},{8,12},{12,8},{16,20},{20,16},{24,28},{28,24},{1,5},{5... | collective-permute-start | bytes 2654216 | tf_op jit(solution)/shard_map/ppermute | solution.py:661
  228.4 21.7 %collective-permute-start.31 = (bf16[3,2,2,2,24,768]{5,4,0,1,2,3:T(8,128)(2,1)S(1)}, bf16[3,2,2,2,24,768]{5,4,0,1,2,3:T(8,128)(2,1)}, u32[]{:S(2)}, u32[]{:S(2)}) collective-permute-start(bf16[3,2,2,2,24,768]{5,4,0,1,2,3:T(8,128)(2,1)S(1)} %fusion.13), channel_id=1, source_target_pairs={{0,2},{1,3},{2,0},{3,1},{4,6},{5,7},{6,4},{7,5},{8,10},{9,11},{10,... | collective-permute-start | bytes 2654216 | tf_op jit(solution)/shard_map/ppermute | solution.py:661
  228.9 21.4 %collective-permute-start.32 = (bf16[3,2,2,2,24,768]{5,4,0,1,2,3:T(8,128)(2,1)S(1)}, bf16[3,2,2,2,24,768]{5,4,0,1,2,3:T(8,128)(2,1)}, u32[]{:S(2)}, u32[]{:S(2)}) collective-permute-start(bf16[3,2,2,2,24,768]{5,4,0,1,2,3:T(8,128)(2,1)S(1)} %fusion.14), channel_id=1, source_target_pairs={{0,8},{4,12},{8,0},{12,4},{16,24},{20,28},{24,16},{28,20},{1,9},{5... | collective-permute-start | bytes 2654216 | tf_op jit(solution)/shard_map/ppermute | solution.py:661
  254.7 19.2 %collective-permute-start.34 = (bf16[3,2,2,24,768]{4,3,0,2,1:T(8,128)(2,1)S(1)}, bf16[3,2,2,24,768]{4,3,0,2,1:T(8,128)(2,1)S(1)}, u32[]{:S(2)}, u32[]{:S(2)}) collective-permute-start(bf16[3,2,2,24,768]{4,3,0,2,1:T(8,128)(2,1)S(1)} %fusion.18), channel_id=1, source_target_pairs={{0,8},{4,12},{8,0},{12,4},{16,24},{20,28},{24,16},{28,20},{1,9},{5... | collective-permute-start | bytes 1327112 | tf_op jit(solution)/shard_map/ppermute | solution.py:661
  256.5 17.4 %collective-permute-start.35 = (bf16[3,2,2,24,768]{4,3,0,1,2:T(8,128)(2,1)S(1)}, bf16[3,2,2,24,768]{4,3,0,1,2:T(8,128)(2,1)S(1)}, u32[]{:S(2)}, u32[]{:S(2)}) collective-permute-start(bf16[3,2,2,24,768]{4,3,0,1,2:T(8,128)(2,1)S(1)} %fusion.19), channel_id=1, source_target_pairs={{0,4},{4,0},{8,12},{12,8},{16,20},{20,16},{24,28},{28,24},{1,5},{5... | collective-permute-start | bytes 1327112 | tf_op jit(solution)/shard_map/ppermute | solution.py:661
  256.9 17.0 %collective-permute-start.36 = (bf16[3,2,2,24,768]{4,3,0,1,2:T(8,128)(2,1)S(1)}, bf16[3,2,2,24,768]{4,3,0,1,2:T(8,128)(2,1)S(1)}, u32[]{:S(2)}, u32[]{:S(2)}) collective-permute-start(bf16[3,2,2,24,768]{4,3,0,1,2:T(8,128)(2,1)S(1)} %fusion.20), channel_id=1, source_target_pairs={{0,2},{1,3},{2,0},{3,1},{4,6},{5,7},{6,4},{7,5},{8,10},{9,11},{10,... | collective-permute-start | bytes 1327112 | tf_op jit(solution)/shard_map/ppermute | solution.py:661
  267.3 7.2 %collective-permute-start.33 = (bf16[2,2,256,768]{3,2,1,0:T(8,128)(2,1)}, bf16[2,2,256,768]{3,2,1,0:T(8,128)(2,1)S(1)}, u32[]{:S(2)}, u32[]{:S(2)}) collective-permute-start(bf16[2,2,256,768]{3,2,1,0:T(8,128)(2,1)} %get-tuple-element.292), channel_id=1, source_target_pairs={{0,1},{1,0},{2,3},{3,2},{4,5},{5,4},{6,7},{7,6},{8,9},{9,8},{10,11... | collective-permute-start | bytes 4718600 | tf_op jit(solution)/shard_map/ppermute | solution.py:661
  276.2 24.3 %collective-permute-start.37 = (bf16[2,256,768]{2,1,0:T(8,128)(2,1)S(1)}, bf16[2,256,768]{2,1,0:T(8,128)(2,1)S(1)}, u32[]{:S(2)}, u32[]{:S(2)}) collective-permute-start(bf16[2,256,768]{2,1,0:T(8,128)(2,1)S(1)} %fusion.15), channel_id=1, source_target_pairs={{0,2},{1,3},{2,0},{3,1},{4,6},{5,7},{6,4},{7,5},{8,10},{9,11},{10,... | collective-permute-start | bytes 2359304 | tf_op jit(solution)/shard_map/ppermute | solution.py:661
  276.8 23.7 %collective-permute-start.38 = (bf16[3,2,24,768]{3,2,0,1:T(8,128)(2,1)S(1)}, bf16[3,2,24,768]{3,2,0,1:T(8,128)(2,1)S(1)}, u32[]{:S(2)}, u32[]{:S(2)}) collective-permute-start(bf16[3,2,24,768]{3,2,0,1:T(8,128)(2,1)S(1)} %fusion.21), channel_id=1, source_target_pairs={{0,16},{4,20},{8,24},{12,28},{16,0},{20,4},{24,8},{28,12},{1,17},{... | collective-permute-start | bytes 663560 | tf_op jit(solution)/shard_map/ppermute | solution.py:661
  279.6 20.9 %collective-permute-start.39 = (bf16[3,2,24,768]{3,2,0,1:T(8,128)(2,1)S(1)}, bf16[3,2,24,768]{3,2,0,1:T(8,128)(2,1)S(1)}, u32[]{:S(2)}, u32[]{:S(2)}) collective-permute-start(bf16[3,2,24,768]{3,2,0,1:T(8,128)(2,1)S(1)} %fusion.22), channel_id=1, source_target_pairs={{0,8},{4,12},{8,0},{12,4},{16,24},{20,28},{24,16},{28,20},{1,9},{5... | collective-permute-start | bytes 663560 | tf_op jit(solution)/shard_map/ppermute | solution.py:661
  279.9 20.6 %collective-permute-start.40 = (bf16[3,2,24,768]{3,2,0,1:T(8,128)(2,1)S(1)}, bf16[3,2,24,768]{3,2,0,1:T(8,128)(2,1)S(1)}, u32[]{:S(2)}, u32[]{:S(2)}) collective-permute-start(bf16[3,2,24,768]{3,2,0,1:T(8,128)(2,1)S(1)} %fusion.23), channel_id=1, source_target_pairs={{0,4},{4,0},{8,12},{12,8},{16,20},{20,16},{24,28},{28,24},{1,5},{5... | collective-permute-start | bytes 663560 | tf_op jit(solution)/shard_map/ppermute | solution.py:661
  300.5 8.8 %copy-start.16 = (bf16[2,256,768]{2,1,0:T(8,128)(2,1)}, bf16[2,256,768]{2,1,0:T(8,128)(2,1)S(1)}, u32[]{:S(2)}) copy-start(bf16[2,256,768]{2,1,0:T(8,128)(2,1)S(1)} %collective-permute-done.37) | copy-start | bytes 2359300
  309.3 9.0 %copy-start.13 = (f32[768,588]{1,0:T(8,128)S(1)}, f32[768,588]{1,0:T(8,128)}, u32[]{:S(2)}) copy-start(f32[768,588]{1,0:T(8,128)} %get-tuple-element.330) | copy-start | bytes 5419012
  318.3 13.8 %collective-permute-start.42 = (bf16[2,2,256,768]{3,2,1,0:T(8,128)(2,1)}, bf16[2,2,256,768]{3,2,1,0:T(8,128)(2,1)S(1)}, u32[]{:S(2)}, u32[]{:S(2)}) collective-permute-start(bf16[2,2,256,768]{3,2,1,0:T(8,128)(2,1)} %get-tuple-element.332), channel_id=1, source_target_pairs={{0,1},{1,0},{2,3},{3,2},{4,5},{5,4},{6,7},{7,6},{8,9},{9,8},{10,11... | collective-permute-start | bytes 4718600 | tf_op jit(solution)/shard_map/ppermute | solution.py:661
  318.4 13.7 %collective-permute-start.41 = (bf16[2,2,4,24,588]{4,3,2,1,0:T(8,128)(2,1)S(1)}, bf16[2,2,4,24,588]{4,3,2,1,0:T(8,128)(2,1)S(1)}, u32[]{:S(2)}, u32[]{:S(2)}) collective-permute-start(bf16[2,2,4,24,588]{4,3,2,1,0:T(8,128)(2,1)S(1)} %fusion.17), channel_id=1, source_target_pairs={{0,4},{4,0},{8,12},{12,8},{16,20},{20,16},{24,28},{28,24},{1,5},{5... | collective-permute-start | bytes 1354760 | tf_op jit(solution)/shard_map/ppermute | solution.py:661
  319.0 13.1 %copy-start.9 = (bf16[2,2,256,768]{3,2,1,0:T(8,128)(2,1)S(1)}, bf16[2,2,256,768]{3,2,1,0:T(8,128)(2,1)}, u32[]{:S(2)}) copy-start(bf16[2,2,256,768]{3,2,1,0:T(8,128)(2,1)} %get-tuple-element.334) | copy-start | bytes 4718596
  321.3 15.7 %collective-permute-start.47 = (bf16[3,24,768]{2,1,0:T(8,128)(2,1)S(1)}, bf16[3,24,768]{2,1,0:T(8,128)(2,1)S(1)}, u32[]{:S(2)}, u32[]{:S(2)}) collective-permute-start(bf16[3,24,768]{2,1,0:T(8,128)(2,1)S(1)} %fusion.27), channel_id=1, source_target_pairs={{0,2},{1,3},{2,0},{3,1},{4,6},{5,7},{6,4},{7,5},{8,10},{9,11},{10,... | collective-permute-start | bytes 331784 | tf_op jit(solution)/shard_map/ppermute | solution.py:661
  322.8 14.4 %collective-permute-start.48 = (bf16[3,24,768]{2,1,0:T(8,128)(2,1)S(1)}, bf16[3,24,768]{2,1,0:T(8,128)(2,1)S(1)}, u32[]{:S(2)}, u32[]{:S(2)}) collective-permute-start(bf16[3,24,768]{2,1,0:T(8,128)(2,1)S(1)} %fusion.28), channel_id=1, source_target_pairs={{0,16},{4,20},{8,24},{12,28},{16,0},{20,4},{24,8},{28,12},{1,17},{... | collective-permute-start | bytes 331784 | tf_op jit(solution)/shard_map/ppermute | solution.py:661
  322.9 16.8 %collective-permute-start.49 = (bf16[3,24,768]{2,1,0:T(8,128)(2,1)S(1)}, bf16[3,24,768]{2,1,0:T(8,128)(2,1)}, u32[]{:S(2)}, u32[]{:S(2)}) collective-permute-start(bf16[3,24,768]{2,1,0:T(8,128)(2,1)S(1)} %fusion.29), channel_id=1, source_target_pairs={{0,16},{4,20},{8,24},{12,28},{16,0},{20,4},{24,8},{28,12},{1,17},{... | collective-permute-start | bytes 331784 | tf_op jit(solution)/shard_map/ppermute | solution.py:661
  333.4 19.5 %collective-permute-start.46 = (bf16[2,256,768]{2,1,0:T(8,128)(2,1)}, bf16[2,256,768]{2,1,0:T(8,128)(2,1)}, u32[]{:S(2)}, u32[]{:S(2)}) collective-permute-start(bf16[2,256,768]{2,1,0:T(8,128)(2,1)} %fusion.16), channel_id=1, source_target_pairs={{0,2},{1,3},{2,0},{3,1},{4,6},{5,7},{6,4},{7,5},{8,10},{9,11},{10,... | collective-permute-start | bytes 2359304 | tf_op jit(solution)/shard_map/ppermute | solution.py:661
  335.3 8.2 %collective-permute-start.43 = (bf16[4,24,588]{2,1,0:T(8,128)(2,1)S(1)}, bf16[4,24,588]{2,1,0:T(8,128)(2,1)S(1)}, u32[]{:S(2)}, u32[]{:S(2)}) collective-permute-start(bf16[4,24,588]{2,1,0:T(8,128)(2,1)S(1)} %get-tuple-element.400), channel_id=1, source_target_pairs={{0,8},{4,12},{8,0},{12,4},{16,24},{20,28},{24,16},{28,20},{1,9},{5... | collective-permute-start | bytes 338696 | tf_op jit(solution)/shard_map/ppermute | solution.py:661
  337.0 10.9 %collective-permute-start.44 = (bf16[4,24,588]{2,1,0:T(8,128)(2,1)S(1)}, bf16[4,24,588]{2,1,0:T(8,128)(2,1)S(1)}, u32[]{:S(2)}, u32[]{:S(2)}) collective-permute-start(bf16[4,24,588]{2,1,0:T(8,128)(2,1)S(1)} %get-tuple-element.399), channel_id=1, source_target_pairs={{0,16},{4,20},{8,24},{12,28},{16,0},{20,4},{24,8},{28,12},{1,17},{... | collective-permute-start | bytes 338696 | tf_op jit(solution)/shard_map/ppermute | solution.py:661
  337.2 10.7 %collective-permute-start.45 = (bf16[4,24,588]{2,1,0:T(8,128)(2,1)S(1)}, bf16[4,24,588]{2,1,0:T(8,128)(2,1)S(1)}, u32[]{:S(2)}, u32[]{:S(2)}) collective-permute-start(bf16[4,24,588]{2,1,0:T(8,128)(2,1)S(1)} %get-tuple-element.398), channel_id=1, source_target_pairs={{0,24},{4,28},{8,16},{12,20},{16,8},{20,12},{24,0},{28,4},{1,25},{... | collective-permute-start | bytes 338696 | tf_op jit(solution)/shard_map/ppermute | solution.py:661
  353.0 8.1 %collective-permute-start.50 = (bf16[24,588]{1,0:T(8,128)(2,1)S(1)}, bf16[24,588]{1,0:T(8,128)(2,1)S(1)}, u32[]{:S(2)}, u32[]{:S(2)}) collective-permute-start(bf16[24,588]{1,0:T(8,128)(2,1)S(1)} %get-tuple-element.367), channel_id=1, source_target_pairs={{0,1},{1,0},{2,3},{3,2},{4,5},{5,4},{6,7},{7,6},{8,9},{9,8},{10,11... | collective-permute-start | bytes 84680 | tf_op jit(solution)/shard_map/ppermute | solution.py:661
  353.1 8.0 %collective-permute-start.51 = (bf16[24,588]{1,0:T(8,128)(2,1)S(1)}, bf16[24,588]{1,0:T(8,128)(2,1)S(1)}, u32[]{:S(2)}, u32[]{:S(2)}) collective-permute-start(bf16[24,588]{1,0:T(8,128)(2,1)S(1)} %get-tuple-element.368), channel_id=1, source_target_pairs={{0,2},{1,3},{2,0},{3,1},{4,6},{5,7},{6,4},{7,5},{8,10},{9,11},{10,... | collective-permute-start | bytes 84680 | tf_op jit(solution)/shard_map/ppermute | solution.py:661
  354.6 6.5 %collective-permute-start.52 = (bf16[24,588]{1,0:T(8,128)(2,1)S(1)}, bf16[24,588]{1,0:T(8,128)(2,1)S(1)}, u32[]{:S(2)}, u32[]{:S(2)}) collective-permute-start(bf16[24,588]{1,0:T(8,128)(2,1)S(1)} %get-tuple-element.369), channel_id=1, source_target_pairs={{0,3},{1,2},{2,1},{3,0},{4,7},{5,6},{6,5},{7,4},{8,11},{9,10},{10,... | collective-permute-start | bytes 84680 | tf_op jit(solution)/shard_map/ppermute | solution.py:661
  (33 other events, 93.3 us)
Sparse Core Ops, SparseCore 0:
  25.0 94.2 all-gather.1
